TPU v7x, 32 devices: a whole 2x2x4 slice. The times are simulated.
32 devices in a mesh: grp: 2 (over y), ex: 4 (over z), feat: 4 (over x, core).
Axes of the slice: x: 2, y: 2, z: 4, core: 2. Of those that a mesh axis runs over, the one named last changes fastest.
Arguments:
- slab_grads: bfloat16 [4096, 4096], P(('grp', 'ex'), 'feat'), parts along dimension 0, may hold values from -6 to 6
- query_grads: bfloat16 [4096, 4096], P(('grp', 'feat'), 'ex'), parts along dimension 0, may hold values from -0.09375 to 0.09375
- example_weights: float32 [4096], P(('grp', 'ex')), parts along dimension 0, may hold values from 0.2 to 2
- tile_owner: int32 [8, 168, 2], P(('grp', 'feat')), parts along dimension 0, may hold values from -1 to 31, as said below
Outputs:
- gram: float32 [8, 168, 128, 128], P(('grp', 'feat'), 'ex'), parts along dimension 0
- scores: float32 [4096, 2048], P(('grp', 'feat'), 'ex'), parts along dimension 0
There are 2 independent parts, one for each index of `grp`. A program takes and returns all parts, laid end to end along the dimension named above; each array names one. Nothing has to cross between parts.
Inputs may be any that keep to these rules, and one draw needn't show every extreme that they name: `tile_owner`: each slot holds a pair (a, b) with a <= b of the 32 feature blocks, or (-1, -1) when empty; every such pair stands in exactly one slot; one column has min(168, 528) live slots.
All inputs are finite; a program needn't handle non-finite values.
Results may differ from a plain program's by a relative error of at most 0.008.
Values may be sent and summed in bfloat16 or wider, within the bound.
No kernel may reach another device: no remote copies, remote signals or barrier semaphores. Data moves between devices by JAX's collectives and lax.ppermute only.
A program may use at most 64 MiB of HBM per device.

v0:
```python
import math

import jax
import jax.numpy as jnp
from jax import lax
from jax.sharding import PartitionSpec as P

B = 128


def select_blocks(blocks3, indices):
    block_ids = lax.broadcasted_iota(jnp.int32, (indices.shape[0], blocks3.shape[1]), 1)
    onehot = (indices[:, None] == block_ids).astype(jnp.bfloat16)
    chosen = jnp.einsum("tnb,gn->tgb", blocks3, onehot, preferred_element_type=jnp.float32)
    return chosen.astype(jnp.bfloat16)


def tile_terms(blocks3, subset):
    group_size = math.gcd(subset.shape[0], 8)
    groups = subset.reshape(-1, group_size, 2)

    def group_tiles(group):
        left_block = select_blocks(blocks3, group[:, 0])
        right_block = select_blocks(blocks3, group[:, 1])
        product = jnp.einsum(
            "tsi,tsj->sij", left_block, right_block, preferred_element_type=jnp.float32
        )
        return jnp.where((group[:, 0] >= 0)[:, None, None], product, jnp.float32(0.0))

    return lax.map(group_tiles, groups).reshape(-1, blocks3.shape[2], blocks3.shape[2])


def local(slab_grads, query_grads, example_weights, tile_owner):
    tile_table = tile_owner[0]
    tok_count = slab_grads.shape[0]
    slab_full = lax.all_gather(slab_grads, "feat", axis=1, tiled=True)
    blocks3 = slab_full.reshape(tok_count, slab_full.shape[1] // B, B)
    row_total = tok_count * lax.axis_size("ex")
    summed = lax.psum_scatter(
        tile_terms(blocks3, tile_table).astype(jnp.bfloat16), "ex", scatter_dimension=0, tiled=True
    ).astype(jnp.float32)
    gram = (summed / row_total)[None]
    summed = lax.dot_general(
        lax.all_gather(query_grads, "ex", axis=1, tiled=True),
        slab_full,
        (((1,), (1,)), ((), ())),
        preferred_element_type=jnp.float32,
    )
    scores = summed * example_weights[None, :]
    return (gram, scores)


def solution(mesh):
    placed = (
        P(("grp", "ex"), "feat"),
        P(("grp", "feat"), "ex"),
        P(("grp", "ex")),
        P(("grp", "feat"), None, None),
    )
    return jax.shard_map(
        local,
        mesh=mesh,
        in_specs=placed,
        out_specs=(P(("grp", "feat"), "ex", None, None), P(("grp", "feat"), "ex")),
        check_vma=False,
    )
```

profile of v0, /device:TPU:9, one launch (start us, length us, event | category | flops | bytes accessed | tf_op | source)
XLA Modules:
  0.0 286.0 jit_solution(8127579421456320305)
XLA Ops:
  9.5 36.2 %all-gather.3.cloned.1.call-done = bf16[512,4096]{1,0:T(8,128)(2,1)} async-done(((bf16[512,1024]{1,0:T(8,128)(2,1)}), bf16[512,4096]{1,0:T(8,128)(2,1)}) %all-gather.3.cloned.1.call-update) | async-done | bytes 4194320 | tf_op jit(solution)/shard_map/all_gather | solution.py:36
  45.6 5.4 %copy.10 = bf16[64,8,32,128]{3,2,1,0:T(8,128)(2,1)} copy(bf16[64,8,32,128]{3,1,2,0:T(8,128)(2,1)} %bitcast.58) | data formatting | bytes 8388608
  51.1 127.0 %while.10 = (s32[]{:T(128)}, bf16[21,8,128,128]{3,2,1,0:T(8,128)(2,1)}, s32[21,8,2]{1,0,2:T(8,128)S(1)}, bf16[512,32,128]{2,1,0:T(8,128)(2,1)}, s32[]{:T(128)}) while((s32[]{:T(128)}, bf16[21,8,128,128]{3,2,1,0:T(8,128)(2,1)}, s32[21,8,2]{1,0,2:T(8,128)S(1)}, bf16[512,32,128]{2,1,0:T(8,128)(2,1)}, s32[]{:T(128)}) %tuple.35), condition=%wide.region_1.2_spmd, body=%wide.region_0.1_spmd.sunk | while | flops 201458176 | bytes 31982040 | solution.py:30
  51.1 3.1 %fusion.33 = bf16[8,512,128]{2,0,1:T(8,128)(2,1)S(1)} fusion(bf16[512,32,128]{2,1,0:T(8,128)(2,1)} %get-tuple-element.81, s32[8]{0:T(128)S(1)} %get-tuple-element.66), kind=kOutput, calls=%fused_computation.12.clone.1 | convolution fusion | flops 33554688 | bytes 5242912 | tf_op jit(solution)/shard_map/while/body/eval_jaxpr/tnb,gn->tgb/dot_general | solution.py:14
  56.1 1.2 fusion.35
  57.3 3.1 %fusion.33 = bf16[8,512,128]{2,0,1:T(8,128)(2,1)S(1)} fusion(bf16[512,32,128]{2,1,0:T(8,128)(2,1)} %get-tuple-element.81, s32[8]{0:T(128)S(1)} %get-tuple-element.66), kind=kOutput, calls=%fused_computation.12.clone.1 | convolution fusion | flops 33554688 | bytes 5242912 | tf_op jit(solution)/shard_map/while/body/eval_jaxpr/tnb,gn->tgb/dot_general | solution.py:14
  62.3 1.2 fusion.35
  63.5 3.1 %fusion.33 = bf16[8,512,128]{2,0,1:T(8,128)(2,1)S(1)} fusion(bf16[512,32,128]{2,1,0:T(8,128)(2,1)} %get-tuple-element.81, s32[8]{0:T(128)S(1)} %get-tuple-element.66), kind=kOutput, calls=%fused_computation.12.clone.1 | convolution fusion | flops 33554688 | bytes 5242912 | tf_op jit(solution)/shard_map/while/body/eval_jaxpr/tnb,gn->tgb/dot_general | solution.py:14
  68.3 1.2 fusion.35
  69.5 3.1 %fusion.33 = bf16[8,512,128]{2,0,1:T(8,128)(2,1)S(1)} fusion(bf16[512,32,128]{2,1,0:T(8,128)(2,1)} %get-tuple-element.81, s32[8]{0:T(128)S(1)} %get-tuple-element.66), kind=kOutput, calls=%fused_computation.12.clone.1 | convolution fusion | flops 33554688 | bytes 5242912 | tf_op jit(solution)/shard_map/while/body/eval_jaxpr/tnb,gn->tgb/dot_general | solution.py:14
  74.3 1.2 fusion.35
  75.5 3.1 %fusion.33 = bf16[8,512,128]{2,0,1:T(8,128)(2,1)S(1)} fusion(bf16[512,32,128]{2,1,0:T(8,128)(2,1)} %get-tuple-element.81, s32[8]{0:T(128)S(1)} %get-tuple-element.66), kind=kOutput, calls=%fused_computation.12.clone.1 | convolution fusion | flops 33554688 | bytes 5242912 | tf_op jit(solution)/shard_map/while/body/eval_jaxpr/tnb,gn->tgb/dot_general | solution.py:14
  80.4 1.2 fusion.35
  81.6 3.1 %fusion.33 = bf16[8,512,128]{2,0,1:T(8,128)(2,1)S(1)} fusion(bf16[512,32,128]{2,1,0:T(8,128)(2,1)} %get-tuple-element.81, s32[8]{0:T(128)S(1)} %get-tuple-element.66), kind=kOutput, calls=%fused_computation.12.clone.1 | convolution fusion | flops 33554688 | bytes 5242912 | tf_op jit(solution)/shard_map/while/body/eval_jaxpr/tnb,gn->tgb/dot_general | solution.py:14
  86.4 1.2 fusion.35
  87.6 3.1 %fusion.33 = bf16[8,512,128]{2,0,1:T(8,128)(2,1)S(1)} fusion(bf16[512,32,128]{2,1,0:T(8,128)(2,1)} %get-tuple-element.81, s32[8]{0:T(128)S(1)} %get-tuple-element.66), kind=kOutput, calls=%fused_computation.12.clone.1 | convolution fusion | flops 33554688 | bytes 5242912 | tf_op jit(solution)/shard_map/while/body/eval_jaxpr/tnb,gn->tgb/dot_general | solution.py:14
  92.4 1.2 fusion.35
  93.6 3.1 %fusion.33 = bf16[8,512,128]{2,0,1:T(8,128)(2,1)S(1)} fusion(bf16[512,32,128]{2,1,0:T(8,128)(2,1)} %get-tuple-element.81, s32[8]{0:T(128)S(1)} %get-tuple-element.66), kind=kOutput, calls=%fused_computation.12.clone.1 | convolution fusion | flops 33554688 | bytes 5242912 | tf_op jit(solution)/shard_map/while/body/eval_jaxpr/tnb,gn->tgb/dot_general | solution.py:14
  98.5 1.2 fusion.35
  99.7 3.1 %fusion.33 = bf16[8,512,128]{2,0,1:T(8,128)(2,1)S(1)} fusion(bf16[512,32,128]{2,1,0:T(8,128)(2,1)} %get-tuple-element.81, s32[8]{0:T(128)S(1)} %get-tuple-element.66), kind=kOutput, calls=%fused_computation.12.clone.1 | convolution fusion | flops 33554688 | bytes 5242912 | tf_op jit(solution)/shard_map/while/body/eval_jaxpr/tnb,gn->tgb/dot_general | solution.py:14
  104.5 1.2 fusion.35
  105.7 3.1 %fusion.33 = bf16[8,512,128]{2,0,1:T(8,128)(2,1)S(1)} fusion(bf16[512,32,128]{2,1,0:T(8,128)(2,1)} %get-tuple-element.81, s32[8]{0:T(128)S(1)} %get-tuple-element.66), kind=kOutput, calls=%fused_computation.12.clone.1 | convolution fusion | flops 33554688 | bytes 5242912 | tf_op jit(solution)/shard_map/while/body/eval_jaxpr/tnb,gn->tgb/dot_general | solution.py:14
  110.5 1.2 fusion.35
  111.7 3.1 %fusion.33 = bf16[8,512,128]{2,0,1:T(8,128)(2,1)S(1)} fusion(bf16[512,32,128]{2,1,0:T(8,128)(2,1)} %get-tuple-element.81, s32[8]{0:T(128)S(1)} %get-tuple-element.66), kind=kOutput, calls=%fused_computation.12.clone.1 | convolution fusion | flops 33554688 | bytes 5242912 | tf_op jit(solution)/shard_map/while/body/eval_jaxpr/tnb,gn->tgb/dot_general | solution.py:14
  116.6 1.2 fusion.35
  117.8 3.1 %fusion.33 = bf16[8,512,128]{2,0,1:T(8,128)(2,1)S(1)} fusion(bf16[512,32,128]{2,1,0:T(8,128)(2,1)} %get-tuple-element.81, s32[8]{0:T(128)S(1)} %get-tuple-element.66), kind=kOutput, calls=%fused_computation.12.clone.1 | convolution fusion | flops 33554688 | bytes 5242912 | tf_op jit(solution)/shard_map/while/body/eval_jaxpr/tnb,gn->tgb/dot_general | solution.py:14
  122.6 1.2 fusion.35
  123.8 3.1 %fusion.33 = bf16[8,512,128]{2,0,1:T(8,128)(2,1)S(1)} fusion(bf16[512,32,128]{2,1,0:T(8,128)(2,1)} %get-tuple-element.81, s32[8]{0:T(128)S(1)} %get-tuple-element.66), kind=kOutput, calls=%fused_computation.12.clone.1 | convolution fusion | flops 33554688 | bytes 5242912 | tf_op jit(solution)/shard_map/while/body/eval_jaxpr/tnb,gn->tgb/dot_general | solution.py:14
  128.6 1.2 fusion.35
  129.8 3.1 %fusion.33 = bf16[8,512,128]{2,0,1:T(8,128)(2,1)S(1)} fusion(bf16[512,32,128]{2,1,0:T(8,128)(2,1)} %get-tuple-element.81, s32[8]{0:T(128)S(1)} %get-tuple-element.66), kind=kOutput, calls=%fused_computation.12.clone.1 | convolution fusion | flops 33554688 | bytes 5242912 | tf_op jit(solution)/shard_map/while/body/eval_jaxpr/tnb,gn->tgb/dot_general | solution.py:14
  134.6 1.2 fusion.35
  135.8 3.1 %fusion.33 = bf16[8,512,128]{2,0,1:T(8,128)(2,1)S(1)} fusion(bf16[512,32,128]{2,1,0:T(8,128)(2,1)} %get-tuple-element.81, s32[8]{0:T(128)S(1)} %get-tuple-element.66), kind=kOutput, calls=%fused_computation.12.clone.1 | convolution fusion | flops 33554688 | bytes 5242912 | tf_op jit(solution)/shard_map/while/body/eval_jaxpr/tnb,gn->tgb/dot_general | solution.py:14
  140.7 1.2 fusion.35
  141.9 3.1 %fusion.33 = bf16[8,512,128]{2,0,1:T(8,128)(2,1)S(1)} fusion(bf16[512,32,128]{2,1,0:T(8,128)(2,1)} %get-tuple-element.81, s32[8]{0:T(128)S(1)} %get-tuple-element.66), kind=kOutput, calls=%fused_computation.12.clone.1 | convolution fusion | flops 33554688 | bytes 5242912 | tf_op jit(solution)/shard_map/while/body/eval_jaxpr/tnb,gn->tgb/dot_general | solution.py:14
  146.7 1.2 fusion.35
  147.9 3.1 %fusion.33 = bf16[8,512,128]{2,0,1:T(8,128)(2,1)S(1)} fusion(bf16[512,32,128]{2,1,0:T(8,128)(2,1)} %get-tuple-element.81, s32[8]{0:T(128)S(1)} %get-tuple-element.66), kind=kOutput, calls=%fused_computation.12.clone.1 | convolution fusion | flops 33554688 | bytes 5242912 | tf_op jit(solution)/shard_map/while/body/eval_jaxpr/tnb,gn->tgb/dot_general | solution.py:14
  152.7 1.2 fusion.35
  153.9 3.1 %fusion.33 = bf16[8,512,128]{2,0,1:T(8,128)(2,1)S(1)} fusion(bf16[512,32,128]{2,1,0:T(8,128)(2,1)} %get-tuple-element.81, s32[8]{0:T(128)S(1)} %get-tuple-element.66), kind=kOutput, calls=%fused_computation.12.clone.1 | convolution fusion | flops 33554688 | bytes 5242912 | tf_op jit(solution)/shard_map/while/body/eval_jaxpr/tnb,gn->tgb/dot_general | solution.py:14
  158.7 1.2 fusion.35
  160.0 3.1 %fusion.33 = bf16[8,512,128]{2,0,1:T(8,128)(2,1)S(1)} fusion(bf16[512,32,128]{2,1,0:T(8,128)(2,1)} %get-tuple-element.81, s32[8]{0:T(128)S(1)} %get-tuple-element.66), kind=kOutput, calls=%fused_computation.12.clone.1 | convolution fusion | flops 33554688 | bytes 5242912 | tf_op jit(solution)/shard_map/while/body/eval_jaxpr/tnb,gn->tgb/dot_general | solution.py:14
  164.8 1.2 fusion.35
  166.0 3.1 %fusion.33 = bf16[8,512,128]{2,0,1:T(8,128)(2,1)S(1)} fusion(bf16[512,32,128]{2,1,0:T(8,128)(2,1)} %get-tuple-element.81, s32[8]{0:T(128)S(1)} %get-tuple-element.66), kind=kOutput, calls=%fused_computation.12.clone.1 | convolution fusion | flops 33554688 | bytes 5242912 | tf_op jit(solution)/shard_map/while/body/eval_jaxpr/tnb,gn->tgb/dot_general | solution.py:14
  170.8 1.2 fusion.35
  172.0 3.1 %fusion.33 = bf16[8,512,128]{2,0,1:T(8,128)(2,1)S(1)} fusion(bf16[512,32,128]{2,1,0:T(8,128)(2,1)} %get-tuple-element.81, s32[8]{0:T(128)S(1)} %get-tuple-element.66), kind=kOutput, calls=%fused_computation.12.clone.1 | convolution fusion | flops 33554688 | bytes 5242912 | tf_op jit(solution)/shard_map/while/body/eval_jaxpr/tnb,gn->tgb/dot_general | solution.py:14
  176.9 1.2 fusion.35
  178.7 6.8 %convolution_multiply_fusion = f32[512,512]{1,0:T(8,128)} fusion(bf16[512,4096]{1,0:T(8,128)(2,1)} %all-gather.5.cloned.1.call-done, bf16[512,4096]{1,0:T(8,128)(2,1)} %all-gather.3.cloned.1.call-done, f32[512]{0:T(512)S(1)} %copy-done.1), kind=kOutput, calls=%fused_computation.20 | convolution fusion | flops 2147745792 | bytes 9439232 | tf_op jit(solution)/shard_map/dot_general | solution.py:43
  185.5 90.8 %reduce-scatter.2.cloned.1.call-done = bf16[42,128,128]{2,1,0:T(8,128)(2,1)} async-done(((bf16[168,128,128]{2,1,0:T(8,128)(2,1)}), bf16[42,128,128]{2,1,0:T(8,128)(2,1)}) %reduce-scatter.2.cloned.1.call-update) | async-done | bytes 1376272 | tf_op jit(solution)/shard_map/reduce_scatter | solution.py:39
  276.3 3.2 %multiply_bitcast_fusion = f32[1,42,128,128]{3,2,1,0:T(8,128)} fusion(bf16[42,128,128]{2,1,0:T(8,128)(2,1)} %reduce-scatter.2.cloned.1.call-done), kind=kLoop, calls=%fused_computation.19 | loop fusion | flops 1376256 | bytes 4128768 | tf_op jit(solution)/shard_map/broadcast_in_dim | solution.py:42
  (158 shorter events, 40.4 us)
Async XLA Ops:
  7.2 38.5 %all-gather.3.cloned.1.call-start = ((), (), s32[]{:S(2)}) async-start(), calls=%async_computation.1 | async-start | bytes 5242880 | tf_op jit(solution)/shard_map/all_gather | solution.py:36
  7.9 170.2 %all-gather.5.cloned.1.call-start = ((), (), s32[]{:S(2)}) async-start(), calls=%async_computation.3 | async-start | bytes 5242880 | tf_op jit(solution)/shard_map/all_gather | solution.py:44
  8.6 267.6 %reduce-scatter.2.cloned.1.call-start = ((), (), s32[]{:S(2)}) async-start(), calls=%async_computation.2 | async-start | bytes 6881280 | tf_op jit(solution)/shard_map/reduce_scatter | solution.py:39
  51.1 3.7 %copy-start = (bf16[512,32,128]{2,1,0:T(8,128)(2,1)S(1)}, bf16[512,32,128]{2,1,0:T(8,128)(2,1)}, u32[]{:S(2)}) copy-start(bf16[512,32,128]{2,1,0:T(8,128)(2,1)} %get-tuple-element.81) | copy-start | bytes 12582916 | tf_op jit(solution)/shard_map/while
  57.3 3.5 %copy-start = (bf16[512,32,128]{2,1,0:T(8,128)(2,1)S(1)}, bf16[512,32,128]{2,1,0:T(8,128)(2,1)}, u32[]{:S(2)}) copy-start(bf16[512,32,128]{2,1,0:T(8,128)(2,1)} %get-tuple-element.81) | copy-start | bytes 12582916 | tf_op jit(solution)/shard_map/while
  63.4 3.5 %copy-start = (bf16[512,32,128]{2,1,0:T(8,128)(2,1)S(1)}, bf16[512,32,128]{2,1,0:T(8,128)(2,1)}, u32[]{:S(2)}) copy-start(bf16[512,32,128]{2,1,0:T(8,128)(2,1)} %get-tuple-element.81) | copy-start | bytes 12582916 | tf_op jit(solution)/shard_map/while
  69.5 3.5 %copy-start = (bf16[512,32,128]{2,1,0:T(8,128)(2,1)S(1)}, bf16[512,32,128]{2,1,0:T(8,128)(2,1)}, u32[]{:S(2)}) copy-start(bf16[512,32,128]{2,1,0:T(8,128)(2,1)} %get-tuple-element.81) | copy-start | bytes 12582916 | tf_op jit(solution)/shard_map/while
  75.5 3.5 %copy-start = (bf16[512,32,128]{2,1,0:T(8,128)(2,1)S(1)}, bf16[512,32,128]{2,1,0:T(8,128)(2,1)}, u32[]{:S(2)}) copy-start(bf16[512,32,128]{2,1,0:T(8,128)(2,1)} %get-tuple-element.81) | copy-start | bytes 12582916 | tf_op jit(solution)/shard_map/while
  81.5 3.4 %copy-start = (bf16[512,32,128]{2,1,0:T(8,128)(2,1)S(1)}, bf16[512,32,128]{2,1,0:T(8,128)(2,1)}, u32[]{:S(2)}) copy-start(bf16[512,32,128]{2,1,0:T(8,128)(2,1)} %get-tuple-element.81) | copy-start | bytes 12582916 | tf_op jit(solution)/shard_map/while
  87.6 3.4 %copy-start = (bf16[512,32,128]{2,1,0:T(8,128)(2,1)S(1)}, bf16[512,32,128]{2,1,0:T(8,128)(2,1)}, u32[]{:S(2)}) copy-start(bf16[512,32,128]{2,1,0:T(8,128)(2,1)} %get-tuple-element.81) | copy-start | bytes 12582916 | tf_op jit(solution)/shard_map/while
  93.6 3.5 %copy-start = (bf16[512,32,128]{2,1,0:T(8,128)(2,1)S(1)}, bf16[512,32,128]{2,1,0:T(8,128)(2,1)}, u32[]{:S(2)}) copy-start(bf16[512,32,128]{2,1,0:T(8,128)(2,1)} %get-tuple-element.81) | copy-start | bytes 12582916 | tf_op jit(solution)/shard_map/while
  99.7 3.5 %copy-start = (bf16[512,32,128]{2,1,0:T(8,128)(2,1)S(1)}, bf16[512,32,128]{2,1,0:T(8,128)(2,1)}, u32[]{:S(2)}) copy-start(bf16[512,32,128]{2,1,0:T(8,128)(2,1)} %get-tuple-element.81) | copy-start | bytes 12582916 | tf_op jit(solution)/shard_map/while
  105.7 3.4 %copy-start = (bf16[512,32,128]{2,1,0:T(8,128)(2,1)S(1)}, bf16[512,32,128]{2,1,0:T(8,128)(2,1)}, u32[]{:S(2)}) copy-start(bf16[512,32,128]{2,1,0:T(8,128)(2,1)} %get-tuple-element.81) | copy-start | bytes 12582916 | tf_op jit(solution)/shard_map/while
  111.7 3.4 %copy-start = (bf16[512,32,128]{2,1,0:T(8,128)(2,1)S(1)}, bf16[512,32,128]{2,1,0:T(8,128)(2,1)}, u32[]{:S(2)}) copy-start(bf16[512,32,128]{2,1,0:T(8,128)(2,1)} %get-tuple-element.81) | copy-start | bytes 12582916 | tf_op jit(solution)/shard_map/while
  117.7 3.4 %copy-start = (bf16[512,32,128]{2,1,0:T(8,128)(2,1)S(1)}, bf16[512,32,128]{2,1,0:T(8,128)(2,1)}, u32[]{:S(2)}) copy-start(bf16[512,32,128]{2,1,0:T(8,128)(2,1)} %get-tuple-element.81) | copy-start | bytes 12582916 | tf_op jit(solution)/shard_map/while
  123.8 3.4 %copy-start = (bf16[512,32,128]{2,1,0:T(8,128)(2,1)S(1)}, bf16[512,32,128]{2,1,0:T(8,128)(2,1)}, u32[]{:S(2)}) copy-start(bf16[512,32,128]{2,1,0:T(8,128)(2,1)} %get-tuple-element.81) | copy-start | bytes 12582916 | tf_op jit(solution)/shard_map/while
  129.8 3.4 %copy-start = (bf16[512,32,128]{2,1,0:T(8,128)(2,1)S(1)}, bf16[512,32,128]{2,1,0:T(8,128)(2,1)}, u32[]{:S(2)}) copy-start(bf16[512,32,128]{2,1,0:T(8,128)(2,1)} %get-tuple-element.81) | copy-start | bytes 12582916 | tf_op jit(solution)/shard_map/while
  135.8 3.4 %copy-start = (bf16[512,32,128]{2,1,0:T(8,128)(2,1)S(1)}, bf16[512,32,128]{2,1,0:T(8,128)(2,1)}, u32[]{:S(2)}) copy-start(bf16[512,32,128]{2,1,0:T(8,128)(2,1)} %get-tuple-element.81) | copy-start | bytes 12582916 | tf_op jit(solution)/shard_map/while
  141.9 3.4 %copy-start = (bf16[512,32,128]{2,1,0:T(8,128)(2,1)S(1)}, bf16[512,32,128]{2,1,0:T(8,128)(2,1)}, u32[]{:S(2)}) copy-start(bf16[512,32,128]{2,1,0:T(8,128)(2,1)} %get-tuple-element.81) | copy-start | bytes 12582916 | tf_op jit(solution)/shard_map/while
  147.9 3.4 %copy-start = (bf16[512,32,128]{2,1,0:T(8,128)(2,1)S(1)}, bf16[512,32,128]{2,1,0:T(8,128)(2,1)}, u32[]{:S(2)}) copy-start(bf16[512,32,128]{2,1,0:T(8,128)(2,1)} %get-tuple-element.81) | copy-start | bytes 12582916 | tf_op jit(solution)/shard_map/while
  153.9 3.4 %copy-start = (bf16[512,32,128]{2,1,0:T(8,128)(2,1)S(1)}, bf16[512,32,128]{2,1,0:T(8,128)(2,1)}, u32[]{:S(2)}) copy-start(bf16[512,32,128]{2,1,0:T(8,128)(2,1)} %get-tuple-element.81) | copy-start | bytes 12582916 | tf_op jit(solution)/shard_map/while
  159.9 3.4 %copy-start = (bf16[512,32,128]{2,1,0:T(8,128)(2,1)S(1)}, bf16[512,32,128]{2,1,0:T(8,128)(2,1)}, u32[]{:S(2)}) copy-start(bf16[512,32,128]{2,1,0:T(8,128)(2,1)} %get-tuple-element.81) | copy-start | bytes 12582916 | tf_op jit(solution)/shard_map/while
  166.0 3.4 %copy-start = (bf16[512,32,128]{2,1,0:T(8,128)(2,1)S(1)}, bf16[512,32,128]{2,1,0:T(8,128)(2,1)}, u32[]{:S(2)}) copy-start(bf16[512,32,128]{2,1,0:T(8,128)(2,1)} %get-tuple-element.81) | copy-start | bytes 12582916 | tf_op jit(solution)/shard_map/while
  172.0 3.4 %copy-start = (bf16[512,32,128]{2,1,0:T(8,128)(2,1)S(1)}, bf16[512,32,128]{2,1,0:T(8,128)(2,1)}, u32[]{:S(2)}) copy-start(bf16[512,32,128]{2,1,0:T(8,128)(2,1)} %get-tuple-element.81) | copy-start | bytes 12582916 | tf_op jit(solution)/shard_map/while
  178.0 0.7 copy-start.1
Sparse Core Ops, SparseCore 0:
  9.6 36.0 all-gather.2
  47.2 77.8 all-gather.4
  178.2 98.0 reduce-scatter.1
where the time goes:
time: 288 us; the launch traced here: 286 us
  waiting for transfers between devices  128 us (44%)
  matrix products  111 us (39%)
  local copies, waits for them, and re-layouts  29.2 us (10%)
  between operations  13.8 us (5%)
  other arithmetic  3.37 us (1%)
    reduce_scatter x1, waiting for transfers between devices, local(): lax.psum_scatter(tile_terms(blocks3, tile_table).astype(jnp.bfloat16), 'e...  90.8 us
    dot_general x42, matrix products, select_blocks(): jnp.einsum('tnb,gn->tgb', blocks3, onehot, preferred_element_type=jnp.flo...  79.2 us
    all_gather x1, waiting for transfers between devices, local(): slab_full = lax.all_gather(slab_grads, 'feat', axis=1, tiled=True)  36.2 us
    dot_general x21, matrix products, group_tiles(): jnp.einsum('tsi,tsj->sij', left_block, right_block, preferred_element_typ...  24.6 us
    dot_general x21, local copies, waits for them, and re-layouts, select_blocks(): jnp.einsum('tnb,gn->tgb', blocks3, onehot, preferred_element_type=jnp.flo...  14.2 us
    while x42, local copies, waits for them, and re-layouts  7.9 us
    dot_general x1, matrix products, local(): lax.dot_general(lax.all_gather(query_grads, 'ex', axis=1, tiled=True), sl...  6.8 us
    unnamed x3, local copies, waits for them, and re-layouts  6.06 us
  transfers between devices with their start and end apart: 3, of which 2 were waited for; matrix products, arithmetic and copies ran while one was open for 46% of the time, Pallas kernels for 0%

commit v1 on v0

--- a/solution.py
+++ b/solution.py
@@ -1,8 +1,11 @@
+import functools
 import math
 
 import jax
 import jax.numpy as jnp
 from jax import lax
+from jax.experimental import pallas as pl
+from jax.experimental.pallas import tpu as pltpu
 from jax.sharding import PartitionSpec as P
 
 B = 128
@@ -30,7 +33,7 @@
     return lax.map(group_tiles, groups).reshape(-1, blocks3.shape[2], blocks3.shape[2])
 
 
-def local(slab_grads, query_grads, example_weights, tile_owner):
+def local_any(slab_grads, query_grads, example_weights, tile_owner):
     tile_table = tile_owner[0]
     tok_count = slab_grads.shape[0]
     slab_full = lax.all_gather(slab_grads, "feat", axis=1, tiled=True)
@@ -50,6 +53,258 @@
     return (gram, scores)
 
 
+PAIR = ((0, 1), (1, 0), (2, 3), (3, 2))
+INNER = ((1, 2), (2, 1))
+TO_END = ((1, 0), (2, 3))
+TO_MID = ((0, 1), (3, 2))
+END_TO_FAR_MID = ((0, 2), (3, 1))
+MID_TO_FAR_END = ((1, 3), (2, 0))
+CORE = ((0, 1), (1, 0), (2, 3), (3, 2))
+ACROSS = ((0, 2), (2, 0), (1, 3), (3, 1))
+
+
+def slot_kernel(slots, carry, final, place, table, *refs):
+    refs = list(refs)
+    pieces = [refs.pop(0) for _ in range(2 * len(slots))]
+    pieces = [p for p in pieces]
+    queries = refs.pop(0), refs.pop(0)
+    acc_in = refs.pop(0) if carry else None
+    outs = [refs.pop(0) for _ in range(2 if final else 1)]
+    scored = [refs.pop(0) for _ in range(len(set(s for s, _ in slots)))]
+    rows, turned, query, row_sem, query_sem = refs
+    tiles = table.shape[0]
+
+    copies = []
+    at = 0
+    for i, (_, count) in enumerate(slots):
+        for half in range(2):
+            copies.append(
+                pltpu.make_async_copy(
+                    pieces[2 * i + half], rows.at[half, pl.ds(at, count)], row_sem.at[2 * i + half]
+                )
+            )
+        at += count
+    for copy in copies:
+        copy.start()
+    query_copies = [
+        pltpu.make_async_copy(queries[j], query.at[j], query_sem.at[j]) for j in range(2)
+    ]
+    middle = place[0] == 1
+
+    @pl.when(middle)
+    def _():
+        for copy in query_copies:
+            copy.start()
+
+    for copy in copies:
+        copy.wait()
+
+    for block in range(32):
+        turned[block] = rows[block // 16, :, (block % 16) * B : (block % 16 + 1) * B].T
+
+    def one(tile, _):
+        left = table[tile, 0]
+        right = table[tile, 1]
+        product = jnp.dot(
+            turned[left],
+            rows[right // 16, :, pl.ds(pl.multiple_of((right % 16) * B, B), B)],
+            preferred_element_type=jnp.float32,
+        )
+        if carry:
+            product += acc_in[tile]
+        return product
+
+    def store(tile, _):
+        outs[0][tile] = one(tile, _)
+        return 0
+
+    def store_sibling(tile, _):
+        outs[0][tile] = one(tile, _).astype(outs[0].dtype)
+        return 0
+
+    def store_own(tile, _):
+        outs[1][tile] = one(tile + tiles // 2, _)
+        return 0
+
+    if final:
+        lax.fori_loop(0, tiles // 2, store_sibling, 0, unroll=6)
+        lax.fori_loop(0, tiles // 2, store_own, 0, unroll=6)
+    else:
+        lax.fori_loop(0, tiles, store, 0, unroll=6)
+
+    @pl.when(middle)
+    def _():
+        for copy in query_copies:
+            copy.wait()
+        group = query.shape[1] // 4
+        quarter = query.shape[2]
+        start = 0
+        for n, ref in enumerate(scored):
+            count = ref.shape[2]
+            for j in range(2):
+                total = None
+                for k in range(4):
+                    spot = place[1 + k]
+                    term = lax.dot_general(
+                        query[j, k * group : (k + 1) * group, :],
+                        rows[
+                            spot // 2,
+                            start : start + count,
+                            pl.ds(pl.multiple_of((spot % 2) * quarter, quarter), quarter),
+                        ],
+                        (((1,), (1,)), ((), ())),
+                        preferred_element_type=jnp.float32,
+                    )
+                    total = term if total is None else total + term
+                ref[j] = total.astype(ref.dtype)
+            start += count
+
+
+def slot_call(place, table, slots, pieces, queries, acc=None, final=False):
+    tiles = table.shape[0]
+    total = sum(count for _, count in slots)
+    wide = pieces[0].shape[1]
+    names = sorted(set(s for s, _ in slots))
+    counts = [sum(c for s, c in slots if s == n) for n in names]
+    group = queries[0].shape[0] // 4
+    if final:
+        outs = [
+            jax.ShapeDtypeStruct((tiles // 2, B, B), jnp.bfloat16),
+            jax.ShapeDtypeStruct((tiles // 2, B, B), jnp.float32),
+        ]
+    else:
+        outs = [jax.ShapeDtypeStruct((tiles, B, B), jnp.float32)]
+    outs += [jax.ShapeDtypeStruct((2, group, c), jnp.bfloat16) for c in counts]
+    carry = acc is not None
+    smem = pl.BlockSpec(memory_space=pltpu.SMEM)
+    vmem = pl.BlockSpec(memory_space=pltpu.VMEM)
+    anywhere = pl.BlockSpec(memory_space=pl.ANY)
+    flops = 2 * tiles * B * B * total + 2 * 2 * group * total * 2 * wide
+    return pl.pallas_call(
+        functools.partial(slot_kernel, slots, carry, final),
+        out_shape=outs,
+        in_specs=[smem, smem]
+        + [anywhere] * (len(pieces) + 2)
+        + ([vmem] if carry else []),
+        out_specs=[vmem] * len(outs),
+        scratch_shapes=[
+            pltpu.VMEM((2, total, wide), jnp.bfloat16),
+            pltpu.VMEM((2 * wide // B, B, total), jnp.bfloat16),
+            pltpu.VMEM((2,) + queries[0].shape, jnp.bfloat16),
+            pltpu.SemaphoreType.DMA((len(pieces),)),
+            pltpu.SemaphoreType.DMA((2,)),
+        ],
+        compiler_params=pltpu.CompilerParams(vmem_limit_bytes=44 * 2**20),
+        cost_estimate=pl.CostEstimate(
+            flops=flops, bytes_accessed=8 * total * wide, transcendentals=0
+        ),
+    )(place, table, *pieces, *queries, *([acc] if carry else []))
+
+
+def local_line(slab_grads, query_grads, example_weights, tile_owner):
+    count, quarter = slab_grads.shape
+    half, piece = count // 2, count // 4
+    e = lax.axis_index("ex")
+    f = lax.axis_index("feat")
+    core = f % 2
+    middle = jnp.logical_or(e == 1, e == 2)
+    late = (e >= 2).astype(jnp.int32)
+
+    def planes(which):
+        return [(p * 4 + g, p * 4 + (g ^ 2)) for p in which for g in range(4)]
+
+    def cores(which):
+        return [(p * 4 + g, p * 4 + (g ^ 1)) for p in which for g in range(4)]
+
+    def move(values, pairs):
+        return [lax.ppermute(v, "ex", pairs) for v in values]
+
+    def across(values):
+        return [lax.ppermute(v, "feat", ACROSS) for v in values]
+
+    keep = lax.dynamic_slice(slab_grads, (core * half, 0), (half, quarter))
+    give = lax.dynamic_slice(slab_grads, ((1 - core) * half, 0), (half, quarter))
+    own = jnp.concatenate([keep, lax.ppermute(give, "feat", CORE)], axis=1)
+    own2 = [own[:piece], own[piece:]]
+
+    near = move(own2, PAIR)
+    inner = move(own2, INNER)
+    outer = move(near, INNER)
+    second = [jnp.where(middle, a, b) for a, b in zip(inner, move(inner, TO_END))]
+    third = [jnp.where(middle, a, b) for a, b in zip(outer, move(outer, TO_END))]
+
+    own_x = across([own])
+    near_x = across(near)
+    second_x = across(second)
+    third_x = across(third)
+
+    q_half = query_grads.shape[0] // 2
+    mine = lax.dynamic_slice(query_grads, (late * q_half, 0), (q_half, quarter))
+    other = lax.dynamic_slice(query_grads, ((1 - late) * q_half, 0), (q_half, quarter))
+    queries = jnp.concatenate(
+        [
+            mine,
+            lax.ppermute(mine, "ex", TO_MID),
+            lax.ppermute(other, "ex", INNER),
+            lax.ppermute(other, "ex", END_TO_FAR_MID),
+        ],
+        axis=0,
+    )
+    queries = (queries, lax.ppermute(queries, ("ex", "feat"), cores((1, 2))))
+
+    slots = tile_owner.shape[1] // 4
+    own_tiles = lax.dynamic_slice(tile_owner[0], (e * slots, 0), (slots, 2))
+    tiles = jnp.concatenate([lax.ppermute(own_tiles, "feat", CORE), own_tiles], axis=0)
+    blocks = quarter // B
+    tiles = jnp.maximum(tiles, 0)
+    table = ((tiles // blocks) ^ f) * blocks + tiles % blocks
+    order = jnp.where(e == 2, jnp.array([2, 3, 1, 0]), jnp.array([1, 0, 2, 3])).astype(jnp.int32)
+    place = jnp.concatenate([middle.astype(jnp.int32)[None], order ^ f])
+
+    acc, r_own, r_near = slot_call(
+        place,
+        table,
+        ((0, half), (1, piece), (1, piece)),
+        [own, own_x[0], near[0], near_x[0], near[1], near_x[1]],
+        queries,
+    )
+    acc, r_second = slot_call(
+        place,
+        table,
+        ((2, piece), (2, piece)),
+        [second[0], second_x[0], second[1], second_x[1]],
+        queries,
+        acc,
+    )
+    for_sibling, for_own, r_third = slot_call(
+        place,
+        table,
+        ((3, piece), (3, piece)),
+        [third[0], third_x[0], third[1], third_x[1]],
+        queries,
+        acc,
+        final=True,
+    )
+
+    gram = for_own + lax.ppermute(for_sibling, "feat", CORE).astype(jnp.float32)
+    gram = gram / (count * 4)
+    gram = jnp.where((own_tiles[:, 0] >= 0)[:, None, None], gram, jnp.float32(0.0))
+
+    to_end = lax.ppermute(r_near, "ex", TO_END)
+    to_mid = lax.ppermute(r_second, "ex", INNER)
+    to_far = lax.ppermute(r_third, "ex", MID_TO_FAR_END)
+    first = jnp.where(middle, r_own, to_end)
+    rest = jnp.where(middle, to_mid, to_far)
+    low = jnp.where(late == 1, rest, first)
+    high = jnp.where(late == 1, first, rest)
+    both = jnp.concatenate([low, high], axis=1)
+    got = lax.ppermute(both[1], "feat", CORE)
+    left = jnp.where(core == 0, both[0], got)
+    right = jnp.where(core == 0, got, both[0])
+    scores = jnp.concatenate([left, right], axis=1).astype(jnp.float32)
+    return gram[None], scores * example_weights[None, :]
+
+
 def solution(mesh):
     placed = (
         P(("grp", "ex"), "feat"),
@@ -57,8 +312,10 @@
         P(("grp", "ex")),
         P(("grp", "feat"), None, None),
     )
+
+    line = mesh.shape["ex"] == 4 and mesh.shape["feat"] == 4
     return jax.shard_map(
-        local,
+        local_line if line else local_any,
         mesh=mesh,
         in_specs=placed,
         out_specs=(P(("grp", "feat"), "ex", None, None), P(("grp", "feat"), "ex")),

time: 288 us -> 173 us (0.60)
  matrix products: 111 us -> 0 us
  waiting for transfers between devices: 128 us -> 73.6 us
  starting transfers between devices: 0.11 us -> 47.2 us
  Pallas kernels: 0 us -> 36.3 us
  local copies, waits for them, and re-layouts: 29.2 us -> 2.47 us
  between operations: 13.8 us -> 1.02 us
  other arithmetic: 3.37 us -> 9.8 us
    dot_general x64 -> x0, matrix products: 111 us -> none  [the longest x42 79.2 us: select_blocks(): jnp.einsum('tnb,gn->tgb', blocks3, onehot, preferred_element_type=jnp.flo...]
    reduce_scatter x1 -> x0, waiting for transfers between devices: 90.8 us -> none  [local(): lax.psum_scatter(tile_terms(blocks3, tile_table).astype(jnp.bfloat16), 'e...]
    ppermute x0 -> x28, waiting for transfers between devices: none -> 73.6 us  [the longest x10 40.5 us: move(): return [lax.ppermute(v, 'ex', pairs) for v in values]]
    ppermute x0 -> x28, starting transfers between devices: none -> 47.2 us  [the longest x10 18.7 us: move(): return [lax.ppermute(v, 'ex', pairs) for v in values]]
    pallas_call x0 -> x3, Pallas kernels: none -> 36.3 us  [slot_call(): pl.pallas_call(functools.partial(slot_kernel, slots, carry, final), out_s...]
    all_gather x2 -> x0, waiting for transfers between devices: 36.2 us -> none  [the longest x1 36.2 us: local(): slab_full = lax.all_gather(slab_grads, 'feat', axis=1, tiled=True)]
    dot_general x21 -> x0, local copies, waits for them, and re-layouts: 14.2 us -> none  [select_blocks(): jnp.einsum('tnb,gn->tgb', blocks3, onehot, preferred_element_type=jnp.flo...]
    while x42 -> x0, local copies, waits for them, and re-layouts: 7.9 us -> none
  transfers between devices with their start and end apart: 3 -> 28, of which waited for: 2 -> 14; matrix products, arithmetic and copies ran while one was open for 46% -> 4% of each run, Pallas kernels for 0% -> 15%
where the time goes in v1:
time: 173 us; the launch traced here: 170 us
  waiting for transfers between devices  73.6 us (43%)
  starting transfers between devices  47.2 us (27%)
  Pallas kernels  36.3 us (21%)
  other arithmetic  9.8 us (6%)
  local copies, waits for them, and re-layouts  2.47 us (1%)
    ppermute x10, waiting for transfers between devices, move(): return [lax.ppermute(v, 'ex', pairs) for v in values]  40.5 us
    pallas_call x3, Pallas kernels, slot_call(): pl.pallas_call(functools.partial(slot_kernel, slots, carry, final), out_s...  36.3 us
    ppermute x7, waiting for transfers between devices, across(): return [lax.ppermute(v, 'feat', ACROSS) for v in values]  20.2 us
    ppermute x10, starting transfers between devices, move(): return [lax.ppermute(v, 'ex', pairs) for v in values]  18.7 us
    ppermute x7, starting transfers between devices, across(): return [lax.ppermute(v, 'feat', ACROSS) for v in values]  7.78 us
    ppermute x1, waiting for transfers between devices, local_line(): lax.ppermute(mine, 'ex', TO_MID)  4.95 us
    ppermute x1, waiting for transfers between devices, local_line(): to_mid = lax.ppermute(r_second, 'ex', INNER)  4.27 us
    ppermute x1, starting transfers between devices, local_line(): queries = (queries, lax.ppermute(queries, ('ex', 'feat'), cores((1, 2))))  3.49 us
  transfers between devices with their start and end apart: 28, of which 14 were waited for; matrix products, arithmetic and copies ran while one was open for 4% of the time, Pallas kernels for 15%

profile of v1, /device:TPU:9, one launch (start us, length us, event | category | flops | bytes accessed | tf_op | source)
XLA Modules:
  0.0 170.4 jit_solution(13238833195311001413)
XLA Ops:
  0.7 1.4 constant_dynamic-slice_fusion.2
  2.1 0.7 collective-permute-start.1
  2.8 0.9 constant_dynamic-slice_fusion.1
  3.7 1.3 collective-permute-start.10
  5.0 3.2 %collective-permute-start.11 = (bf16[256,1024]{1,0:T(8,128)(2,1)}, bf16[256,1024]{1,0:T(8,128)(2,1)}, u32[]{:S(2)}, u32[]{:S(2)}) collective-permute-start(bf16[256,1024]{1,0:T(8,128)(2,1)} %get-tuple-element.21), channel_id=1, source_target_pairs={{4,8},{8,4},{5,9},{9,5},{6,10},{10,6},{7,11},{11,7},{20,24},{24,20... | collective-permute-start | bytes 1572872 | tf_op jit(solution)/shard_map/ppermute | solution.py:248
  8.2 1.0 fusion.1
  9.2 2.1 %collective-permute-start.14 = (bf16[128,2048]{1,0:T(8,128)(2,1)}, bf16[128,2048]{1,0:T(8,128)(2,1)S(1)}, u32[]{:S(2)}, u32[]{:S(2)}) collective-permute-start(bf16[128,2048]{1,0:T(8,128)(2,1)} %get-tuple-element.23), channel_id=1, source_target_pairs={{4,8},{8,4},{5,9},{9,5},{6,10},{10,6},{7,11},{11,7},{20,24},{24,20... | collective-permute-start | bytes 1572872 | tf_op jit(solution)/shard_map/ppermute | solution.py:220
  12.1 0.8 collective-permute-done
  12.9 1.3 collective-permute-start.12
  14.2 4.9 %collective-permute-done.10 = bf16[256,1024]{1,0:T(8,128)(2,1)} collective-permute-done((bf16[256,1024]{1,0:T(8,128)(2,1)S(1)}, bf16[256,1024]{1,0:T(8,128)(2,1)}, u32[]{:S(2)}, u32[]{:S(2)}) %collective-permute-start.10) | collective-permute-done | bytes 524320 | tf_op jit(solution)/shard_map/ppermute | solution.py:247
  19.2 1.5 collective-permute-done.11
  20.7 3.2 %collective-permute-start.17 = (bf16[128,2048]{1,0:T(8,128)(2,1)}, bf16[128,2048]{1,0:T(8,128)(2,1)}, u32[]{:S(2)}, u32[]{:S(2)}) collective-permute-start(bf16[128,2048]{1,0:T(8,128)(2,1)} %get-tuple-element.22), channel_id=1, source_target_pairs={{4,8},{8,4},{5,9},{9,5},{6,10},{10,6},{7,11},{11,7},{20,24},{24,20... | collective-permute-start | bytes 1572872 | tf_op jit(solution)/shard_map/ppermute | solution.py:220
  24.0 18.1 %collective-permute-done.14 = bf16[128,2048]{1,0:T(8,128)(2,1)S(1)} collective-permute-done((bf16[128,2048]{1,0:T(8,128)(2,1)}, bf16[128,2048]{1,0:T(8,128)(2,1)S(1)}, u32[]{:S(2)}, u32[]{:S(2)}) %collective-permute-start.14) | collective-permute-done | bytes 524320 | tf_op jit(solution)/shard_map/ppermute | solution.py:220
  42.1 2.1 %collective-permute-start.15 = (bf16[128,2048]{1,0:T(8,128)(2,1)S(1)}, bf16[128,2048]{1,0:T(8,128)(2,1)}, u32[]{:S(2)}, u32[]{:S(2)}) collective-permute-start(bf16[128,2048]{1,0:T(8,128)(2,1)S(1)} %collective-permute-done.14), channel_id=1, source_target_pairs={{4,0},{8,12},{5,1},{9,13},{6,2},{10,14},{7,3},{11,15},{20,16},{24,... | collective-permute-start | bytes 1572872 | tf_op jit(solution)/shard_map/ppermute | solution.py:220
  44.2 4.1 %collective-permute-start.7 = (bf16[128,2048]{1,0:T(8,128)(2,1)S(1)}, bf16[128,2048]{1,0:T(8,128)(2,1)}, u32[]{:S(2)}, u32[]{:S(2)}) collective-permute-start(bf16[128,2048]{1,0:T(8,128)(2,1)S(1)} %collective-permute-done.6.refs_4_), channel_id=1, source_target_pairs={{4,8},{8,4},{5,9},{9,5},{6,10},{10,6},{7,11},{11,7},{20,24},{24,20... | collective-permute-start | bytes 1572872 | tf_op jit(solution)/shard_map/ppermute | solution.py:220
  48.6 1.3 collective-permute-start.20
  49.9 4.5 %collective-permute-done.17 = bf16[128,2048]{1,0:T(8,128)(2,1)} collective-permute-done((bf16[128,2048]{1,0:T(8,128)(2,1)}, bf16[128,2048]{1,0:T(8,128)(2,1)}, u32[]{:S(2)}, u32[]{:S(2)}) %collective-permute-start.17) | collective-permute-done | bytes 524320 | tf_op jit(solution)/shard_map/ppermute | solution.py:220
  54.4 1.3 collective-permute-start.18
  55.7 3.2 %collective-permute-start.3 = (bf16[128,2048]{1,0:T(8,128)(2,1)S(1)}, bf16[128,2048]{1,0:T(8,128)(2,1)S(1)}, u32[]{:S(2)}, u32[]{:S(2)}) collective-permute-start(bf16[128,2048]{1,0:T(8,128)(2,1)S(1)} %collective-permute-done.2.refs_2_), channel_id=1, source_target_pairs={{4,8},{8,4},{5,9},{9,5},{6,10},{10,6},{7,11},{11,7},{20,24},{24,20... | collective-permute-start | bytes 1572872 | tf_op jit(solution)/shard_map/ppermute | solution.py:220
  58.9 1.5 pad_maximum_fusion.refs_6_.refs_4_
  60.5 3.5 %collective-permute-start.13 = (bf16[1024,1024]{1,0:T(8,128)(2,1)S(1)}, bf16[1024,1024]{1,0:T(8,128)(2,1)S(1)}, u32[]{:S(2)}, u32[]{:S(2)}) collective-permute-start(bf16[1024,1024]{1,0:T(8,128)(2,1)S(1)} %pad_maximum_fusion.refs_6_.refs_4_), channel_id=1, source_target_pairs={{4,5},{5,4},{6,7},{7,6},{8,9},{9,8},{10,11},{11,10},{20,21},{21,20... | collective-permute-start | bytes 6291464 | tf_op jit(solution)/shard_map/ppermute | solution.py:253
  64.0 1.7 collective-permute-done.7
  65.6 1.3 collective-permute-start.8
  67.0 1.3 collective-permute-start.21
  68.3 8.4 %collective-permute-done.3 = bf16[128,2048]{1,0:T(8,128)(2,1)S(1)} collective-permute-done((bf16[128,2048]{1,0:T(8,128)(2,1)S(1)}, bf16[128,2048]{1,0:T(8,128)(2,1)S(1)}, u32[]{:S(2)}, u32[]{:S(2)}) %collective-permute-start.3) | collective-permute-done | bytes 524320 | tf_op jit(solution)/shard_map/ppermute | solution.py:220
  76.8 1.3 collective-permute-start.4
  78.1 1.1 broadcast_select_fusion.refs_2_
  79.2 1.3 collective-permute-start.22
  80.5 1.1 broadcast_select_fusion.2.refs_2_
  81.6 7.8 %collective-permute-done.4 = bf16[128,2048]{1,0:T(8,128)(2,1)S(1)} collective-permute-done((bf16[128,2048]{1,0:T(8,128)(2,1)S(1)}, bf16[128,2048]{1,0:T(8,128)(2,1)S(1)}, u32[]{:S(2)}, u32[]{:S(2)}) %collective-permute-start.4) | collective-permute-done | bytes 524320 | tf_op jit(solution)/shard_map/ppermute | solution.py:220
  89.4 1.2 collective-permute-start.16
  91.0 1.2 collective-permute-start.9
  92.2 2.0 %collective-permute-done.22.refs_5_ = bf16[128,2048]{1,0:T(8,128)(2,1)S(1)} collective-permute-done((bf16[128,2048]{1,0:T(8,128)(2,1)S(1)}, bf16[128,2048]{1,0:T(8,128)(2,1)S(1)}, u32[]{:S(2)}, u32[]{:S(2)}) %collective-permute-start.22) | collective-permute-done | bytes 524320 | tf_op jit(solution)/shard_map/ppermute | solution.py:223
  94.2 1.2 collective-permute-start.5
  95.5 13.7 %shard_map.77 = (f32[84,128,128]{2,1,0:T(8,128)}, bf16[2,256,256]{2,1,0:T(8,128)(2,1)S(1)}, bf16[2,256,256]{2,1,0:T(8,128)(2,1)S(1)}) custom-call(s32[5]{0:T(128)S(1)} %pad_add_fusion.1.place, s32[84,2]{1,0:T(8,128)S(1)} %fusion.7.table, bf16[256,2048]{1,0:T(8,128)(2,1)S(1)} %pad_maximum_fusion.1.refs_0_, ...), custom_call_target="tpu_custom_call" | custom-call | flops 3556769792 | bytes 8388608 | tf_op jit(solution)/shard_map/pallas_call | solution.py:183
  109.2 7.5 %collective-permute-done.19.refs_3_ = bf16[128,2048]{1,0:T(8,128)(2,1)S(1)} collective-permute-done((bf16[128,2048]{1,0:T(8,128)(2,1)S(1)}, bf16[128,2048]{1,0:T(8,128)(2,1)S(1)}, u32[]{:S(2)}, u32[]{:S(2)}) %collective-permute-start.19) | collective-permute-done | bytes 524320 | tf_op jit(solution)/shard_map/ppermute | solution.py:223
  116.7 11.8 %shard_map.78 = (f32[84,128,128]{2,1,0:T(8,128)}, bf16[2,256,256]{2,1,0:T(8,128)(2,1)S(1)}) custom-call(s32[5]{0:T(128)S(1)} %pad_add_fusion.1.place, s32[84,2]{1,0:T(8,128)S(1)} %fusion.7.table, bf16[128,2048]{1,0:T(8,128)(2,1)S(1)} %broadcast_select_fusion.1.refs_0_, bf16[128,2048]{1,0:T(8,128)(2,1)S(1)} %collective-permute-done.16.refs_1_, ...), custom_call_target="tpu_custom_call" | custom-call | flops 1778384896 | bytes 4194304 | tf_op jit(solution)/shard_map/pallas_call | solution.py:183
  128.5 10.7 %collective-permute-done.5.refs_1_ = bf16[128,2048]{1,0:T(8,128)(2,1)S(1)} collective-permute-done((bf16[128,2048]{1,0:T(8,128)(2,1)S(1)}, bf16[128,2048]{1,0:T(8,128)(2,1)S(1)}, u32[]{:S(2)}, u32[]{:S(2)}) %collective-permute-start.5) | collective-permute-done | bytes 524320 | tf_op jit(solution)/shard_map/ppermute | solution.py:223
  139.2 10.8 %shard_map.79 = (bf16[42,128,128]{2,1,0:T(8,128)(2,1)S(1)}, f32[42,128,128]{2,1,0:T(8,128)}, bf16[2,256,256]{2,1,0:T(8,128)(2,1)S(1)}) custom-call(s32[5]{0:T(128)S(1)} %pad_add_fusion.1.place, s32[84,2]{1,0:T(8,128)S(1)} %fusion.7.table, bf16[128,2048]{1,0:T(8,128)(2,1)S(1)} %broadcast_select_fusion.3.refs_0_, ...), custom_call_target="tpu_custom_call" | custom-call | flops 1778384896 | bytes 4194304 | tf_op jit(solution)/shard_map/pallas_call | solution.py:183
  150.0 1.3 collective-permute-start.25
  151.3 2.3 %collective-permute-start.24 = (bf16[2,256,256]{2,1,0:T(8,128)(2,1)S(1)}, bf16[2,256,256]{2,1,0:T(8,128)(2,1)S(1)}, u32[]{:S(2)}, u32[]{:S(2)}) collective-permute-start(bf16[2,256,256]{2,1,0:T(8,128)(2,1)S(1)} %get-tuple-element.14), channel_id=1, source_target_pairs={{4,8},{8,4},{5,9},{9,5},{6,10},{10,6},{7,11},{11,7},{20,24},{24,20... | collective-permute-start | bytes 786440 | tf_op jit(solution)/shard_map/ppermute | solution.py:294
  153.6 1.3 collective-permute-start.26
  154.9 2.5 %collective-permute-start.23 = (bf16[42,128,128]{2,1,0:T(8,128)(2,1)S(1)}, bf16[42,128,128]{2,1,0:T(8,128)(2,1)}, u32[]{:S(2)}, u32[]{:S(2)}) collective-permute-start(bf16[42,128,128]{2,1,0:T(8,128)(2,1)S(1)} %get-tuple-element.13), channel_id=1, source_target_pairs={{0,1},{1,0},{2,3},{3,2},{4,5},{5,4},{6,7},{7,6},{8,9},{9,8},{10,11... | collective-permute-start | bytes 4128776 | tf_op jit(solution)/shard_map/ppermute | solution.py:289
  157.4 4.3 %collective-permute-done.24 = bf16[2,256,256]{2,1,0:T(8,128)(2,1)S(1)} collective-permute-done((bf16[2,256,256]{2,1,0:T(8,128)(2,1)S(1)}, bf16[2,256,256]{2,1,0:T(8,128)(2,1)S(1)}, u32[]{:S(2)}, u32[]{:S(2)}) %collective-permute-start.24) | collective-permute-done | bytes 262176 | tf_op jit(solution)/shard_map/ppermute | solution.py:294
  162.0 2.7 %collective-permute-start.27 = (bf16[512,256]{1,0:T(8,128)(2,1)S(1)}, bf16[512,256]{1,0:T(8,128)(2,1)S(1)}, u32[]{:S(2)}, u32[]{:S(2)}) collective-permute-start(bf16[512,256]{1,0:T(8,128)(2,1)S(1)} %fusion.4), channel_id=1, source_target_pairs={{0,1},{1,0},{2,3},{3,2},{4,5},{5,4},{6,7},{7,6},{8,9},{9,8},{10,11... | collective-permute-start | bytes 786440 | tf_op jit(solution)/shard_map/ppermute | solution.py:301
  164.7 1.2 collective-permute-done.27
  166.0 1.1 convert_multiply_fusion
  167.1 3.3 %select_bitcast_fusion = f32[1,42,128,128]{3,2,1,0:T(8,128)} fusion(f32[42,128,128]{2,1,0:T(8,128)S(1)} %copy-done.1, bf16[42,128,128]{2,1,0:T(8,128)(2,1)} %collective-permute-done.23, pred[42]{0:T(512)(128)(4,1)S(1)} %compare_bitcast_fusion), kind=kLoop, calls=%fused_computation | loop fusion | flops 2752512 | bytes 6881322 | tf_op jit(solution)/shard_map/broadcast_in_dim | solution.py:305
  (44 shorter events, 2.1 us)
Async XLA Ops:
  0.6 10.8 %copy-start = (s32[1,168,2]{1,2,0:T(2,128)S(1)}, s32[1,168,2]{1,2,0:T(2,128)}, u32[]{:S(2)}) copy-start(s32[1,168,2]{1,2,0:T(2,128)} %param.9) | copy-start | bytes 4036
  0.6 2.2 %copy-start.2 = (bf16[512,1024]{1,0:T(8,128)(2,1)S(1)}, bf16[512,1024]{1,0:T(8,128)(2,1)}, u32[]{:S(2)}) copy-start(bf16[512,1024]{1,0:T(8,128)(2,1)} %param.7) | copy-start | bytes 3145732
  0.7 23.2 %copy-start.4 = (s32[4]{0:T(128)S(1)}, s32[4]{0:T(128)}, u32[]{:S(2)}) copy-start(s32[4]{0:T(128)} %constant.74.clone) | copy-start | bytes 52
  0.7 23.2 %copy-start.5 = (s32[4]{0:T(128)S(1)}, s32[4]{0:T(128)}, u32[]{:S(2)}) copy-start(s32[4]{0:T(128)} %constant.75.clone) | copy-start | bytes 52
  2.1 6.1 %collective-permute-start.1 = (bf16[256,1024]{1,0:T(8,128)(2,1)S(1)}, bf16[256,1024]{1,0:T(8,128)(2,1)S(1)}, u32[]{:S(2)}, u32[]{:S(2)}) collective-permute-start(bf16[256,1024]{1,0:T(8,128)(2,1)S(1)} %get-tuple-element.24), channel_id=1, source_target_pairs={{0,1},{1,0},{2,3},{3,2},{4,5},{5,4},{6,7},{7,6},{8,9},{9,8},{10,11... | collective-permute-start | bytes 1572872 | tf_op jit(solution)/shard_map/ppermute | solution.py:227
  3.7 15.5 %collective-permute-start.10 = (bf16[256,1024]{1,0:T(8,128)(2,1)S(1)}, bf16[256,1024]{1,0:T(8,128)(2,1)}, u32[]{:S(2)}, u32[]{:S(2)}) collective-permute-start(bf16[256,1024]{1,0:T(8,128)(2,1)S(1)} %get-tuple-element.20), channel_id=1, source_target_pairs={{0,4},{12,8},{1,5},{13,9},{2,6},{14,10},{3,7},{15,11},{16,20},{28,... | collective-permute-start | bytes 1572872 | tf_op jit(solution)/shard_map/ppermute | solution.py:247
  5.0 15.7 %collective-permute-start.11 = (bf16[256,1024]{1,0:T(8,128)(2,1)}, bf16[256,1024]{1,0:T(8,128)(2,1)}, u32[]{:S(2)}, u32[]{:S(2)}) collective-permute-start(bf16[256,1024]{1,0:T(8,128)(2,1)} %get-tuple-element.21), channel_id=1, source_target_pairs={{4,8},{8,4},{5,9},{9,5},{6,10},{10,6},{7,11},{11,7},{20,24},{24,20... | collective-permute-start | bytes 1572872 | tf_op jit(solution)/shard_map/ppermute | solution.py:248
  9.2 32.9 %collective-permute-start.14 = (bf16[128,2048]{1,0:T(8,128)(2,1)}, bf16[128,2048]{1,0:T(8,128)(2,1)S(1)}, u32[]{:S(2)}, u32[]{:S(2)}) collective-permute-start(bf16[128,2048]{1,0:T(8,128)(2,1)} %get-tuple-element.23), channel_id=1, source_target_pairs={{4,8},{8,4},{5,9},{9,5},{6,10},{10,6},{7,11},{11,7},{20,24},{24,20... | collective-permute-start | bytes 1572872 | tf_op jit(solution)/shard_map/ppermute | solution.py:220
  11.3 32.9 %collective-permute-start.6 = (bf16[128,2048]{1,0:T(8,128)(2,1)}, bf16[128,2048]{1,0:T(8,128)(2,1)S(1)}, u32[]{:S(2)}, u32[]{:S(2)}) collective-permute-start(bf16[128,2048]{1,0:T(8,128)(2,1)} %get-tuple-element.22), channel_id=1, source_target_pairs={{0,4},{4,0},{8,12},{12,8},{1,5},{5,1},{9,13},{13,9},{2,6},{6,2},{1... | collective-permute-start | bytes 1572872 | tf_op jit(solution)/shard_map/ppermute | solution.py:220
  11.5 1.5 collective-permute-start
  12.9 35.7 %collective-permute-start.12 = (bf16[256,1024]{1,0:T(8,128)(2,1)}, bf16[256,1024]{1,0:T(8,128)(2,1)}, u32[]{:S(2)}, u32[]{:S(2)}) collective-permute-start(bf16[256,1024]{1,0:T(8,128)(2,1)} %get-tuple-element.21), channel_id=1, source_target_pairs={{0,8},{12,4},{1,9},{13,5},{2,10},{14,6},{3,11},{15,7},{16,24},{28,... | collective-permute-start | bytes 1572872 | tf_op jit(solution)/shard_map/ppermute | solution.py:249
  19.2 36.5 %collective-permute-start.2 = (bf16[128,2048]{1,0:T(8,128)(2,1)}, bf16[128,2048]{1,0:T(8,128)(2,1)S(1)}, u32[]{:S(2)}, u32[]{:S(2)}) collective-permute-start(bf16[128,2048]{1,0:T(8,128)(2,1)} %get-tuple-element.23), channel_id=1, source_target_pairs={{0,4},{4,0},{8,12},{12,8},{1,5},{5,1},{9,13},{13,9},{2,6},{6,2},{1... | collective-permute-start | bytes 1572872 | tf_op jit(solution)/shard_map/ppermute | solution.py:220
  20.7 33.7 %collective-permute-start.17 = (bf16[128,2048]{1,0:T(8,128)(2,1)}, bf16[128,2048]{1,0:T(8,128)(2,1)}, u32[]{:S(2)}, u32[]{:S(2)}) collective-permute-start(bf16[128,2048]{1,0:T(8,128)(2,1)} %get-tuple-element.22), channel_id=1, source_target_pairs={{4,8},{8,4},{5,9},{9,5},{6,10},{10,6},{7,11},{11,7},{20,24},{24,20... | collective-permute-start | bytes 1572872 | tf_op jit(solution)/shard_map/ppermute | solution.py:220
  42.1 18.4 %collective-permute-start.15 = (bf16[128,2048]{1,0:T(8,128)(2,1)S(1)}, bf16[128,2048]{1,0:T(8,128)(2,1)}, u32[]{:S(2)}, u32[]{:S(2)}) collective-permute-start(bf16[128,2048]{1,0:T(8,128)(2,1)S(1)} %collective-permute-done.14), channel_id=1, source_target_pairs={{4,0},{8,12},{5,1},{9,13},{6,2},{10,14},{7,3},{11,15},{20,16},{24,... | collective-permute-start | bytes 1572872 | tf_op jit(solution)/shard_map/ppermute | solution.py:220
  44.2 21.4 %collective-permute-start.7 = (bf16[128,2048]{1,0:T(8,128)(2,1)S(1)}, bf16[128,2048]{1,0:T(8,128)(2,1)}, u32[]{:S(2)}, u32[]{:S(2)}) collective-permute-start(bf16[128,2048]{1,0:T(8,128)(2,1)S(1)} %collective-permute-done.6.refs_4_), channel_id=1, source_target_pairs={{4,8},{8,4},{5,9},{9,5},{6,10},{10,6},{7,11},{11,7},{20,24},{24,20... | collective-permute-start | bytes 1572872 | tf_op jit(solution)/shard_map/ppermute | solution.py:220
  48.6 42.0 %collective-permute-start.20 = (bf16[256,2048]{1,0:T(8,128)(2,1)S(1)}, bf16[256,2048]{1,0:T(8,128)(2,1)S(1)}, u32[]{:S(2)}, u32[]{:S(2)}) collective-permute-start(bf16[256,2048]{1,0:T(8,128)(2,1)S(1)} %pad_maximum_fusion.1.refs_0_), channel_id=1, source_target_pairs={{0,2},{2,0},{1,3},{3,1},{4,6},{6,4},{5,7},{7,5},{8,10},{10,8},{9,1... | collective-permute-start | bytes 3145736 | tf_op jit(solution)/shard_map/ppermute | solution.py:223
  54.4 12.6 %collective-permute-start.18 = (bf16[128,2048]{1,0:T(8,128)(2,1)}, bf16[128,2048]{1,0:T(8,128)(2,1)S(1)}, u32[]{:S(2)}, u32[]{:S(2)}) collective-permute-start(bf16[128,2048]{1,0:T(8,128)(2,1)} %collective-permute-done.17), channel_id=1, source_target_pairs={{4,0},{8,12},{5,1},{9,13},{6,2},{10,14},{7,3},{11,15},{20,16},{24,... | collective-permute-start | bytes 1572872 | tf_op jit(solution)/shard_map/ppermute | solution.py:220
  55.7 21.0 %collective-permute-start.3 = (bf16[128,2048]{1,0:T(8,128)(2,1)S(1)}, bf16[128,2048]{1,0:T(8,128)(2,1)S(1)}, u32[]{:S(2)}, u32[]{:S(2)}) collective-permute-start(bf16[128,2048]{1,0:T(8,128)(2,1)S(1)} %collective-permute-done.2.refs_2_), channel_id=1, source_target_pairs={{4,8},{8,4},{5,9},{9,5},{6,10},{10,6},{7,11},{11,7},{20,24},{24,20... | collective-permute-start | bytes 1572872 | tf_op jit(solution)/shard_map/ppermute | solution.py:220
  60.5 35.0 %collective-permute-start.13 = (bf16[1024,1024]{1,0:T(8,128)(2,1)S(1)}, bf16[1024,1024]{1,0:T(8,128)(2,1)S(1)}, u32[]{:S(2)}, u32[]{:S(2)}) collective-permute-start(bf16[1024,1024]{1,0:T(8,128)(2,1)S(1)} %pad_maximum_fusion.refs_6_.refs_4_), channel_id=1, source_target_pairs={{4,5},{5,4},{6,7},{7,6},{8,9},{9,8},{10,11},{11,10},{20,21},{21,20... | collective-permute-start | bytes 6291464 | tf_op jit(solution)/shard_map/ppermute | solution.py:253
  65.6 13.6 %collective-permute-start.8 = (bf16[128,2048]{1,0:T(8,128)(2,1)}, bf16[128,2048]{1,0:T(8,128)(2,1)S(1)}, u32[]{:S(2)}, u32[]{:S(2)}) collective-permute-start(bf16[128,2048]{1,0:T(8,128)(2,1)} %collective-permute-done.7), channel_id=1, source_target_pairs={{4,0},{8,12},{5,1},{9,13},{6,2},{10,14},{7,3},{11,15},{20,16},{24,... | collective-permute-start | bytes 1572872 | tf_op jit(solution)/shard_map/ppermute | solution.py:220
  67.0 23.9 %collective-permute-start.21 = (bf16[128,2048]{1,0:T(8,128)(2,1)S(1)}, bf16[128,2048]{1,0:T(8,128)(2,1)S(1)}, u32[]{:S(2)}, u32[]{:S(2)}) collective-permute-start(bf16[128,2048]{1,0:T(8,128)(2,1)S(1)} %collective-permute-done.2.refs_2_), channel_id=1, source_target_pairs={{0,2},{2,0},{1,3},{3,1},{4,6},{6,4},{5,7},{7,5},{8,10},{10,8},{9,1... | collective-permute-start | bytes 1572872 | tf_op jit(solution)/shard_map/ppermute | solution.py:223
  76.8 12.6 %collective-permute-start.4 = (bf16[128,2048]{1,0:T(8,128)(2,1)S(1)}, bf16[128,2048]{1,0:T(8,128)(2,1)S(1)}, u32[]{:S(2)}, u32[]{:S(2)}) collective-permute-start(bf16[128,2048]{1,0:T(8,128)(2,1)S(1)} %collective-permute-done.3), channel_id=1, source_target_pairs={{4,0},{8,12},{5,1},{9,13},{6,2},{10,14},{7,3},{11,15},{20,16},{24,... | collective-permute-start | bytes 1572872 | tf_op jit(solution)/shard_map/ppermute | solution.py:220
  79.2 15.0 %collective-permute-start.22 = (bf16[128,2048]{1,0:T(8,128)(2,1)S(1)}, bf16[128,2048]{1,0:T(8,128)(2,1)S(1)}, u32[]{:S(2)}, u32[]{:S(2)}) collective-permute-start(bf16[128,2048]{1,0:T(8,128)(2,1)S(1)} %collective-permute-done.6.refs_4_), channel_id=1, source_target_pairs={{0,2},{2,0},{1,3},{3,1},{4,6},{6,4},{5,7},{7,5},{8,10},{10,8},{9,1... | collective-permute-start | bytes 1572872 | tf_op jit(solution)/shard_map/ppermute | solution.py:223
  89.4 19.8 %collective-permute-start.16 = (bf16[128,2048]{1,0:T(8,128)(2,1)S(1)}, bf16[128,2048]{1,0:T(8,128)(2,1)S(1)}, u32[]{:S(2)}, u32[]{:S(2)}) collective-permute-start(bf16[128,2048]{1,0:T(8,128)(2,1)S(1)} %broadcast_select_fusion.1.refs_0_), channel_id=1, source_target_pairs={{0,2},{2,0},{1,3},{3,1},{4,6},{6,4},{5,7},{7,5},{8,10},{10,8},{9,1... | collective-permute-start | bytes 1572872 | tf_op jit(solution)/shard_map/ppermute | solution.py:223
  90.6 26.0 %collective-permute-start.19 = (bf16[128,2048]{1,0:T(8,128)(2,1)S(1)}, bf16[128,2048]{1,0:T(8,128)(2,1)S(1)}, u32[]{:S(2)}, u32[]{:S(2)}) collective-permute-start(bf16[128,2048]{1,0:T(8,128)(2,1)S(1)} %broadcast_select_fusion.refs_2_), channel_id=1, source_target_pairs={{0,2},{2,0},{1,3},{3,1},{4,6},{6,4},{5,7},{7,5},{8,10},{10,8},{9,1... | collective-permute-start | bytes 1572872 | tf_op jit(solution)/shard_map/ppermute | solution.py:223
  91.0 37.5 %collective-permute-start.9 = (bf16[128,2048]{1,0:T(8,128)(2,1)S(1)}, bf16[128,2048]{1,0:T(8,128)(2,1)S(1)}, u32[]{:S(2)}, u32[]{:S(2)}) collective-permute-start(bf16[128,2048]{1,0:T(8,128)(2,1)S(1)} %broadcast_select_fusion.2.refs_2_), channel_id=1, source_target_pairs={{0,2},{2,0},{1,3},{3,1},{4,6},{6,4},{5,7},{7,5},{8,10},{10,8},{9,1... | collective-permute-start | bytes 1572872 | tf_op jit(solution)/shard_map/ppermute | solution.py:223
  94.2 44.9 %collective-permute-start.5 = (bf16[128,2048]{1,0:T(8,128)(2,1)S(1)}, bf16[128,2048]{1,0:T(8,128)(2,1)S(1)}, u32[]{:S(2)}, u32[]{:S(2)}) collective-permute-start(bf16[128,2048]{1,0:T(8,128)(2,1)S(1)} %broadcast_select_fusion.3.refs_0_), channel_id=1, source_target_pairs={{0,2},{2,0},{1,3},{3,1},{4,6},{6,4},{5,7},{7,5},{8,10},{10,8},{9,1... | collective-permute-start | bytes 1572872 | tf_op jit(solution)/shard_map/ppermute | solution.py:223
  150.0 16.0 %copy-start.3 = (f32[512]{0:T(512)S(1)}, f32[512]{0:T(512)}, u32[]{:S(2)}) copy-start(f32[512]{0:T(512)} %param.8) | copy-start | bytes 6148
  150.0 7.4 %collective-permute-start.25 = (bf16[2,256,256]{2,1,0:T(8,128)(2,1)S(1)}, bf16[2,256,256]{2,1,0:T(8,128)(2,1)S(1)}, u32[]{:S(2)}, u32[]{:S(2)}) collective-permute-start(bf16[2,256,256]{2,1,0:T(8,128)(2,1)S(1)} %get-tuple-element.15), channel_id=1, source_target_pairs={{4,12},{8,0},{5,13},{9,1},{6,14},{10,2},{7,15},{11,3},{20,28},{24,... | collective-permute-start | bytes 786440 | tf_op jit(solution)/shard_map/ppermute | solution.py:295
  151.3 10.4 %collective-permute-start.24 = (bf16[2,256,256]{2,1,0:T(8,128)(2,1)S(1)}, bf16[2,256,256]{2,1,0:T(8,128)(2,1)S(1)}, u32[]{:S(2)}, u32[]{:S(2)}) collective-permute-start(bf16[2,256,256]{2,1,0:T(8,128)(2,1)S(1)} %get-tuple-element.14), channel_id=1, source_target_pairs={{4,8},{8,4},{5,9},{9,5},{6,10},{10,6},{7,11},{11,7},{20,24},{24,20... | collective-permute-start | bytes 786440 | tf_op jit(solution)/shard_map/ppermute | solution.py:294
  153.6 8.3 %collective-permute-start.26 = (bf16[2,256,256]{2,1,0:T(8,128)(2,1)S(1)}, bf16[2,256,256]{2,1,0:T(8,128)(2,1)S(1)}, u32[]{:S(2)}, u32[]{:S(2)}) collective-permute-start(bf16[2,256,256]{2,1,0:T(8,128)(2,1)S(1)} %get-tuple-element.17), channel_id=1, source_target_pairs={{4,0},{8,12},{5,1},{9,13},{6,2},{10,14},{7,3},{11,15},{20,16},{24,... | collective-permute-start | bytes 786440 | tf_op jit(solution)/shard_map/ppermute | solution.py:293
  154.9 12.2 %collective-permute-start.23 = (bf16[42,128,128]{2,1,0:T(8,128)(2,1)S(1)}, bf16[42,128,128]{2,1,0:T(8,128)(2,1)}, u32[]{:S(2)}, u32[]{:S(2)}) collective-permute-start(bf16[42,128,128]{2,1,0:T(8,128)(2,1)S(1)} %get-tuple-element.13), channel_id=1, source_target_pairs={{0,1},{1,0},{2,3},{3,2},{4,5},{5,4},{6,7},{7,6},{8,9},{9,8},{10,11... | collective-permute-start | bytes 4128776 | tf_op jit(solution)/shard_map/ppermute | solution.py:289
  162.0 3.9 %collective-permute-start.27 = (bf16[512,256]{1,0:T(8,128)(2,1)S(1)}, bf16[512,256]{1,0:T(8,128)(2,1)S(1)}, u32[]{:S(2)}, u32[]{:S(2)}) collective-permute-start(bf16[512,256]{1,0:T(8,128)(2,1)S(1)} %fusion.4), channel_id=1, source_target_pairs={{0,1},{1,0},{2,3},{3,2},{4,5},{5,4},{6,7},{7,6},{8,9},{9,8},{10,11... | collective-permute-start | bytes 786440 | tf_op jit(solution)/shard_map/ppermute | solution.py:301
  164.7 2.4 %copy-start.1 = (f32[42,128,128]{2,1,0:T(8,128)S(1)}, f32[42,128,128]{2,1,0:T(8,128)}, u32[]{:S(2)}) copy-start(f32[42,128,128]{2,1,0:T(8,128)} %get-tuple-element.12) | copy-start | bytes 8257540

commit v2 on v0

--- a/solution.py
+++ b/solution.py
@@ -3,6 +3,8 @@
 import jax
 import jax.numpy as jnp
 from jax import lax
+from jax.experimental import pallas as pl
+from jax.experimental.pallas import tpu as pltpu
 from jax.sharding import PartitionSpec as P
 
 B = 128
@@ -30,7 +32,7 @@
     return lax.map(group_tiles, groups).reshape(-1, blocks3.shape[2], blocks3.shape[2])
 
 
-def local(slab_grads, query_grads, example_weights, tile_owner):
+def local_any(slab_grads, query_grads, example_weights, tile_owner):
     tile_table = tile_owner[0]
     tok_count = slab_grads.shape[0]
     slab_full = lax.all_gather(slab_grads, "feat", axis=1, tiled=True)
@@ -50,6 +52,286 @@
     return (gram, scores)
 
 
+PAIR = ((0, 1), (1, 0), (2, 3), (3, 2))
+INNER = ((1, 2), (2, 1))
+TO_END = ((1, 0), (2, 3))
+TO_MID = ((0, 1), (3, 2))
+END_TO_FAR_MID = ((0, 2), (3, 1))
+MID_TO_FAR_END = ((1, 3), (2, 0))
+CORE = ((0, 1), (1, 0), (2, 3), (3, 2))
+ACROSS = ((0, 2), (2, 0), (1, 3), (3, 1))
+
+
+def tile_call(place, table, always, on_middle=(), on_ends=(), carried=()):
+    tiles = table.shape[0]
+    lists = [list(always), list(on_middle), list(on_ends)]
+    arrays = [x for pairs in lists for pair in pairs for x in pair]
+    n = len(arrays)
+    wide = arrays[0].shape[1]
+    first = sum(pair[0].shape[0] for pair in always)
+    total = first + sum(pair[0].shape[0] for pair in on_middle)
+    half = tiles // 2
+    per = wide // B
+    unroll = max(u for u in range(1, 22) if half % u == 0)
+
+    def kernel(place_ref, table_ref, *refs):
+        row_refs = refs[:n]
+        carried_refs = refs[n : n + len(carried)]
+        out_sibling, out_own, rows, turned, sems = refs[n + len(carried) :]
+        copies = [[], [], []]
+        at = 0
+        for which, pairs in enumerate(lists):
+            start = 0 if which == 0 else first
+            for pair in pairs:
+                count = pair[0].shape[0]
+                for side in range(2):
+                    copies[which].append(
+                        pltpu.make_async_copy(
+                            row_refs[at], rows.at[side, pl.ds(start, count)], sems.at[at]
+                        )
+                    )
+                    at += 1
+                start += count
+
+        def run(some):
+            for copy in some:
+                copy.start()
+            for copy in some:
+                copy.wait()
+
+        if on_middle:
+            pl.when(place_ref[0] == 1)(lambda: run(copies[1]))
+            pl.when(place_ref[0] == 0)(lambda: run(copies[2]))
+        run(copies[0])
+
+        for block in range(2 * per):
+            side, column = divmod(block * B, wide)
+            turned[block] = rows[side, :, column : column + B].T
+
+        def product(tile):
+            right = table_ref[tile, 1]
+            return jnp.dot(
+                turned[table_ref[tile, 0]],
+                rows[right // per, :, pl.ds(pl.multiple_of((right % per) * B, B), B)],
+                preferred_element_type=jnp.float32,
+            )
+
+        def sibling(tile, _):
+            out_sibling[tile] = product(tile).astype(out_sibling.dtype)
+            return 0
+
+        def mine(tile, _):
+            sum_ = product(tile + half)
+            for ref in carried_refs:
+                sum_ += ref[tile].astype(jnp.float32)
+            out_own[tile] = sum_
+            return 0
+
+        lax.fori_loop(0, half, sibling, 0, unroll=unroll)
+        lax.fori_loop(0, half, mine, 0, unroll=unroll)
+
+    smem = pl.BlockSpec(memory_space=pltpu.SMEM)
+    vmem = pl.BlockSpec(memory_space=pltpu.VMEM)
+    hbm = pl.BlockSpec(memory_space=pltpu.HBM)
+    return pl.pallas_call(
+        kernel,
+        out_shape=[
+            jax.ShapeDtypeStruct((half, B, B), jnp.bfloat16),
+            jax.ShapeDtypeStruct((half, B, B), jnp.float32),
+        ],
+        in_specs=[smem, smem] + [hbm] * n + [vmem] * len(carried),
+        out_specs=[vmem, vmem],
+        scratch_shapes=[
+            pltpu.VMEM((2, total, wide), jnp.bfloat16),
+            pltpu.VMEM((2 * per, B, total), jnp.bfloat16),
+            pltpu.SemaphoreType.DMA((n,)),
+        ],
+        compiler_params=pltpu.CompilerParams(vmem_limit_bytes=24 * 2**20),
+        cost_estimate=pl.CostEstimate(flops=0, bytes_accessed=0, transcendentals=0),
+    )(place, table, *arrays, *carried)
+
+
+def score_call(place, parts, own, across):
+    n, m = len(own), len(parts)
+    count = tuple(x.shape[0] for x in own)
+    wide = own[0].shape[1]
+    quarter = parts[0][0].shape[1]
+    lengths = [pair[0].shape[0] for pair in parts]
+    group = sum(lengths) // 4
+    per = wide // quarter
+
+    def kernel(place_ref, *refs):
+        row_refs = refs[: 2 * n]
+        query_refs = refs[2 * n : 2 * n + 2 * m]
+        outs = refs[2 * n + 2 * m : 3 * n + 2 * m]
+        rows, query, sems = refs[3 * n + 2 * m :]
+
+        @pl.when(place_ref[0] == 1)
+        def _():
+            copies = []
+            for i in range(2 * n):
+                into = rows.at[i % 2, pl.ds(sum(count[: i // 2]), count[i // 2])]
+                copies.append(pltpu.make_async_copy(row_refs[i], into, sems.at[i]))
+            for i in range(2 * m):
+                into = query.at[i % 2, pl.ds(sum(lengths[: i // 2]), lengths[i // 2])]
+                copies.append(pltpu.make_async_copy(query_refs[i], into, sems.at[2 * n + i]))
+            for copy in copies:
+                copy.start()
+            for copy in copies:
+                copy.wait()
+            for i in range(n):
+                for j in range(2):
+                    total = None
+                    for k in range(4):
+                        spot = place_ref[1 + k]
+                        term = lax.dot_general(
+                            query[j, k * group : (k + 1) * group, :],
+                            rows[
+                                spot // per,
+                                sum(count[:i]) : sum(count[: i + 1]),
+                                pl.ds(pl.multiple_of((spot % per) * quarter, quarter), quarter),
+                            ],
+                            (((1,), (1,)), ((), ())),
+                            preferred_element_type=jnp.float32,
+                        )
+                        total = term if total is None else total + term
+                    outs[i][j] = total.astype(outs[i].dtype)
+
+    smem = pl.BlockSpec(memory_space=pltpu.SMEM)
+    hbm = pl.BlockSpec(memory_space=pltpu.HBM)
+    vmem = pl.BlockSpec(memory_space=pltpu.VMEM)
+    arrays = [x for pair in zip(own, across) for x in pair] + [x for pair in parts for x in pair]
+    return pl.pallas_call(
+        kernel,
+        out_shape=[jax.ShapeDtypeStruct((2, group, c), jnp.bfloat16) for c in count],
+        in_specs=[smem] + [hbm] * len(arrays),
+        out_specs=[vmem] * n,
+        scratch_shapes=[
+            pltpu.VMEM((2, sum(count), wide), jnp.bfloat16),
+            pltpu.VMEM((2, 4 * group, quarter), jnp.bfloat16),
+            pltpu.SemaphoreType.DMA((len(arrays),)),
+        ],
+        compiler_params=pltpu.CompilerParams(vmem_limit_bytes=24 * 2**20),
+        cost_estimate=pl.CostEstimate(flops=0, bytes_accessed=0, transcendentals=0),
+    )(place, *arrays)
+
+
+def after(values, *done):
+    return lax.optimization_barrier(tuple(values) + done)[: len(values)]
+
+
+def local_line(slab_grads, query_grads, example_weights, tile_owner):
+    count, quarter = slab_grads.shape
+    half, piece = count // 2, count // 4
+    e = lax.axis_index("ex")
+    f = lax.axis_index("feat")
+    core = f % 2
+    middle = jnp.logical_or(e == 1, e == 2)
+    late = (e >= 2).astype(jnp.int32)
+
+    def move(value, pairs):
+        return lax.ppermute(value, "ex", pairs)
+
+    def across(value):
+        return lax.ppermute(value, "feat", ACROSS)
+
+    def across_on(value, which):
+        pairs = [(p * 4 + g, p * 4 + (g ^ 2)) for p in which for g in range(4)]
+        return lax.ppermute(value, ("ex", "feat"), pairs)
+
+    def join(*values):
+        return jnp.concatenate(values, axis=0)
+
+    def cores(value):
+        pairs = [(p * 4 + g, p * 4 + (g ^ 1)) for p in (1, 2) for g in range(4)]
+        return lax.ppermute(value, ("ex", "feat"), pairs)
+
+    slots = tile_owner.shape[1] // 4
+    own_tiles = lax.dynamic_slice(tile_owner[0], (e * slots, 0), (slots, 2))
+    tiles = jnp.concatenate([lax.ppermute(own_tiles, "feat", CORE), own_tiles], axis=0)
+    blocks = quarter // B
+    tiles = jnp.maximum(tiles, 0)
+    table = ((tiles // blocks) ^ f) * blocks + tiles % blocks
+    order = jnp.where(e == 2, jnp.array([2, 3, 1, 0]), jnp.array([1, 0, 2, 3])).astype(jnp.int32)
+    place = jnp.concatenate([middle.astype(jnp.int32)[None], order ^ f])
+
+    keep = lax.dynamic_slice(slab_grads, (core * half, 0), (half, quarter))
+    give = lax.dynamic_slice(slab_grads, ((1 - core) * half, 0), (half, quarter))
+    own = jnp.concatenate([keep, lax.ppermute(give, "feat", CORE)], axis=1)
+
+    own_x = across(own)
+    near = move(own, PAIR)
+    inner = move(own, INNER)
+
+    near, inner, query_grads, table = after((near, inner, query_grads, table), own_x)
+    near_x = across(near)
+    outer = move(near, INNER)
+    inner_end = move(inner, TO_END)
+    q_end = move(query_grads, TO_MID)
+    q_half = query_grads.shape[0] // 2
+    mine = lax.dynamic_slice(query_grads, (late * q_half, 0), (q_half, quarter))
+    other = lax.dynamic_slice(query_grads, ((1 - late) * q_half, 0), (q_half, quarter))
+
+    inner, inner_end, outer, near, near_x = after((inner, inner_end, outer, near, near_x))
+    second = jnp.where(middle, inner, inner_end)
+    second_x = across(second)
+    outer_end0 = move(outer[:piece], TO_END)
+    outer_end1 = move(outer[piece:], TO_END)
+    outer_x = across_on(outer, (1, 2))
+
+    q_end, near, mine = after((q_end, near, mine), second)
+    end_mine = lax.dynamic_slice(q_end, (late * q_half, 0), (q_half, quarter))
+    end_other = lax.dynamic_slice(q_end, ((1 - late) * q_half, 0), (q_half, quarter))
+    q_inner = move(join(other, end_other), INNER)
+    sibling1, sum1 = tile_call(place, table, [(own, own_x), (near, near_x)])
+
+    outer_end0, outer_end1, end_mine, mine, sibling1 = after(
+        (outer_end0, outer_end1, end_mine, mine, sibling1), sum1
+    )
+    outer_end_x0 = across_on(outer_end0, (0, 3))
+    outer_end_x1 = across_on(outer_end1, (0, 3))
+
+    mine, end_mine, q_inner, sibling1 = after((mine, end_mine, q_inner, sibling1), outer_end1)
+    sibling1 = lax.ppermute(sibling1, "feat", CORE)
+    parts = [(mine, cores(mine)), (end_mine, cores(end_mine)), (q_inner, cores(q_inner))]
+
+    own, second = after((own, second), second_x, outer_end_x0)
+    r_own, r_near, r_inner = score_call(place, parts, [own, near, second], [own_x, near_x, second_x])
+    to_end = move(r_near, TO_END)
+    to_mid = move(r_inner, INNER)
+    second, second_x = after((second, second_x), r_own)
+    sibling2, sum2 = tile_call(place, table, [(second, second_x)], carried=[sum1, sibling1])
+    sibling2 = lax.ppermute(sibling2, "feat", CORE)
+
+    outer, outer_x = after((outer, outer_x), sum2)
+    (r_outer,) = score_call(place, parts, [outer], [outer_x])
+    to_far = move(r_outer, MID_TO_FAR_END)
+    outer, outer_x = after((outer, outer_x), r_outer)
+    sibling3, sum3 = tile_call(
+        place,
+        table,
+        [],
+        [(outer, outer_x)],
+        [(outer_end0, outer_end_x0), (outer_end1, outer_end_x1)],
+        [sum2],
+    )
+    sibling3 = lax.ppermute(sibling3, "feat", CORE)
+    gram = sum3 + sibling2.astype(jnp.float32) + sibling3.astype(jnp.float32)
+    gram = gram / (count * 4)
+    gram = jnp.where((own_tiles[:, 0] >= 0)[:, None, None], gram, jnp.float32(0.0))
+
+    first = jnp.where(middle, r_own, to_end)
+    rest = jnp.where(middle, to_mid, to_far)
+    low = jnp.where(late == 1, rest, first)
+    high = jnp.where(late == 1, first, rest)
+    both = jnp.concatenate([low, high], axis=1)
+    got = lax.ppermute(both[1], "feat", CORE)
+    left = jnp.where(core == 0, both[0], got)
+    right = jnp.where(core == 0, got, both[0])
+    scores = jnp.concatenate([left, right], axis=1).astype(jnp.float32)
+    return gram[None], scores * example_weights[None, :]
+
+
 def solution(mesh):
     placed = (
         P(("grp", "ex"), "feat"),
@@ -57,8 +339,10 @@
         P(("grp", "ex")),
         P(("grp", "feat"), None, None),
     )
+
+    line = mesh.shape["ex"] == 4 and mesh.shape["feat"] == 4
     return jax.shard_map(
-        local,
+        local_line if line else local_any,
         mesh=mesh,
         in_specs=placed,
         out_specs=(P(("grp", "feat"), "ex", None, None), P(("grp", "feat"), "ex")),

time: 288 us -> 150 us (0.52)
  matrix products: 111 us -> 0 us
  waiting for transfers between devices: 128 us -> 51.3 us
  starting transfers between devices: 0.11 us -> 44.6 us
  Pallas kernels: 0 us -> 29.7 us
  local copies, waits for them, and re-layouts: 29.2 us -> 12.4 us
  between operations: 13.8 us -> 1 us
  other arithmetic: 3.37 us -> 9 us
    dot_general x64 -> x0, matrix products: 111 us -> none  [the longest x42 79.2 us: select_blocks(): jnp.einsum('tnb,gn->tgb', blocks3, onehot, preferred_element_type=jnp.flo...]
    reduce_scatter x1 -> x0, waiting for transfers between devices: 90.8 us -> none  [local(): lax.psum_scatter(tile_terms(blocks3, tile_table).astype(jnp.bfloat16), 'e...]
    ppermute x0 -> x26, waiting for transfers between devices: none -> 51.3 us  [the longest x11 44.2 us: move(): return lax.ppermute(value, 'ex', pairs)]
    ppermute x0 -> x26, starting transfers between devices: none -> 44.6 us  [the longest x11 23.5 us: move(): return lax.ppermute(value, 'ex', pairs)]
    all_gather x2 -> x0, waiting for transfers between devices: 36.2 us -> none  [the longest x1 36.2 us: local(): slab_full = lax.all_gather(slab_grads, 'feat', axis=1, tiled=True)]
    pallas_call x0 -> x5, Pallas kernels: none -> 29.7 us  [the longest x3 19.6 us: tile_call(): pl.pallas_call(kernel, out_shape=[jax.ShapeDtypeStruct((half, B, B), jnp....]
    dot_general x21 -> x0, local copies, waits for them, and re-layouts: 14.2 us -> none  [select_blocks(): jnp.einsum('tnb,gn->tgb', blocks3, onehot, preferred_element_type=jnp.flo...]
    while x42 -> x0, local copies, waits for them, and re-layouts: 7.9 us -> none
  transfers between devices with their start and end apart: 3 -> 26, of which waited for: 2 -> 13; matrix products, arithmetic and copies ran while one was open for 46% -> 5% of each run, Pallas kernels for 0% -> 20%
where the time goes in v2:
time: 150 us; the launch traced here: 148 us
  waiting for transfers between devices  51.3 us (34%)
  starting transfers between devices  44.6 us (30%)
  Pallas kernels  29.7 us (20%)
  local copies, waits for them, and re-layouts  12.4 us (8%)
  other arithmetic  9 us (6%)
    ppermute x11, waiting for transfers between devices, move(): return lax.ppermute(value, 'ex', pairs)  44.2 us
    ppermute x11, starting transfers between devices, move(): return lax.ppermute(value, 'ex', pairs)  23.5 us
    pallas_call x3, Pallas kernels, tile_call(): pl.pallas_call(kernel, out_shape=[jax.ShapeDtypeStruct((half, B, B), jnp....  19.6 us
    pallas_call x2, Pallas kernels, score_call(): pl.pallas_call(kernel, out_shape=[jax.ShapeDtypeStruct((2, group, c), jnp...  10.2 us
    ppermute x3, starting transfers between devices, cores(): return lax.ppermute(value, ('ex', 'feat'), pairs)  6.51 us
    unnamed x30, local copies, waits for them, and re-layouts  5.68 us
    ppermute x1, starting transfers between devices, local_line(): sibling1 = lax.ppermute(sibling1, 'feat', CORE)  4.3 us
    broadcast_in_dim x1, other arithmetic, local_line(): return (gram[None], scores * example_weights[None, :])  4.04 us
  transfers between devices with their start and end apart: 26, of which 13 were waited for; matrix products, arithmetic and copies ran while one was open for 5% of the time, Pallas kernels for 20%

profile of v2, /device:TPU:9, one launch (start us, length us, event | category | flops | bytes accessed | tf_op | source)
XLA Modules:
  0.0 148.0 jit_solution(4017006547887716037)
XLA Ops:
  0.7 1.3 constant_dynamic-slice_fusion.5
  2.7 1.5 %collective-permute-done = bf16[256,1024]{1,0:T(8,128)(2,1)S(1)} collective-permute-done((bf16[256,1024]{1,0:T(8,128)(2,1)S(1)}, bf16[256,1024]{1,0:T(8,128)(2,1)S(1)}, u32[]{:S(2)}, u32[]{:S(2)}) %collective-permute-start) | collective-permute-done | bytes 524320 | tf_op jit(solution)/shard_map/ppermute | solution.py:260
  4.4 4.5 %collective-permute-start.2 = (bf16[256,2048]{1,0:T(8,128)(2,1)S(1)}, bf16[256,2048]{1,0:T(8,128)(2,1)}, u32[]{:S(2)}, u32[]{:S(2)}) collective-permute-start(bf16[256,2048]{1,0:T(8,128)(2,1)S(1)} %pad_maximum_fusion.refs_0_), channel_id=1, source_target_pairs={{4,8},{8,4},{5,9},{9,5},{6,10},{10,6},{7,11},{11,7},{20,24},{24,20... | collective-permute-start | bytes 3145736 | tf_op jit(solution)/shard_map/ppermute | solution.py:233
  8.9 1.3 collective-permute-start.4
  10.2 1.2 collective-permute-start.3
  11.4 0.8 collective-permute-done.3
  12.5 16.4 %collective-permute-done.1.refs_2_ = bf16[256,2048]{1,0:T(8,128)(2,1)S(1)} collective-permute-done((bf16[256,2048]{1,0:T(8,128)(2,1)S(1)}, bf16[256,2048]{1,0:T(8,128)(2,1)S(1)}, u32[]{:S(2)}, u32[]{:S(2)}) %collective-permute-start.1) | collective-permute-done | bytes 1048608 | tf_op jit(solution)/shard_map/ppermute | solution.py:233
  28.9 3.0 %collective-permute-done.2 = bf16[256,2048]{1,0:T(8,128)(2,1)} collective-permute-done((bf16[256,2048]{1,0:T(8,128)(2,1)S(1)}, bf16[256,2048]{1,0:T(8,128)(2,1)}, u32[]{:S(2)}, u32[]{:S(2)}) %collective-permute-start.2) | collective-permute-done | bytes 1048608 | tf_op jit(solution)/shard_map/ppermute | solution.py:233
  31.9 0.8 collective-permute-done.4.refs_1_
  32.7 1.0 copy-done.6
  33.7 2.3 %collective-permute-start.5 = (bf16[256,2048]{1,0:T(8,128)(2,1)}, bf16[256,2048]{1,0:T(8,128)(2,1)}, u32[]{:S(2)}, u32[]{:S(2)}) collective-permute-start(bf16[256,2048]{1,0:T(8,128)(2,1)} %collective-permute-done.2), channel_id=1, source_target_pairs={{4,0},{8,12},{5,1},{9,13},{6,2},{10,14},{7,3},{11,15},{20,16},{24,... | collective-permute-start | bytes 3145736 | tf_op jit(solution)/shard_map/ppermute | solution.py:233
  35.9 2.7 %collective-permute-start.6 = (bf16[256,2048]{1,0:T(8,128)(2,1)S(1)}, bf16[256,2048]{1,0:T(8,128)(2,1)S(1)}, u32[]{:S(2)}, u32[]{:S(2)}) collective-permute-start(bf16[256,2048]{1,0:T(8,128)(2,1)S(1)} %collective-permute-done.1.refs_2_), channel_id=1, source_target_pairs={{4,8},{8,4},{5,9},{9,5},{6,10},{10,6},{7,11},{11,7},{20,24},{24,20... | collective-permute-start | bytes 3145736 | tf_op jit(solution)/shard_map/ppermute | solution.py:233
  38.6 1.3 collective-permute-start.7
  39.9 1.3 collective-permute-start.12
  41.2 2.1 %constant_dynamic-slice_fusion.1 = (bf16[256,1024]{1,0:T(8,128)(2,1)S(1)}, bf16[256,1024]{1,0:T(8,128)(2,1)}) fusion(bf16[512,1024]{1,0:T(8,128)(2,1)} %param.7, s32[]{:T(128)S(6)} %select_n.97, s32[]{:T(128)S(6)} %mul.33), kind=kLoop, calls=%fused_computation.27 | loop fusion | bytes 2097160 | tf_op jit(solution)/shard_map/dynamic_slice | solution.py:273
  43.2 12.9 %collective-permute-done.5 = bf16[256,2048]{1,0:T(8,128)(2,1)} collective-permute-done((bf16[256,2048]{1,0:T(8,128)(2,1)}, bf16[256,2048]{1,0:T(8,128)(2,1)}, u32[]{:S(2)}, u32[]{:S(2)}) %collective-permute-start.5) | collective-permute-done | bytes 1048608 | tf_op jit(solution)/shard_map/ppermute | solution.py:233
  56.1 4.6 %collective-permute-done.6.refs_0_ = bf16[256,2048]{1,0:T(8,128)(2,1)S(1)} collective-permute-done((bf16[256,2048]{1,0:T(8,128)(2,1)S(1)}, bf16[256,2048]{1,0:T(8,128)(2,1)S(1)}, u32[]{:S(2)}, u32[]{:S(2)}) %collective-permute-start.6) | collective-permute-done | bytes 1048608 | tf_op jit(solution)/shard_map/ppermute | solution.py:233
  61.3 1.3 broadcast_select_fusion.refs_4_.refs_0_
  62.7 1.7 %collective-permute-done.12 = bf16[512,1024]{1,0:T(8,128)(2,1)} collective-permute-done((bf16[512,1024]{1,0:T(8,128)(2,1)}, bf16[512,1024]{1,0:T(8,128)(2,1)}, u32[]{:S(2)}, u32[]{:S(2)}) %collective-permute-start.12) | collective-permute-done | bytes 1048608 | tf_op jit(solution)/shard_map/ppermute | solution.py:233
  64.3 2.1 %constant_dynamic-slice_fusion = (bf16[256,1024]{1,0:T(8,128)(2,1)S(1)}, bf16[256,1024]{1,0:T(8,128)(2,1)}) fusion(bf16[512,1024]{1,0:T(8,128)(2,1)} %collective-permute-done.12, s32[]{:T(128)S(6)} %select_n.97, s32[]{:T(128)S(6)} %mul.33), kind=kLoop, calls=%fused_computation.26 | loop fusion | bytes 2097160 | tf_op jit(solution)/shard_map/dynamic_slice | solution.py:284
  66.4 1.1 pad_maximum_fusion.1
  67.5 2.6 %collective-permute-start.14 = (bf16[512,1024]{1,0:T(8,128)(2,1)}, bf16[512,1024]{1,0:T(8,128)(2,1)}, u32[]{:S(2)}, u32[]{:S(2)}) collective-permute-start(bf16[512,1024]{1,0:T(8,128)(2,1)} %pad_maximum_fusion.1), channel_id=1, source_target_pairs={{4,8},{8,4},{5,9},{9,5},{6,10},{10,6},{7,11},{11,7},{20,24},{24,20... | collective-permute-start | bytes 3145736 | tf_op jit(solution)/shard_map/ppermute | solution.py:233
  70.1 1.1 fusion.9
  71.2 2.1 %collective-permute-start.10 = (bf16[128,2048]{1,0:T(8,128)(2,1)}, bf16[128,2048]{1,0:T(8,128)(2,1)}, u32[]{:S(2)}, u32[]{:S(2)}) collective-permute-start(bf16[128,2048]{1,0:T(8,128)(2,1)} %get-tuple-element.85), channel_id=1, source_target_pairs={{4,0},{8,12},{5,1},{9,13},{6,2},{10,14},{7,3},{11,15},{20,16},{24,... | collective-permute-start | bytes 1572872 | tf_op jit(solution)/shard_map/ppermute | solution.py:233
  73.2 2.1 %collective-permute-start.11 = (bf16[128,2048]{1,0:T(8,128)(2,1)}, bf16[128,2048]{1,0:T(8,128)(2,1)}, u32[]{:S(2)}, u32[]{:S(2)}) collective-permute-start(bf16[128,2048]{1,0:T(8,128)(2,1)} %get-tuple-element.84), channel_id=1, source_target_pairs={{4,0},{8,12},{5,1},{9,13},{6,2},{10,14},{7,3},{11,15},{20,16},{24,... | collective-permute-start | bytes 1572872 | tf_op jit(solution)/shard_map/ppermute | solution.py:233
  75.8 1.2 copy-done.4
  77.0 1.2 copy-done.7
  78.2 8.0 %shard_map.77 = (bf16[42,128,128]{2,1,0:T(8,128)(2,1)S(1)}, f32[42,128,128]{2,1,0:T(8,128)S(1)}) custom-call(s32[5]{0:T(128)S(1)} %pad_add_fusion.1.place_ref, s32[84,2]{1,0:T(8,128)S(1)} %fusion.5.table_ref, bf16[256,2048]{1,0:T(8,128)(2,1)S(1)} %pad_maximum_fusion.refs_0_, bf16[256,2048]{1,0:T(8,128)(2,1)S(1)} %copy-done.7, ...), custom_call_target="tpu_custom_call" | custom-call | tf_op jit(solution)/shard_map/pallas_call | solution.py:136
  86.3 5.6 %collective-permute-done.11.refs_4_ = bf16[128,2048]{1,0:T(8,128)(2,1)} collective-permute-done((bf16[128,2048]{1,0:T(8,128)(2,1)}, bf16[128,2048]{1,0:T(8,128)(2,1)}, u32[]{:S(2)}, u32[]{:S(2)}) %collective-permute-start.11) | collective-permute-done | bytes 524320 | tf_op jit(solution)/shard_map/ppermute | solution.py:233
  92.6 4.3 %collective-permute-start.18 = (bf16[42,128,128]{2,1,0:T(8,128)(2,1)S(1)}, bf16[42,128,128]{2,1,0:T(8,128)(2,1)S(1)}, u32[]{:S(2)}, u32[]{:S(2)}) collective-permute-start(bf16[42,128,128]{2,1,0:T(8,128)(2,1)S(1)} %get-tuple-element.67), channel_id=1, source_target_pairs={{0,1},{1,0},{2,3},{3,2},{4,5},{5,4},{6,7},{7,6},{8,9},{9,8},{10,11... | collective-permute-start | bytes 4128776 | tf_op jit(solution)/shard_map/ppermute | solution.py:295
  96.9 1.9 %collective-permute-start.17 = (bf16[512,1024]{1,0:T(8,128)(2,1)}, bf16[512,1024]{1,0:T(8,128)(2,1)S(1)}, u32[]{:S(2)}, u32[]{:S(2)}) collective-permute-start(bf16[512,1024]{1,0:T(8,128)(2,1)} %collective-permute-done.14.refs_10_.refs_6_), channel_id=1, source_target_pairs={{4,5},{5,4},{6,7},{7,6},{8,9},{9,8},{10,11},{11,10},{20,21},{21,20... | collective-permute-start | bytes 3145736 | tf_op jit(solution)/shard_map/ppermute | solution.py:247
  98.8 2.2 %collective-permute-start.8 = (bf16[256,2048]{1,0:T(8,128)(2,1)S(1)}, bf16[256,2048]{1,0:T(8,128)(2,1)S(1)}, u32[]{:S(2)}, u32[]{:S(2)}) collective-permute-start(bf16[256,2048]{1,0:T(8,128)(2,1)S(1)} %collective-permute-done.6.refs_0_), channel_id=1, source_target_pairs={{4,6},{5,7},{6,4},{7,5},{8,10},{9,11},{10,8},{11,9},{20,22},{21,23... | collective-permute-start | bytes 3145736 | tf_op jit(solution)/shard_map/ppermute | solution.py:240
  101.0 2.7 %collective-permute-start.15 = (bf16[256,1024]{1,0:T(8,128)(2,1)S(1)}, bf16[256,1024]{1,0:T(8,128)(2,1)S(1)}, u32[]{:S(2)}, u32[]{:S(2)}) collective-permute-start(bf16[256,1024]{1,0:T(8,128)(2,1)S(1)} %copy-done.1), channel_id=1, source_target_pairs={{4,5},{5,4},{6,7},{7,6},{8,9},{9,8},{10,11},{11,10},{20,21},{21,20... | collective-permute-start | bytes 1572872 | tf_op jit(solution)/shard_map/ppermute | solution.py:247
  103.7 1.9 %collective-permute-start.16 = (bf16[256,1024]{1,0:T(8,128)(2,1)S(1)}, bf16[256,1024]{1,0:T(8,128)(2,1)S(1)}, u32[]{:S(2)}, u32[]{:S(2)}) collective-permute-start(bf16[256,1024]{1,0:T(8,128)(2,1)S(1)} %copy-done.2), channel_id=1, source_target_pairs={{4,5},{5,4},{6,7},{7,6},{8,9},{9,8},{10,11},{11,10},{20,21},{21,20... | collective-permute-start | bytes 1572872 | tf_op jit(solution)/shard_map/ppermute | solution.py:247
  106.3 1.2 collective-permute-done.16.refs_9_.refs_5_
  107.5 6.7 %shard_map.78 = (bf16[2,256,256]{2,1,0:T(8,128)(2,1)S(1)}, bf16[2,256,256]{2,1,0:T(8,128)(2,1)}, bf16[2,256,256]{2,1,0:T(8,128)(2,1)}) custom-call(s32[5]{0:T(128)S(1)} %pad_add_fusion.1.place_ref, bf16[256,2048]{1,0:T(8,128)(2,1)S(1)} %pad_maximum_fusion.refs_0_, bf16[256,2048]{1,0:T(8,128)(2,1)S(1)} %copy-done.8, bf16[256,2048]{1,0:T(8,128)(2,1)S(1)} %copy-done.5, ...), custom_call_target="tpu_custom_call" | custom-call | tf_op jit(solution)/shard_map/pallas_call | solution.py:204
  114.3 2.7 %collective-permute-start.22 = (bf16[2,256,256]{2,1,0:T(8,128)(2,1)}, bf16[2,256,256]{2,1,0:T(8,128)(2,1)S(1)}, u32[]{:S(2)}, u32[]{:S(2)}) collective-permute-start(bf16[2,256,256]{2,1,0:T(8,128)(2,1)} %get-tuple-element.76), channel_id=1, source_target_pairs={{4,8},{8,4},{5,9},{9,5},{6,10},{10,6},{7,11},{11,7},{20,24},{24,20... | collective-permute-start | bytes 786440 | tf_op jit(solution)/shard_map/ppermute | solution.py:233
  117.0 2.0 %collective-permute-start.24 = (bf16[2,256,256]{2,1,0:T(8,128)(2,1)}, bf16[2,256,256]{2,1,0:T(8,128)(2,1)}, u32[]{:S(2)}, u32[]{:S(2)}) collective-permute-start(bf16[2,256,256]{2,1,0:T(8,128)(2,1)} %get-tuple-element.77), channel_id=1, source_target_pairs={{4,0},{8,12},{5,1},{9,13},{6,2},{10,14},{7,3},{11,15},{20,16},{24,... | collective-permute-start | bytes 786440 | tf_op jit(solution)/shard_map/ppermute | solution.py:233
  119.0 5.9 %shard_map.79 = (bf16[42,128,128]{2,1,0:T(8,128)(2,1)}, f32[42,128,128]{2,1,0:T(8,128)S(1)}) custom-call(s32[5]{0:T(128)S(1)} %pad_add_fusion.1.place_ref, s32[84,2]{1,0:T(8,128)S(1)} %fusion.5.table_ref, bf16[256,2048]{1,0:T(8,128)(2,1)S(1)} %broadcast_select_fusion.refs_4_.refs_0_, bf16[256,2048]{1,0:T(8,128)(2,1)S(1)} %collective-permute-done.9.refs_5_.refs_1_, ...), custom_call_target="tpu_custom_call" | custom-call | tf_op jit(solution)/shard_map/pallas_call | solution.py:136
  124.9 3.4 %shard_map.80 = bf16[2,256,256]{2,1,0:T(8,128)(2,1)S(1)} custom-call(s32[5]{0:T(128)S(1)} %pad_add_fusion.1.place_ref, bf16[256,2048]{1,0:T(8,128)(2,1)S(1)} %collective-permute-done.6.refs_0_, bf16[256,2048]{1,0:T(8,128)(2,1)S(1)} %collective-permute-done.8.refs_1_, bf16[256,1024]{1,0:T(8,128)(2,1)S(1)} %copy-done.1, ...), custom_call_target="tpu_custom_call" | custom-call | tf_op jit(solution)/shard_map/pallas_call | solution.py:204
  128.4 1.3 collective-permute-start.23
  129.7 5.7 %shard_map.81 = (bf16[42,128,128]{2,1,0:T(8,128)(2,1)}, f32[42,128,128]{2,1,0:T(8,128)S(1)}) custom-call(s32[5]{0:T(128)S(1)} %pad_add_fusion.1.place_ref, s32[84,2]{1,0:T(8,128)S(1)} %fusion.5.table_ref, bf16[256,2048]{1,0:T(8,128)(2,1)S(1)} %collective-permute-done.6.refs_0_, bf16[256,2048]{1,0:T(8,128)(2,1)S(1)} %collective-permute-done.8.refs_1_, ...), custom_call_target="tpu_custom_call" | custom-call | tf_op jit(solution)/shard_map/pallas_call | solution.py:136
  135.4 1.5 %copy-done.9 = f32[42,128,128]{2,1,0:T(8,128)} copy-done((f32[42,128,128]{2,1,0:T(8,128)}, f32[42,128,128]{2,1,0:T(8,128)S(1)}, u32[]{:S(2)}) %copy-start.9) | copy-done | bytes 2752536
  136.9 1.3 collective-permute-start.21
  139.7 2.1 %collective-permute-done.25 = bf16[512,256]{1,0:T(8,128)(2,1)S(1)} collective-permute-done((bf16[512,256]{1,0:T(8,128)(2,1)S(1)}, bf16[512,256]{1,0:T(8,128)(2,1)S(1)}, u32[]{:S(2)}, u32[]{:S(2)}) %collective-permute-start.25) | collective-permute-done | bytes 262176 | tf_op jit(solution)/shard_map/ppermute | solution.py:328
  141.8 1.1 broadcast_select_fusion.6
  142.9 1.1 convert_multiply_fusion
  144.0 4.0 %select_bitcast_fusion = f32[1,42,128,128]{3,2,1,0:T(8,128)} fusion(bf16[42,128,128]{2,1,0:T(8,128)(2,1)} %collective-permute-done.21, f32[42,128,128]{2,1,0:T(8,128)S(1)} %copy-done.10, bf16[42,128,128]{2,1,0:T(8,128)(2,1)} %collective-permute-done.20, pred[42]{0:T(512)(128)(4,1)S(1)} %compare_bitcast_fusion), kind=kLoop, calls=%fused_computation | loop fusion | flops 4128768 | bytes 8257578 | tf_op jit(solution)/shard_map/broadcast_in_dim | solution.py:332
  (58 shorter events, 5.1 us)
Async XLA Ops:
  0.6 9.5 %copy-start = (s32[1,168,2]{1,2,0:T(2,128)S(1)}, s32[1,168,2]{1,2,0:T(2,128)}, u32[]{:S(2)}) copy-start(s32[1,168,2]{1,2,0:T(2,128)} %param.9) | copy-start | bytes 4036
  1.9 2.3 %collective-permute-start = (bf16[256,1024]{1,0:T(8,128)(2,1)S(1)}, bf16[256,1024]{1,0:T(8,128)(2,1)S(1)}, u32[]{:S(2)}, u32[]{:S(2)}) collective-permute-start(bf16[256,1024]{1,0:T(8,128)(2,1)S(1)} %get-tuple-element.87), channel_id=1, source_target_pairs={{0,1},{1,0},{2,3},{3,2},{4,5},{5,4},{6,7},{7,6},{8,9},{9,8},{10,11... | collective-permute-start | bytes 1572872 | tf_op jit(solution)/shard_map/ppermute | solution.py:260
  4.3 24.5 %collective-permute-start.1 = (bf16[256,2048]{1,0:T(8,128)(2,1)S(1)}, bf16[256,2048]{1,0:T(8,128)(2,1)S(1)}, u32[]{:S(2)}, u32[]{:S(2)}) collective-permute-start(bf16[256,2048]{1,0:T(8,128)(2,1)S(1)} %pad_maximum_fusion.refs_0_), channel_id=1, source_target_pairs={{0,4},{4,0},{8,12},{12,8},{1,5},{5,1},{9,13},{13,9},{2,6},{6,2},{1... | collective-permute-start | bytes 3145736 | tf_op jit(solution)/shard_map/ppermute | solution.py:233
  4.4 27.5 %collective-permute-start.2 = (bf16[256,2048]{1,0:T(8,128)(2,1)S(1)}, bf16[256,2048]{1,0:T(8,128)(2,1)}, u32[]{:S(2)}, u32[]{:S(2)}) collective-permute-start(bf16[256,2048]{1,0:T(8,128)(2,1)S(1)} %pad_maximum_fusion.refs_0_), channel_id=1, source_target_pairs={{4,8},{8,4},{5,9},{9,5},{6,10},{10,6},{7,11},{11,7},{20,24},{24,20... | collective-permute-start | bytes 3145736 | tf_op jit(solution)/shard_map/ppermute | solution.py:233
  8.9 23.8 %collective-permute-start.4 = (bf16[256,2048]{1,0:T(8,128)(2,1)S(1)}, bf16[256,2048]{1,0:T(8,128)(2,1)S(1)}, u32[]{:S(2)}, u32[]{:S(2)}) collective-permute-start(bf16[256,2048]{1,0:T(8,128)(2,1)S(1)} %pad_maximum_fusion.refs_0_), channel_id=1, source_target_pairs={{0,2},{2,0},{1,3},{3,1},{4,6},{6,4},{5,7},{7,5},{8,10},{10,8},{9,1... | collective-permute-start | bytes 3145736 | tf_op jit(solution)/shard_map/ppermute | solution.py:236
  10.2 2.0 %collective-permute-start.3 = (s32[42,2]{0,1:T(2,128)S(1)}, s32[42,2]{0,1:T(2,128)S(1)}, u32[]{:S(2)}, u32[]{:S(2)}) collective-permute-start(s32[42,2]{0,1:T(2,128)S(1)} %fusion.7), channel_id=1, source_target_pairs={{0,1},{1,0},{2,3},{3,2},{4,5},{5,4},{6,7},{7,6},{8,9},{9,8},{10,11... | collective-permute-start | bytes 1016 | tf_op jit(solution)/shard_map/ppermute | solution.py:251
  28.9 31.9 %copy-start.3 = (bf16[256,2048]{1,0:T(8,128)(2,1)}, bf16[256,2048]{1,0:T(8,128)(2,1)S(1)}, u32[]{:S(2)}) copy-start(bf16[256,2048]{1,0:T(8,128)(2,1)S(1)} %collective-permute-done.1.refs_2_) | copy-start | bytes 3145732
  32.7 1.0 copy-start.6
  33.7 22.5 %collective-permute-start.5 = (bf16[256,2048]{1,0:T(8,128)(2,1)}, bf16[256,2048]{1,0:T(8,128)(2,1)}, u32[]{:S(2)}, u32[]{:S(2)}) collective-permute-start(bf16[256,2048]{1,0:T(8,128)(2,1)} %collective-permute-done.2), channel_id=1, source_target_pairs={{4,0},{8,12},{5,1},{9,13},{6,2},{10,14},{7,3},{11,15},{20,16},{24,... | collective-permute-start | bytes 3145736 | tf_op jit(solution)/shard_map/ppermute | solution.py:233
  35.9 24.8 %collective-permute-start.6 = (bf16[256,2048]{1,0:T(8,128)(2,1)S(1)}, bf16[256,2048]{1,0:T(8,128)(2,1)S(1)}, u32[]{:S(2)}, u32[]{:S(2)}) collective-permute-start(bf16[256,2048]{1,0:T(8,128)(2,1)S(1)} %collective-permute-done.1.refs_2_), channel_id=1, source_target_pairs={{4,8},{8,4},{5,9},{9,5},{6,10},{10,6},{7,11},{11,7},{20,24},{24,20... | collective-permute-start | bytes 3145736 | tf_op jit(solution)/shard_map/ppermute | solution.py:233
  38.6 22.7 %collective-permute-start.7 = (bf16[256,2048]{1,0:T(8,128)(2,1)S(1)}, bf16[256,2048]{1,0:T(8,128)(2,1)}, u32[]{:S(2)}, u32[]{:S(2)}) collective-permute-start(bf16[256,2048]{1,0:T(8,128)(2,1)S(1)} %collective-permute-done.1.refs_2_), channel_id=1, source_target_pairs={{0,2},{2,0},{1,3},{3,1},{4,6},{6,4},{5,7},{7,5},{8,10},{10,8},{9,1... | collective-permute-start | bytes 3145736 | tf_op jit(solution)/shard_map/ppermute | solution.py:236
  39.9 24.5 %collective-permute-start.12 = (bf16[512,1024]{1,0:T(8,128)(2,1)}, bf16[512,1024]{1,0:T(8,128)(2,1)}, u32[]{:S(2)}, u32[]{:S(2)}) collective-permute-start(bf16[512,1024]{1,0:T(8,128)(2,1)} %param.7), channel_id=1, source_target_pairs={{0,4},{12,8},{1,5},{13,9},{2,6},{14,10},{3,7},{15,11},{16,20},{28,... | collective-permute-start | bytes 3145736 | tf_op jit(solution)/shard_map/ppermute | solution.py:233
  66.4 8.9 %copy-start.13 = (s32[4]{0:T(128)S(1)}, s32[4]{0:T(128)}, u32[]{:S(2)}) copy-start(s32[4]{0:T(128)} %constant.74.clone) | copy-start | bytes 52
  66.4 8.9 %copy-start.14 = (s32[4]{0:T(128)S(1)}, s32[4]{0:T(128)}, u32[]{:S(2)}) copy-start(s32[4]{0:T(128)} %constant.75.clone) | copy-start | bytes 52
  67.5 25.1 %collective-permute-start.14 = (bf16[512,1024]{1,0:T(8,128)(2,1)}, bf16[512,1024]{1,0:T(8,128)(2,1)}, u32[]{:S(2)}, u32[]{:S(2)}) collective-permute-start(bf16[512,1024]{1,0:T(8,128)(2,1)} %pad_maximum_fusion.1), channel_id=1, source_target_pairs={{4,8},{8,4},{5,9},{9,5},{6,10},{10,6},{7,11},{11,7},{20,24},{24,20... | collective-permute-start | bytes 3145736 | tf_op jit(solution)/shard_map/ppermute | solution.py:233
  71.2 15.1 %collective-permute-start.10 = (bf16[128,2048]{1,0:T(8,128)(2,1)}, bf16[128,2048]{1,0:T(8,128)(2,1)}, u32[]{:S(2)}, u32[]{:S(2)}) collective-permute-start(bf16[128,2048]{1,0:T(8,128)(2,1)} %get-tuple-element.85), channel_id=1, source_target_pairs={{4,0},{8,12},{5,1},{9,13},{6,2},{10,14},{7,3},{11,15},{20,16},{24,... | collective-permute-start | bytes 1572872 | tf_op jit(solution)/shard_map/ppermute | solution.py:233
  73.2 18.6 %collective-permute-start.11 = (bf16[128,2048]{1,0:T(8,128)(2,1)}, bf16[128,2048]{1,0:T(8,128)(2,1)}, u32[]{:S(2)}, u32[]{:S(2)}) collective-permute-start(bf16[128,2048]{1,0:T(8,128)(2,1)} %get-tuple-element.84), channel_id=1, source_target_pairs={{4,0},{8,12},{5,1},{9,13},{6,2},{10,14},{7,3},{11,15},{20,16},{24,... | collective-permute-start | bytes 1572872 | tf_op jit(solution)/shard_map/ppermute | solution.py:233
  75.4 28.3 %collective-permute-start.9 = (bf16[256,2048]{1,0:T(8,128)(2,1)S(1)}, bf16[256,2048]{1,0:T(8,128)(2,1)S(1)}, u32[]{:S(2)}, u32[]{:S(2)}) collective-permute-start(bf16[256,2048]{1,0:T(8,128)(2,1)S(1)} %broadcast_select_fusion.refs_4_.refs_0_), channel_id=1, source_target_pairs={{0,2},{2,0},{1,3},{3,1},{4,6},{6,4},{5,7},{7,5},{8,10},{10,8},{9,1... | collective-permute-start | bytes 3145736 | tf_op jit(solution)/shard_map/ppermute | solution.py:236
  75.8 1.2 copy-start.4
  77.0 1.2 copy-start.7
  78.2 22.8 %copy-start.1 = (bf16[256,1024]{1,0:T(8,128)(2,1)S(1)}, bf16[256,1024]{1,0:T(8,128)(2,1)}, u32[]{:S(2)}) copy-start(bf16[256,1024]{1,0:T(8,128)(2,1)} %get-tuple-element.61.refs_6_.refs_2_) | copy-start | bytes 1572868
  78.2 25.5 %copy-start.2 = (bf16[256,1024]{1,0:T(8,128)(2,1)S(1)}, bf16[256,1024]{1,0:T(8,128)(2,1)}, u32[]{:S(2)}) copy-start(bf16[256,1024]{1,0:T(8,128)(2,1)} %get-tuple-element.62.refs_8_.refs_4_) | copy-start | bytes 1572868
  78.2 29.3 %copy-start.5 = (bf16[256,2048]{1,0:T(8,128)(2,1)S(1)}, bf16[256,2048]{1,0:T(8,128)(2,1)}, u32[]{:S(2)}) copy-start(bf16[256,2048]{1,0:T(8,128)(2,1)} %copy-done.3) | copy-start | bytes 3145732
  78.2 29.3 %copy-start.8 = (bf16[256,2048]{1,0:T(8,128)(2,1)S(1)}, bf16[256,2048]{1,0:T(8,128)(2,1)}, u32[]{:S(2)}) copy-start(bf16[256,2048]{1,0:T(8,128)(2,1)} %copy-done.6) | copy-start | bytes 3145732
  91.9 9.1 %collective-permute-start.13 = (bf16[128,2048]{1,0:T(8,128)(2,1)}, bf16[128,2048]{1,0:T(8,128)(2,1)S(1)}, u32[]{:S(2)}, u32[]{:S(2)}) collective-permute-start(bf16[128,2048]{1,0:T(8,128)(2,1)} %collective-permute-done.10.refs_2_), channel_id=1, source_target_pairs={{0,2},{1,3},{2,0},{3,1},{12,14},{13,15},{14,12},{15,13},{16,18},{1... | collective-permute-start | bytes 1572872 | tf_op jit(solution)/shard_map/ppermute | solution.py:240
  92.6 26.4 %collective-permute-start.18 = (bf16[42,128,128]{2,1,0:T(8,128)(2,1)S(1)}, bf16[42,128,128]{2,1,0:T(8,128)(2,1)S(1)}, u32[]{:S(2)}, u32[]{:S(2)}) collective-permute-start(bf16[42,128,128]{2,1,0:T(8,128)(2,1)S(1)} %get-tuple-element.67), channel_id=1, source_target_pairs={{0,1},{1,0},{2,3},{3,2},{4,5},{5,4},{6,7},{7,6},{8,9},{9,8},{10,11... | collective-permute-start | bytes 4128776 | tf_op jit(solution)/shard_map/ppermute | solution.py:295
  96.9 10.6 %collective-permute-start.17 = (bf16[512,1024]{1,0:T(8,128)(2,1)}, bf16[512,1024]{1,0:T(8,128)(2,1)S(1)}, u32[]{:S(2)}, u32[]{:S(2)}) collective-permute-start(bf16[512,1024]{1,0:T(8,128)(2,1)} %collective-permute-done.14.refs_10_.refs_6_), channel_id=1, source_target_pairs={{4,5},{5,4},{6,7},{7,6},{8,9},{9,8},{10,11},{11,10},{20,21},{21,20... | collective-permute-start | bytes 3145736 | tf_op jit(solution)/shard_map/ppermute | solution.py:247
  98.8 26.1 %collective-permute-start.8 = (bf16[256,2048]{1,0:T(8,128)(2,1)S(1)}, bf16[256,2048]{1,0:T(8,128)(2,1)S(1)}, u32[]{:S(2)}, u32[]{:S(2)}) collective-permute-start(bf16[256,2048]{1,0:T(8,128)(2,1)S(1)} %collective-permute-done.6.refs_0_), channel_id=1, source_target_pairs={{4,6},{5,7},{6,4},{7,5},{8,10},{9,11},{10,8},{11,9},{20,22},{21,23... | collective-permute-start | bytes 3145736 | tf_op jit(solution)/shard_map/ppermute | solution.py:240
  101.0 4.6 %collective-permute-start.15 = (bf16[256,1024]{1,0:T(8,128)(2,1)S(1)}, bf16[256,1024]{1,0:T(8,128)(2,1)S(1)}, u32[]{:S(2)}, u32[]{:S(2)}) collective-permute-start(bf16[256,1024]{1,0:T(8,128)(2,1)S(1)} %copy-done.1), channel_id=1, source_target_pairs={{4,5},{5,4},{6,7},{7,6},{8,9},{9,8},{10,11},{11,10},{20,21},{21,20... | collective-permute-start | bytes 1572872 | tf_op jit(solution)/shard_map/ppermute | solution.py:247
  103.7 3.8 %collective-permute-start.16 = (bf16[256,1024]{1,0:T(8,128)(2,1)S(1)}, bf16[256,1024]{1,0:T(8,128)(2,1)S(1)}, u32[]{:S(2)}, u32[]{:S(2)}) collective-permute-start(bf16[256,1024]{1,0:T(8,128)(2,1)S(1)} %copy-done.2), channel_id=1, source_target_pairs={{4,5},{5,4},{6,7},{7,6},{8,9},{9,8},{10,11},{11,10},{20,21},{21,20... | collective-permute-start | bytes 1572872 | tf_op jit(solution)/shard_map/ppermute | solution.py:247
  105.6 24.1 %collective-permute-start.19 = (bf16[128,2048]{1,0:T(8,128)(2,1)}, bf16[128,2048]{1,0:T(8,128)(2,1)S(1)}, u32[]{:S(2)}, u32[]{:S(2)}) collective-permute-start(bf16[128,2048]{1,0:T(8,128)(2,1)} %collective-permute-done.11.refs_4_), channel_id=1, source_target_pairs={{0,2},{1,3},{2,0},{3,1},{12,14},{13,15},{14,12},{15,13},{16,18},{1... | collective-permute-start | bytes 1572872 | tf_op jit(solution)/shard_map/ppermute | solution.py:240
  114.3 24.0 %collective-permute-start.22 = (bf16[2,256,256]{2,1,0:T(8,128)(2,1)}, bf16[2,256,256]{2,1,0:T(8,128)(2,1)S(1)}, u32[]{:S(2)}, u32[]{:S(2)}) collective-permute-start(bf16[2,256,256]{2,1,0:T(8,128)(2,1)} %get-tuple-element.76), channel_id=1, source_target_pairs={{4,8},{8,4},{5,9},{9,5},{6,10},{10,6},{7,11},{11,7},{20,24},{24,20... | collective-permute-start | bytes 786440 | tf_op jit(solution)/shard_map/ppermute | solution.py:233
  117.0 21.3 %collective-permute-start.24 = (bf16[2,256,256]{2,1,0:T(8,128)(2,1)}, bf16[2,256,256]{2,1,0:T(8,128)(2,1)}, u32[]{:S(2)}, u32[]{:S(2)}) collective-permute-start(bf16[2,256,256]{2,1,0:T(8,128)(2,1)} %get-tuple-element.77), channel_id=1, source_target_pairs={{4,0},{8,12},{5,1},{9,13},{6,2},{10,14},{7,3},{11,15},{20,16},{24,... | collective-permute-start | bytes 786440 | tf_op jit(solution)/shard_map/ppermute | solution.py:233
  128.4 9.9 %collective-permute-start.23 = (bf16[2,256,256]{2,1,0:T(8,128)(2,1)S(1)}, bf16[2,256,256]{2,1,0:T(8,128)(2,1)S(1)}, u32[]{:S(2)}, u32[]{:S(2)}) collective-permute-start(bf16[2,256,256]{2,1,0:T(8,128)(2,1)S(1)} %shard_map.80), channel_id=1, source_target_pairs={{4,12},{8,0},{5,13},{9,1},{6,14},{10,2},{7,15},{11,3},{20,28},{24,... | collective-permute-start | bytes 786440 | tf_op jit(solution)/shard_map/ppermute | solution.py:233
  135.4 1.5 %copy-start.9 = (f32[42,128,128]{2,1,0:T(8,128)}, f32[42,128,128]{2,1,0:T(8,128)S(1)}, u32[]{:S(2)}) copy-start(f32[42,128,128]{2,1,0:T(8,128)S(1)} %get-tuple-element.73) | copy-start | bytes 8257540
  136.9 5.9 %copy-start.12 = (f32[512]{0:T(512)S(1)}, f32[512]{0:T(512)}, u32[]{:S(2)}) copy-start(f32[512]{0:T(512)} %param.8) | copy-start | bytes 6148
  136.9 7.1 %collective-permute-start.21 = (bf16[42,128,128]{2,1,0:T(8,128)(2,1)}, bf16[42,128,128]{2,1,0:T(8,128)(2,1)}, u32[]{:S(2)}, u32[]{:S(2)}) collective-permute-start(bf16[42,128,128]{2,1,0:T(8,128)(2,1)} %get-tuple-element.75), channel_id=1, source_target_pairs={{0,1},{1,0},{2,3},{3,2},{4,5},{5,4},{6,7},{7,6},{8,9},{9,8},{10,11... | collective-permute-start | bytes 4128776 | tf_op jit(solution)/shard_map/ppermute | solution.py:318
  138.3 5.7 %collective-permute-start.20 = (bf16[42,128,128]{2,1,0:T(8,128)(2,1)}, bf16[42,128,128]{2,1,0:T(8,128)(2,1)}, u32[]{:S(2)}, u32[]{:S(2)}) collective-permute-start(bf16[42,128,128]{2,1,0:T(8,128)(2,1)} %get-tuple-element.74), channel_id=1, source_target_pairs={{0,1},{1,0},{2,3},{3,2},{4,5},{5,4},{6,7},{7,6},{8,9},{9,8},{10,11... | collective-permute-start | bytes 4128776 | tf_op jit(solution)/shard_map/ppermute | solution.py:304
  138.4 0.7 copy-start.11
  138.4 5.6 %copy-start.10 = (f32[42,128,128]{2,1,0:T(8,128)S(1)}, f32[42,128,128]{2,1,0:T(8,128)}, u32[]{:S(2)}) copy-start(f32[42,128,128]{2,1,0:T(8,128)} %copy-done.9) | copy-start | bytes 8257540
  139.1 2.7 %collective-permute-start.25 = (bf16[512,256]{1,0:T(8,128)(2,1)S(1)}, bf16[512,256]{1,0:T(8,128)(2,1)S(1)}, u32[]{:S(2)}, u32[]{:S(2)}) collective-permute-start(bf16[512,256]{1,0:T(8,128)(2,1)S(1)} %fusion.2), channel_id=1, source_target_pairs={{0,1},{1,0},{2,3},{3,2},{4,5},{5,4},{6,7},{7,6},{8,9},{9,8},{10,11... | collective-permute-start | bytes 786440 | tf_op jit(solution)/shard_map/ppermute | solution.py:328

commit v3 on v0

--- a/solution.py
+++ b/solution.py
@@ -3,6 +3,8 @@
 import jax
 import jax.numpy as jnp
 from jax import lax
+from jax.experimental import pallas as pl
+from jax.experimental.pallas import tpu as pltpu
 from jax.sharding import PartitionSpec as P
 
 B = 128
@@ -30,7 +32,7 @@
     return lax.map(group_tiles, groups).reshape(-1, blocks3.shape[2], blocks3.shape[2])
 
 
-def local(slab_grads, query_grads, example_weights, tile_owner):
+def local_any(slab_grads, query_grads, example_weights, tile_owner):
     tile_table = tile_owner[0]
     tok_count = slab_grads.shape[0]
     slab_full = lax.all_gather(slab_grads, "feat", axis=1, tiled=True)
@@ -50,6 +52,434 @@
     return (gram, scores)
 
 
+PAIR = ((0, 1), (1, 0), (2, 3), (3, 2))
+INNER = ((1, 2), (2, 1))
+TO_END = ((1, 0), (2, 3))
+TO_MID = ((0, 1), (3, 2))
+END_TO_FAR_MID = ((0, 2), (3, 1))
+MID_TO_FAR_END = ((1, 3), (2, 0))
+CORE = ((0, 1), (1, 0), (2, 3), (3, 2))
+ACROSS = ((0, 2), (2, 0), (1, 3), (3, 1))
+
+
+def plan(batches, own_count):
+    out = []
+    for sides in batches:
+        for side in range(2):
+            at = own_count
+            for given, start, count, *flip in sides[side]:
+                for plane, array in zip((1, 0), given) if isinstance(given, tuple) else [(2, given)]:
+                    wide = array.shape[1]
+                    if any(flip):
+                        out.append((array, start, count, side, at, 0, wide // 2, wide // 2, plane))
+                        out.append((array, start, count, side, at, wide // 2, 0, wide // 2, plane))
+                    else:
+                        out.append((array, start, count, side, at, 0, 0, wide, plane))
+                at += count
+    return out
+
+
+def rows_of(batches):
+    return sum(entry[2] for sides in batches[:1] for entry in sides[0])
+
+
+def tile_call(place, table, always, carried=(), carried_sibling=None, part="both", scores=None):
+    tiles = table.shape[0]
+    moves = [plan([always], 0)]
+    arrays = []
+    for some in moves:
+        for array, *_ in some:
+            if not any(array is x for x in arrays):
+                arrays.append(array)
+    where = [[next(i for i, x in enumerate(arrays) if x is m[0]) for m in some] for some in moves]
+    n = len(arrays)
+    n_moves = sum(len(some) for some in moves)
+    wide = arrays[0].shape[1]
+    total = rows_of([always])
+    half = tiles // 2
+    per = wide // B
+    extra = [] if carried_sibling is None else [carried_sibling]
+    carried = list(carried) + extra
+    n_own = len(carried) - len(extra)
+    unroll = max(u for u in range(1, 22) if half // 2 % u == 0)
+    n_out = 2 if part == "both" else 1
+
+    n_scores = len(scores.count) if scores else 0
+    score_arrays = scores.arrays if scores else []
+    n_in = n + len(carried) + len(score_arrays)
+
+    def kernel(place_ref, table_ref, *refs):
+        score_sources = refs[n + len(carried) : n_in]
+        score_outs = refs[n_in + n_out : n_in + n_out + n_scores]
+        refs = refs[: n + len(carried)] + refs[n_in : n_in + n_out] + refs[n_in + n_out + n_scores :]
+        if scores:
+            score_scratch, refs = refs[-3:], refs[:-3]
+            score_copies = scores.copies(score_sources, *score_scratch)
+        row_refs = refs[:n]
+        carried_refs = refs[n : n + len(carried)]
+        out_refs = refs[n + len(carried) : n + len(carried) + n_out]
+        outs = refs[n + len(carried) + n_out : -3 - len(carried)]
+        held = refs[-3 - len(carried) : -3]
+        rows, turned, sems = refs[-3:]
+        held_copies = [
+            pltpu.make_async_copy(ref, held[i], sems.at[n_moves + i])
+            for i, ref in enumerate(carried_refs)
+        ]
+        parts = []
+        for i in range(n_out):
+            for j in range(2):
+                some = pl.ds(j * (half // 2), half // 2)
+                sem = sems.at[n_moves + len(carried) + 2 * i + j]
+                parts.append(pltpu.make_async_copy(outs[i].at[some], out_refs[i].at[some], sem))
+        copies = [[], [], []]
+        at = 0
+        for i, some in enumerate(moves):
+            for (_, start, count, side, to, left, right, columns, plane), index in zip(some, where[i]):
+                source = row_refs[index].at[pl.ds(start, count), pl.ds(left, columns)]
+                into = rows.at[side, pl.ds(to, count), pl.ds(right, columns)]
+                copies[plane].append(pltpu.make_async_copy(source, into, sems.at[at]))
+                at += 1
+
+        def each(some, do):
+            for copy in some:
+                do(copy)
+
+        def rows_do(do):
+            each(copies[2], do)
+            for plane in range(2):
+                if copies[plane]:
+                    pl.when(place_ref[0] == plane)(lambda plane=plane: each(copies[plane], do))
+
+        rows_do(lambda copy: copy.start())
+        each(held_copies, lambda copy: copy.start())
+        if scores:
+            pl.when(place_ref[0] == 1)(lambda: each(score_copies, lambda copy: copy.start()))
+        rows_do(lambda copy: copy.wait())
+
+        for block in range(2 * per):
+            side, column = divmod(block * B, wide)
+            turned[block] = rows[side, :, column : column + B].T
+
+        def product(tile):
+            right = table_ref[tile, 1]
+            return jnp.dot(
+                turned[table_ref[tile, 0]],
+                rows[right // per, :, pl.ds(pl.multiple_of((right % per) * B, B), B)],
+                preferred_element_type=jnp.float32,
+            )
+
+        def sibling(tile, _):
+            sum_ = product(tile)
+            for ref in held[n_own:]:
+                sum_ += ref[tile].astype(jnp.float32)
+            outs[0][tile] = sum_.astype(outs[0].dtype)
+            return 0
+
+        def mine(tile, _):
+            sum_ = product(tile + half)
+            for ref in held[:n_own]:
+                sum_ += ref[tile].astype(jnp.float32)
+            if part == "own":
+                scale = 1.0 / place_ref[7].astype(jnp.float32)
+                sum_ = sum_ * jnp.where(table_ref[tile + half, 2] == 1, scale, 0.0)
+            outs[-1][tile] = sum_
+            return 0
+
+        if part != "own":
+            for copy in held_copies[n_own:]:
+                copy.wait()
+            for j in range(2):
+                lax.fori_loop(j * (half // 2), (j + 1) * (half // 2), sibling, 0, unroll=unroll)
+                parts[j].start()
+        if part != "sibling":
+            for copy in held_copies[:n_own]:
+                copy.wait()
+            for j in range(2):
+                lax.fori_loop(j * (half // 2), (j + 1) * (half // 2), mine, 0, unroll=unroll)
+                parts[j - 2].start()
+        if scores:
+
+            @pl.when(place_ref[0] == 1)
+            def _():
+                scores.compute(place_ref, score_outs, *score_scratch[:2], score_copies)
+
+        for copy in parts:
+            copy.wait()
+
+    smem = pl.BlockSpec(memory_space=pltpu.SMEM)
+    hbm = pl.BlockSpec(memory_space=pltpu.HBM)
+    outs = []
+    if part != "own":
+        outs.append(jax.ShapeDtypeStruct((half, B, B), jnp.bfloat16))
+    if part != "sibling":
+        outs.append(jax.ShapeDtypeStruct((half, B, B), jnp.float32))
+    return pl.pallas_call(
+        kernel,
+        out_shape=outs + (scores.out_shape if scores else []),
+        in_specs=[smem, smem] + [hbm] * n_in,
+        out_specs=[hbm] * n_out + [pl.BlockSpec(memory_space=pltpu.VMEM)] * n_scores,
+        scratch_shapes=[pltpu.VMEM(x.shape, x.dtype) for x in outs + list(carried)]
+        + [
+            pltpu.VMEM((2, total, wide), jnp.bfloat16),
+            pltpu.VMEM((2 * per, B, total), jnp.bfloat16),
+            pltpu.SemaphoreType.DMA((n_moves + len(carried) + 2 * n_out,)),
+        ]
+        + (scores.scratch if scores else []),
+        compiler_params=pltpu.CompilerParams(vmem_limit_bytes=18 * 2**20),
+        cost_estimate=pl.CostEstimate(flops=0, bytes_accessed=0, transcendentals=0),
+    )(place, table, *arrays, *carried, *score_arrays)
+
+
+class Scores:
+    def __init__(self, parts, slots):
+        self.count = [rows_of([slot]) for slot in slots]
+        self.moves = []
+        for i, slot in enumerate(slots):
+            self.moves += plan([slot], sum(self.count[:i]))
+        self.quarter = parts[0][0].shape[1]
+        lengths = [pair[0].shape[0] for pair in parts]
+        for i, pair in enumerate(parts):
+            for j in range(2):
+                at = sum(lengths[:i])
+                self.moves.append((pair[j], 0, lengths[i], 2 + j, at, 0, 0, self.quarter, 2))
+        self.wide = self.moves[0][0].shape[1]
+        self.group = sum(lengths) // 4
+        self.arrays = [move[0] for move in self.moves]
+        self.out_shape = [
+            jax.ShapeDtypeStruct((2, self.group, c), jnp.bfloat16) for c in self.count
+        ]
+        self.scratch = [
+            pltpu.VMEM((2, sum(self.count), self.wide), jnp.bfloat16),
+            pltpu.VMEM((2, 4 * self.group, self.quarter), jnp.bfloat16),
+            pltpu.SemaphoreType.DMA((len(self.moves),)),
+        ]
+
+    def copies(self, sources, rows, query, sems):
+        out = []
+        for i, (_, start, count, side, to, *_) in enumerate(self.moves):
+            into = rows.at[side, pl.ds(to, count)] if side < 2 else query.at[side - 2, pl.ds(to, count)]
+            out.append(pltpu.make_async_copy(sources[i].at[pl.ds(start, count)], into, sems.at[i]))
+        return out
+
+    def compute(self, place_ref, outs, rows, query, copies):
+        group, quarter = self.group, self.quarter
+        per = self.wide // quarter
+        for copy, move in zip(copies, self.moves):
+            if move[3] >= 2:
+                copy.wait()
+        for i, out in enumerate(outs):
+            first = sum(self.count[:i])
+            for copy, move in zip(copies, self.moves):
+                if move[3] < 2 and first <= move[4] < first + self.count[i]:
+                    copy.wait()
+            for j in range(2):
+                total = None
+                for k in range(4):
+                    spot = place_ref[1 + k]
+                    columns = pl.ds(pl.multiple_of((spot % per) * quarter, quarter), quarter)
+                    term = lax.dot_general(
+                        query[j, k * group : (k + 1) * group, :],
+                        rows[spot // per, first : first + self.count[i], columns],
+                        (((1,), (1,)), ((), ())),
+                        preferred_element_type=jnp.float32,
+                    )
+                    total = term if total is None else total + term
+                out[j] = total.astype(out.dtype)
+
+
+def score_call(place, parts, slots):
+    scores = Scores(parts, slots)
+    n, m = len(slots), len(scores.moves)
+
+    def kernel(place_ref, *refs):
+        outs = refs[m : m + n]
+        rows, query, sems = refs[m + n :]
+
+        @pl.when(place_ref[0] == 1)
+        def _():
+            copies = scores.copies(refs[:m], rows, query, sems)
+            for copy, move in zip(copies, scores.moves):
+                if move[3] >= 2:
+                    copy.start()
+            for copy, move in zip(copies, scores.moves):
+                if move[3] < 2:
+                    copy.start()
+            scores.compute(place_ref, outs, rows, query, copies)
+
+    smem = pl.BlockSpec(memory_space=pltpu.SMEM)
+    hbm = pl.BlockSpec(memory_space=pltpu.HBM)
+    vmem = pl.BlockSpec(memory_space=pltpu.VMEM)
+    return pl.pallas_call(
+        kernel,
+        out_shape=scores.out_shape,
+        in_specs=[smem] + [hbm] * m,
+        out_specs=[vmem] * n,
+        scratch_shapes=scores.scratch,
+        compiler_params=pltpu.CompilerParams(vmem_limit_bytes=18 * 2**20),
+        cost_estimate=pl.CostEstimate(flops=0, bytes_accessed=0, transcendentals=0),
+    )(place, *scores.arrays)
+
+
+def weigh_call(place, on_middle, on_ends, swapped, weights):
+    group, count = swapped[0].shape
+
+    def kernel(place_ref, *refs):
+        late, core = place_ref[5], place_ref[6]
+        weight, out = refs[6], refs[7]
+
+        def put(i, block, own_rows):
+            row = late if i == 0 else 1 - late
+            column = core if own_rows else 1 - core
+            across = pl.ds(pl.multiple_of(column * count, count), count)
+            down = pl.ds(pl.multiple_of(row * group, group), group)
+            out[down, across] = block.astype(jnp.float32) * weight[:, across]
+
+        for i in range(2):
+            pl.when(place_ref[0] == 1)(lambda i=i: put(i, refs[i][0], True))
+            pl.when(place_ref[0] == 0)(lambda i=i: put(i, refs[2 + i][0], True))
+            put(i, refs[4 + i][...], False)
+
+    smem = pl.BlockSpec(memory_space=pltpu.SMEM)
+    vmem = pl.BlockSpec(memory_space=pltpu.VMEM)
+    return pl.pallas_call(
+        kernel,
+        out_shape=jax.ShapeDtypeStruct((2 * group, 2 * count), jnp.float32),
+        in_specs=[smem] + [vmem] * 7,
+        out_specs=vmem,
+        cost_estimate=pl.CostEstimate(flops=0, bytes_accessed=0, transcendentals=0),
+    )(place, *on_middle, *on_ends, *swapped, weights)
+
+
+def after(values, *done):
+    return lax.optimization_barrier(tuple(values) + done)[: len(values)]
+
+
+def local_line(slab_grads, query_grads, example_weights, tile_owner):
+    count, quarter = slab_grads.shape
+    half, piece = count // 2, count // 4
+    e = lax.axis_index("ex")
+    f = lax.axis_index("feat")
+    core = f % 2
+    middle = jnp.logical_or(e == 1, e == 2)
+    late = (e >= 2).astype(jnp.int32)
+
+    def move(value, pairs):
+        return lax.ppermute(value, "ex", pairs)
+
+    def across(value):
+        return lax.ppermute(value, "feat", ACROSS)
+
+    def swap(value):
+        return lax.ppermute(value, "feat", CORE)
+
+    def across_on(value, which):
+        pairs = [(p * 4 + g, p * 4 + (g ^ 2)) for p in which for g in range(4)]
+        return lax.ppermute(value, ("ex", "feat"), pairs)
+
+    def swap_on(value, which):
+        pairs = [(p * 4 + g, p * 4 + (g ^ 1)) for p in which for g in range(4)]
+        return lax.ppermute(value, ("ex", "feat"), pairs)
+
+    mids, ends = (1, 2), (0, 3)
+
+    def whole(a, b):
+        return ([(a, 0, half)], [(b, 0, half)])
+
+    slots = tile_owner.shape[1] // 4
+    own_tiles = lax.dynamic_slice(tile_owner[0], (e * slots, 0), (slots, 2))
+    tiles = jnp.concatenate([swap(own_tiles), own_tiles], axis=0)
+    blocks = quarter // B
+    valid = (tiles[:, :1] >= 0).astype(jnp.int32)
+    tiles = jnp.maximum(tiles, 0)
+    table = ((tiles // blocks) ^ f) * blocks + tiles % blocks
+    table = jnp.concatenate([table, valid], axis=1)
+    order = jnp.where(e == 2, jnp.array([2, 3, 1, 0]), jnp.array([1, 0, 2, 3])).astype(jnp.int32)
+    place = jnp.concatenate(
+        [
+            middle.astype(jnp.int32)[None],
+            order ^ f,
+            late[None],
+            core[None],
+            jnp.array([4 * count], jnp.int32),
+        ]
+    )
+
+    keep = lax.dynamic_slice(slab_grads, (core * half, 0), (half, quarter))
+    give = lax.dynamic_slice(slab_grads, ((1 - core) * half, 0), (half, quarter))
+    own = jnp.concatenate([keep, swap(give)], axis=1)
+    q_half = query_grads.shape[0] // 2
+
+    own_x = across(own)
+    near = move(own, PAIR)
+    inner = move(own, INNER)
+
+    def halves(value, which):
+        return lax.dynamic_slice(value, (which * q_half, 0), (q_half, quarter))
+
+    q_mine, q_other = halves(query_grads, late), halves(query_grads, 1 - late)
+    near, inner, own, own_x, q_mine, q_other, table = after(
+        (near, inner, own, own_x, q_mine, q_other, table)
+    )
+    near_x = across(near)
+    outer = move(near, INNER)
+    inner_end = move(inner, TO_END)
+    q_end_other = move(q_other, TO_MID)
+    q_mine_sibling = swap(q_mine)
+    sibling0, sum0 = tile_call(place, table, whole(own, own_x))
+
+    inner, inner_end, outer, near, near_x, q_end_other, q_mine, sibling0, sum0 = after(
+        (inner, inner_end, outer, near, near_x, q_end_other, q_mine, sibling0, sum0)
+    )
+    second = jnp.where(middle, outer, inner_end)
+    second_x = across(second)
+    outer_end = move(outer, TO_END)
+    q_inner = move(q_other, INNER)
+    q_far = move(q_end_other, INNER)
+    q_end = move(q_mine, TO_MID)
+    sibling1, sum1 = tile_call(place, table, whole(near, near_x), [sum0], sibling0)
+
+    second, second_x, outer_end, inner, sum1, sibling1 = after(
+        (second, second_x, outer_end, inner, sum1, sibling1)
+    )
+    third = jnp.where(middle, inner, outer_end)
+    third_x = across(third)
+    parts = [(q_mine, q_mine_sibling)] + [(x, swap(x)) for x in (q_end, q_inner, q_far)]
+    slots3 = [whole(own, own_x), whole(near, near_x), whole(second, second_x)]
+    r_own, r_near, r_outer = score_call(place, parts, slots3)
+    to_far = move(r_outer, MID_TO_FAR_END)
+    to_end = move(r_near, TO_END)
+    sibling2, sum2 = tile_call(place, table, whole(second, second_x), [sum1], sibling1)
+    third_sibling = swap(third)
+
+    third_x, to_end, sibling2 = after((third_x, to_end, sibling2), sum2, r_own)
+    third_x_sibling = swap(third_x)
+    (r_inner,) = score_call(place, parts, [whole(third, third_x)])
+    sibling2 = swap(sibling2)
+    sibling2, r_inner, third_x_sibling = after((sibling2, r_inner, third_x_sibling))
+    to_mid = move(r_inner, INNER)
+    (gram,) = tile_call(
+        place,
+        table,
+        (
+            [(third, 0, half), (third_sibling, 0, half, True)],
+            [(third_x, 0, half), (third_x_sibling, 0, half, True)],
+        ),
+        [sum2, sibling2],
+        part="own",
+    )
+    to_end, to_far, to_mid, gram = after((to_end, to_far, to_mid, gram))
+    first_sibling = swap(jnp.where(middle, r_own[1], to_end[1]))
+    rest_sibling = swap(jnp.where(middle, to_mid[1], to_far[1]))
+    scores = weigh_call(
+        place,
+        (r_own, to_mid),
+        (to_end, to_far),
+        (first_sibling, rest_sibling),
+        example_weights[None, :],
+    )
+    return gram[None], scores
+
+
 def solution(mesh):
     placed = (
         P(("grp", "ex"), "feat"),
@@ -57,8 +487,10 @@
         P(("grp", "ex")),
         P(("grp", "feat"), None, None),
     )
+
+    line = mesh.shape["ex"] == 4 and mesh.shape["feat"] == 4
     return jax.shard_map(
-        local,
+        local_line if line else local_any,
         mesh=mesh,
         in_specs=placed,
         out_specs=(P(("grp", "feat"), "ex", None, None), P(("grp", "feat"), "ex")),

time: 288 us -> 134 us (0.47)
  matrix products: 111 us -> 0 us
  waiting for transfers between devices: 128 us -> 46.6 us
  starting transfers between devices: 0.11 us -> 43.8 us
  Pallas kernels: 0 us -> 35.2 us
  local copies, waits for them, and re-layouts: 29.2 us -> 3.5 us
  between operations: 13.8 us -> 0.98 us
    dot_general x64 -> x0, matrix products: 111 us -> none  [the longest x42 79.2 us: select_blocks(): jnp.einsum('tnb,gn->tgb', blocks3, onehot, preferred_element_type=jnp.flo...]
    reduce_scatter x1 -> x0, waiting for transfers between devices: 90.8 us -> none  [local(): lax.psum_scatter(tile_terms(blocks3, tile_table).astype(jnp.bfloat16), 'e...]
    ppermute x0 -> x27, waiting for transfers between devices: none -> 46.6 us  [the longest x12 34.6 us: move(): return lax.ppermute(value, 'ex', pairs)]
    ppermute x0 -> x27, starting transfers between devices: none -> 43.8 us  [the longest x12 26.1 us: move(): return lax.ppermute(value, 'ex', pairs)]
    all_gather x2 -> x0, waiting for transfers between devices: 36.2 us -> none  [the longest x1 36.2 us: local(): slab_full = lax.all_gather(slab_grads, 'feat', axis=1, tiled=True)]
    pallas_call x0 -> x7, Pallas kernels: none -> 35.2 us  [the longest x4 25.1 us: tile_call(): pl.pallas_call(kernel, out_shape=outs + (scores.out_shape if scores else...]
    dot_general x21 -> x0, local copies, waits for them, and re-layouts: 14.2 us -> none  [select_blocks(): jnp.einsum('tnb,gn->tgb', blocks3, onehot, preferred_element_type=jnp.flo...]
    while x42 -> x0, local copies, waits for them, and re-layouts: 7.9 us -> none
  transfers between devices with their start and end apart: 3 -> 27, of which waited for: 2 -> 16; matrix products, arithmetic and copies ran while one was open for 46% -> 2% of each run, Pallas kernels for 0% -> 25%
where the time goes in v3:
time: 134 us; the launch traced here: 133 us
  waiting for transfers between devices  46.6 us (35%)
  starting transfers between devices  43.8 us (33%)
  Pallas kernels  35.2 us (26%)
  local copies, waits for them, and re-layouts  3.5 us (3%)
  other arithmetic  2.89 us (2%)
    ppermute x12, waiting for transfers between devices, move(): return lax.ppermute(value, 'ex', pairs)  34.6 us
    ppermute x12, starting transfers between devices, move(): return lax.ppermute(value, 'ex', pairs)  26.1 us
    pallas_call x4, Pallas kernels, tile_call(): pl.pallas_call(kernel, out_shape=outs + (scores.out_shape if scores else...  25.1 us
    ppermute x11, starting transfers between devices, swap(): return lax.ppermute(value, 'feat', CORE)  13.2 us
    pallas_call x2, Pallas kernels, score_call(): pl.pallas_call(kernel, out_shape=scores.out_shape, in_specs=[smem] + [hbm...  7.8 us
    ppermute x4, waiting for transfers between devices, across(): return lax.ppermute(value, 'feat', ACROSS)  6.91 us
    ppermute x11, waiting for transfers between devices, swap(): return lax.ppermute(value, 'feat', CORE)  5.09 us
    ppermute x4, starting transfers between devices, across(): return lax.ppermute(value, 'feat', ACROSS)  4.52 us
  transfers between devices with their start and end apart: 27, of which 16 were waited for; matrix products, arithmetic and copies ran while one was open for 2% of the time, Pallas kernels for 25%

profile of v3, /device:TPU:9, one launch (start us, length us, event | category | flops | bytes accessed | tf_op | source)
XLA Modules:
  0.0 133.0 jit_solution(1508123863121792184)
XLA Ops:
  0.7 1.3 constant_dynamic-slice_fusion.4
  1.9 0.7 collective-permute-start
  2.7 1.5 %collective-permute-done = bf16[256,1024]{1,0:T(8,128)(2,1)S(1)} collective-permute-done((bf16[256,1024]{1,0:T(8,128)(2,1)S(1)}, bf16[256,1024]{1,0:T(8,128)(2,1)S(1)}, u32[]{:S(2)}, u32[]{:S(2)}) %collective-permute-start) | collective-permute-done | bytes 524320 | tf_op jit(solution)/shard_map/ppermute | solution.py:373
  4.4 4.5 %collective-permute-start.2 = (bf16[256,2048]{1,0:T(8,128)(2,1)S(1)}, bf16[256,2048]{1,0:T(8,128)(2,1)}, u32[]{:S(2)}, u32[]{:S(2)}) collective-permute-start(bf16[256,2048]{1,0:T(8,128)(2,1)S(1)} %pad_maximum_fusion.refs_0_), channel_id=1, source_target_pairs={{4,8},{8,4},{5,9},{9,5},{6,10},{10,6},{7,11},{11,7},{20,24},{24,20... | collective-permute-start | bytes 3145736 | tf_op jit(solution)/shard_map/ppermute | solution.py:367
  8.9 1.3 collective-permute-start.3
  10.2 1.2 collective-permute-start.4
  11.4 1.3 constant_dynamic-slice_fusion.1
  12.8 16.0 %collective-permute-done.1.refs_0_.refs_2_ = bf16[256,2048]{1,0:T(8,128)(2,1)} collective-permute-done((bf16[256,2048]{1,0:T(8,128)(2,1)S(1)}, bf16[256,2048]{1,0:T(8,128)(2,1)}, u32[]{:S(2)}, u32[]{:S(2)}) %collective-permute-start.1) | collective-permute-done | bytes 1048608 | tf_op jit(solution)/shard_map/ppermute | solution.py:367
  28.9 3.0 %collective-permute-done.2 = bf16[256,2048]{1,0:T(8,128)(2,1)} collective-permute-done((bf16[256,2048]{1,0:T(8,128)(2,1)S(1)}, bf16[256,2048]{1,0:T(8,128)(2,1)}, u32[]{:S(2)}, u32[]{:S(2)}) %collective-permute-start.2) | collective-permute-done | bytes 1048608 | tf_op jit(solution)/shard_map/ppermute | solution.py:367
  31.9 0.8 collective-permute-done.3.refs_1_
  32.7 2.3 %collective-permute-start.5 = (bf16[256,2048]{1,0:T(8,128)(2,1)}, bf16[256,2048]{1,0:T(8,128)(2,1)}, u32[]{:S(2)}, u32[]{:S(2)}) collective-permute-start(bf16[256,2048]{1,0:T(8,128)(2,1)} %collective-permute-done.2), channel_id=1, source_target_pairs={{4,0},{8,12},{5,1},{9,13},{6,2},{10,14},{7,3},{11,15},{20,16},{24,... | collective-permute-start | bytes 3145736 | tf_op jit(solution)/shard_map/ppermute | solution.py:367
  35.0 2.6 %collective-permute-start.6 = (bf16[256,2048]{1,0:T(8,128)(2,1)}, bf16[256,2048]{1,0:T(8,128)(2,1)}, u32[]{:S(2)}, u32[]{:S(2)}) collective-permute-start(bf16[256,2048]{1,0:T(8,128)(2,1)} %collective-permute-done.1.refs_0_.refs_2_), channel_id=1, source_target_pairs={{4,8},{8,4},{5,9},{9,5},{6,10},{10,6},{7,11},{11,7},{20,24},{24,20... | collective-permute-start | bytes 3145736 | tf_op jit(solution)/shard_map/ppermute | solution.py:367
  37.6 1.3 collective-permute-start.7
  38.9 1.3 collective-permute-start.8
  40.4 5.3 %shard_map.86 = (bf16[42,128,128]{2,1,0:T(8,128)(2,1)S(1)}, f32[42,128,128]{2,1,0:T(8,128)S(1)}) custom-call(s32[8]{0:T(128)S(1)} %concatenate.15.place_ref, s32[84,3]{1,0:T(8,128)S(1)} %copy.11.table_ref, bf16[256,2048]{1,0:T(8,128)(2,1)S(1)} %pad_maximum_fusion.refs_0_, bf16[256,2048]{1,0:T(8,128)(2,1)S(1)} %collective-permute-done.3.refs_1_), custom_call_target="tpu_custom_call" | custom-call | tf_op jit(solution)/shard_map/pallas_call | solution.py:216
  45.7 6.2 %collective-permute-done.8 = bf16[256,1024]{1,0:T(8,128)(2,1)} collective-permute-done((bf16[256,1024]{1,0:T(8,128)(2,1)S(1)}, bf16[256,1024]{1,0:T(8,128)(2,1)}, u32[]{:S(2)}, u32[]{:S(2)}) %collective-permute-start.8) | collective-permute-done | bytes 524320 | tf_op jit(solution)/shard_map/ppermute | solution.py:367
  51.9 3.2 %collective-permute-done.5 = bf16[256,2048]{1,0:T(8,128)(2,1)} collective-permute-done((bf16[256,2048]{1,0:T(8,128)(2,1)}, bf16[256,2048]{1,0:T(8,128)(2,1)}, u32[]{:S(2)}, u32[]{:S(2)}) %collective-permute-start.5) | collective-permute-done | bytes 1048608 | tf_op jit(solution)/shard_map/ppermute | solution.py:367
  55.2 4.8 %collective-permute-done.6 = bf16[256,2048]{1,0:T(8,128)(2,1)} collective-permute-done((bf16[256,2048]{1,0:T(8,128)(2,1)}, bf16[256,2048]{1,0:T(8,128)(2,1)}, u32[]{:S(2)}, u32[]{:S(2)}) %collective-permute-start.6) | collective-permute-done | bytes 1048608 | tf_op jit(solution)/shard_map/ppermute | solution.py:367
  60.0 0.6 collective-permute-done.7.refs_1_.refs_3_
  60.6 1.3 %broadcast_select_fusion.1.refs_4_.refs_0_ = bf16[256,2048]{1,0:T(8,128)(2,1)S(1)} fusion(bf16[256,2048]{1,0:T(8,128)(2,1)} %collective-permute-done.6, bf16[256,2048]{1,0:T(8,128)(2,1)} %collective-permute-done.5, pred[]{:T(512)S(6)} %or.3), kind=kLoop, calls=%fused_computation.2 | loop fusion | flops 524288 | bytes 3145729 | tf_op jit(solution)/shard_map/jit(_where)/select_n | solution.py:433
  61.9 1.3 collective-permute-start.9
  63.2 1.3 %collective-permute-start.10 = (bf16[256,2048]{1,0:T(8,128)(2,1)}, bf16[256,2048]{1,0:T(8,128)(2,1)S(1)}, u32[]{:S(2)}, u32[]{:S(2)}) collective-permute-start(bf16[256,2048]{1,0:T(8,128)(2,1)} %collective-permute-done.6), channel_id=1, source_target_pairs={{4,0},{8,12},{5,1},{9,13},{6,2},{10,14},{7,3},{11,15},{20,16},{24,... | collective-permute-start | bytes 3145736 | tf_op jit(solution)/shard_map/ppermute | solution.py:367
  64.5 2.6 %collective-permute-start.15 = (bf16[256,1024]{1,0:T(8,128)(2,1)S(1)}, bf16[256,1024]{1,0:T(8,128)(2,1)S(1)}, u32[]{:S(2)}, u32[]{:S(2)}) collective-permute-start(bf16[256,1024]{1,0:T(8,128)(2,1)S(1)} %get-tuple-element.45), channel_id=1, source_target_pairs={{4,8},{8,4},{5,9},{9,5},{6,10},{10,6},{7,11},{11,7},{20,24},{24,20... | collective-permute-start | bytes 1572872 | tf_op jit(solution)/shard_map/ppermute | solution.py:367
  67.1 1.3 collective-permute-start.13
  68.4 2.7 %collective-permute-start.17 = (bf16[256,1024]{1,0:T(8,128)(2,1)}, bf16[256,1024]{1,0:T(8,128)(2,1)S(1)}, u32[]{:S(2)}, u32[]{:S(2)}) collective-permute-start(bf16[256,1024]{1,0:T(8,128)(2,1)} %collective-permute-done.8), channel_id=1, source_target_pairs={{4,8},{8,4},{5,9},{9,5},{6,10},{10,6},{7,11},{11,7},{20,24},{24,20... | collective-permute-start | bytes 1572872 | tf_op jit(solution)/shard_map/ppermute | solution.py:367
  71.1 7.0 %shard_map.87 = (bf16[42,128,128]{2,1,0:T(8,128)(2,1)S(1)}, f32[42,128,128]{2,1,0:T(8,128)S(1)}) custom-call(s32[8]{0:T(128)S(1)} %concatenate.15.place_ref, s32[84,3]{1,0:T(8,128)S(1)} %copy.11.table_ref, bf16[256,2048]{1,0:T(8,128)(2,1)} %collective-permute-done.1.refs_0_.refs_2_, bf16[256,2048]{1,0:T(8,128)(2,1)} %collective-permute-done.7.refs_1_.refs_3_, ...), custom_call_target="tpu_custom_call" | custom-call | tf_op jit(solution)/shard_map/pallas_call | solution.py:216
  78.1 5.5 %collective-permute-done.9.refs_5_.refs_1_ = bf16[256,2048]{1,0:T(8,128)(2,1)S(1)} collective-permute-done((bf16[256,2048]{1,0:T(8,128)(2,1)S(1)}, bf16[256,2048]{1,0:T(8,128)(2,1)S(1)}, u32[]{:S(2)}, u32[]{:S(2)}) %collective-permute-start.9) | collective-permute-done | bytes 1048608 | tf_op jit(solution)/shard_map/ppermute | solution.py:370
  83.6 0.6 collective-permute-done.10
  84.2 1.3 broadcast_select_fusion.refs_0_
  85.6 0.7 collective-permute-start.11
  86.2 4.2 %collective-permute-start.12 = (bf16[256,1024]{1,0:T(8,128)(2,1)S(1)}, bf16[256,1024]{1,0:T(8,128)(2,1)S(1)}, u32[]{:S(2)}, u32[]{:S(2)}) collective-permute-start(bf16[256,1024]{1,0:T(8,128)(2,1)S(1)} %get-tuple-element.65.refs_6_.refs_2_), channel_id=1, source_target_pairs={{0,1},{1,0},{2,3},{3,2},{4,5},{5,4},{6,7},{7,6},{8,9},{9,8},{10,11... | collective-permute-start | bytes 1572872 | tf_op jit(solution)/shard_map/ppermute | solution.py:373
  91.0 1.0 collective-permute-start.18
  92.0 0.7 collective-permute-done.16.refs_11_.refs_7_
  92.7 0.7 collective-permute-done.14.refs_9_.refs_5_
  93.5 0.7 collective-permute-done.18.refs_13_.refs_9_
  94.2 5.4 %shard_map.88 = (bf16[2,256,256]{2,1,0:T(8,128)(2,1)S(1)}, bf16[2,256,256]{2,1,0:T(8,128)(2,1)S(1)}, bf16[2,256,256]{2,1,0:T(8,128)(2,1)S(1)}) custom-call(s32[8]{0:T(128)S(1)} %concatenate.15.place_ref, bf16[256,2048]{1,0:T(8,128)(2,1)S(1)} %pad_maximum_fusion.refs_0_, bf16[256,2048]{1,0:T(8,128)(2,1)S(1)} %collective-permute-done.3.refs_1_, ...), custom_call_target="tpu_custom_call" | custom-call | tf_op jit(solution)/shard_map/pallas_call | solution.py:312
  99.7 1.3 collective-permute-start.19
  101.0 6.1 %shard_map.89 = (bf16[42,128,128]{2,1,0:T(8,128)(2,1)S(1)}, f32[42,128,128]{2,1,0:T(8,128)S(1)}) custom-call(s32[8]{0:T(128)S(1)} %concatenate.15.place_ref, s32[84,3]{1,0:T(8,128)S(1)} %copy.11.table_ref, bf16[256,2048]{1,0:T(8,128)(2,1)S(1)} %broadcast_select_fusion.1.refs_4_.refs_0_, bf16[256,2048]{1,0:T(8,128)(2,1)S(1)} %collective-permute-done.9.refs_5_.refs_1_, ...), custom_call_target="tpu_custom_call" | custom-call | tf_op jit(solution)/shard_map/pallas_call | solution.py:216
  107.1 4.1 %collective-permute-start.21 = (bf16[42,128,128]{2,1,0:T(8,128)(2,1)S(1)}, bf16[42,128,128]{2,1,0:T(8,128)(2,1)S(1)}, u32[]{:S(2)}, u32[]{:S(2)}) collective-permute-start(bf16[42,128,128]{2,1,0:T(8,128)(2,1)S(1)} %get-tuple-element.75), channel_id=1, source_target_pairs={{0,1},{1,0},{2,3},{3,2},{4,5},{5,4},{6,7},{7,6},{8,9},{9,8},{10,11... | collective-permute-start | bytes 4128776 | tf_op jit(solution)/shard_map/ppermute | solution.py:373
  111.2 0.5 collective-permute-start.24
  111.7 3.2 %collective-permute-start.20 = (bf16[2,256,256]{2,1,0:T(8,128)(2,1)S(1)}, bf16[2,256,256]{2,1,0:T(8,128)(2,1)S(1)}, u32[]{:S(2)}, u32[]{:S(2)}) collective-permute-start(bf16[2,256,256]{2,1,0:T(8,128)(2,1)S(1)} %get-tuple-element.74), channel_id=1, source_target_pairs={{4,12},{8,0},{5,13},{9,1},{6,14},{10,2},{7,15},{11,3},{20,28},{24,... | collective-permute-start | bytes 786440 | tf_op jit(solution)/shard_map/ppermute | solution.py:367
  114.9 2.4 %shard_map.90 = bf16[2,256,256]{2,1,0:T(8,128)(2,1)S(1)} custom-call(s32[8]{0:T(128)S(1)} %concatenate.15.place_ref, bf16[256,2048]{1,0:T(8,128)(2,1)S(1)} %broadcast_select_fusion.refs_0_, bf16[256,2048]{1,0:T(8,128)(2,1)S(1)} %collective-permute-done.11.refs_1_.refs_2_, bf16[256,1024]{1,0:T(8,128)(2,1)S(1)} %get-tuple-element.65.refs_6_.refs_2_, ...), custom_call_target="tpu_custom_call" | custom-call | tf_op jit(solution)/shard_map/pallas_call | solution.py:312
  117.3 2.9 %collective-permute-start.23 = (bf16[2,256,256]{2,1,0:T(8,128)(2,1)S(1)}, bf16[2,256,256]{2,1,0:T(8,128)(2,1)S(1)}, u32[]{:S(2)}, u32[]{:S(2)}) collective-permute-start(bf16[2,256,256]{2,1,0:T(8,128)(2,1)S(1)} %shard_map.90), channel_id=1, source_target_pairs={{4,8},{8,4},{5,9},{9,5},{6,10},{10,6},{7,11},{11,7},{20,24},{24,20... | collective-permute-start | bytes 786440 | tf_op jit(solution)/shard_map/ppermute | solution.py:367
  120.3 6.8 %shard_map.91 = f32[42,128,128]{2,1,0:T(8,128)} custom-call(s32[8]{0:T(128)S(1)} %concatenate.15.place_ref, s32[84,3]{1,0:T(8,128)S(1)} %copy.11.table_ref, bf16[256,2048]{1,0:T(8,128)(2,1)S(1)} %broadcast_select_fusion.refs_0_, bf16[256,2048]{1,0:T(8,128)(2,1)S(1)} %collective-permute-done.24.refs_1_, ...), custom_call_target="tpu_custom_call" | custom-call | tf_op jit(solution)/shard_map/pallas_call | solution.py:216
  127.0 0.7 collective-permute-done.23.refs_1_
  127.8 0.8 collective-permute-start.25
  128.7 0.9 collective-permute-done.25.refs_4_
  130.7 2.3 %shard_map.92 = f32[512,512]{1,0:T(8,128)} custom-call(s32[8]{0:T(128)} %copy-done.2, bf16[2,256,256]{2,1,0:T(8,128)(2,1)} %copy-done.1, bf16[2,256,256]{2,1,0:T(8,128)(2,1)} %copy-done.5, bf16[2,256,256]{2,1,0:T(8,128)(2,1)} %copy-done.3, bf16[2,256,256]{2,1,0:T(8,128)(2,1)} %copy-done.4, bf16[256,256]{1,0:T(8,128)(2,1)} %copy-done.6, ...), custom_call_target="tpu_custom_call" | custom-call | tf_op jit(solution)/shard_map/pallas_call | solution.py:344
  (47 shorter events, 2.3 us)
Async XLA Ops:
  0.6 9.5 %copy-start = (s32[1,168,2]{1,2,0:T(2,128)S(1)}, s32[1,168,2]{1,2,0:T(2,128)}, u32[]{:S(2)}) copy-start(s32[1,168,2]{1,2,0:T(2,128)} %param.10) | copy-start | bytes 4036
  1.9 2.3 %collective-permute-start = (bf16[256,1024]{1,0:T(8,128)(2,1)S(1)}, bf16[256,1024]{1,0:T(8,128)(2,1)S(1)}, u32[]{:S(2)}, u32[]{:S(2)}) collective-permute-start(bf16[256,1024]{1,0:T(8,128)(2,1)S(1)} %get-tuple-element.89), channel_id=1, source_target_pairs={{0,1},{1,0},{2,3},{3,2},{4,5},{5,4},{6,7},{7,6},{8,9},{9,8},{10,11... | collective-permute-start | bytes 1572872 | tf_op jit(solution)/shard_map/ppermute | solution.py:373
  4.2 36.0 %copy-start.8 = (s32[4]{0:T(128)S(1)}, s32[4]{0:T(128)}, u32[]{:S(2)}) copy-start(s32[4]{0:T(128)} %constant.71.clone) | copy-start | bytes 52
  4.2 36.0 %copy-start.9 = (s32[4]{0:T(128)S(1)}, s32[4]{0:T(128)}, u32[]{:S(2)}) copy-start(s32[4]{0:T(128)} %constant.72.clone) | copy-start | bytes 52
  4.3 24.5 %collective-permute-start.1 = (bf16[256,2048]{1,0:T(8,128)(2,1)S(1)}, bf16[256,2048]{1,0:T(8,128)(2,1)}, u32[]{:S(2)}, u32[]{:S(2)}) collective-permute-start(bf16[256,2048]{1,0:T(8,128)(2,1)S(1)} %pad_maximum_fusion.refs_0_), channel_id=1, source_target_pairs={{0,4},{4,0},{8,12},{12,8},{1,5},{5,1},{9,13},{13,9},{2,6},{6,2},{1... | collective-permute-start | bytes 3145736 | tf_op jit(solution)/shard_map/ppermute | solution.py:367
  4.4 27.5 %collective-permute-start.2 = (bf16[256,2048]{1,0:T(8,128)(2,1)S(1)}, bf16[256,2048]{1,0:T(8,128)(2,1)}, u32[]{:S(2)}, u32[]{:S(2)}) collective-permute-start(bf16[256,2048]{1,0:T(8,128)(2,1)S(1)} %pad_maximum_fusion.refs_0_), channel_id=1, source_target_pairs={{4,8},{8,4},{5,9},{9,5},{6,10},{10,6},{7,11},{11,7},{20,24},{24,20... | collective-permute-start | bytes 3145736 | tf_op jit(solution)/shard_map/ppermute | solution.py:367
  8.9 23.8 %collective-permute-start.3 = (bf16[256,2048]{1,0:T(8,128)(2,1)S(1)}, bf16[256,2048]{1,0:T(8,128)(2,1)S(1)}, u32[]{:S(2)}, u32[]{:S(2)}) collective-permute-start(bf16[256,2048]{1,0:T(8,128)(2,1)S(1)} %pad_maximum_fusion.refs_0_), channel_id=1, source_target_pairs={{0,2},{2,0},{1,3},{3,1},{4,6},{6,4},{5,7},{7,5},{8,10},{10,8},{9,1... | collective-permute-start | bytes 3145736 | tf_op jit(solution)/shard_map/ppermute | solution.py:370
  10.2 2.5 %collective-permute-start.4 = (s32[42,2]{0,1:T(2,128)S(1)}, s32[42,2]{0,1:T(2,128)S(1)}, u32[]{:S(2)}, u32[]{:S(2)}) collective-permute-start(s32[42,2]{0,1:T(2,128)S(1)} %fusion), channel_id=1, source_target_pairs={{0,1},{1,0},{2,3},{3,2},{4,5},{5,4},{6,7},{7,6},{8,9},{9,8},{10,11... | collective-permute-start | bytes 1016 | tf_op jit(solution)/shard_map/ppermute | solution.py:373
  32.7 22.5 %collective-permute-start.5 = (bf16[256,2048]{1,0:T(8,128)(2,1)}, bf16[256,2048]{1,0:T(8,128)(2,1)}, u32[]{:S(2)}, u32[]{:S(2)}) collective-permute-start(bf16[256,2048]{1,0:T(8,128)(2,1)} %collective-permute-done.2), channel_id=1, source_target_pairs={{4,0},{8,12},{5,1},{9,13},{6,2},{10,14},{7,3},{11,15},{20,16},{24,... | collective-permute-start | bytes 3145736 | tf_op jit(solution)/shard_map/ppermute | solution.py:367
  35.0 25.0 %collective-permute-start.6 = (bf16[256,2048]{1,0:T(8,128)(2,1)}, bf16[256,2048]{1,0:T(8,128)(2,1)}, u32[]{:S(2)}, u32[]{:S(2)}) collective-permute-start(bf16[256,2048]{1,0:T(8,128)(2,1)} %collective-permute-done.1.refs_0_.refs_2_), channel_id=1, source_target_pairs={{4,8},{8,4},{5,9},{9,5},{6,10},{10,6},{7,11},{11,7},{20,24},{24,20... | collective-permute-start | bytes 3145736 | tf_op jit(solution)/shard_map/ppermute | solution.py:367
  37.6 22.9 %collective-permute-start.7 = (bf16[256,2048]{1,0:T(8,128)(2,1)}, bf16[256,2048]{1,0:T(8,128)(2,1)}, u32[]{:S(2)}, u32[]{:S(2)}) collective-permute-start(bf16[256,2048]{1,0:T(8,128)(2,1)} %collective-permute-done.1.refs_0_.refs_2_), channel_id=1, source_target_pairs={{0,2},{2,0},{1,3},{3,1},{4,6},{6,4},{5,7},{7,5},{8,10},{10,8},{9,1... | collective-permute-start | bytes 3145736 | tf_op jit(solution)/shard_map/ppermute | solution.py:370
  38.9 13.0 %collective-permute-start.8 = (bf16[256,1024]{1,0:T(8,128)(2,1)S(1)}, bf16[256,1024]{1,0:T(8,128)(2,1)}, u32[]{:S(2)}, u32[]{:S(2)}) collective-permute-start(bf16[256,1024]{1,0:T(8,128)(2,1)S(1)} %get-tuple-element.45), channel_id=1, source_target_pairs={{0,4},{12,8},{1,5},{13,9},{2,6},{14,10},{3,7},{15,11},{16,20},{28,... | collective-permute-start | bytes 1572872 | tf_op jit(solution)/shard_map/ppermute | solution.py:367
  40.3 79.9 %copy-start.2 = (s32[8]{0:T(128)}, s32[8]{0:T(128)S(1)}, u32[]{:S(2)}) copy-start(s32[8]{0:T(128)S(1)} %concatenate.15.place_ref) | copy-start | bytes 100
  61.9 21.7 %collective-permute-start.9 = (bf16[256,2048]{1,0:T(8,128)(2,1)S(1)}, bf16[256,2048]{1,0:T(8,128)(2,1)S(1)}, u32[]{:S(2)}, u32[]{:S(2)}) collective-permute-start(bf16[256,2048]{1,0:T(8,128)(2,1)S(1)} %broadcast_select_fusion.1.refs_4_.refs_0_), channel_id=1, source_target_pairs={{0,2},{2,0},{1,3},{3,1},{4,6},{6,4},{5,7},{7,5},{8,10},{10,8},{9,1... | collective-permute-start | bytes 3145736 | tf_op jit(solution)/shard_map/ppermute | solution.py:370
  63.2 21.0 %collective-permute-start.10 = (bf16[256,2048]{1,0:T(8,128)(2,1)}, bf16[256,2048]{1,0:T(8,128)(2,1)S(1)}, u32[]{:S(2)}, u32[]{:S(2)}) collective-permute-start(bf16[256,2048]{1,0:T(8,128)(2,1)} %collective-permute-done.6), channel_id=1, source_target_pairs={{4,0},{8,12},{5,1},{9,13},{6,2},{10,14},{7,3},{11,15},{20,16},{24,... | collective-permute-start | bytes 3145736 | tf_op jit(solution)/shard_map/ppermute | solution.py:367
  64.5 25.9 %collective-permute-start.15 = (bf16[256,1024]{1,0:T(8,128)(2,1)S(1)}, bf16[256,1024]{1,0:T(8,128)(2,1)S(1)}, u32[]{:S(2)}, u32[]{:S(2)}) collective-permute-start(bf16[256,1024]{1,0:T(8,128)(2,1)S(1)} %get-tuple-element.45), channel_id=1, source_target_pairs={{4,8},{8,4},{5,9},{9,5},{6,10},{10,6},{7,11},{11,7},{20,24},{24,20... | collective-permute-start | bytes 1572872 | tf_op jit(solution)/shard_map/ppermute | solution.py:367
  67.1 23.3 %collective-permute-start.13 = (bf16[256,1024]{1,0:T(8,128)(2,1)S(1)}, bf16[256,1024]{1,0:T(8,128)(2,1)S(1)}, u32[]{:S(2)}, u32[]{:S(2)}) collective-permute-start(bf16[256,1024]{1,0:T(8,128)(2,1)S(1)} %get-tuple-element.65.refs_6_.refs_2_), channel_id=1, source_target_pairs={{0,4},{12,8},{1,5},{13,9},{2,6},{14,10},{3,7},{15,11},{16,20},{28,... | collective-permute-start | bytes 1572872 | tf_op jit(solution)/shard_map/ppermute | solution.py:367
  68.4 22.5 %collective-permute-start.17 = (bf16[256,1024]{1,0:T(8,128)(2,1)}, bf16[256,1024]{1,0:T(8,128)(2,1)S(1)}, u32[]{:S(2)}, u32[]{:S(2)}) collective-permute-start(bf16[256,1024]{1,0:T(8,128)(2,1)} %collective-permute-done.8), channel_id=1, source_target_pairs={{4,8},{8,4},{5,9},{9,5},{6,10},{10,6},{7,11},{11,7},{20,24},{24,20... | collective-permute-start | bytes 1572872 | tf_op jit(solution)/shard_map/ppermute | solution.py:367
  85.6 21.6 %collective-permute-start.11 = (bf16[256,2048]{1,0:T(8,128)(2,1)S(1)}, bf16[256,2048]{1,0:T(8,128)(2,1)S(1)}, u32[]{:S(2)}, u32[]{:S(2)}) collective-permute-start(bf16[256,2048]{1,0:T(8,128)(2,1)S(1)} %broadcast_select_fusion.refs_0_), channel_id=1, source_target_pairs={{0,2},{2,0},{1,3},{3,1},{4,6},{6,4},{5,7},{7,5},{8,10},{10,8},{9,1... | collective-permute-start | bytes 3145736 | tf_op jit(solution)/shard_map/ppermute | solution.py:370
  86.2 5.8 %collective-permute-start.12 = (bf16[256,1024]{1,0:T(8,128)(2,1)S(1)}, bf16[256,1024]{1,0:T(8,128)(2,1)S(1)}, u32[]{:S(2)}, u32[]{:S(2)}) collective-permute-start(bf16[256,1024]{1,0:T(8,128)(2,1)S(1)} %get-tuple-element.65.refs_6_.refs_2_), channel_id=1, source_target_pairs={{0,1},{1,0},{2,3},{3,2},{4,5},{5,4},{6,7},{7,6},{8,9},{9,8},{10,11... | collective-permute-start | bytes 1572872 | tf_op jit(solution)/shard_map/ppermute | solution.py:373
  90.5 2.3 %collective-permute-start.16 = (bf16[256,1024]{1,0:T(8,128)(2,1)S(1)}, bf16[256,1024]{1,0:T(8,128)(2,1)S(1)}, u32[]{:S(2)}, u32[]{:S(2)}) collective-permute-start(bf16[256,1024]{1,0:T(8,128)(2,1)S(1)} %collective-permute-done.15.refs_10_.refs_6_), channel_id=1, source_target_pairs={{0,1},{1,0},{2,3},{3,2},{4,5},{5,4},{6,7},{7,6},{8,9},{9,8},{10,11... | collective-permute-start | bytes 1572872 | tf_op jit(solution)/shard_map/ppermute | solution.py:373
  90.5 3.0 %collective-permute-start.14 = (bf16[256,1024]{1,0:T(8,128)(2,1)S(1)}, bf16[256,1024]{1,0:T(8,128)(2,1)S(1)}, u32[]{:S(2)}, u32[]{:S(2)}) collective-permute-start(bf16[256,1024]{1,0:T(8,128)(2,1)S(1)} %collective-permute-done.13.refs_8_.refs_4_), channel_id=1, source_target_pairs={{0,1},{1,0},{2,3},{3,2},{4,5},{5,4},{6,7},{7,6},{8,9},{9,8},{10,11... | collective-permute-start | bytes 1572872 | tf_op jit(solution)/shard_map/ppermute | solution.py:373
  91.0 3.3 %collective-permute-start.18 = (bf16[256,1024]{1,0:T(8,128)(2,1)S(1)}, bf16[256,1024]{1,0:T(8,128)(2,1)S(1)}, u32[]{:S(2)}, u32[]{:S(2)}) collective-permute-start(bf16[256,1024]{1,0:T(8,128)(2,1)S(1)} %collective-permute-done.17.refs_12_.refs_8_), channel_id=1, source_target_pairs={{0,1},{1,0},{2,3},{3,2},{4,5},{5,4},{6,7},{7,6},{8,9},{9,8},{10,11... | collective-permute-start | bytes 1572872 | tf_op jit(solution)/shard_map/ppermute | solution.py:373
  99.7 28.1 %copy-start.1 = (bf16[2,256,256]{2,1,0:T(8,128)(2,1)}, bf16[2,256,256]{2,1,0:T(8,128)(2,1)S(1)}, u32[]{:S(2)}) copy-start(bf16[2,256,256]{2,1,0:T(8,128)(2,1)S(1)} %get-tuple-element.72.refs_0_) | copy-start | bytes 786436
  99.7 7.4 %collective-permute-start.19 = (bf16[2,256,256]{2,1,0:T(8,128)(2,1)S(1)}, bf16[2,256,256]{2,1,0:T(8,128)(2,1)S(1)}, u32[]{:S(2)}, u32[]{:S(2)}) collective-permute-start(bf16[2,256,256]{2,1,0:T(8,128)(2,1)S(1)} %get-tuple-element.67), channel_id=1, source_target_pairs={{4,0},{8,12},{5,1},{9,13},{6,2},{10,14},{7,3},{11,15},{20,16},{24,... | collective-permute-start | bytes 786440 | tf_op jit(solution)/shard_map/ppermute | solution.py:367
  107.1 20.6 %copy-start.3 = (bf16[2,256,256]{2,1,0:T(8,128)(2,1)}, bf16[2,256,256]{2,1,0:T(8,128)(2,1)S(1)}, u32[]{:S(2)}) copy-start(bf16[2,256,256]{2,1,0:T(8,128)(2,1)S(1)} %collective-permute-done.19.refs_2_) | copy-start | bytes 786436
  107.1 10.2 %collective-permute-start.21 = (bf16[42,128,128]{2,1,0:T(8,128)(2,1)S(1)}, bf16[42,128,128]{2,1,0:T(8,128)(2,1)S(1)}, u32[]{:S(2)}, u32[]{:S(2)}) collective-permute-start(bf16[42,128,128]{2,1,0:T(8,128)(2,1)S(1)} %get-tuple-element.75), channel_id=1, source_target_pairs={{0,1},{1,0},{2,3},{3,2},{4,5},{5,4},{6,7},{7,6},{8,9},{9,8},{10,11... | collective-permute-start | bytes 4128776 | tf_op jit(solution)/shard_map/ppermute | solution.py:373
  111.2 6.1 %collective-permute-start.22 = (bf16[256,2048]{1,0:T(8,128)(2,1)S(1)}, bf16[256,2048]{1,0:T(8,128)(2,1)S(1)}, u32[]{:S(2)}, u32[]{:S(2)}) collective-permute-start(bf16[256,2048]{1,0:T(8,128)(2,1)S(1)} %collective-permute-done.11.refs_1_.refs_2_), channel_id=1, source_target_pairs={{0,1},{1,0},{2,3},{3,2},{4,5},{5,4},{6,7},{7,6},{8,9},{9,8},{10,11... | collective-permute-start | bytes 3145736 | tf_op jit(solution)/shard_map/ppermute | solution.py:373
  111.2 9.0 %collective-permute-start.24 = (bf16[256,2048]{1,0:T(8,128)(2,1)S(1)}, bf16[256,2048]{1,0:T(8,128)(2,1)S(1)}, u32[]{:S(2)}, u32[]{:S(2)}) collective-permute-start(bf16[256,2048]{1,0:T(8,128)(2,1)S(1)} %broadcast_select_fusion.refs_0_), channel_id=1, source_target_pairs={{0,1},{1,0},{2,3},{3,2},{4,5},{5,4},{6,7},{7,6},{8,9},{9,8},{10,11... | collective-permute-start | bytes 3145736 | tf_op jit(solution)/shard_map/ppermute | solution.py:373
  111.7 15.3 %collective-permute-start.20 = (bf16[2,256,256]{2,1,0:T(8,128)(2,1)S(1)}, bf16[2,256,256]{2,1,0:T(8,128)(2,1)S(1)}, u32[]{:S(2)}, u32[]{:S(2)}) collective-permute-start(bf16[2,256,256]{2,1,0:T(8,128)(2,1)S(1)} %get-tuple-element.74), channel_id=1, source_target_pairs={{4,12},{8,0},{5,13},{9,1},{6,14},{10,2},{7,15},{11,3},{20,28},{24,... | collective-permute-start | bytes 786440 | tf_op jit(solution)/shard_map/ppermute | solution.py:367
  117.3 10.4 %collective-permute-start.23 = (bf16[2,256,256]{2,1,0:T(8,128)(2,1)S(1)}, bf16[2,256,256]{2,1,0:T(8,128)(2,1)S(1)}, u32[]{:S(2)}, u32[]{:S(2)}) collective-permute-start(bf16[2,256,256]{2,1,0:T(8,128)(2,1)S(1)} %shard_map.90), channel_id=1, source_target_pairs={{4,8},{8,4},{5,9},{9,5},{6,10},{10,6},{7,11},{11,7},{20,24},{24,20... | collective-permute-start | bytes 786440 | tf_op jit(solution)/shard_map/ppermute | solution.py:367
  127.0 3.0 %copy-start.4 = (bf16[2,256,256]{2,1,0:T(8,128)(2,1)}, bf16[2,256,256]{2,1,0:T(8,128)(2,1)S(1)}, u32[]{:S(2)}) copy-start(bf16[2,256,256]{2,1,0:T(8,128)(2,1)S(1)} %collective-permute-done.20.refs_3_) | copy-start | bytes 786436
  127.7 2.3 %copy-start.5 = (bf16[2,256,256]{2,1,0:T(8,128)(2,1)}, bf16[2,256,256]{2,1,0:T(8,128)(2,1)S(1)}, u32[]{:S(2)}) copy-start(bf16[2,256,256]{2,1,0:T(8,128)(2,1)S(1)} %collective-permute-done.23.refs_1_) | copy-start | bytes 786436
  127.8 1.8 %collective-permute-start.25 = (bf16[256,256]{1,0:T(8,128)(2,1)S(1)}, bf16[256,256]{1,0:T(8,128)(2,1)S(1)}, u32[]{:S(2)}, u32[]{:S(2)}) collective-permute-start(bf16[256,256]{1,0:T(8,128)(2,1)S(1)} %select_bitcast_fusion.1), channel_id=1, source_target_pairs={{0,1},{1,0},{2,3},{3,2},{4,5},{5,4},{6,7},{7,6},{8,9},{9,8},{10,11... | collective-permute-start | bytes 393224 | tf_op jit(solution)/shard_map/ppermute | solution.py:373
  128.6 1.4 %collective-permute-start.26 = (bf16[256,256]{1,0:T(8,128)(2,1)S(1)}, bf16[256,256]{1,0:T(8,128)(2,1)S(1)}, u32[]{:S(2)}, u32[]{:S(2)}) collective-permute-start(bf16[256,256]{1,0:T(8,128)(2,1)S(1)} %select_bitcast_fusion), channel_id=1, source_target_pairs={{0,1},{1,0},{2,3},{3,2},{4,5},{5,4},{6,7},{7,6},{8,9},{9,8},{10,11... | collective-permute-start | bytes 393224 | tf_op jit(solution)/shard_map/ppermute | solution.py:373
  129.6 0.7 copy-start.6
  130.0 0.7 copy-start.7

commit v4 on v3

--- a/solution.py
+++ b/solution.py
@@ -446,17 +446,21 @@
     parts = [(q_mine, q_mine_sibling)] + [(x, swap(x)) for x in (q_end, q_inner, q_far)]
     slots3 = [whole(own, own_x), whole(near, near_x), whole(second, second_x)]
     r_own, r_near, r_outer = score_call(place, parts, slots3)
-    to_far = move(r_outer, MID_TO_FAR_END)
+    far = move(r_outer, INNER)
     to_end = move(r_near, TO_END)
     sibling2, sum2 = tile_call(place, table, whole(second, second_x), [sum1], sibling1)
     third_sibling = swap(third)
 
-    third_x, to_end, sibling2 = after((third_x, to_end, sibling2), sum2, r_own)
+    first = jnp.where(middle, r_own[1], to_end[1])
+    third_x, to_end, far, sibling2, first = after((third_x, to_end, far, sibling2, first), sum2, r_own)
+    first_sibling = swap(first)
     third_x_sibling = swap(third_x)
     (r_inner,) = score_call(place, parts, [whole(third, third_x)])
     sibling2 = swap(sibling2)
-    sibling2, r_inner, third_x_sibling = after((sibling2, r_inner, third_x_sibling))
+    r_inner, far = after((r_inner, far))
+    to_far = move(far, TO_END)
     to_mid = move(r_inner, INNER)
+    sibling2, third_x_sibling = after((sibling2, third_x_sibling), r_inner)
     (gram,) = tile_call(
         place,
         table,
@@ -468,7 +472,6 @@
         part="own",
     )
     to_end, to_far, to_mid, gram = after((to_end, to_far, to_mid, gram))
-    first_sibling = swap(jnp.where(middle, r_own[1], to_end[1]))
     rest_sibling = swap(jnp.where(middle, to_mid[1], to_far[1]))
     scores = weigh_call(
         place,

time: 134 us -> 131 us (0.978)
  starting transfers between devices: 43.8 us -> 41.7 us
    ppermute x11, starting transfers between devices: 13.2 us -> 10.5 us  [swap(): return lax.ppermute(value, 'feat', CORE)]
    ppermute x12 -> x13, starting transfers between devices: 26.1 us -> 26.7 us  [move(): return lax.ppermute(value, 'ex', pairs)]
    ppermute x12 -> x13, waiting for transfers between devices: 34.6 us -> 34.5 us  [move(): return lax.ppermute(value, 'ex', pairs)]
  transfers between devices with their start and end apart: 27 -> 28, of which waited for: 16 -> 15; matrix products, arithmetic and copies ran while one was open for 2% -> 2% of each run, Pallas kernels for 25% -> 25%
where the time goes in v4:
time: 131 us
  waiting for transfers between devices  46.2 us (35%)
  starting transfers between devices  41.7 us (32%)
  Pallas kernels  35.3 us (27%)
  local copies, waits for them, and re-layouts  3.51 us (3%)
  other arithmetic  2.89 us (2%)
    ppermute x13, waiting for transfers between devices, move(): return lax.ppermute(value, 'ex', pairs)  34.5 us
    ppermute x13, starting transfers between devices, move(): return lax.ppermute(value, 'ex', pairs)  26.7 us
    pallas_call x4, Pallas kernels, tile_call(): pl.pallas_call(kernel, out_shape=outs + (scores.out_shape if scores else...  25.1 us
    ppermute x11, starting transfers between devices, swap(): return lax.ppermute(value, 'feat', CORE)  10.5 us
    pallas_call x2, Pallas kernels, score_call(): pl.pallas_call(kernel, out_shape=scores.out_shape, in_specs=[smem] + [hbm...  7.8 us
    ppermute x4, waiting for transfers between devices, across(): return lax.ppermute(value, 'feat', ACROSS)  6.92 us
    ppermute x11, waiting for transfers between devices, swap(): return lax.ppermute(value, 'feat', CORE)  4.75 us
    ppermute x4, starting transfers between devices, across(): return lax.ppermute(value, 'feat', ACROSS)  4.52 us
  transfers between devices with their start and end apart: 28, of which 15 were waited for; matrix products, arithmetic and copies ran while one was open for 2% of the time, Pallas kernels for 25%

profile of v4, /device:TPU:9, one launch (start us, length us, event | category | flops | bytes accessed | tf_op | source)
XLA Modules:
  0.0 130.5 jit_solution(414014796936622897)
XLA Ops:
  0.7 1.3 constant_dynamic-slice_fusion.4
  1.9 0.7 collective-permute-start
  2.7 1.5 %collective-permute-done = bf16[256,1024]{1,0:T(8,128)(2,1)S(1)} collective-permute-done((bf16[256,1024]{1,0:T(8,128)(2,1)S(1)}, bf16[256,1024]{1,0:T(8,128)(2,1)S(1)}, u32[]{:S(2)}, u32[]{:S(2)}) %collective-permute-start) | collective-permute-done | bytes 524320 | tf_op jit(solution)/shard_map/ppermute | solution.py:373
  4.4 4.5 %collective-permute-start.2 = (bf16[256,2048]{1,0:T(8,128)(2,1)S(1)}, bf16[256,2048]{1,0:T(8,128)(2,1)}, u32[]{:S(2)}, u32[]{:S(2)}) collective-permute-start(bf16[256,2048]{1,0:T(8,128)(2,1)S(1)} %pad_maximum_fusion.refs_0_), channel_id=1, source_target_pairs={{4,8},{8,4},{5,9},{9,5},{6,10},{10,6},{7,11},{11,7},{20,24},{24,20... | collective-permute-start | bytes 3145736 | tf_op jit(solution)/shard_map/ppermute | solution.py:367
  8.9 1.3 collective-permute-start.3
  10.2 1.2 collective-permute-start.4
  11.4 1.3 constant_dynamic-slice_fusion.1
  12.8 16.0 %collective-permute-done.1.refs_0_.refs_2_ = bf16[256,2048]{1,0:T(8,128)(2,1)} collective-permute-done((bf16[256,2048]{1,0:T(8,128)(2,1)S(1)}, bf16[256,2048]{1,0:T(8,128)(2,1)}, u32[]{:S(2)}, u32[]{:S(2)}) %collective-permute-start.1) | collective-permute-done | bytes 1048608 | tf_op jit(solution)/shard_map/ppermute | solution.py:367
  28.9 3.0 %collective-permute-done.2 = bf16[256,2048]{1,0:T(8,128)(2,1)} collective-permute-done((bf16[256,2048]{1,0:T(8,128)(2,1)S(1)}, bf16[256,2048]{1,0:T(8,128)(2,1)}, u32[]{:S(2)}, u32[]{:S(2)}) %collective-permute-start.2) | collective-permute-done | bytes 1048608 | tf_op jit(solution)/shard_map/ppermute | solution.py:367
  31.9 0.8 collective-permute-done.3.refs_1_
  32.7 2.3 %collective-permute-start.5 = (bf16[256,2048]{1,0:T(8,128)(2,1)}, bf16[256,2048]{1,0:T(8,128)(2,1)}, u32[]{:S(2)}, u32[]{:S(2)}) collective-permute-start(bf16[256,2048]{1,0:T(8,128)(2,1)} %collective-permute-done.2), channel_id=1, source_target_pairs={{4,0},{8,12},{5,1},{9,13},{6,2},{10,14},{7,3},{11,15},{20,16},{24,... | collective-permute-start | bytes 3145736 | tf_op jit(solution)/shard_map/ppermute | solution.py:367
  35.0 2.7 %collective-permute-start.6 = (bf16[256,2048]{1,0:T(8,128)(2,1)}, bf16[256,2048]{1,0:T(8,128)(2,1)}, u32[]{:S(2)}, u32[]{:S(2)}) collective-permute-start(bf16[256,2048]{1,0:T(8,128)(2,1)} %collective-permute-done.1.refs_0_.refs_2_), channel_id=1, source_target_pairs={{4,8},{8,4},{5,9},{9,5},{6,10},{10,6},{7,11},{11,7},{20,24},{24,20... | collective-permute-start | bytes 3145736 | tf_op jit(solution)/shard_map/ppermute | solution.py:367
  37.6 1.3 collective-permute-start.7
  38.9 1.3 collective-permute-start.8
  40.5 5.4 %shard_map.86 = (bf16[42,128,128]{2,1,0:T(8,128)(2,1)S(1)}, f32[42,128,128]{2,1,0:T(8,128)S(1)}) custom-call(s32[8]{0:T(128)S(1)} %concatenate.15.place_ref, s32[84,3]{1,0:T(8,128)S(1)} %copy.11.table_ref, bf16[256,2048]{1,0:T(8,128)(2,1)S(1)} %pad_maximum_fusion.refs_0_, bf16[256,2048]{1,0:T(8,128)(2,1)S(1)} %collective-permute-done.3.refs_1_), custom_call_target="tpu_custom_call" | custom-call | tf_op jit(solution)/shard_map/pallas_call | solution.py:216
  45.8 6.1 %collective-permute-done.8 = bf16[256,1024]{1,0:T(8,128)(2,1)} collective-permute-done((bf16[256,1024]{1,0:T(8,128)(2,1)S(1)}, bf16[256,1024]{1,0:T(8,128)(2,1)}, u32[]{:S(2)}, u32[]{:S(2)}) %collective-permute-start.8) | collective-permute-done | bytes 524320 | tf_op jit(solution)/shard_map/ppermute | solution.py:367
  52.0 3.2 %collective-permute-done.5 = bf16[256,2048]{1,0:T(8,128)(2,1)} collective-permute-done((bf16[256,2048]{1,0:T(8,128)(2,1)}, bf16[256,2048]{1,0:T(8,128)(2,1)}, u32[]{:S(2)}, u32[]{:S(2)}) %collective-permute-start.5) | collective-permute-done | bytes 1048608 | tf_op jit(solution)/shard_map/ppermute | solution.py:367
  55.2 4.8 %collective-permute-done.6 = bf16[256,2048]{1,0:T(8,128)(2,1)} collective-permute-done((bf16[256,2048]{1,0:T(8,128)(2,1)}, bf16[256,2048]{1,0:T(8,128)(2,1)}, u32[]{:S(2)}, u32[]{:S(2)}) %collective-permute-start.6) | collective-permute-done | bytes 1048608 | tf_op jit(solution)/shard_map/ppermute | solution.py:367
  60.0 0.6 collective-permute-done.7.refs_1_.refs_3_
  60.6 1.3 %broadcast_select_fusion.1.refs_4_.refs_0_ = bf16[256,2048]{1,0:T(8,128)(2,1)S(1)} fusion(bf16[256,2048]{1,0:T(8,128)(2,1)} %collective-permute-done.6, bf16[256,2048]{1,0:T(8,128)(2,1)} %collective-permute-done.5, pred[]{:T(512)S(6)} %or.3), kind=kLoop, calls=%fused_computation.2 | loop fusion | flops 524288 | bytes 3145729 | tf_op jit(solution)/shard_map/jit(_where)/select_n | solution.py:433
  61.9 1.3 collective-permute-start.9
  63.2 1.3 %collective-permute-start.10 = (bf16[256,2048]{1,0:T(8,128)(2,1)}, bf16[256,2048]{1,0:T(8,128)(2,1)S(1)}, u32[]{:S(2)}, u32[]{:S(2)}) collective-permute-start(bf16[256,2048]{1,0:T(8,128)(2,1)} %collective-permute-done.6), channel_id=1, source_target_pairs={{4,0},{8,12},{5,1},{9,13},{6,2},{10,14},{7,3},{11,15},{20,16},{24,... | collective-permute-start | bytes 3145736 | tf_op jit(solution)/shard_map/ppermute | solution.py:367
  64.6 2.6 %collective-permute-start.15 = (bf16[256,1024]{1,0:T(8,128)(2,1)S(1)}, bf16[256,1024]{1,0:T(8,128)(2,1)S(1)}, u32[]{:S(2)}, u32[]{:S(2)}) collective-permute-start(bf16[256,1024]{1,0:T(8,128)(2,1)S(1)} %get-tuple-element.48), channel_id=1, source_target_pairs={{4,8},{8,4},{5,9},{9,5},{6,10},{10,6},{7,11},{11,7},{20,24},{24,20... | collective-permute-start | bytes 1572872 | tf_op jit(solution)/shard_map/ppermute | solution.py:367
  67.2 1.3 collective-permute-start.13
  68.5 2.7 %collective-permute-start.17 = (bf16[256,1024]{1,0:T(8,128)(2,1)}, bf16[256,1024]{1,0:T(8,128)(2,1)S(1)}, u32[]{:S(2)}, u32[]{:S(2)}) collective-permute-start(bf16[256,1024]{1,0:T(8,128)(2,1)} %collective-permute-done.8), channel_id=1, source_target_pairs={{4,8},{8,4},{5,9},{9,5},{6,10},{10,6},{7,11},{11,7},{20,24},{24,20... | collective-permute-start | bytes 1572872 | tf_op jit(solution)/shard_map/ppermute | solution.py:367
  71.2 7.0 %shard_map.87 = (bf16[42,128,128]{2,1,0:T(8,128)(2,1)S(1)}, f32[42,128,128]{2,1,0:T(8,128)S(1)}) custom-call(s32[8]{0:T(128)S(1)} %concatenate.15.place_ref, s32[84,3]{1,0:T(8,128)S(1)} %copy.11.table_ref, bf16[256,2048]{1,0:T(8,128)(2,1)} %collective-permute-done.1.refs_0_.refs_2_, bf16[256,2048]{1,0:T(8,128)(2,1)} %collective-permute-done.7.refs_1_.refs_3_, ...), custom_call_target="tpu_custom_call" | custom-call | tf_op jit(solution)/shard_map/pallas_call | solution.py:216
  78.1 5.5 %collective-permute-done.9.refs_5_.refs_1_ = bf16[256,2048]{1,0:T(8,128)(2,1)S(1)} collective-permute-done((bf16[256,2048]{1,0:T(8,128)(2,1)S(1)}, bf16[256,2048]{1,0:T(8,128)(2,1)S(1)}, u32[]{:S(2)}, u32[]{:S(2)}) %collective-permute-start.9) | collective-permute-done | bytes 1048608 | tf_op jit(solution)/shard_map/ppermute | solution.py:370
  84.2 1.3 %broadcast_select_fusion.refs_0_ = bf16[256,2048]{1,0:T(8,128)(2,1)S(1)} fusion(bf16[256,2048]{1,0:T(8,128)(2,1)} %collective-permute-done.2, bf16[256,2048]{1,0:T(8,128)(2,1)S(1)} %collective-permute-done.10, pred[]{:T(512)S(6)} %or.3), kind=kLoop, calls=%fused_computation.1 | loop fusion | flops 524288 | bytes 3145729 | tf_op jit(solution)/shard_map/jit(_where)/select_n | solution.py:444
  85.6 0.7 collective-permute-start.11
  86.3 4.2 %collective-permute-start.12 = (bf16[256,1024]{1,0:T(8,128)(2,1)S(1)}, bf16[256,1024]{1,0:T(8,128)(2,1)S(1)}, u32[]{:S(2)}, u32[]{:S(2)}) collective-permute-start(bf16[256,1024]{1,0:T(8,128)(2,1)S(1)} %get-tuple-element.68.refs_6_.refs_2_), channel_id=1, source_target_pairs={{0,1},{1,0},{2,3},{3,2},{4,5},{5,4},{6,7},{7,6},{8,9},{9,8},{10,11... | collective-permute-start | bytes 1572872 | tf_op jit(solution)/shard_map/ppermute | solution.py:373
  91.0 1.0 collective-permute-start.18
  92.0 0.7 collective-permute-done.16.refs_11_.refs_7_
  92.8 0.7 collective-permute-done.14.refs_9_.refs_5_
  93.5 0.7 collective-permute-done.18.refs_13_.refs_9_
  94.3 5.4 %shard_map.88 = (bf16[2,256,256]{2,1,0:T(8,128)(2,1)S(1)}, bf16[2,256,256]{2,1,0:T(8,128)(2,1)S(1)}, bf16[2,256,256]{2,1,0:T(8,128)(2,1)S(1)}) custom-call(s32[8]{0:T(128)S(1)} %concatenate.15.place_ref, bf16[256,2048]{1,0:T(8,128)(2,1)S(1)} %pad_maximum_fusion.refs_0_, bf16[256,2048]{1,0:T(8,128)(2,1)S(1)} %collective-permute-done.3.refs_1_, ...), custom_call_target="tpu_custom_call" | custom-call | tf_op jit(solution)/shard_map/pallas_call | solution.py:312
  99.7 1.3 %collective-permute-start.19 = (bf16[2,256,256]{2,1,0:T(8,128)(2,1)S(1)}, bf16[2,256,256]{2,1,0:T(8,128)(2,1)S(1)}, u32[]{:S(2)}, u32[]{:S(2)}) collective-permute-start(bf16[2,256,256]{2,1,0:T(8,128)(2,1)S(1)} %get-tuple-element.70), channel_id=1, source_target_pairs={{4,0},{8,12},{5,1},{9,13},{6,2},{10,14},{7,3},{11,15},{20,16},{24,... | collective-permute-start | bytes 786440 | tf_op jit(solution)/shard_map/ppermute | solution.py:367
  101.0 2.6 %collective-permute-start.20 = (bf16[2,256,256]{2,1,0:T(8,128)(2,1)S(1)}, bf16[2,256,256]{2,1,0:T(8,128)(2,1)S(1)}, u32[]{:S(2)}, u32[]{:S(2)}) collective-permute-start(bf16[2,256,256]{2,1,0:T(8,128)(2,1)S(1)} %get-tuple-element.71), channel_id=1, source_target_pairs={{4,8},{8,4},{5,9},{9,5},{6,10},{10,6},{7,11},{11,7},{20,24},{24,20... | collective-permute-start | bytes 786440 | tf_op jit(solution)/shard_map/ppermute | solution.py:367
  103.6 6.1 %shard_map.89 = (bf16[42,128,128]{2,1,0:T(8,128)(2,1)S(1)}, f32[42,128,128]{2,1,0:T(8,128)S(1)}) custom-call(s32[8]{0:T(128)S(1)} %concatenate.15.place_ref, s32[84,3]{1,0:T(8,128)S(1)} %copy.11.table_ref, bf16[256,2048]{1,0:T(8,128)(2,1)S(1)} %broadcast_select_fusion.1.refs_4_.refs_0_, bf16[256,2048]{1,0:T(8,128)(2,1)S(1)} %collective-permute-done.9.refs_5_.refs_1_, ...), custom_call_target="tpu_custom_call" | custom-call | tf_op jit(solution)/shard_map/pallas_call | solution.py:216
  109.7 0.7 collective-permute-done.20
  110.4 1.2 collective-permute-start.24
  112.1 2.4 %shard_map.90 = bf16[2,256,256]{2,1,0:T(8,128)(2,1)S(1)} custom-call(s32[8]{0:T(128)S(1)} %concatenate.15.place_ref, bf16[256,2048]{1,0:T(8,128)(2,1)S(1)} %broadcast_select_fusion.refs_0_, bf16[256,2048]{1,0:T(8,128)(2,1)S(1)} %collective-permute-done.11.refs_1_.refs_2_, bf16[256,1024]{1,0:T(8,128)(2,1)S(1)} %get-tuple-element.68.refs_6_.refs_2_, ...), custom_call_target="tpu_custom_call" | custom-call | tf_op jit(solution)/shard_map/pallas_call | solution.py:312
  114.5 1.3 %collective-permute-start.21 = (bf16[2,256,256]{2,1,0:T(8,128)(2,1)S(1)}, bf16[2,256,256]{2,1,0:T(8,128)(2,1)S(1)}, u32[]{:S(2)}, u32[]{:S(2)}) collective-permute-start(bf16[2,256,256]{2,1,0:T(8,128)(2,1)S(1)} %collective-permute-done.20), channel_id=1, source_target_pairs={{4,0},{8,12},{5,1},{9,13},{6,2},{10,14},{7,3},{11,15},{20,16},{24,... | collective-permute-start | bytes 786440 | tf_op jit(solution)/shard_map/ppermute | solution.py:367
  115.9 2.8 %collective-permute-start.22 = (bf16[2,256,256]{2,1,0:T(8,128)(2,1)S(1)}, bf16[2,256,256]{2,1,0:T(8,128)(2,1)S(1)}, u32[]{:S(2)}, u32[]{:S(2)}) collective-permute-start(bf16[2,256,256]{2,1,0:T(8,128)(2,1)S(1)} %shard_map.90), channel_id=1, source_target_pairs={{4,8},{8,4},{5,9},{9,5},{6,10},{10,6},{7,11},{11,7},{20,24},{24,20... | collective-permute-start | bytes 786440 | tf_op jit(solution)/shard_map/ppermute | solution.py:367
  119.0 6.7 %shard_map.91 = f32[42,128,128]{2,1,0:T(8,128)} custom-call(s32[8]{0:T(128)S(1)} %concatenate.15.place_ref, s32[84,3]{1,0:T(8,128)S(1)} %copy.11.table_ref, bf16[256,2048]{1,0:T(8,128)(2,1)S(1)} %broadcast_select_fusion.refs_0_, bf16[256,2048]{1,0:T(8,128)(2,1)S(1)} %collective-permute-done.23.refs_1_, ...), custom_call_target="tpu_custom_call" | custom-call | tf_op jit(solution)/shard_map/pallas_call | solution.py:216
  125.8 0.8 collective-permute-start.27
  126.6 1.0 collective-permute-done.27.refs_5_
  127.6 0.7 copy-done.7
  128.2 2.3 %shard_map.92 = f32[512,512]{1,0:T(8,128)} custom-call(s32[8]{0:T(128)} %copy-done.2, bf16[2,256,256]{2,1,0:T(8,128)(2,1)} %copy-done.1, bf16[2,256,256]{2,1,0:T(8,128)(2,1)} %copy-done.5, bf16[2,256,256]{2,1,0:T(8,128)(2,1)} %copy-done.3, bf16[2,256,256]{2,1,0:T(8,128)(2,1)} %copy-done.4, bf16[256,256]{1,0:T(8,128)(2,1)} %copy-done.6, ...), custom_call_target="tpu_custom_call" | custom-call | tf_op jit(solution)/shard_map/pallas_call | solution.py:344
  (49 shorter events, 2.6 us)
Async XLA Ops:
  0.6 9.5 %copy-start = (s32[1,168,2]{1,2,0:T(2,128)S(1)}, s32[1,168,2]{1,2,0:T(2,128)}, u32[]{:S(2)}) copy-start(s32[1,168,2]{1,2,0:T(2,128)} %param.10) | copy-start | bytes 4036
  1.9 2.3 %collective-permute-start = (bf16[256,1024]{1,0:T(8,128)(2,1)S(1)}, bf16[256,1024]{1,0:T(8,128)(2,1)S(1)}, u32[]{:S(2)}, u32[]{:S(2)}) collective-permute-start(bf16[256,1024]{1,0:T(8,128)(2,1)S(1)} %get-tuple-element.95), channel_id=1, source_target_pairs={{0,1},{1,0},{2,3},{3,2},{4,5},{5,4},{6,7},{7,6},{8,9},{9,8},{10,11... | collective-permute-start | bytes 1572872 | tf_op jit(solution)/shard_map/ppermute | solution.py:373
  4.2 36.0 %copy-start.8 = (s32[4]{0:T(128)S(1)}, s32[4]{0:T(128)}, u32[]{:S(2)}) copy-start(s32[4]{0:T(128)} %constant.71.clone) | copy-start | bytes 52
  4.2 36.0 %copy-start.9 = (s32[4]{0:T(128)S(1)}, s32[4]{0:T(128)}, u32[]{:S(2)}) copy-start(s32[4]{0:T(128)} %constant.72.clone) | copy-start | bytes 52
  4.3 24.5 %collective-permute-start.1 = (bf16[256,2048]{1,0:T(8,128)(2,1)S(1)}, bf16[256,2048]{1,0:T(8,128)(2,1)}, u32[]{:S(2)}, u32[]{:S(2)}) collective-permute-start(bf16[256,2048]{1,0:T(8,128)(2,1)S(1)} %pad_maximum_fusion.refs_0_), channel_id=1, source_target_pairs={{0,4},{4,0},{8,12},{12,8},{1,5},{5,1},{9,13},{13,9},{2,6},{6,2},{1... | collective-permute-start | bytes 3145736 | tf_op jit(solution)/shard_map/ppermute | solution.py:367
  4.4 27.5 %collective-permute-start.2 = (bf16[256,2048]{1,0:T(8,128)(2,1)S(1)}, bf16[256,2048]{1,0:T(8,128)(2,1)}, u32[]{:S(2)}, u32[]{:S(2)}) collective-permute-start(bf16[256,2048]{1,0:T(8,128)(2,1)S(1)} %pad_maximum_fusion.refs_0_), channel_id=1, source_target_pairs={{4,8},{8,4},{5,9},{9,5},{6,10},{10,6},{7,11},{11,7},{20,24},{24,20... | collective-permute-start | bytes 3145736 | tf_op jit(solution)/shard_map/ppermute | solution.py:367
  8.9 23.8 %collective-permute-start.3 = (bf16[256,2048]{1,0:T(8,128)(2,1)S(1)}, bf16[256,2048]{1,0:T(8,128)(2,1)S(1)}, u32[]{:S(2)}, u32[]{:S(2)}) collective-permute-start(bf16[256,2048]{1,0:T(8,128)(2,1)S(1)} %pad_maximum_fusion.refs_0_), channel_id=1, source_target_pairs={{0,2},{2,0},{1,3},{3,1},{4,6},{6,4},{5,7},{7,5},{8,10},{10,8},{9,1... | collective-permute-start | bytes 3145736 | tf_op jit(solution)/shard_map/ppermute | solution.py:370
  10.2 2.5 %collective-permute-start.4 = (s32[42,2]{0,1:T(2,128)S(1)}, s32[42,2]{0,1:T(2,128)S(1)}, u32[]{:S(2)}, u32[]{:S(2)}) collective-permute-start(s32[42,2]{0,1:T(2,128)S(1)} %fusion.1), channel_id=1, source_target_pairs={{0,1},{1,0},{2,3},{3,2},{4,5},{5,4},{6,7},{7,6},{8,9},{9,8},{10,11... | collective-permute-start | bytes 1016 | tf_op jit(solution)/shard_map/ppermute | solution.py:373
  32.7 22.5 %collective-permute-start.5 = (bf16[256,2048]{1,0:T(8,128)(2,1)}, bf16[256,2048]{1,0:T(8,128)(2,1)}, u32[]{:S(2)}, u32[]{:S(2)}) collective-permute-start(bf16[256,2048]{1,0:T(8,128)(2,1)} %collective-permute-done.2), channel_id=1, source_target_pairs={{4,0},{8,12},{5,1},{9,13},{6,2},{10,14},{7,3},{11,15},{20,16},{24,... | collective-permute-start | bytes 3145736 | tf_op jit(solution)/shard_map/ppermute | solution.py:367
  35.0 25.0 %collective-permute-start.6 = (bf16[256,2048]{1,0:T(8,128)(2,1)}, bf16[256,2048]{1,0:T(8,128)(2,1)}, u32[]{:S(2)}, u32[]{:S(2)}) collective-permute-start(bf16[256,2048]{1,0:T(8,128)(2,1)} %collective-permute-done.1.refs_0_.refs_2_), channel_id=1, source_target_pairs={{4,8},{8,4},{5,9},{9,5},{6,10},{10,6},{7,11},{11,7},{20,24},{24,20... | collective-permute-start | bytes 3145736 | tf_op jit(solution)/shard_map/ppermute | solution.py:367
  37.6 22.9 %collective-permute-start.7 = (bf16[256,2048]{1,0:T(8,128)(2,1)}, bf16[256,2048]{1,0:T(8,128)(2,1)}, u32[]{:S(2)}, u32[]{:S(2)}) collective-permute-start(bf16[256,2048]{1,0:T(8,128)(2,1)} %collective-permute-done.1.refs_0_.refs_2_), channel_id=1, source_target_pairs={{0,2},{2,0},{1,3},{3,1},{4,6},{6,4},{5,7},{7,5},{8,10},{10,8},{9,1... | collective-permute-start | bytes 3145736 | tf_op jit(solution)/shard_map/ppermute | solution.py:370
  38.9 13.0 %collective-permute-start.8 = (bf16[256,1024]{1,0:T(8,128)(2,1)S(1)}, bf16[256,1024]{1,0:T(8,128)(2,1)}, u32[]{:S(2)}, u32[]{:S(2)}) collective-permute-start(bf16[256,1024]{1,0:T(8,128)(2,1)S(1)} %get-tuple-element.48), channel_id=1, source_target_pairs={{0,4},{12,8},{1,5},{13,9},{2,6},{14,10},{3,7},{15,11},{16,20},{28,... | collective-permute-start | bytes 1572872 | tf_op jit(solution)/shard_map/ppermute | solution.py:367
  40.3 78.7 %copy-start.2 = (s32[8]{0:T(128)}, s32[8]{0:T(128)S(1)}, u32[]{:S(2)}) copy-start(s32[8]{0:T(128)S(1)} %concatenate.15.place_ref) | copy-start | bytes 100
  61.9 21.7 %collective-permute-start.9 = (bf16[256,2048]{1,0:T(8,128)(2,1)S(1)}, bf16[256,2048]{1,0:T(8,128)(2,1)S(1)}, u32[]{:S(2)}, u32[]{:S(2)}) collective-permute-start(bf16[256,2048]{1,0:T(8,128)(2,1)S(1)} %broadcast_select_fusion.1.refs_4_.refs_0_), channel_id=1, source_target_pairs={{0,2},{2,0},{1,3},{3,1},{4,6},{6,4},{5,7},{7,5},{8,10},{10,8},{9,1... | collective-permute-start | bytes 3145736 | tf_op jit(solution)/shard_map/ppermute | solution.py:370
  63.2 21.0 %collective-permute-start.10 = (bf16[256,2048]{1,0:T(8,128)(2,1)}, bf16[256,2048]{1,0:T(8,128)(2,1)S(1)}, u32[]{:S(2)}, u32[]{:S(2)}) collective-permute-start(bf16[256,2048]{1,0:T(8,128)(2,1)} %collective-permute-done.6), channel_id=1, source_target_pairs={{4,0},{8,12},{5,1},{9,13},{6,2},{10,14},{7,3},{11,15},{20,16},{24,... | collective-permute-start | bytes 3145736 | tf_op jit(solution)/shard_map/ppermute | solution.py:367
  64.6 25.9 %collective-permute-start.15 = (bf16[256,1024]{1,0:T(8,128)(2,1)S(1)}, bf16[256,1024]{1,0:T(8,128)(2,1)S(1)}, u32[]{:S(2)}, u32[]{:S(2)}) collective-permute-start(bf16[256,1024]{1,0:T(8,128)(2,1)S(1)} %get-tuple-element.48), channel_id=1, source_target_pairs={{4,8},{8,4},{5,9},{9,5},{6,10},{10,6},{7,11},{11,7},{20,24},{24,20... | collective-permute-start | bytes 1572872 | tf_op jit(solution)/shard_map/ppermute | solution.py:367
  67.2 23.3 %collective-permute-start.13 = (bf16[256,1024]{1,0:T(8,128)(2,1)S(1)}, bf16[256,1024]{1,0:T(8,128)(2,1)S(1)}, u32[]{:S(2)}, u32[]{:S(2)}) collective-permute-start(bf16[256,1024]{1,0:T(8,128)(2,1)S(1)} %get-tuple-element.68.refs_6_.refs_2_), channel_id=1, source_target_pairs={{0,4},{12,8},{1,5},{13,9},{2,6},{14,10},{3,7},{15,11},{16,20},{28,... | collective-permute-start | bytes 1572872 | tf_op jit(solution)/shard_map/ppermute | solution.py:367
  68.5 22.5 %collective-permute-start.17 = (bf16[256,1024]{1,0:T(8,128)(2,1)}, bf16[256,1024]{1,0:T(8,128)(2,1)S(1)}, u32[]{:S(2)}, u32[]{:S(2)}) collective-permute-start(bf16[256,1024]{1,0:T(8,128)(2,1)} %collective-permute-done.8), channel_id=1, source_target_pairs={{4,8},{8,4},{5,9},{9,5},{6,10},{10,6},{7,11},{11,7},{20,24},{24,20... | collective-permute-start | bytes 1572872 | tf_op jit(solution)/shard_map/ppermute | solution.py:367
  85.6 24.9 %collective-permute-start.11 = (bf16[256,2048]{1,0:T(8,128)(2,1)S(1)}, bf16[256,2048]{1,0:T(8,128)(2,1)S(1)}, u32[]{:S(2)}, u32[]{:S(2)}) collective-permute-start(bf16[256,2048]{1,0:T(8,128)(2,1)S(1)} %broadcast_select_fusion.refs_0_), channel_id=1, source_target_pairs={{0,2},{2,0},{1,3},{3,1},{4,6},{6,4},{5,7},{7,5},{8,10},{10,8},{9,1... | collective-permute-start | bytes 3145736 | tf_op jit(solution)/shard_map/ppermute | solution.py:370
  86.3 5.8 %collective-permute-start.12 = (bf16[256,1024]{1,0:T(8,128)(2,1)S(1)}, bf16[256,1024]{1,0:T(8,128)(2,1)S(1)}, u32[]{:S(2)}, u32[]{:S(2)}) collective-permute-start(bf16[256,1024]{1,0:T(8,128)(2,1)S(1)} %get-tuple-element.68.refs_6_.refs_2_), channel_id=1, source_target_pairs={{0,1},{1,0},{2,3},{3,2},{4,5},{5,4},{6,7},{7,6},{8,9},{9,8},{10,11... | collective-permute-start | bytes 1572872 | tf_op jit(solution)/shard_map/ppermute | solution.py:373
  90.5 2.3 %collective-permute-start.16 = (bf16[256,1024]{1,0:T(8,128)(2,1)S(1)}, bf16[256,1024]{1,0:T(8,128)(2,1)S(1)}, u32[]{:S(2)}, u32[]{:S(2)}) collective-permute-start(bf16[256,1024]{1,0:T(8,128)(2,1)S(1)} %collective-permute-done.15.refs_10_.refs_6_), channel_id=1, source_target_pairs={{0,1},{1,0},{2,3},{3,2},{4,5},{5,4},{6,7},{7,6},{8,9},{9,8},{10,11... | collective-permute-start | bytes 1572872 | tf_op jit(solution)/shard_map/ppermute | solution.py:373
  90.5 3.0 %collective-permute-start.14 = (bf16[256,1024]{1,0:T(8,128)(2,1)S(1)}, bf16[256,1024]{1,0:T(8,128)(2,1)S(1)}, u32[]{:S(2)}, u32[]{:S(2)}) collective-permute-start(bf16[256,1024]{1,0:T(8,128)(2,1)S(1)} %collective-permute-done.13.refs_8_.refs_4_), channel_id=1, source_target_pairs={{0,1},{1,0},{2,3},{3,2},{4,5},{5,4},{6,7},{7,6},{8,9},{9,8},{10,11... | collective-permute-start | bytes 1572872 | tf_op jit(solution)/shard_map/ppermute | solution.py:373
  91.0 3.3 %collective-permute-start.18 = (bf16[256,1024]{1,0:T(8,128)(2,1)S(1)}, bf16[256,1024]{1,0:T(8,128)(2,1)S(1)}, u32[]{:S(2)}, u32[]{:S(2)}) collective-permute-start(bf16[256,1024]{1,0:T(8,128)(2,1)S(1)} %collective-permute-done.17.refs_12_.refs_8_), channel_id=1, source_target_pairs={{0,1},{1,0},{2,3},{3,2},{4,5},{5,4},{6,7},{7,6},{8,9},{9,8},{10,11... | collective-permute-start | bytes 1572872 | tf_op jit(solution)/shard_map/ppermute | solution.py:373
  99.7 10.0 %copy-start.1 = (bf16[2,256,256]{2,1,0:T(8,128)(2,1)}, bf16[2,256,256]{2,1,0:T(8,128)(2,1)S(1)}, u32[]{:S(2)}) copy-start(bf16[2,256,256]{2,1,0:T(8,128)(2,1)S(1)} %get-tuple-element.75.refs_0_) | copy-start | bytes 786436
  99.7 10.0 %collective-permute-start.19 = (bf16[2,256,256]{2,1,0:T(8,128)(2,1)S(1)}, bf16[2,256,256]{2,1,0:T(8,128)(2,1)S(1)}, u32[]{:S(2)}, u32[]{:S(2)}) collective-permute-start(bf16[2,256,256]{2,1,0:T(8,128)(2,1)S(1)} %get-tuple-element.70), channel_id=1, source_target_pairs={{4,0},{8,12},{5,1},{9,13},{6,2},{10,14},{7,3},{11,15},{20,16},{24,... | collective-permute-start | bytes 786440 | tf_op jit(solution)/shard_map/ppermute | solution.py:367
  101.0 9.4 %collective-permute-start.20 = (bf16[2,256,256]{2,1,0:T(8,128)(2,1)S(1)}, bf16[2,256,256]{2,1,0:T(8,128)(2,1)S(1)}, u32[]{:S(2)}, u32[]{:S(2)}) collective-permute-start(bf16[2,256,256]{2,1,0:T(8,128)(2,1)S(1)} %get-tuple-element.71), channel_id=1, source_target_pairs={{4,8},{8,4},{5,9},{9,5},{6,10},{10,6},{7,11},{11,7},{20,24},{24,20... | collective-permute-start | bytes 786440 | tf_op jit(solution)/shard_map/ppermute | solution.py:367
  109.7 4.8 %copy-start.3 = (bf16[2,256,256]{2,1,0:T(8,128)(2,1)}, bf16[2,256,256]{2,1,0:T(8,128)(2,1)S(1)}, u32[]{:S(2)}) copy-start(bf16[2,256,256]{2,1,0:T(8,128)(2,1)S(1)} %collective-permute-done.19.refs_2_) | copy-start | bytes 786436
  110.4 8.6 %collective-permute-start.24 = (bf16[42,128,128]{2,1,0:T(8,128)(2,1)S(1)}, bf16[42,128,128]{2,1,0:T(8,128)(2,1)S(1)}, u32[]{:S(2)}, u32[]{:S(2)}) collective-permute-start(bf16[42,128,128]{2,1,0:T(8,128)(2,1)S(1)} %get-tuple-element.82), channel_id=1, source_target_pairs={{0,1},{1,0},{2,3},{3,2},{4,5},{5,4},{6,7},{7,6},{8,9},{9,8},{10,11... | collective-permute-start | bytes 4128776 | tf_op jit(solution)/shard_map/ppermute | solution.py:373
  111.6 7.0 %collective-permute-start.25 = (bf16[256,2048]{1,0:T(8,128)(2,1)S(1)}, bf16[256,2048]{1,0:T(8,128)(2,1)S(1)}, u32[]{:S(2)}, u32[]{:S(2)}) collective-permute-start(bf16[256,2048]{1,0:T(8,128)(2,1)S(1)} %collective-permute-done.11.refs_1_.refs_2_), channel_id=1, source_target_pairs={{0,1},{1,0},{2,3},{3,2},{4,5},{5,4},{6,7},{7,6},{8,9},{9,8},{10,11... | collective-permute-start | bytes 3145736 | tf_op jit(solution)/shard_map/ppermute | solution.py:373
  111.6 7.4 %collective-permute-start.23 = (bf16[256,2048]{1,0:T(8,128)(2,1)S(1)}, bf16[256,2048]{1,0:T(8,128)(2,1)S(1)}, u32[]{:S(2)}, u32[]{:S(2)}) collective-permute-start(bf16[256,2048]{1,0:T(8,128)(2,1)S(1)} %broadcast_select_fusion.refs_0_), channel_id=1, source_target_pairs={{0,1},{1,0},{2,3},{3,2},{4,5},{5,4},{6,7},{7,6},{8,9},{9,8},{10,11... | collective-permute-start | bytes 3145736 | tf_op jit(solution)/shard_map/ppermute | solution.py:373
  114.5 11.2 %collective-permute-start.21 = (bf16[2,256,256]{2,1,0:T(8,128)(2,1)S(1)}, bf16[2,256,256]{2,1,0:T(8,128)(2,1)S(1)}, u32[]{:S(2)}, u32[]{:S(2)}) collective-permute-start(bf16[2,256,256]{2,1,0:T(8,128)(2,1)S(1)} %collective-permute-done.20), channel_id=1, source_target_pairs={{4,0},{8,12},{5,1},{9,13},{6,2},{10,14},{7,3},{11,15},{20,16},{24,... | collective-permute-start | bytes 786440 | tf_op jit(solution)/shard_map/ppermute | solution.py:367
  115.9 9.9 %collective-permute-start.22 = (bf16[2,256,256]{2,1,0:T(8,128)(2,1)S(1)}, bf16[2,256,256]{2,1,0:T(8,128)(2,1)S(1)}, u32[]{:S(2)}, u32[]{:S(2)}) collective-permute-start(bf16[2,256,256]{2,1,0:T(8,128)(2,1)S(1)} %shard_map.90), channel_id=1, source_target_pairs={{4,8},{8,4},{5,9},{9,5},{6,10},{10,6},{7,11},{11,7},{20,24},{24,20... | collective-permute-start | bytes 786440 | tf_op jit(solution)/shard_map/ppermute | solution.py:367
  118.7 7.9 %collective-permute-start.26 = (bf16[256,256]{1,0:T(8,128)(2,1)S(1)}, bf16[256,256]{1,0:T(8,128)(2,1)S(1)}, u32[]{:S(2)}, u32[]{:S(2)}) collective-permute-start(bf16[256,256]{1,0:T(8,128)(2,1)S(1)} %fusion), channel_id=1, source_target_pairs={{0,1},{1,0},{2,3},{3,2},{4,5},{5,4},{6,7},{7,6},{8,9},{9,8},{10,11... | collective-permute-start | bytes 393224 | tf_op jit(solution)/shard_map/ppermute | solution.py:373
  125.7 1.8 %copy-start.4 = (bf16[2,256,256]{2,1,0:T(8,128)(2,1)}, bf16[2,256,256]{2,1,0:T(8,128)(2,1)S(1)}, u32[]{:S(2)}) copy-start(bf16[2,256,256]{2,1,0:T(8,128)(2,1)S(1)} %collective-permute-done.21.refs_3_) | copy-start | bytes 786436
  125.8 1.8 %copy-start.5 = (bf16[2,256,256]{2,1,0:T(8,128)(2,1)}, bf16[2,256,256]{2,1,0:T(8,128)(2,1)S(1)}, u32[]{:S(2)}) copy-start(bf16[2,256,256]{2,1,0:T(8,128)(2,1)S(1)} %collective-permute-done.22.refs_1_) | copy-start | bytes 786436
  125.8 1.7 %collective-permute-start.27 = (bf16[256,256]{1,0:T(8,128)(2,1)S(1)}, bf16[256,256]{1,0:T(8,128)(2,1)S(1)}, u32[]{:S(2)}, u32[]{:S(2)}) collective-permute-start(bf16[256,256]{1,0:T(8,128)(2,1)S(1)} %select_bitcast_fusion), channel_id=1, source_target_pairs={{0,1},{1,0},{2,3},{3,2},{4,5},{5,4},{6,7},{7,6},{8,9},{9,8},{10,11... | collective-permute-start | bytes 393224 | tf_op jit(solution)/shard_map/ppermute | solution.py:373
  126.6 1.0 copy-start.6
  127.5 0.7 copy-start.7

commit v5 on v4

--- a/solution.py
+++ b/solution.py
@@ -346,6 +346,7 @@
         out_shape=jax.ShapeDtypeStruct((2 * group, 2 * count), jnp.float32),
         in_specs=[smem] + [vmem] * 7,
         out_specs=vmem,
+        compiler_params=pltpu.CompilerParams(vmem_limit_bytes=8 * 2**20),
         cost_estimate=pl.CostEstimate(flops=0, bytes_accessed=0, transcendentals=0),
     )(place, *on_middle, *on_ends, *swapped, weights)
 

time: 131 us -> 130 us (level)
  no operation moved by 1% of the time
where the time goes in v5:
time: 130 us; the launch traced here: 129 us
  waiting for transfers between devices  46.3 us (36%)
  starting transfers between devices  41.7 us (32%)
  Pallas kernels  34.5 us (27%)
  other arithmetic  2.89 us (2%)
  local copies, waits for them, and re-layouts  2.84 us (2%)
    ppermute x13, waiting for transfers between devices, move(): return lax.ppermute(value, 'ex', pairs)  34.6 us
    ppermute x13, starting transfers between devices, move(): return lax.ppermute(value, 'ex', pairs)  26.7 us
    pallas_call x4, Pallas kernels, tile_call(): pl.pallas_call(kernel, out_shape=outs + (scores.out_shape if scores else...  25.1 us
    ppermute x11, starting transfers between devices, swap(): return lax.ppermute(value, 'feat', CORE)  10.5 us
    pallas_call x2, Pallas kernels, score_call(): pl.pallas_call(kernel, out_shape=scores.out_shape, in_specs=[smem] + [hbm...  7.79 us
    ppermute x4, waiting for transfers between devices, across(): return lax.ppermute(value, 'feat', ACROSS)  6.92 us
    ppermute x11, waiting for transfers between devices, swap(): return lax.ppermute(value, 'feat', CORE)  4.75 us
    ppermute x4, starting transfers between devices, across(): return lax.ppermute(value, 'feat', ACROSS)  4.52 us
  transfers between devices with their start and end apart: 28, of which 15 were waited for; matrix products, arithmetic and copies ran while one was open for 2% of the time, Pallas kernels for 25%

profile of v5, /device:TPU:9, one launch (start us, length us, event | category | flops | bytes accessed | tf_op | source)
XLA Modules:
  0.0 129.2 jit_solution(10302040932021019385)
XLA Ops:
  0.7 1.3 constant_dynamic-slice_fusion.4
  1.9 0.7 collective-permute-start
  2.7 1.5 %collective-permute-done = bf16[256,1024]{1,0:T(8,128)(2,1)S(1)} collective-permute-done((bf16[256,1024]{1,0:T(8,128)(2,1)S(1)}, bf16[256,1024]{1,0:T(8,128)(2,1)S(1)}, u32[]{:S(2)}, u32[]{:S(2)}) %collective-permute-start) | collective-permute-done | bytes 524320 | tf_op jit(solution)/shard_map/ppermute | solution.py:374
  4.4 4.5 %collective-permute-start.2 = (bf16[256,2048]{1,0:T(8,128)(2,1)S(1)}, bf16[256,2048]{1,0:T(8,128)(2,1)}, u32[]{:S(2)}, u32[]{:S(2)}) collective-permute-start(bf16[256,2048]{1,0:T(8,128)(2,1)S(1)} %pad_maximum_fusion.refs_0_), channel_id=1, source_target_pairs={{4,8},{8,4},{5,9},{9,5},{6,10},{10,6},{7,11},{11,7},{20,24},{24,20... | collective-permute-start | bytes 3145736 | tf_op jit(solution)/shard_map/ppermute | solution.py:368
  8.9 1.3 collective-permute-start.3
  10.2 1.2 collective-permute-start.4
  11.4 1.3 constant_dynamic-slice_fusion.1
  12.8 16.0 %collective-permute-done.1.refs_0_.refs_2_ = bf16[256,2048]{1,0:T(8,128)(2,1)} collective-permute-done((bf16[256,2048]{1,0:T(8,128)(2,1)S(1)}, bf16[256,2048]{1,0:T(8,128)(2,1)}, u32[]{:S(2)}, u32[]{:S(2)}) %collective-permute-start.1) | collective-permute-done | bytes 1048608 | tf_op jit(solution)/shard_map/ppermute | solution.py:368
  28.9 3.0 %collective-permute-done.2 = bf16[256,2048]{1,0:T(8,128)(2,1)} collective-permute-done((bf16[256,2048]{1,0:T(8,128)(2,1)S(1)}, bf16[256,2048]{1,0:T(8,128)(2,1)}, u32[]{:S(2)}, u32[]{:S(2)}) %collective-permute-start.2) | collective-permute-done | bytes 1048608 | tf_op jit(solution)/shard_map/ppermute | solution.py:368
  31.9 0.8 collective-permute-done.3.refs_1_
  32.7 2.3 %collective-permute-start.5 = (bf16[256,2048]{1,0:T(8,128)(2,1)}, bf16[256,2048]{1,0:T(8,128)(2,1)}, u32[]{:S(2)}, u32[]{:S(2)}) collective-permute-start(bf16[256,2048]{1,0:T(8,128)(2,1)} %collective-permute-done.2), channel_id=1, source_target_pairs={{4,0},{8,12},{5,1},{9,13},{6,2},{10,14},{7,3},{11,15},{20,16},{24,... | collective-permute-start | bytes 3145736 | tf_op jit(solution)/shard_map/ppermute | solution.py:368
  35.0 2.7 %collective-permute-start.6 = (bf16[256,2048]{1,0:T(8,128)(2,1)}, bf16[256,2048]{1,0:T(8,128)(2,1)}, u32[]{:S(2)}, u32[]{:S(2)}) collective-permute-start(bf16[256,2048]{1,0:T(8,128)(2,1)} %collective-permute-done.1.refs_0_.refs_2_), channel_id=1, source_target_pairs={{4,8},{8,4},{5,9},{9,5},{6,10},{10,6},{7,11},{11,7},{20,24},{24,20... | collective-permute-start | bytes 3145736 | tf_op jit(solution)/shard_map/ppermute | solution.py:368
  37.7 1.3 collective-permute-start.7
  38.9 1.3 collective-permute-start.8
  40.5 5.3 %shard_map.86 = (bf16[42,128,128]{2,1,0:T(8,128)(2,1)S(1)}, f32[42,128,128]{2,1,0:T(8,128)S(1)}) custom-call(s32[8]{0:T(128)S(1)} %concatenate.15.place_ref, s32[84,3]{1,0:T(8,128)S(1)} %copy.11.table_ref, bf16[256,2048]{1,0:T(8,128)(2,1)S(1)} %pad_maximum_fusion.refs_0_, bf16[256,2048]{1,0:T(8,128)(2,1)S(1)} %collective-permute-done.3.refs_1_), custom_call_target="tpu_custom_call" | custom-call | tf_op jit(solution)/shard_map/pallas_call | solution.py:216
  45.8 6.2 %collective-permute-done.8 = bf16[256,1024]{1,0:T(8,128)(2,1)} collective-permute-done((bf16[256,1024]{1,0:T(8,128)(2,1)S(1)}, bf16[256,1024]{1,0:T(8,128)(2,1)}, u32[]{:S(2)}, u32[]{:S(2)}) %collective-permute-start.8) | collective-permute-done | bytes 524320 | tf_op jit(solution)/shard_map/ppermute | solution.py:368
  52.0 3.2 %collective-permute-done.5 = bf16[256,2048]{1,0:T(8,128)(2,1)} collective-permute-done((bf16[256,2048]{1,0:T(8,128)(2,1)}, bf16[256,2048]{1,0:T(8,128)(2,1)}, u32[]{:S(2)}, u32[]{:S(2)}) %collective-permute-start.5) | collective-permute-done | bytes 1048608 | tf_op jit(solution)/shard_map/ppermute | solution.py:368
  55.2 4.8 %collective-permute-done.6 = bf16[256,2048]{1,0:T(8,128)(2,1)} collective-permute-done((bf16[256,2048]{1,0:T(8,128)(2,1)}, bf16[256,2048]{1,0:T(8,128)(2,1)}, u32[]{:S(2)}, u32[]{:S(2)}) %collective-permute-start.6) | collective-permute-done | bytes 1048608 | tf_op jit(solution)/shard_map/ppermute | solution.py:368
  60.0 0.6 collective-permute-done.7.refs_1_.refs_3_
  60.6 1.3 %broadcast_select_fusion.1.refs_4_.refs_0_ = bf16[256,2048]{1,0:T(8,128)(2,1)S(1)} fusion(bf16[256,2048]{1,0:T(8,128)(2,1)} %collective-permute-done.6, bf16[256,2048]{1,0:T(8,128)(2,1)} %collective-permute-done.5, pred[]{:T(512)S(6)} %or.3), kind=kLoop, calls=%fused_computation.2 | loop fusion | flops 524288 | bytes 3145729 | tf_op jit(solution)/shard_map/jit(_where)/select_n | solution.py:434
  61.9 1.3 collective-permute-start.9
  63.2 1.3 %collective-permute-start.10 = (bf16[256,2048]{1,0:T(8,128)(2,1)}, bf16[256,2048]{1,0:T(8,128)(2,1)S(1)}, u32[]{:S(2)}, u32[]{:S(2)}) collective-permute-start(bf16[256,2048]{1,0:T(8,128)(2,1)} %collective-permute-done.6), channel_id=1, source_target_pairs={{4,0},{8,12},{5,1},{9,13},{6,2},{10,14},{7,3},{11,15},{20,16},{24,... | collective-permute-start | bytes 3145736 | tf_op jit(solution)/shard_map/ppermute | solution.py:368
  64.6 2.6 %collective-permute-start.15 = (bf16[256,1024]{1,0:T(8,128)(2,1)S(1)}, bf16[256,1024]{1,0:T(8,128)(2,1)S(1)}, u32[]{:S(2)}, u32[]{:S(2)}) collective-permute-start(bf16[256,1024]{1,0:T(8,128)(2,1)S(1)} %get-tuple-element.48), channel_id=1, source_target_pairs={{4,8},{8,4},{5,9},{9,5},{6,10},{10,6},{7,11},{11,7},{20,24},{24,20... | collective-permute-start | bytes 1572872 | tf_op jit(solution)/shard_map/ppermute | solution.py:368
  67.2 1.3 %collective-permute-start.13 = (bf16[256,1024]{1,0:T(8,128)(2,1)S(1)}, bf16[256,1024]{1,0:T(8,128)(2,1)S(1)}, u32[]{:S(2)}, u32[]{:S(2)}) collective-permute-start(bf16[256,1024]{1,0:T(8,128)(2,1)S(1)} %get-tuple-element.68.refs_6_.refs_2_), channel_id=1, source_target_pairs={{0,4},{12,8},{1,5},{13,9},{2,6},{14,10},{3,7},{15,11},{16,20},{28,... | collective-permute-start | bytes 1572872 | tf_op jit(solution)/shard_map/ppermute | solution.py:368
  68.5 2.7 %collective-permute-start.17 = (bf16[256,1024]{1,0:T(8,128)(2,1)}, bf16[256,1024]{1,0:T(8,128)(2,1)S(1)}, u32[]{:S(2)}, u32[]{:S(2)}) collective-permute-start(bf16[256,1024]{1,0:T(8,128)(2,1)} %collective-permute-done.8), channel_id=1, source_target_pairs={{4,8},{8,4},{5,9},{9,5},{6,10},{10,6},{7,11},{11,7},{20,24},{24,20... | collective-permute-start | bytes 1572872 | tf_op jit(solution)/shard_map/ppermute | solution.py:368
  71.2 7.0 %shard_map.87 = (bf16[42,128,128]{2,1,0:T(8,128)(2,1)S(1)}, f32[42,128,128]{2,1,0:T(8,128)S(1)}) custom-call(s32[8]{0:T(128)S(1)} %concatenate.15.place_ref, s32[84,3]{1,0:T(8,128)S(1)} %copy.11.table_ref, bf16[256,2048]{1,0:T(8,128)(2,1)} %collective-permute-done.1.refs_0_.refs_2_, bf16[256,2048]{1,0:T(8,128)(2,1)} %collective-permute-done.7.refs_1_.refs_3_, ...), custom_call_target="tpu_custom_call" | custom-call | tf_op jit(solution)/shard_map/pallas_call | solution.py:216
  78.1 5.5 %collective-permute-done.9.refs_5_.refs_1_ = bf16[256,2048]{1,0:T(8,128)(2,1)S(1)} collective-permute-done((bf16[256,2048]{1,0:T(8,128)(2,1)S(1)}, bf16[256,2048]{1,0:T(8,128)(2,1)S(1)}, u32[]{:S(2)}, u32[]{:S(2)}) %collective-permute-start.9) | collective-permute-done | bytes 1048608 | tf_op jit(solution)/shard_map/ppermute | solution.py:371
  83.7 0.6 collective-permute-done.10
  84.3 1.3 %broadcast_select_fusion.refs_0_ = bf16[256,2048]{1,0:T(8,128)(2,1)S(1)} fusion(bf16[256,2048]{1,0:T(8,128)(2,1)} %collective-permute-done.2, bf16[256,2048]{1,0:T(8,128)(2,1)S(1)} %collective-permute-done.10, pred[]{:T(512)S(6)} %or.3), kind=kLoop, calls=%fused_computation.1 | loop fusion | flops 524288 | bytes 3145729 | tf_op jit(solution)/shard_map/jit(_where)/select_n | solution.py:445
  85.6 0.7 collective-permute-start.11
  86.3 4.2 %collective-permute-start.12 = (bf16[256,1024]{1,0:T(8,128)(2,1)S(1)}, bf16[256,1024]{1,0:T(8,128)(2,1)S(1)}, u32[]{:S(2)}, u32[]{:S(2)}) collective-permute-start(bf16[256,1024]{1,0:T(8,128)(2,1)S(1)} %get-tuple-element.68.refs_6_.refs_2_), channel_id=1, source_target_pairs={{0,1},{1,0},{2,3},{3,2},{4,5},{5,4},{6,7},{7,6},{8,9},{9,8},{10,11... | collective-permute-start | bytes 1572872 | tf_op jit(solution)/shard_map/ppermute | solution.py:374
  91.0 1.0 collective-permute-start.18
  92.0 0.7 collective-permute-done.16.refs_11_.refs_7_
  92.8 0.7 collective-permute-done.14.refs_9_.refs_5_
  93.5 0.7 collective-permute-done.18.refs_13_.refs_9_
  94.3 5.4 %shard_map.88 = (bf16[2,256,256]{2,1,0:T(8,128)(2,1)S(1)}, bf16[2,256,256]{2,1,0:T(8,128)(2,1)S(1)}, bf16[2,256,256]{2,1,0:T(8,128)(2,1)S(1)}) custom-call(s32[8]{0:T(128)S(1)} %concatenate.15.place_ref, bf16[256,2048]{1,0:T(8,128)(2,1)S(1)} %pad_maximum_fusion.refs_0_, bf16[256,2048]{1,0:T(8,128)(2,1)S(1)} %collective-permute-done.3.refs_1_, ...), custom_call_target="tpu_custom_call" | custom-call | tf_op jit(solution)/shard_map/pallas_call | solution.py:312
  99.7 1.3 %collective-permute-start.19 = (bf16[2,256,256]{2,1,0:T(8,128)(2,1)S(1)}, bf16[2,256,256]{2,1,0:T(8,128)(2,1)S(1)}, u32[]{:S(2)}, u32[]{:S(2)}) collective-permute-start(bf16[2,256,256]{2,1,0:T(8,128)(2,1)S(1)} %get-tuple-element.70), channel_id=1, source_target_pairs={{4,0},{8,12},{5,1},{9,13},{6,2},{10,14},{7,3},{11,15},{20,16},{24,... | collective-permute-start | bytes 786440 | tf_op jit(solution)/shard_map/ppermute | solution.py:368
  101.0 2.6 %collective-permute-start.20 = (bf16[2,256,256]{2,1,0:T(8,128)(2,1)S(1)}, bf16[2,256,256]{2,1,0:T(8,128)(2,1)S(1)}, u32[]{:S(2)}, u32[]{:S(2)}) collective-permute-start(bf16[2,256,256]{2,1,0:T(8,128)(2,1)S(1)} %get-tuple-element.71), channel_id=1, source_target_pairs={{4,8},{8,4},{5,9},{9,5},{6,10},{10,6},{7,11},{11,7},{20,24},{24,20... | collective-permute-start | bytes 786440 | tf_op jit(solution)/shard_map/ppermute | solution.py:368
  103.6 6.1 %shard_map.89 = (bf16[42,128,128]{2,1,0:T(8,128)(2,1)S(1)}, f32[42,128,128]{2,1,0:T(8,128)S(1)}) custom-call(s32[8]{0:T(128)S(1)} %concatenate.15.place_ref, s32[84,3]{1,0:T(8,128)S(1)} %copy.11.table_ref, bf16[256,2048]{1,0:T(8,128)(2,1)S(1)} %broadcast_select_fusion.1.refs_4_.refs_0_, bf16[256,2048]{1,0:T(8,128)(2,1)S(1)} %collective-permute-done.9.refs_5_.refs_1_, ...), custom_call_target="tpu_custom_call" | custom-call | tf_op jit(solution)/shard_map/pallas_call | solution.py:216
  109.7 0.7 collective-permute-done.20
  110.4 1.2 collective-permute-start.24
  112.1 2.4 %shard_map.90 = bf16[2,256,256]{2,1,0:T(8,128)(2,1)S(1)} custom-call(s32[8]{0:T(128)S(1)} %concatenate.15.place_ref, bf16[256,2048]{1,0:T(8,128)(2,1)S(1)} %broadcast_select_fusion.refs_0_, bf16[256,2048]{1,0:T(8,128)(2,1)S(1)} %collective-permute-done.11.refs_1_.refs_2_, bf16[256,1024]{1,0:T(8,128)(2,1)S(1)} %get-tuple-element.68.refs_6_.refs_2_, ...), custom_call_target="tpu_custom_call" | custom-call | tf_op jit(solution)/shard_map/pallas_call | solution.py:312
  114.5 1.3 %collective-permute-start.21 = (bf16[2,256,256]{2,1,0:T(8,128)(2,1)S(1)}, bf16[2,256,256]{2,1,0:T(8,128)(2,1)S(1)}, u32[]{:S(2)}, u32[]{:S(2)}) collective-permute-start(bf16[2,256,256]{2,1,0:T(8,128)(2,1)S(1)} %collective-permute-done.20), channel_id=1, source_target_pairs={{4,0},{8,12},{5,1},{9,13},{6,2},{10,14},{7,3},{11,15},{20,16},{24,... | collective-permute-start | bytes 786440 | tf_op jit(solution)/shard_map/ppermute | solution.py:368
  115.8 2.8 %collective-permute-start.22 = (bf16[2,256,256]{2,1,0:T(8,128)(2,1)S(1)}, bf16[2,256,256]{2,1,0:T(8,128)(2,1)S(1)}, u32[]{:S(2)}, u32[]{:S(2)}) collective-permute-start(bf16[2,256,256]{2,1,0:T(8,128)(2,1)S(1)} %shard_map.90), channel_id=1, source_target_pairs={{4,8},{8,4},{5,9},{9,5},{6,10},{10,6},{7,11},{11,7},{20,24},{24,20... | collective-permute-start | bytes 786440 | tf_op jit(solution)/shard_map/ppermute | solution.py:368
  119.0 6.7 %shard_map.91 = f32[42,128,128]{2,1,0:T(8,128)} custom-call(s32[8]{0:T(128)S(1)} %concatenate.15.place_ref, s32[84,3]{1,0:T(8,128)S(1)} %copy.11.table_ref, bf16[256,2048]{1,0:T(8,128)(2,1)S(1)} %broadcast_select_fusion.refs_0_, bf16[256,2048]{1,0:T(8,128)(2,1)S(1)} %collective-permute-done.23.refs_1_, ...), custom_call_target="tpu_custom_call" | custom-call | tf_op jit(solution)/shard_map/pallas_call | solution.py:216
  125.8 0.7 collective-permute-start.27
  126.6 1.0 collective-permute-done.27.refs_5_
  127.5 1.6 %shard_map.92 = f32[512,512]{1,0:T(8,128)} custom-call(s32[8]{0:T(128)S(1)} %concatenate.15.place_ref, bf16[2,256,256]{2,1,0:T(8,128)(2,1)S(1)} %get-tuple-element.75.refs_0_, bf16[2,256,256]{2,1,0:T(8,128)(2,1)S(1)} %collective-permute-done.22.refs_1_, bf16[2,256,256]{2,1,0:T(8,128)(2,1)S(1)} %collective-permute-done.19.refs_2_, ...), custom_call_target="tpu_custom_call" | custom-call | tf_op jit(solution)/shard_map/pallas_call | solution.py:344
  (37 shorter events, 2.0 us)
Async XLA Ops:
  0.6 9.5 %copy-start = (s32[1,168,2]{1,2,0:T(2,128)S(1)}, s32[1,168,2]{1,2,0:T(2,128)}, u32[]{:S(2)}) copy-start(s32[1,168,2]{1,2,0:T(2,128)} %param.10) | copy-start | bytes 4036
  1.9 2.3 %collective-permute-start = (bf16[256,1024]{1,0:T(8,128)(2,1)S(1)}, bf16[256,1024]{1,0:T(8,128)(2,1)S(1)}, u32[]{:S(2)}, u32[]{:S(2)}) collective-permute-start(bf16[256,1024]{1,0:T(8,128)(2,1)S(1)} %get-tuple-element.95), channel_id=1, source_target_pairs={{0,1},{1,0},{2,3},{3,2},{4,5},{5,4},{6,7},{7,6},{8,9},{9,8},{10,11... | collective-permute-start | bytes 1572872 | tf_op jit(solution)/shard_map/ppermute | solution.py:374
  4.2 36.0 %copy-start.2 = (s32[4]{0:T(128)S(1)}, s32[4]{0:T(128)}, u32[]{:S(2)}) copy-start(s32[4]{0:T(128)} %constant.71.clone) | copy-start | bytes 52
  4.2 36.0 %copy-start.3 = (s32[4]{0:T(128)S(1)}, s32[4]{0:T(128)}, u32[]{:S(2)}) copy-start(s32[4]{0:T(128)} %constant.72.clone) | copy-start | bytes 52
  4.3 24.5 %collective-permute-start.1 = (bf16[256,2048]{1,0:T(8,128)(2,1)S(1)}, bf16[256,2048]{1,0:T(8,128)(2,1)}, u32[]{:S(2)}, u32[]{:S(2)}) collective-permute-start(bf16[256,2048]{1,0:T(8,128)(2,1)S(1)} %pad_maximum_fusion.refs_0_), channel_id=1, source_target_pairs={{0,4},{4,0},{8,12},{12,8},{1,5},{5,1},{9,13},{13,9},{2,6},{6,2},{1... | collective-permute-start | bytes 3145736 | tf_op jit(solution)/shard_map/ppermute | solution.py:368
  4.4 27.5 %collective-permute-start.2 = (bf16[256,2048]{1,0:T(8,128)(2,1)S(1)}, bf16[256,2048]{1,0:T(8,128)(2,1)}, u32[]{:S(2)}, u32[]{:S(2)}) collective-permute-start(bf16[256,2048]{1,0:T(8,128)(2,1)S(1)} %pad_maximum_fusion.refs_0_), channel_id=1, source_target_pairs={{4,8},{8,4},{5,9},{9,5},{6,10},{10,6},{7,11},{11,7},{20,24},{24,20... | collective-permute-start | bytes 3145736 | tf_op jit(solution)/shard_map/ppermute | solution.py:368
  8.9 23.8 %collective-permute-start.3 = (bf16[256,2048]{1,0:T(8,128)(2,1)S(1)}, bf16[256,2048]{1,0:T(8,128)(2,1)S(1)}, u32[]{:S(2)}, u32[]{:S(2)}) collective-permute-start(bf16[256,2048]{1,0:T(8,128)(2,1)S(1)} %pad_maximum_fusion.refs_0_), channel_id=1, source_target_pairs={{0,2},{2,0},{1,3},{3,1},{4,6},{6,4},{5,7},{7,5},{8,10},{10,8},{9,1... | collective-permute-start | bytes 3145736 | tf_op jit(solution)/shard_map/ppermute | solution.py:371
  10.2 2.5 %collective-permute-start.4 = (s32[42,2]{0,1:T(2,128)S(1)}, s32[42,2]{0,1:T(2,128)S(1)}, u32[]{:S(2)}, u32[]{:S(2)}) collective-permute-start(s32[42,2]{0,1:T(2,128)S(1)} %fusion.1), channel_id=1, source_target_pairs={{0,1},{1,0},{2,3},{3,2},{4,5},{5,4},{6,7},{7,6},{8,9},{9,8},{10,11... | collective-permute-start | bytes 1016 | tf_op jit(solution)/shard_map/ppermute | solution.py:374
  32.7 22.5 %collective-permute-start.5 = (bf16[256,2048]{1,0:T(8,128)(2,1)}, bf16[256,2048]{1,0:T(8,128)(2,1)}, u32[]{:S(2)}, u32[]{:S(2)}) collective-permute-start(bf16[256,2048]{1,0:T(8,128)(2,1)} %collective-permute-done.2), channel_id=1, source_target_pairs={{4,0},{8,12},{5,1},{9,13},{6,2},{10,14},{7,3},{11,15},{20,16},{24,... | collective-permute-start | bytes 3145736 | tf_op jit(solution)/shard_map/ppermute | solution.py:368
  35.0 25.0 %collective-permute-start.6 = (bf16[256,2048]{1,0:T(8,128)(2,1)}, bf16[256,2048]{1,0:T(8,128)(2,1)}, u32[]{:S(2)}, u32[]{:S(2)}) collective-permute-start(bf16[256,2048]{1,0:T(8,128)(2,1)} %collective-permute-done.1.refs_0_.refs_2_), channel_id=1, source_target_pairs={{4,8},{8,4},{5,9},{9,5},{6,10},{10,6},{7,11},{11,7},{20,24},{24,20... | collective-permute-start | bytes 3145736 | tf_op jit(solution)/shard_map/ppermute | solution.py:368
  37.7 22.9 %collective-permute-start.7 = (bf16[256,2048]{1,0:T(8,128)(2,1)}, bf16[256,2048]{1,0:T(8,128)(2,1)}, u32[]{:S(2)}, u32[]{:S(2)}) collective-permute-start(bf16[256,2048]{1,0:T(8,128)(2,1)} %collective-permute-done.1.refs_0_.refs_2_), channel_id=1, source_target_pairs={{0,2},{2,0},{1,3},{3,1},{4,6},{6,4},{5,7},{7,5},{8,10},{10,8},{9,1... | collective-permute-start | bytes 3145736 | tf_op jit(solution)/shard_map/ppermute | solution.py:371
  38.9 13.0 %collective-permute-start.8 = (bf16[256,1024]{1,0:T(8,128)(2,1)S(1)}, bf16[256,1024]{1,0:T(8,128)(2,1)}, u32[]{:S(2)}, u32[]{:S(2)}) collective-permute-start(bf16[256,1024]{1,0:T(8,128)(2,1)S(1)} %get-tuple-element.48), channel_id=1, source_target_pairs={{0,4},{12,8},{1,5},{13,9},{2,6},{14,10},{3,7},{15,11},{16,20},{28,... | collective-permute-start | bytes 1572872 | tf_op jit(solution)/shard_map/ppermute | solution.py:368
  61.9 21.7 %collective-permute-start.9 = (bf16[256,2048]{1,0:T(8,128)(2,1)S(1)}, bf16[256,2048]{1,0:T(8,128)(2,1)S(1)}, u32[]{:S(2)}, u32[]{:S(2)}) collective-permute-start(bf16[256,2048]{1,0:T(8,128)(2,1)S(1)} %broadcast_select_fusion.1.refs_4_.refs_0_), channel_id=1, source_target_pairs={{0,2},{2,0},{1,3},{3,1},{4,6},{6,4},{5,7},{7,5},{8,10},{10,8},{9,1... | collective-permute-start | bytes 3145736 | tf_op jit(solution)/shard_map/ppermute | solution.py:371
  63.2 21.0 %collective-permute-start.10 = (bf16[256,2048]{1,0:T(8,128)(2,1)}, bf16[256,2048]{1,0:T(8,128)(2,1)S(1)}, u32[]{:S(2)}, u32[]{:S(2)}) collective-permute-start(bf16[256,2048]{1,0:T(8,128)(2,1)} %collective-permute-done.6), channel_id=1, source_target_pairs={{4,0},{8,12},{5,1},{9,13},{6,2},{10,14},{7,3},{11,15},{20,16},{24,... | collective-permute-start | bytes 3145736 | tf_op jit(solution)/shard_map/ppermute | solution.py:368
  64.6 25.9 %collective-permute-start.15 = (bf16[256,1024]{1,0:T(8,128)(2,1)S(1)}, bf16[256,1024]{1,0:T(8,128)(2,1)S(1)}, u32[]{:S(2)}, u32[]{:S(2)}) collective-permute-start(bf16[256,1024]{1,0:T(8,128)(2,1)S(1)} %get-tuple-element.48), channel_id=1, source_target_pairs={{4,8},{8,4},{5,9},{9,5},{6,10},{10,6},{7,11},{11,7},{20,24},{24,20... | collective-permute-start | bytes 1572872 | tf_op jit(solution)/shard_map/ppermute | solution.py:368
  67.2 23.3 %collective-permute-start.13 = (bf16[256,1024]{1,0:T(8,128)(2,1)S(1)}, bf16[256,1024]{1,0:T(8,128)(2,1)S(1)}, u32[]{:S(2)}, u32[]{:S(2)}) collective-permute-start(bf16[256,1024]{1,0:T(8,128)(2,1)S(1)} %get-tuple-element.68.refs_6_.refs_2_), channel_id=1, source_target_pairs={{0,4},{12,8},{1,5},{13,9},{2,6},{14,10},{3,7},{15,11},{16,20},{28,... | collective-permute-start | bytes 1572872 | tf_op jit(solution)/shard_map/ppermute | solution.py:368
  68.5 22.5 %collective-permute-start.17 = (bf16[256,1024]{1,0:T(8,128)(2,1)}, bf16[256,1024]{1,0:T(8,128)(2,1)S(1)}, u32[]{:S(2)}, u32[]{:S(2)}) collective-permute-start(bf16[256,1024]{1,0:T(8,128)(2,1)} %collective-permute-done.8), channel_id=1, source_target_pairs={{4,8},{8,4},{5,9},{9,5},{6,10},{10,6},{7,11},{11,7},{20,24},{24,20... | collective-permute-start | bytes 1572872 | tf_op jit(solution)/shard_map/ppermute | solution.py:368
  85.6 24.9 %collective-permute-start.11 = (bf16[256,2048]{1,0:T(8,128)(2,1)S(1)}, bf16[256,2048]{1,0:T(8,128)(2,1)S(1)}, u32[]{:S(2)}, u32[]{:S(2)}) collective-permute-start(bf16[256,2048]{1,0:T(8,128)(2,1)S(1)} %broadcast_select_fusion.refs_0_), channel_id=1, source_target_pairs={{0,2},{2,0},{1,3},{3,1},{4,6},{6,4},{5,7},{7,5},{8,10},{10,8},{9,1... | collective-permute-start | bytes 3145736 | tf_op jit(solution)/shard_map/ppermute | solution.py:371
  86.3 5.8 %collective-permute-start.12 = (bf16[256,1024]{1,0:T(8,128)(2,1)S(1)}, bf16[256,1024]{1,0:T(8,128)(2,1)S(1)}, u32[]{:S(2)}, u32[]{:S(2)}) collective-permute-start(bf16[256,1024]{1,0:T(8,128)(2,1)S(1)} %get-tuple-element.68.refs_6_.refs_2_), channel_id=1, source_target_pairs={{0,1},{1,0},{2,3},{3,2},{4,5},{5,4},{6,7},{7,6},{8,9},{9,8},{10,11... | collective-permute-start | bytes 1572872 | tf_op jit(solution)/shard_map/ppermute | solution.py:374
  90.5 2.3 %collective-permute-start.16 = (bf16[256,1024]{1,0:T(8,128)(2,1)S(1)}, bf16[256,1024]{1,0:T(8,128)(2,1)S(1)}, u32[]{:S(2)}, u32[]{:S(2)}) collective-permute-start(bf16[256,1024]{1,0:T(8,128)(2,1)S(1)} %collective-permute-done.15.refs_10_.refs_6_), channel_id=1, source_target_pairs={{0,1},{1,0},{2,3},{3,2},{4,5},{5,4},{6,7},{7,6},{8,9},{9,8},{10,11... | collective-permute-start | bytes 1572872 | tf_op jit(solution)/shard_map/ppermute | solution.py:374
  90.5 3.0 %collective-permute-start.14 = (bf16[256,1024]{1,0:T(8,128)(2,1)S(1)}, bf16[256,1024]{1,0:T(8,128)(2,1)S(1)}, u32[]{:S(2)}, u32[]{:S(2)}) collective-permute-start(bf16[256,1024]{1,0:T(8,128)(2,1)S(1)} %collective-permute-done.13.refs_8_.refs_4_), channel_id=1, source_target_pairs={{0,1},{1,0},{2,3},{3,2},{4,5},{5,4},{6,7},{7,6},{8,9},{9,8},{10,11... | collective-permute-start | bytes 1572872 | tf_op jit(solution)/shard_map/ppermute | solution.py:374
  91.0 3.3 %collective-permute-start.18 = (bf16[256,1024]{1,0:T(8,128)(2,1)S(1)}, bf16[256,1024]{1,0:T(8,128)(2,1)S(1)}, u32[]{:S(2)}, u32[]{:S(2)}) collective-permute-start(bf16[256,1024]{1,0:T(8,128)(2,1)S(1)} %collective-permute-done.17.refs_12_.refs_8_), channel_id=1, source_target_pairs={{0,1},{1,0},{2,3},{3,2},{4,5},{5,4},{6,7},{7,6},{8,9},{9,8},{10,11... | collective-permute-start | bytes 1572872 | tf_op jit(solution)/shard_map/ppermute | solution.py:374
  99.7 10.0 %collective-permute-start.19 = (bf16[2,256,256]{2,1,0:T(8,128)(2,1)S(1)}, bf16[2,256,256]{2,1,0:T(8,128)(2,1)S(1)}, u32[]{:S(2)}, u32[]{:S(2)}) collective-permute-start(bf16[2,256,256]{2,1,0:T(8,128)(2,1)S(1)} %get-tuple-element.70), channel_id=1, source_target_pairs={{4,0},{8,12},{5,1},{9,13},{6,2},{10,14},{7,3},{11,15},{20,16},{24,... | collective-permute-start | bytes 786440 | tf_op jit(solution)/shard_map/ppermute | solution.py:368
  101.0 9.4 %collective-permute-start.20 = (bf16[2,256,256]{2,1,0:T(8,128)(2,1)S(1)}, bf16[2,256,256]{2,1,0:T(8,128)(2,1)S(1)}, u32[]{:S(2)}, u32[]{:S(2)}) collective-permute-start(bf16[2,256,256]{2,1,0:T(8,128)(2,1)S(1)} %get-tuple-element.71), channel_id=1, source_target_pairs={{4,8},{8,4},{5,9},{9,5},{6,10},{10,6},{7,11},{11,7},{20,24},{24,20... | collective-permute-start | bytes 786440 | tf_op jit(solution)/shard_map/ppermute | solution.py:368
  110.4 8.6 %collective-permute-start.24 = (bf16[42,128,128]{2,1,0:T(8,128)(2,1)S(1)}, bf16[42,128,128]{2,1,0:T(8,128)(2,1)S(1)}, u32[]{:S(2)}, u32[]{:S(2)}) collective-permute-start(bf16[42,128,128]{2,1,0:T(8,128)(2,1)S(1)} %get-tuple-element.82), channel_id=1, source_target_pairs={{0,1},{1,0},{2,3},{3,2},{4,5},{5,4},{6,7},{7,6},{8,9},{9,8},{10,11... | collective-permute-start | bytes 4128776 | tf_op jit(solution)/shard_map/ppermute | solution.py:374
  111.6 7.0 %collective-permute-start.25 = (bf16[256,2048]{1,0:T(8,128)(2,1)S(1)}, bf16[256,2048]{1,0:T(8,128)(2,1)S(1)}, u32[]{:S(2)}, u32[]{:S(2)}) collective-permute-start(bf16[256,2048]{1,0:T(8,128)(2,1)S(1)} %collective-permute-done.11.refs_1_.refs_2_), channel_id=1, source_target_pairs={{0,1},{1,0},{2,3},{3,2},{4,5},{5,4},{6,7},{7,6},{8,9},{9,8},{10,11... | collective-permute-start | bytes 3145736 | tf_op jit(solution)/shard_map/ppermute | solution.py:374
  111.6 7.4 %collective-permute-start.23 = (bf16[256,2048]{1,0:T(8,128)(2,1)S(1)}, bf16[256,2048]{1,0:T(8,128)(2,1)S(1)}, u32[]{:S(2)}, u32[]{:S(2)}) collective-permute-start(bf16[256,2048]{1,0:T(8,128)(2,1)S(1)} %broadcast_select_fusion.refs_0_), channel_id=1, source_target_pairs={{0,1},{1,0},{2,3},{3,2},{4,5},{5,4},{6,7},{7,6},{8,9},{9,8},{10,11... | collective-permute-start | bytes 3145736 | tf_op jit(solution)/shard_map/ppermute | solution.py:374
  114.5 13.0 %copy-start.1 = (f32[512]{0:T(512)S(1)}, f32[512]{0:T(512)}, u32[]{:S(2)}) copy-start(f32[512]{0:T(512)} %param.9) | copy-start | bytes 6148
  114.5 11.2 %collective-permute-start.21 = (bf16[2,256,256]{2,1,0:T(8,128)(2,1)S(1)}, bf16[2,256,256]{2,1,0:T(8,128)(2,1)S(1)}, u32[]{:S(2)}, u32[]{:S(2)}) collective-permute-start(bf16[2,256,256]{2,1,0:T(8,128)(2,1)S(1)} %collective-permute-done.20), channel_id=1, source_target_pairs={{4,0},{8,12},{5,1},{9,13},{6,2},{10,14},{7,3},{11,15},{20,16},{24,... | collective-permute-start | bytes 786440 | tf_op jit(solution)/shard_map/ppermute | solution.py:368
  115.8 9.9 %collective-permute-start.22 = (bf16[2,256,256]{2,1,0:T(8,128)(2,1)S(1)}, bf16[2,256,256]{2,1,0:T(8,128)(2,1)S(1)}, u32[]{:S(2)}, u32[]{:S(2)}) collective-permute-start(bf16[2,256,256]{2,1,0:T(8,128)(2,1)S(1)} %shard_map.90), channel_id=1, source_target_pairs={{4,8},{8,4},{5,9},{9,5},{6,10},{10,6},{7,11},{11,7},{20,24},{24,20... | collective-permute-start | bytes 786440 | tf_op jit(solution)/shard_map/ppermute | solution.py:368
  118.7 7.9 %collective-permute-start.26 = (bf16[256,256]{1,0:T(8,128)(2,1)S(1)}, bf16[256,256]{1,0:T(8,128)(2,1)S(1)}, u32[]{:S(2)}, u32[]{:S(2)}) collective-permute-start(bf16[256,256]{1,0:T(8,128)(2,1)S(1)} %fusion), channel_id=1, source_target_pairs={{0,1},{1,0},{2,3},{3,2},{4,5},{5,4},{6,7},{7,6},{8,9},{9,8},{10,11... | collective-permute-start | bytes 393224 | tf_op jit(solution)/shard_map/ppermute | solution.py:374
  125.8 1.7 %collective-permute-start.27 = (bf16[256,256]{1,0:T(8,128)(2,1)S(1)}, bf16[256,256]{1,0:T(8,128)(2,1)S(1)}, u32[]{:S(2)}, u32[]{:S(2)}) collective-permute-start(bf16[256,256]{1,0:T(8,128)(2,1)S(1)} %select_bitcast_fusion), channel_id=1, source_target_pairs={{0,1},{1,0},{2,3},{3,2},{4,5},{5,4},{6,7},{7,6},{8,9},{9,8},{10,11... | collective-permute-start | bytes 393224 | tf_op jit(solution)/shard_map/ppermute | solution.py:374

commit v6 on v5

--- a/solution.py
+++ b/solution.py
@@ -103,6 +103,7 @@
     n_own = len(carried) - len(extra)
     unroll = max(u for u in range(1, 22) if half // 2 % u == 0)
     n_out = 2 if part == "both" else 1
+    inside = part == "both"
 
     n_scores = len(scores.count) if scores else 0
     score_arrays = scores.arrays if scores else []
@@ -118,15 +119,11 @@
         row_refs = refs[:n]
         carried_refs = refs[n : n + len(carried)]
         out_refs = refs[n + len(carried) : n + len(carried) + n_out]
-        outs = refs[n + len(carried) + n_out : -3 - len(carried)]
-        held = refs[-3 - len(carried) : -3]
+        outs = out_refs if inside else refs[n + len(carried) + n_out : -3]
+        held = carried_refs
         rows, turned, sems = refs[-3:]
-        held_copies = [
-            pltpu.make_async_copy(ref, held[i], sems.at[n_moves + i])
-            for i, ref in enumerate(carried_refs)
-        ]
         parts = []
-        for i in range(n_out):
+        for i in range(0 if inside else n_out):
             for j in range(2):
                 some = pl.ds(j * (half // 2), half // 2)
                 sem = sems.at[n_moves + len(carried) + 2 * i + j]
@@ -151,7 +148,6 @@
                     pl.when(place_ref[0] == plane)(lambda plane=plane: each(copies[plane], do))
 
         rows_do(lambda copy: copy.start())
-        each(held_copies, lambda copy: copy.start())
         if scores:
             pl.when(place_ref[0] == 1)(lambda: each(score_copies, lambda copy: copy.start()))
         rows_do(lambda copy: copy.wait())
@@ -186,17 +182,15 @@
             return 0
 
         if part != "own":
-            for copy in held_copies[n_own:]:
-                copy.wait()
             for j in range(2):
                 lax.fori_loop(j * (half // 2), (j + 1) * (half // 2), sibling, 0, unroll=unroll)
-                parts[j].start()
+                if parts:
+                    parts[j].start()
         if part != "sibling":
-            for copy in held_copies[:n_own]:
-                copy.wait()
             for j in range(2):
                 lax.fori_loop(j * (half // 2), (j + 1) * (half // 2), mine, 0, unroll=unroll)
-                parts[j - 2].start()
+                if parts:
+                    parts[j - 2].start()
         if scores:
 
             @pl.when(place_ref[0] == 1)
@@ -208,6 +202,7 @@
 
     smem = pl.BlockSpec(memory_space=pltpu.SMEM)
     hbm = pl.BlockSpec(memory_space=pltpu.HBM)
+    vmem = pl.BlockSpec(memory_space=pltpu.VMEM)
     outs = []
     if part != "own":
         outs.append(jax.ShapeDtypeStruct((half, B, B), jnp.bfloat16))
@@ -216,16 +211,16 @@
     return pl.pallas_call(
         kernel,
         out_shape=outs + (scores.out_shape if scores else []),
-        in_specs=[smem, smem] + [hbm] * n_in,
-        out_specs=[hbm] * n_out + [pl.BlockSpec(memory_space=pltpu.VMEM)] * n_scores,
-        scratch_shapes=[pltpu.VMEM(x.shape, x.dtype) for x in outs + list(carried)]
+        in_specs=[smem, smem] + [hbm] * n + [vmem] * len(carried) + [hbm] * len(score_arrays),
+        out_specs=[vmem if inside else hbm] * n_out + [pl.BlockSpec(memory_space=pltpu.VMEM)] * n_scores,
+        scratch_shapes=[pltpu.VMEM(x.shape, x.dtype) for x in outs if not inside]
         + [
             pltpu.VMEM((2, total, wide), jnp.bfloat16),
             pltpu.VMEM((2 * per, B, total), jnp.bfloat16),
             pltpu.SemaphoreType.DMA((n_moves + len(carried) + 2 * n_out,)),
         ]
         + (scores.scratch if scores else []),
-        compiler_params=pltpu.CompilerParams(vmem_limit_bytes=18 * 2**20),
+        compiler_params=pltpu.CompilerParams(vmem_limit_bytes=13 * 2**20),
         cost_estimate=pl.CostEstimate(flops=0, bytes_accessed=0, transcendentals=0),
     )(place, table, *arrays, *carried, *score_arrays)
 
@@ -238,10 +233,7 @@
             self.moves += plan([slot], sum(self.count[:i]))
         self.quarter = parts[0][0].shape[1]
         lengths = [pair[0].shape[0] for pair in parts]
-        for i, pair in enumerate(parts):
-            for j in range(2):
-                at = sum(lengths[:i])
-                self.moves.append((pair[j], 0, lengths[i], 2 + j, at, 0, 0, self.quarter, 2))
+        self.queries = [x for pair in parts for x in pair]
         self.wide = self.moves[0][0].shape[1]
         self.group = sum(lengths) // 4
         self.arrays = [move[0] for move in self.moves]
@@ -250,23 +242,19 @@
         ]
         self.scratch = [
             pltpu.VMEM((2, sum(self.count), self.wide), jnp.bfloat16),
-            pltpu.VMEM((2, 4 * self.group, self.quarter), jnp.bfloat16),
             pltpu.SemaphoreType.DMA((len(self.moves),)),
         ]
 
-    def copies(self, sources, rows, query, sems):
+    def copies(self, sources, rows, sems):
         out = []
         for i, (_, start, count, side, to, *_) in enumerate(self.moves):
-            into = rows.at[side, pl.ds(to, count)] if side < 2 else query.at[side - 2, pl.ds(to, count)]
+            into = rows.at[side, pl.ds(to, count)]
             out.append(pltpu.make_async_copy(sources[i].at[pl.ds(start, count)], into, sems.at[i]))
         return out
 
     def compute(self, place_ref, outs, rows, query, copies):
         group, quarter = self.group, self.quarter
         per = self.wide // quarter
-        for copy, move in zip(copies, self.moves):
-            if move[3] >= 2:
-                copy.wait()
         for i, out in enumerate(outs):
             first = sum(self.count[:i])
             for copy, move in zip(copies, self.moves):
@@ -278,7 +266,7 @@
                     spot = place_ref[1 + k]
                     columns = pl.ds(pl.multiple_of((spot % per) * quarter, quarter), quarter)
                     term = lax.dot_general(
-                        query[j, k * group : (k + 1) * group, :],
+                        query[2 * k + j][...],
                         rows[spot // per, first : first + self.count[i], columns],
                         (((1,), (1,)), ((), ())),
                         preferred_element_type=jnp.float32,
@@ -292,19 +280,15 @@
     n, m = len(slots), len(scores.moves)
 
     def kernel(place_ref, *refs):
-        outs = refs[m : m + n]
-        rows, query, sems = refs[m + n :]
+        outs = refs[m + 8 : m + 8 + n]
+        rows, sems = refs[m + 8 + n :]
 
         @pl.when(place_ref[0] == 1)
         def _():
-            copies = scores.copies(refs[:m], rows, query, sems)
-            for copy, move in zip(copies, scores.moves):
-                if move[3] >= 2:
-                    copy.start()
-            for copy, move in zip(copies, scores.moves):
-                if move[3] < 2:
-                    copy.start()
-            scores.compute(place_ref, outs, rows, query, copies)
+            copies = scores.copies(refs[:m], rows, sems)
+            for copy in copies:
+                copy.start()
+            scores.compute(place_ref, outs, rows, refs[m : m + 8], copies)
 
     smem = pl.BlockSpec(memory_space=pltpu.SMEM)
     hbm = pl.BlockSpec(memory_space=pltpu.HBM)
@@ -312,12 +296,12 @@
     return pl.pallas_call(
         kernel,
         out_shape=scores.out_shape,
-        in_specs=[smem] + [hbm] * m,
+        in_specs=[smem] + [hbm] * m + [vmem] * 8,
         out_specs=[vmem] * n,
         scratch_shapes=scores.scratch,
-        compiler_params=pltpu.CompilerParams(vmem_limit_bytes=18 * 2**20),
+        compiler_params=pltpu.CompilerParams(vmem_limit_bytes=9 * 2**20),
         cost_estimate=pl.CostEstimate(flops=0, bytes_accessed=0, transcendentals=0),
-    )(place, *scores.arrays)
+    )(place, *scores.arrays, *scores.queries)
 
 
 def weigh_call(place, on_middle, on_ends, swapped, weights):

time: 130 us -> 129 us (level)
  Pallas kernels: 34.5 us -> 28.5 us
  waiting for transfers between devices: 46.3 us -> 50.7 us
    pallas_call x4, Pallas kernels: 25.1 us -> 20 us  [tile_call(): pl.pallas_call(kernel, out_shape=outs + (scores.out_shape if scores else...]
    ppermute x13, waiting for transfers between devices: 34.6 us -> 37.7 us  [move(): return lax.ppermute(value, 'ex', pairs)]
  transfers between devices with their start and end apart: 28 -> 28, of which waited for: 15 -> 16; matrix products, arithmetic and copies ran while one was open for 2% -> 2% of each run, Pallas kernels for 25% -> 21%
where the time goes in v6:
time: 129 us; the launch traced here: 128 us
  waiting for transfers between devices  50.7 us (39%)
  starting transfers between devices  42.6 us (33%)
  Pallas kernels  28.5 us (22%)
  other arithmetic  2.88 us (2%)
  local copies, waits for them, and re-layouts  2.84 us (2%)
    ppermute x13, waiting for transfers between devices, move(): return lax.ppermute(value, 'ex', pairs)  37.7 us
    ppermute x13, starting transfers between devices, move(): return lax.ppermute(value, 'ex', pairs)  26.7 us
    pallas_call x4, Pallas kernels, tile_call(): pl.pallas_call(kernel, out_shape=outs + (scores.out_shape if scores else...  20 us
    ppermute x11, starting transfers between devices, swap(): return lax.ppermute(value, 'feat', CORE)  11.4 us
    ppermute x4, waiting for transfers between devices, across(): return lax.ppermute(value, 'feat', ACROSS)  8.2 us
    pallas_call x2, Pallas kernels, score_call(): pl.pallas_call(kernel, out_shape=scores.out_shape, in_specs=[smem] + [hbm...  6.85 us
    ppermute x11, waiting for transfers between devices, swap(): return lax.ppermute(value, 'feat', CORE)  4.75 us
    ppermute x4, starting transfers between devices, across(): return lax.ppermute(value, 'feat', ACROSS)  4.52 us
  transfers between devices with their start and end apart: 28, of which 16 were waited for; matrix products, arithmetic and copies ran while one was open for 2% of the time, Pallas kernels for 21%

profile of v6, /device:TPU:9, one launch (start us, length us, event | category | flops | bytes accessed | tf_op | source)
XLA Modules:
  0.0 128.4 jit_solution(16383893801900237733)
XLA Ops:
  0.7 1.3 constant_dynamic-slice_fusion.4
  1.9 0.7 collective-permute-start
  2.7 1.5 %collective-permute-done = bf16[256,1024]{1,0:T(8,128)(2,1)S(1)} collective-permute-done((bf16[256,1024]{1,0:T(8,128)(2,1)S(1)}, bf16[256,1024]{1,0:T(8,128)(2,1)S(1)}, u32[]{:S(2)}, u32[]{:S(2)}) %collective-permute-start) | collective-permute-done | bytes 524320 | tf_op jit(solution)/shard_map/ppermute | solution.py:358
  4.4 4.5 %collective-permute-start.2 = (bf16[256,2048]{1,0:T(8,128)(2,1)S(1)}, bf16[256,2048]{1,0:T(8,128)(2,1)}, u32[]{:S(2)}, u32[]{:S(2)}) collective-permute-start(bf16[256,2048]{1,0:T(8,128)(2,1)S(1)} %pad_maximum_fusion.refs_0_), channel_id=1, source_target_pairs={{4,8},{8,4},{5,9},{9,5},{6,10},{10,6},{7,11},{11,7},{20,24},{24,20... | collective-permute-start | bytes 3145736 | tf_op jit(solution)/shard_map/ppermute | solution.py:352
  8.9 1.3 collective-permute-start.3
  10.2 1.2 collective-permute-start.4
  11.4 1.3 constant_dynamic-slice_fusion.1
  12.8 16.0 %collective-permute-done.1.refs_0_.refs_2_ = bf16[256,2048]{1,0:T(8,128)(2,1)} collective-permute-done((bf16[256,2048]{1,0:T(8,128)(2,1)S(1)}, bf16[256,2048]{1,0:T(8,128)(2,1)}, u32[]{:S(2)}, u32[]{:S(2)}) %collective-permute-start.1) | collective-permute-done | bytes 1048608 | tf_op jit(solution)/shard_map/ppermute | solution.py:352
  28.9 3.0 %collective-permute-done.2 = bf16[256,2048]{1,0:T(8,128)(2,1)} collective-permute-done((bf16[256,2048]{1,0:T(8,128)(2,1)S(1)}, bf16[256,2048]{1,0:T(8,128)(2,1)}, u32[]{:S(2)}, u32[]{:S(2)}) %collective-permute-start.2) | collective-permute-done | bytes 1048608 | tf_op jit(solution)/shard_map/ppermute | solution.py:352
  31.9 0.8 collective-permute-done.3.refs_1_
  32.7 2.3 %collective-permute-start.5 = (bf16[256,2048]{1,0:T(8,128)(2,1)}, bf16[256,2048]{1,0:T(8,128)(2,1)}, u32[]{:S(2)}, u32[]{:S(2)}) collective-permute-start(bf16[256,2048]{1,0:T(8,128)(2,1)} %collective-permute-done.2), channel_id=1, source_target_pairs={{4,0},{8,12},{5,1},{9,13},{6,2},{10,14},{7,3},{11,15},{20,16},{24,... | collective-permute-start | bytes 3145736 | tf_op jit(solution)/shard_map/ppermute | solution.py:352
  35.0 2.7 %collective-permute-start.6 = (bf16[256,2048]{1,0:T(8,128)(2,1)}, bf16[256,2048]{1,0:T(8,128)(2,1)}, u32[]{:S(2)}, u32[]{:S(2)}) collective-permute-start(bf16[256,2048]{1,0:T(8,128)(2,1)} %collective-permute-done.1.refs_0_.refs_2_), channel_id=1, source_target_pairs={{4,8},{8,4},{5,9},{9,5},{6,10},{10,6},{7,11},{11,7},{20,24},{24,20... | collective-permute-start | bytes 3145736 | tf_op jit(solution)/shard_map/ppermute | solution.py:352
  37.7 1.3 collective-permute-start.7
  38.9 1.3 collective-permute-start.8
  40.5 3.9 %shard_map.86 = (bf16[42,128,128]{2,1,0:T(8,128)(2,1)S(1)}, f32[42,128,128]{2,1,0:T(8,128)S(1)}) custom-call(s32[8]{0:T(128)S(1)} %concatenate.15.place_ref, s32[84,3]{1,0:T(8,128)S(1)} %copy.11.table_ref, bf16[256,2048]{1,0:T(8,128)(2,1)S(1)} %pad_maximum_fusion.refs_0_, bf16[256,2048]{1,0:T(8,128)(2,1)S(1)} %collective-permute-done.3.refs_1_), custom_call_target="tpu_custom_call" | custom-call | tf_op jit(solution)/shard_map/pallas_call | solution.py:211
  44.4 7.6 %collective-permute-done.8 = bf16[256,1024]{1,0:T(8,128)(2,1)} collective-permute-done((bf16[256,1024]{1,0:T(8,128)(2,1)S(1)}, bf16[256,1024]{1,0:T(8,128)(2,1)}, u32[]{:S(2)}, u32[]{:S(2)}) %collective-permute-start.8) | collective-permute-done | bytes 524320 | tf_op jit(solution)/shard_map/ppermute | solution.py:352
  52.0 3.2 %collective-permute-done.5 = bf16[256,2048]{1,0:T(8,128)(2,1)} collective-permute-done((bf16[256,2048]{1,0:T(8,128)(2,1)}, bf16[256,2048]{1,0:T(8,128)(2,1)}, u32[]{:S(2)}, u32[]{:S(2)}) %collective-permute-start.5) | collective-permute-done | bytes 1048608 | tf_op jit(solution)/shard_map/ppermute | solution.py:352
  55.2 4.8 %collective-permute-done.6 = bf16[256,2048]{1,0:T(8,128)(2,1)} collective-permute-done((bf16[256,2048]{1,0:T(8,128)(2,1)}, bf16[256,2048]{1,0:T(8,128)(2,1)}, u32[]{:S(2)}, u32[]{:S(2)}) %collective-permute-start.6) | collective-permute-done | bytes 1048608 | tf_op jit(solution)/shard_map/ppermute | solution.py:352
  60.0 0.6 collective-permute-done.7.refs_1_.refs_3_
  60.6 1.3 %broadcast_select_fusion.1.refs_4_.refs_0_ = bf16[256,2048]{1,0:T(8,128)(2,1)S(1)} fusion(bf16[256,2048]{1,0:T(8,128)(2,1)} %collective-permute-done.6, bf16[256,2048]{1,0:T(8,128)(2,1)} %collective-permute-done.5, pred[]{:T(512)S(6)} %or.3), kind=kLoop, calls=%fused_computation.2 | loop fusion | flops 524288 | bytes 3145729 | tf_op jit(solution)/shard_map/jit(_where)/select_n | solution.py:418
  61.9 1.3 collective-permute-start.9
  63.2 1.3 %collective-permute-start.10 = (bf16[256,2048]{1,0:T(8,128)(2,1)}, bf16[256,2048]{1,0:T(8,128)(2,1)S(1)}, u32[]{:S(2)}, u32[]{:S(2)}) collective-permute-start(bf16[256,2048]{1,0:T(8,128)(2,1)} %collective-permute-done.6), channel_id=1, source_target_pairs={{4,0},{8,12},{5,1},{9,13},{6,2},{10,14},{7,3},{11,15},{20,16},{24,... | collective-permute-start | bytes 3145736 | tf_op jit(solution)/shard_map/ppermute | solution.py:352
  64.6 2.6 %collective-permute-start.15 = (bf16[256,1024]{1,0:T(8,128)(2,1)S(1)}, bf16[256,1024]{1,0:T(8,128)(2,1)S(1)}, u32[]{:S(2)}, u32[]{:S(2)}) collective-permute-start(bf16[256,1024]{1,0:T(8,128)(2,1)S(1)} %get-tuple-element.48), channel_id=1, source_target_pairs={{4,8},{8,4},{5,9},{9,5},{6,10},{10,6},{7,11},{11,7},{20,24},{24,20... | collective-permute-start | bytes 1572872 | tf_op jit(solution)/shard_map/ppermute | solution.py:352
  67.2 1.3 %collective-permute-start.13 = (bf16[256,1024]{1,0:T(8,128)(2,1)S(1)}, bf16[256,1024]{1,0:T(8,128)(2,1)S(1)}, u32[]{:S(2)}, u32[]{:S(2)}) collective-permute-start(bf16[256,1024]{1,0:T(8,128)(2,1)S(1)} %get-tuple-element.68.refs_6_.refs_2_), channel_id=1, source_target_pairs={{0,4},{12,8},{1,5},{13,9},{2,6},{14,10},{3,7},{15,11},{16,20},{28,... | collective-permute-start | bytes 1572872 | tf_op jit(solution)/shard_map/ppermute | solution.py:352
  68.5 2.7 %collective-permute-start.17 = (bf16[256,1024]{1,0:T(8,128)(2,1)}, bf16[256,1024]{1,0:T(8,128)(2,1)S(1)}, u32[]{:S(2)}, u32[]{:S(2)}) collective-permute-start(bf16[256,1024]{1,0:T(8,128)(2,1)} %collective-permute-done.8), channel_id=1, source_target_pairs={{4,8},{8,4},{5,9},{9,5},{6,10},{10,6},{7,11},{11,7},{20,24},{24,20... | collective-permute-start | bytes 1572872 | tf_op jit(solution)/shard_map/ppermute | solution.py:352
  71.2 5.7 %shard_map.87 = (bf16[42,128,128]{2,1,0:T(8,128)(2,1)S(1)}, f32[42,128,128]{2,1,0:T(8,128)S(1)}) custom-call(s32[8]{0:T(128)S(1)} %concatenate.15.place_ref, s32[84,3]{1,0:T(8,128)S(1)} %copy.11.table_ref, bf16[256,2048]{1,0:T(8,128)(2,1)} %collective-permute-done.1.refs_0_.refs_2_, bf16[256,2048]{1,0:T(8,128)(2,1)} %collective-permute-done.7.refs_1_.refs_3_, ...), custom_call_target="tpu_custom_call" | custom-call | tf_op jit(solution)/shard_map/pallas_call | solution.py:211
  76.9 6.8 %collective-permute-done.9.refs_5_.refs_1_ = bf16[256,2048]{1,0:T(8,128)(2,1)S(1)} collective-permute-done((bf16[256,2048]{1,0:T(8,128)(2,1)S(1)}, bf16[256,2048]{1,0:T(8,128)(2,1)S(1)}, u32[]{:S(2)}, u32[]{:S(2)}) %collective-permute-start.9) | collective-permute-done | bytes 1048608 | tf_op jit(solution)/shard_map/ppermute | solution.py:355
  84.3 1.3 %broadcast_select_fusion.refs_0_ = bf16[256,2048]{1,0:T(8,128)(2,1)S(1)} fusion(bf16[256,2048]{1,0:T(8,128)(2,1)} %collective-permute-done.2, bf16[256,2048]{1,0:T(8,128)(2,1)S(1)} %collective-permute-done.10, pred[]{:T(512)S(6)} %or.3), kind=kLoop, calls=%fused_computation.1 | loop fusion | flops 524288 | bytes 3145729 | tf_op jit(solution)/shard_map/jit(_where)/select_n | solution.py:429
  85.6 0.7 collective-permute-start.11
  86.3 4.2 %collective-permute-start.12 = (bf16[256,1024]{1,0:T(8,128)(2,1)S(1)}, bf16[256,1024]{1,0:T(8,128)(2,1)S(1)}, u32[]{:S(2)}, u32[]{:S(2)}) collective-permute-start(bf16[256,1024]{1,0:T(8,128)(2,1)S(1)} %get-tuple-element.68.refs_6_.refs_2_), channel_id=1, source_target_pairs={{0,1},{1,0},{2,3},{3,2},{4,5},{5,4},{6,7},{7,6},{8,9},{9,8},{10,11... | collective-permute-start | bytes 1572872 | tf_op jit(solution)/shard_map/ppermute | solution.py:358
  91.0 1.0 collective-permute-start.18
  92.0 0.7 collective-permute-done.16.refs_11_.refs_7_
  92.8 0.7 collective-permute-done.14.refs_9_.refs_5_
  93.5 0.7 collective-permute-done.18.refs_13_.refs_9_
  94.3 4.8 %shard_map.88 = (bf16[2,256,256]{2,1,0:T(8,128)(2,1)S(1)}, bf16[2,256,256]{2,1,0:T(8,128)(2,1)S(1)}, bf16[2,256,256]{2,1,0:T(8,128)(2,1)S(1)}) custom-call(s32[8]{0:T(128)S(1)} %concatenate.15.place_ref, bf16[256,2048]{1,0:T(8,128)(2,1)S(1)} %pad_maximum_fusion.refs_0_, bf16[256,2048]{1,0:T(8,128)(2,1)S(1)} %collective-permute-done.3.refs_1_, ...), custom_call_target="tpu_custom_call" | custom-call | tf_op jit(solution)/shard_map/pallas_call | solution.py:296
  99.1 1.3 %collective-permute-start.19 = (bf16[2,256,256]{2,1,0:T(8,128)(2,1)S(1)}, bf16[2,256,256]{2,1,0:T(8,128)(2,1)S(1)}, u32[]{:S(2)}, u32[]{:S(2)}) collective-permute-start(bf16[2,256,256]{2,1,0:T(8,128)(2,1)S(1)} %get-tuple-element.70), channel_id=1, source_target_pairs={{4,0},{8,12},{5,1},{9,13},{6,2},{10,14},{7,3},{11,15},{20,16},{24,... | collective-permute-start | bytes 786440 | tf_op jit(solution)/shard_map/ppermute | solution.py:352
  100.4 2.8 %collective-permute-start.20 = (bf16[2,256,256]{2,1,0:T(8,128)(2,1)S(1)}, bf16[2,256,256]{2,1,0:T(8,128)(2,1)S(1)}, u32[]{:S(2)}, u32[]{:S(2)}) collective-permute-start(bf16[2,256,256]{2,1,0:T(8,128)(2,1)S(1)} %get-tuple-element.71), channel_id=1, source_target_pairs={{4,8},{8,4},{5,9},{9,5},{6,10},{10,6},{7,11},{11,7},{20,24},{24,20... | collective-permute-start | bytes 786440 | tf_op jit(solution)/shard_map/ppermute | solution.py:352
  103.2 4.3 %shard_map.89 = (bf16[42,128,128]{2,1,0:T(8,128)(2,1)S(1)}, f32[42,128,128]{2,1,0:T(8,128)S(1)}) custom-call(s32[8]{0:T(128)S(1)} %concatenate.15.place_ref, s32[84,3]{1,0:T(8,128)S(1)} %copy.11.table_ref, bf16[256,2048]{1,0:T(8,128)(2,1)S(1)} %broadcast_select_fusion.1.refs_4_.refs_0_, bf16[256,2048]{1,0:T(8,128)(2,1)S(1)} %collective-permute-done.9.refs_5_.refs_1_, ...), custom_call_target="tpu_custom_call" | custom-call | tf_op jit(solution)/shard_map/pallas_call | solution.py:211
  107.5 2.3 %collective-permute-done.20 = bf16[2,256,256]{2,1,0:T(8,128)(2,1)S(1)} collective-permute-done((bf16[2,256,256]{2,1,0:T(8,128)(2,1)S(1)}, bf16[2,256,256]{2,1,0:T(8,128)(2,1)S(1)}, u32[]{:S(2)}, u32[]{:S(2)}) %collective-permute-start.20) | collective-permute-done | bytes 262176 | tf_op jit(solution)/shard_map/ppermute | solution.py:352
  109.9 1.4 %collective-permute-start.24 = (bf16[42,128,128]{2,1,0:T(8,128)(2,1)S(1)}, bf16[42,128,128]{2,1,0:T(8,128)(2,1)S(1)}, u32[]{:S(2)}, u32[]{:S(2)}) collective-permute-start(bf16[42,128,128]{2,1,0:T(8,128)(2,1)S(1)} %get-tuple-element.82), channel_id=1, source_target_pairs={{0,1},{1,0},{2,3},{3,2},{4,5},{5,4},{6,7},{7,6},{8,9},{9,8},{10,11... | collective-permute-start | bytes 4128776 | tf_op jit(solution)/shard_map/ppermute | solution.py:358
  111.7 2.0 %shard_map.90 = bf16[2,256,256]{2,1,0:T(8,128)(2,1)S(1)} custom-call(s32[8]{0:T(128)S(1)} %concatenate.15.place_ref, bf16[256,2048]{1,0:T(8,128)(2,1)S(1)} %broadcast_select_fusion.refs_0_, bf16[256,2048]{1,0:T(8,128)(2,1)S(1)} %collective-permute-done.11.refs_1_.refs_2_, bf16[256,1024]{1,0:T(8,128)(2,1)S(1)} %get-tuple-element.68.refs_6_.refs_2_, ...), custom_call_target="tpu_custom_call" | custom-call | tf_op jit(solution)/shard_map/pallas_call | solution.py:296
  113.8 1.4 %collective-permute-start.21 = (bf16[2,256,256]{2,1,0:T(8,128)(2,1)S(1)}, bf16[2,256,256]{2,1,0:T(8,128)(2,1)S(1)}, u32[]{:S(2)}, u32[]{:S(2)}) collective-permute-start(bf16[2,256,256]{2,1,0:T(8,128)(2,1)S(1)} %collective-permute-done.20), channel_id=1, source_target_pairs={{4,0},{8,12},{5,1},{9,13},{6,2},{10,14},{7,3},{11,15},{20,16},{24,... | collective-permute-start | bytes 786440 | tf_op jit(solution)/shard_map/ppermute | solution.py:352
  115.1 2.6 %collective-permute-start.22 = (bf16[2,256,256]{2,1,0:T(8,128)(2,1)S(1)}, bf16[2,256,256]{2,1,0:T(8,128)(2,1)S(1)}, u32[]{:S(2)}, u32[]{:S(2)}) collective-permute-start(bf16[2,256,256]{2,1,0:T(8,128)(2,1)S(1)} %shard_map.90), channel_id=1, source_target_pairs={{4,8},{8,4},{5,9},{9,5},{6,10},{10,6},{7,11},{11,7},{20,24},{24,20... | collective-permute-start | bytes 786440 | tf_op jit(solution)/shard_map/ppermute | solution.py:352
  117.7 0.6 collective-permute-start.26
  118.3 6.1 %shard_map.91 = f32[42,128,128]{2,1,0:T(8,128)} custom-call(s32[8]{0:T(128)S(1)} %concatenate.15.place_ref, s32[84,3]{1,0:T(8,128)S(1)} %copy.11.table_ref, bf16[256,2048]{1,0:T(8,128)(2,1)S(1)} %broadcast_select_fusion.refs_0_, bf16[256,2048]{1,0:T(8,128)(2,1)S(1)} %collective-permute-done.23.refs_1_, ...), custom_call_target="tpu_custom_call" | custom-call | tf_op jit(solution)/shard_map/pallas_call | solution.py:211
  124.7 1.2 collective-permute-start.27
  125.8 1.0 collective-permute-done.27.refs_5_
  126.8 1.6 %shard_map.92 = f32[512,512]{1,0:T(8,128)} custom-call(s32[8]{0:T(128)S(1)} %concatenate.15.place_ref, bf16[2,256,256]{2,1,0:T(8,128)(2,1)S(1)} %get-tuple-element.75.refs_0_, bf16[2,256,256]{2,1,0:T(8,128)(2,1)S(1)} %collective-permute-done.22.refs_1_, bf16[2,256,256]{2,1,0:T(8,128)(2,1)S(1)} %collective-permute-done.19.refs_2_, ...), custom_call_target="tpu_custom_call" | custom-call | tf_op jit(solution)/shard_map/pallas_call | solution.py:328
  (37 shorter events, 2.4 us)
Async XLA Ops:
  0.6 9.5 %copy-start = (s32[1,168,2]{1,2,0:T(2,128)S(1)}, s32[1,168,2]{1,2,0:T(2,128)}, u32[]{:S(2)}) copy-start(s32[1,168,2]{1,2,0:T(2,128)} %param.10) | copy-start | bytes 4036
  1.9 2.3 %collective-permute-start = (bf16[256,1024]{1,0:T(8,128)(2,1)S(1)}, bf16[256,1024]{1,0:T(8,128)(2,1)S(1)}, u32[]{:S(2)}, u32[]{:S(2)}) collective-permute-start(bf16[256,1024]{1,0:T(8,128)(2,1)S(1)} %get-tuple-element.95), channel_id=1, source_target_pairs={{0,1},{1,0},{2,3},{3,2},{4,5},{5,4},{6,7},{7,6},{8,9},{9,8},{10,11... | collective-permute-start | bytes 1572872 | tf_op jit(solution)/shard_map/ppermute | solution.py:358
  4.2 36.0 %copy-start.2 = (s32[4]{0:T(128)S(1)}, s32[4]{0:T(128)}, u32[]{:S(2)}) copy-start(s32[4]{0:T(128)} %constant.71.clone) | copy-start | bytes 52
  4.2 36.0 %copy-start.3 = (s32[4]{0:T(128)S(1)}, s32[4]{0:T(128)}, u32[]{:S(2)}) copy-start(s32[4]{0:T(128)} %constant.72.clone) | copy-start | bytes 52
  4.3 24.5 %collective-permute-start.1 = (bf16[256,2048]{1,0:T(8,128)(2,1)S(1)}, bf16[256,2048]{1,0:T(8,128)(2,1)}, u32[]{:S(2)}, u32[]{:S(2)}) collective-permute-start(bf16[256,2048]{1,0:T(8,128)(2,1)S(1)} %pad_maximum_fusion.refs_0_), channel_id=1, source_target_pairs={{0,4},{4,0},{8,12},{12,8},{1,5},{5,1},{9,13},{13,9},{2,6},{6,2},{1... | collective-permute-start | bytes 3145736 | tf_op jit(solution)/shard_map/ppermute | solution.py:352
  4.4 27.5 %collective-permute-start.2 = (bf16[256,2048]{1,0:T(8,128)(2,1)S(1)}, bf16[256,2048]{1,0:T(8,128)(2,1)}, u32[]{:S(2)}, u32[]{:S(2)}) collective-permute-start(bf16[256,2048]{1,0:T(8,128)(2,1)S(1)} %pad_maximum_fusion.refs_0_), channel_id=1, source_target_pairs={{4,8},{8,4},{5,9},{9,5},{6,10},{10,6},{7,11},{11,7},{20,24},{24,20... | collective-permute-start | bytes 3145736 | tf_op jit(solution)/shard_map/ppermute | solution.py:352
  8.9 23.8 %collective-permute-start.3 = (bf16[256,2048]{1,0:T(8,128)(2,1)S(1)}, bf16[256,2048]{1,0:T(8,128)(2,1)S(1)}, u32[]{:S(2)}, u32[]{:S(2)}) collective-permute-start(bf16[256,2048]{1,0:T(8,128)(2,1)S(1)} %pad_maximum_fusion.refs_0_), channel_id=1, source_target_pairs={{0,2},{2,0},{1,3},{3,1},{4,6},{6,4},{5,7},{7,5},{8,10},{10,8},{9,1... | collective-permute-start | bytes 3145736 | tf_op jit(solution)/shard_map/ppermute | solution.py:355
  10.2 2.5 %collective-permute-start.4 = (s32[42,2]{0,1:T(2,128)S(1)}, s32[42,2]{0,1:T(2,128)S(1)}, u32[]{:S(2)}, u32[]{:S(2)}) collective-permute-start(s32[42,2]{0,1:T(2,128)S(1)} %fusion.1), channel_id=1, source_target_pairs={{0,1},{1,0},{2,3},{3,2},{4,5},{5,4},{6,7},{7,6},{8,9},{9,8},{10,11... | collective-permute-start | bytes 1016 | tf_op jit(solution)/shard_map/ppermute | solution.py:358
  32.7 22.5 %collective-permute-start.5 = (bf16[256,2048]{1,0:T(8,128)(2,1)}, bf16[256,2048]{1,0:T(8,128)(2,1)}, u32[]{:S(2)}, u32[]{:S(2)}) collective-permute-start(bf16[256,2048]{1,0:T(8,128)(2,1)} %collective-permute-done.2), channel_id=1, source_target_pairs={{4,0},{8,12},{5,1},{9,13},{6,2},{10,14},{7,3},{11,15},{20,16},{24,... | collective-permute-start | bytes 3145736 | tf_op jit(solution)/shard_map/ppermute | solution.py:352
  35.0 25.0 %collective-permute-start.6 = (bf16[256,2048]{1,0:T(8,128)(2,1)}, bf16[256,2048]{1,0:T(8,128)(2,1)}, u32[]{:S(2)}, u32[]{:S(2)}) collective-permute-start(bf16[256,2048]{1,0:T(8,128)(2,1)} %collective-permute-done.1.refs_0_.refs_2_), channel_id=1, source_target_pairs={{4,8},{8,4},{5,9},{9,5},{6,10},{10,6},{7,11},{11,7},{20,24},{24,20... | collective-permute-start | bytes 3145736 | tf_op jit(solution)/shard_map/ppermute | solution.py:352
  37.7 22.9 %collective-permute-start.7 = (bf16[256,2048]{1,0:T(8,128)(2,1)}, bf16[256,2048]{1,0:T(8,128)(2,1)}, u32[]{:S(2)}, u32[]{:S(2)}) collective-permute-start(bf16[256,2048]{1,0:T(8,128)(2,1)} %collective-permute-done.1.refs_0_.refs_2_), channel_id=1, source_target_pairs={{0,2},{2,0},{1,3},{3,1},{4,6},{6,4},{5,7},{7,5},{8,10},{10,8},{9,1... | collective-permute-start | bytes 3145736 | tf_op jit(solution)/shard_map/ppermute | solution.py:355
  38.9 13.0 %collective-permute-start.8 = (bf16[256,1024]{1,0:T(8,128)(2,1)S(1)}, bf16[256,1024]{1,0:T(8,128)(2,1)}, u32[]{:S(2)}, u32[]{:S(2)}) collective-permute-start(bf16[256,1024]{1,0:T(8,128)(2,1)S(1)} %get-tuple-element.48), channel_id=1, source_target_pairs={{0,4},{12,8},{1,5},{13,9},{2,6},{14,10},{3,7},{15,11},{16,20},{28,... | collective-permute-start | bytes 1572872 | tf_op jit(solution)/shard_map/ppermute | solution.py:352
  61.9 21.7 %collective-permute-start.9 = (bf16[256,2048]{1,0:T(8,128)(2,1)S(1)}, bf16[256,2048]{1,0:T(8,128)(2,1)S(1)}, u32[]{:S(2)}, u32[]{:S(2)}) collective-permute-start(bf16[256,2048]{1,0:T(8,128)(2,1)S(1)} %broadcast_select_fusion.1.refs_4_.refs_0_), channel_id=1, source_target_pairs={{0,2},{2,0},{1,3},{3,1},{4,6},{6,4},{5,7},{7,5},{8,10},{10,8},{9,1... | collective-permute-start | bytes 3145736 | tf_op jit(solution)/shard_map/ppermute | solution.py:355
  63.2 21.0 %collective-permute-start.10 = (bf16[256,2048]{1,0:T(8,128)(2,1)}, bf16[256,2048]{1,0:T(8,128)(2,1)S(1)}, u32[]{:S(2)}, u32[]{:S(2)}) collective-permute-start(bf16[256,2048]{1,0:T(8,128)(2,1)} %collective-permute-done.6), channel_id=1, source_target_pairs={{4,0},{8,12},{5,1},{9,13},{6,2},{10,14},{7,3},{11,15},{20,16},{24,... | collective-permute-start | bytes 3145736 | tf_op jit(solution)/shard_map/ppermute | solution.py:352
  64.6 25.9 %collective-permute-start.15 = (bf16[256,1024]{1,0:T(8,128)(2,1)S(1)}, bf16[256,1024]{1,0:T(8,128)(2,1)S(1)}, u32[]{:S(2)}, u32[]{:S(2)}) collective-permute-start(bf16[256,1024]{1,0:T(8,128)(2,1)S(1)} %get-tuple-element.48), channel_id=1, source_target_pairs={{4,8},{8,4},{5,9},{9,5},{6,10},{10,6},{7,11},{11,7},{20,24},{24,20... | collective-permute-start | bytes 1572872 | tf_op jit(solution)/shard_map/ppermute | solution.py:352
  67.2 23.3 %collective-permute-start.13 = (bf16[256,1024]{1,0:T(8,128)(2,1)S(1)}, bf16[256,1024]{1,0:T(8,128)(2,1)S(1)}, u32[]{:S(2)}, u32[]{:S(2)}) collective-permute-start(bf16[256,1024]{1,0:T(8,128)(2,1)S(1)} %get-tuple-element.68.refs_6_.refs_2_), channel_id=1, source_target_pairs={{0,4},{12,8},{1,5},{13,9},{2,6},{14,10},{3,7},{15,11},{16,20},{28,... | collective-permute-start | bytes 1572872 | tf_op jit(solution)/shard_map/ppermute | solution.py:352
  68.5 22.5 %collective-permute-start.17 = (bf16[256,1024]{1,0:T(8,128)(2,1)}, bf16[256,1024]{1,0:T(8,128)(2,1)S(1)}, u32[]{:S(2)}, u32[]{:S(2)}) collective-permute-start(bf16[256,1024]{1,0:T(8,128)(2,1)} %collective-permute-done.8), channel_id=1, source_target_pairs={{4,8},{8,4},{5,9},{9,5},{6,10},{10,6},{7,11},{11,7},{20,24},{24,20... | collective-permute-start | bytes 1572872 | tf_op jit(solution)/shard_map/ppermute | solution.py:352
  85.6 24.3 %collective-permute-start.11 = (bf16[256,2048]{1,0:T(8,128)(2,1)S(1)}, bf16[256,2048]{1,0:T(8,128)(2,1)S(1)}, u32[]{:S(2)}, u32[]{:S(2)}) collective-permute-start(bf16[256,2048]{1,0:T(8,128)(2,1)S(1)} %broadcast_select_fusion.refs_0_), channel_id=1, source_target_pairs={{0,2},{2,0},{1,3},{3,1},{4,6},{6,4},{5,7},{7,5},{8,10},{10,8},{9,1... | collective-permute-start | bytes 3145736 | tf_op jit(solution)/shard_map/ppermute | solution.py:355
  86.3 5.8 %collective-permute-start.12 = (bf16[256,1024]{1,0:T(8,128)(2,1)S(1)}, bf16[256,1024]{1,0:T(8,128)(2,1)S(1)}, u32[]{:S(2)}, u32[]{:S(2)}) collective-permute-start(bf16[256,1024]{1,0:T(8,128)(2,1)S(1)} %get-tuple-element.68.refs_6_.refs_2_), channel_id=1, source_target_pairs={{0,1},{1,0},{2,3},{3,2},{4,5},{5,4},{6,7},{7,6},{8,9},{9,8},{10,11... | collective-permute-start | bytes 1572872 | tf_op jit(solution)/shard_map/ppermute | solution.py:358
  90.5 2.3 %collective-permute-start.16 = (bf16[256,1024]{1,0:T(8,128)(2,1)S(1)}, bf16[256,1024]{1,0:T(8,128)(2,1)S(1)}, u32[]{:S(2)}, u32[]{:S(2)}) collective-permute-start(bf16[256,1024]{1,0:T(8,128)(2,1)S(1)} %collective-permute-done.15.refs_10_.refs_6_), channel_id=1, source_target_pairs={{0,1},{1,0},{2,3},{3,2},{4,5},{5,4},{6,7},{7,6},{8,9},{9,8},{10,11... | collective-permute-start | bytes 1572872 | tf_op jit(solution)/shard_map/ppermute | solution.py:358
  90.5 3.0 %collective-permute-start.14 = (bf16[256,1024]{1,0:T(8,128)(2,1)S(1)}, bf16[256,1024]{1,0:T(8,128)(2,1)S(1)}, u32[]{:S(2)}, u32[]{:S(2)}) collective-permute-start(bf16[256,1024]{1,0:T(8,128)(2,1)S(1)} %collective-permute-done.13.refs_8_.refs_4_), channel_id=1, source_target_pairs={{0,1},{1,0},{2,3},{3,2},{4,5},{5,4},{6,7},{7,6},{8,9},{9,8},{10,11... | collective-permute-start | bytes 1572872 | tf_op jit(solution)/shard_map/ppermute | solution.py:358
  91.0 3.3 %collective-permute-start.18 = (bf16[256,1024]{1,0:T(8,128)(2,1)S(1)}, bf16[256,1024]{1,0:T(8,128)(2,1)S(1)}, u32[]{:S(2)}, u32[]{:S(2)}) collective-permute-start(bf16[256,1024]{1,0:T(8,128)(2,1)S(1)} %collective-permute-done.17.refs_12_.refs_8_), channel_id=1, source_target_pairs={{0,1},{1,0},{2,3},{3,2},{4,5},{5,4},{6,7},{7,6},{8,9},{9,8},{10,11... | collective-permute-start | bytes 1572872 | tf_op jit(solution)/shard_map/ppermute | solution.py:358
  99.1 8.4 %collective-permute-start.19 = (bf16[2,256,256]{2,1,0:T(8,128)(2,1)S(1)}, bf16[2,256,256]{2,1,0:T(8,128)(2,1)S(1)}, u32[]{:S(2)}, u32[]{:S(2)}) collective-permute-start(bf16[2,256,256]{2,1,0:T(8,128)(2,1)S(1)} %get-tuple-element.70), channel_id=1, source_target_pairs={{4,0},{8,12},{5,1},{9,13},{6,2},{10,14},{7,3},{11,15},{20,16},{24,... | collective-permute-start | bytes 786440 | tf_op jit(solution)/shard_map/ppermute | solution.py:352
  100.4 9.4 %collective-permute-start.20 = (bf16[2,256,256]{2,1,0:T(8,128)(2,1)S(1)}, bf16[2,256,256]{2,1,0:T(8,128)(2,1)S(1)}, u32[]{:S(2)}, u32[]{:S(2)}) collective-permute-start(bf16[2,256,256]{2,1,0:T(8,128)(2,1)S(1)} %get-tuple-element.71), channel_id=1, source_target_pairs={{4,8},{8,4},{5,9},{9,5},{6,10},{10,6},{7,11},{11,7},{20,24},{24,20... | collective-permute-start | bytes 786440 | tf_op jit(solution)/shard_map/ppermute | solution.py:352
  109.9 8.5 %collective-permute-start.24 = (bf16[42,128,128]{2,1,0:T(8,128)(2,1)S(1)}, bf16[42,128,128]{2,1,0:T(8,128)(2,1)S(1)}, u32[]{:S(2)}, u32[]{:S(2)}) collective-permute-start(bf16[42,128,128]{2,1,0:T(8,128)(2,1)S(1)} %get-tuple-element.82), channel_id=1, source_target_pairs={{0,1},{1,0},{2,3},{3,2},{4,5},{5,4},{6,7},{7,6},{8,9},{9,8},{10,11... | collective-permute-start | bytes 4128776 | tf_op jit(solution)/shard_map/ppermute | solution.py:358
  111.2 6.5 %collective-permute-start.25 = (bf16[256,2048]{1,0:T(8,128)(2,1)S(1)}, bf16[256,2048]{1,0:T(8,128)(2,1)S(1)}, u32[]{:S(2)}, u32[]{:S(2)}) collective-permute-start(bf16[256,2048]{1,0:T(8,128)(2,1)S(1)} %collective-permute-done.11.refs_1_.refs_2_), channel_id=1, source_target_pairs={{0,1},{1,0},{2,3},{3,2},{4,5},{5,4},{6,7},{7,6},{8,9},{9,8},{10,11... | collective-permute-start | bytes 3145736 | tf_op jit(solution)/shard_map/ppermute | solution.py:358
  111.2 7.1 %collective-permute-start.23 = (bf16[256,2048]{1,0:T(8,128)(2,1)S(1)}, bf16[256,2048]{1,0:T(8,128)(2,1)S(1)}, u32[]{:S(2)}, u32[]{:S(2)}) collective-permute-start(bf16[256,2048]{1,0:T(8,128)(2,1)S(1)} %broadcast_select_fusion.refs_0_), channel_id=1, source_target_pairs={{0,1},{1,0},{2,3},{3,2},{4,5},{5,4},{6,7},{7,6},{8,9},{9,8},{10,11... | collective-permute-start | bytes 3145736 | tf_op jit(solution)/shard_map/ppermute | solution.py:358
  113.7 13.1 %copy-start.1 = (f32[512]{0:T(512)S(1)}, f32[512]{0:T(512)}, u32[]{:S(2)}) copy-start(f32[512]{0:T(512)} %param.9) | copy-start | bytes 6148
  113.8 10.7 %collective-permute-start.21 = (bf16[2,256,256]{2,1,0:T(8,128)(2,1)S(1)}, bf16[2,256,256]{2,1,0:T(8,128)(2,1)S(1)}, u32[]{:S(2)}, u32[]{:S(2)}) collective-permute-start(bf16[2,256,256]{2,1,0:T(8,128)(2,1)S(1)} %collective-permute-done.20), channel_id=1, source_target_pairs={{4,0},{8,12},{5,1},{9,13},{6,2},{10,14},{7,3},{11,15},{20,16},{24,... | collective-permute-start | bytes 786440 | tf_op jit(solution)/shard_map/ppermute | solution.py:352
  115.1 9.5 %collective-permute-start.22 = (bf16[2,256,256]{2,1,0:T(8,128)(2,1)S(1)}, bf16[2,256,256]{2,1,0:T(8,128)(2,1)S(1)}, u32[]{:S(2)}, u32[]{:S(2)}) collective-permute-start(bf16[2,256,256]{2,1,0:T(8,128)(2,1)S(1)} %shard_map.90), channel_id=1, source_target_pairs={{4,8},{8,4},{5,9},{9,5},{6,10},{10,6},{7,11},{11,7},{20,24},{24,20... | collective-permute-start | bytes 786440 | tf_op jit(solution)/shard_map/ppermute | solution.py:352
  117.7 8.1 %collective-permute-start.26 = (bf16[256,256]{1,0:T(8,128)(2,1)S(1)}, bf16[256,256]{1,0:T(8,128)(2,1)S(1)}, u32[]{:S(2)}, u32[]{:S(2)}) collective-permute-start(bf16[256,256]{1,0:T(8,128)(2,1)S(1)} %fusion), channel_id=1, source_target_pairs={{0,1},{1,0},{2,3},{3,2},{4,5},{5,4},{6,7},{7,6},{8,9},{9,8},{10,11... | collective-permute-start | bytes 393224 | tf_op jit(solution)/shard_map/ppermute | solution.py:358
  124.7 2.2 %collective-permute-start.27 = (bf16[256,256]{1,0:T(8,128)(2,1)S(1)}, bf16[256,256]{1,0:T(8,128)(2,1)S(1)}, u32[]{:S(2)}, u32[]{:S(2)}) collective-permute-start(bf16[256,256]{1,0:T(8,128)(2,1)S(1)} %select_bitcast_fusion), channel_id=1, source_target_pairs={{0,1},{1,0},{2,3},{3,2},{4,5},{5,4},{6,7},{7,6},{8,9},{9,8},{10,11... | collective-permute-start | bytes 393224 | tf_op jit(solution)/shard_map/ppermute | solution.py:358

commit v7 on v6

--- a/solution.py
+++ b/solution.py
@@ -389,8 +389,9 @@
         ]
     )
 
+    give = lax.dynamic_slice(slab_grads, ((1 - core) * half, 0), (half, quarter))
+    (slab_grads,) = after((slab_grads,), give)
     keep = lax.dynamic_slice(slab_grads, (core * half, 0), (half, quarter))
-    give = lax.dynamic_slice(slab_grads, ((1 - core) * half, 0), (half, quarter))
     own = jnp.concatenate([keep, swap(give)], axis=1)
     q_half = query_grads.shape[0] // 2
 
@@ -402,14 +403,14 @@
         return lax.dynamic_slice(value, (which * q_half, 0), (q_half, quarter))
 
     q_mine, q_other = halves(query_grads, late), halves(query_grads, 1 - late)
-    near, inner, own, own_x, q_mine, q_other, table = after(
-        (near, inner, own, own_x, q_mine, q_other, table)
+    q_mine_sibling = swap(q_mine)
+    near, inner, own, own_x, q_mine, q_other, table, q_mine_sibling = after(
+        (near, inner, own, own_x, q_mine, q_other, table, q_mine_sibling)
     )
     near_x = across(near)
     outer = move(near, INNER)
     inner_end = move(inner, TO_END)
     q_end_other = move(q_other, TO_MID)
-    q_mine_sibling = swap(q_mine)
     sibling0, sum0 = tile_call(place, table, whole(own, own_x))
 
     inner, inner_end, outer, near, near_x, q_end_other, q_mine, sibling0, sum0 = after(
@@ -445,7 +446,6 @@
     r_inner, far = after((r_inner, far))
     to_far = move(far, TO_END)
     to_mid = move(r_inner, INNER)
-    sibling2, third_x_sibling = after((sibling2, third_x_sibling), r_inner)
     (gram,) = tile_call(
         place,
         table,

time: 129 us -> 129 us (level)
  waiting for transfers between devices: 50.7 us -> 48 us
  Pallas kernels: 28.5 us -> 30.6 us
    ppermute x13, waiting for transfers between devices: 37.7 us -> 34.3 us  [move(): return lax.ppermute(value, 'ex', pairs)]
  transfers between devices with their start and end apart: 28 -> 28, of which waited for: 16 -> 16; matrix products, arithmetic and copies ran while one was open for 2% -> 3% of each run, Pallas kernels for 21% -> 23%
where the time goes in v7:
time: 129 us; the launch traced here: 128 us
  waiting for transfers between devices  48 us (37%)
  starting transfers between devices  42.3 us (33%)
  Pallas kernels  30.6 us (24%)
  local copies, waits for them, and re-layouts  3.64 us (3%)
  other arithmetic  2.89 us (2%)
    ppermute x13, waiting for transfers between devices, move(): return lax.ppermute(value, 'ex', pairs)  34.3 us
    ppermute x13, starting transfers between devices, move(): return lax.ppermute(value, 'ex', pairs)  26.6 us
    pallas_call x4, Pallas kernels, tile_call(): pl.pallas_call(kernel, out_shape=outs + (scores.out_shape if scores else...  21.3 us
    ppermute x11, starting transfers between devices, swap(): return lax.ppermute(value, 'feat', CORE)  11.2 us
    ppermute x4, waiting for transfers between devices, across(): return lax.ppermute(value, 'feat', ACROSS)  8.26 us
    pallas_call x2, Pallas kernels, score_call(): pl.pallas_call(kernel, out_shape=scores.out_shape, in_specs=[smem] + [hbm...  7.75 us
    ppermute x11, waiting for transfers between devices, swap(): return lax.ppermute(value, 'feat', CORE)  5.44 us
    ppermute x4, starting transfers between devices, across(): return lax.ppermute(value, 'feat', ACROSS)  4.52 us
  transfers between devices with their start and end apart: 28, of which 16 were waited for; matrix products, arithmetic and copies ran while one was open for 3% of the time, Pallas kernels for 23%

profile of v7, /device:TPU:9, one launch (start us, length us, event | category | flops | bytes accessed | tf_op | source)
XLA Modules:
  0.0 128.5 jit_solution(1697838981565302284)
XLA Ops:
  0.7 1.2 copy-done
  1.9 0.7 collective-permute-start
  2.7 1.5 %collective-permute-done = bf16[256,1024]{1,0:T(8,128)(2,1)S(1)} collective-permute-done((bf16[256,1024]{1,0:T(8,128)(2,1)S(1)}, bf16[256,1024]{1,0:T(8,128)(2,1)S(1)}, u32[]{:S(2)}, u32[]{:S(2)}) %collective-permute-start) | collective-permute-done | bytes 524320 | tf_op jit(solution)/shard_map/ppermute | solution.py:358
  4.3 4.5 %collective-permute-start.2 = (bf16[256,2048]{1,0:T(8,128)(2,1)S(1)}, bf16[256,2048]{1,0:T(8,128)(2,1)}, u32[]{:S(2)}, u32[]{:S(2)}) collective-permute-start(bf16[256,2048]{1,0:T(8,128)(2,1)S(1)} %pad_maximum_fusion.refs_0_), channel_id=1, source_target_pairs={{4,8},{8,4},{5,9},{9,5},{6,10},{10,6},{7,11},{11,7},{20,24},{24,20... | collective-permute-start | bytes 3145736 | tf_op jit(solution)/shard_map/ppermute | solution.py:352
  8.8 1.3 collective-permute-start.3
  10.1 2.1 %constant_dynamic-slice_fusion.1 = (bf16[256,1024]{1,0:T(8,128)(2,1)}, bf16[256,1024]{1,0:T(8,128)(2,1)S(1)}) fusion(bf16[512,1024]{1,0:T(8,128)(2,1)} %param.8, s32[]{:T(128)S(6)} %select_n.73, s32[]{:T(128)S(6)} %mul.21), kind=kLoop, calls=%fused_computation.11 | loop fusion | bytes 2097160 | tf_op jit(solution)/shard_map/dynamic_slice | solution.py:403
  12.2 1.2 collective-permute-start.5
  13.5 1.4 %collective-permute-done.4 = s32[42,2]{0,1:T(2,128)S(1)} collective-permute-done((s32[42,2]{0,1:T(2,128)S(1)}, s32[42,2]{0,1:T(2,128)S(1)}, u32[]{:S(2)}, u32[]{:S(2)}) %collective-permute-start.4) | collective-permute-done | bytes 368 | tf_op jit(solution)/shard_map/ppermute | solution.py:358
  15.0 13.8 %collective-permute-done.1.refs_0_.refs_2_ = bf16[256,2048]{1,0:T(8,128)(2,1)} collective-permute-done((bf16[256,2048]{1,0:T(8,128)(2,1)S(1)}, bf16[256,2048]{1,0:T(8,128)(2,1)}, u32[]{:S(2)}, u32[]{:S(2)}) %collective-permute-start.1) | collective-permute-done | bytes 1048608 | tf_op jit(solution)/shard_map/ppermute | solution.py:352
  28.8 3.0 %collective-permute-done.2 = bf16[256,2048]{1,0:T(8,128)(2,1)} collective-permute-done((bf16[256,2048]{1,0:T(8,128)(2,1)S(1)}, bf16[256,2048]{1,0:T(8,128)(2,1)}, u32[]{:S(2)}, u32[]{:S(2)}) %collective-permute-start.2) | collective-permute-done | bytes 1048608 | tf_op jit(solution)/shard_map/ppermute | solution.py:352
  31.8 0.9 collective-permute-done.3.refs_1_
  32.7 2.3 %collective-permute-start.6 = (bf16[256,2048]{1,0:T(8,128)(2,1)}, bf16[256,2048]{1,0:T(8,128)(2,1)}, u32[]{:S(2)}, u32[]{:S(2)}) collective-permute-start(bf16[256,2048]{1,0:T(8,128)(2,1)} %collective-permute-done.2), channel_id=1, source_target_pairs={{4,0},{8,12},{5,1},{9,13},{6,2},{10,14},{7,3},{11,15},{20,16},{24,... | collective-permute-start | bytes 3145736 | tf_op jit(solution)/shard_map/ppermute | solution.py:352
  35.0 2.7 %collective-permute-start.7 = (bf16[256,2048]{1,0:T(8,128)(2,1)}, bf16[256,2048]{1,0:T(8,128)(2,1)}, u32[]{:S(2)}, u32[]{:S(2)}) collective-permute-start(bf16[256,2048]{1,0:T(8,128)(2,1)} %collective-permute-done.1.refs_0_.refs_2_), channel_id=1, source_target_pairs={{4,8},{8,4},{5,9},{9,5},{6,10},{10,6},{7,11},{11,7},{20,24},{24,20... | collective-permute-start | bytes 3145736 | tf_op jit(solution)/shard_map/ppermute | solution.py:352
  37.7 1.3 collective-permute-start.8
  39.0 1.3 collective-permute-start.9
  40.5 5.1 %shard_map.86 = (bf16[42,128,128]{2,1,0:T(8,128)(2,1)S(1)}, f32[42,128,128]{2,1,0:T(8,128)S(1)}) custom-call(s32[8]{0:T(128)S(1)} %concatenate.15.place_ref, s32[84,3]{1,0:T(8,128)S(1)} %copy.11.table_ref, bf16[256,2048]{1,0:T(8,128)(2,1)S(1)} %pad_maximum_fusion.refs_0_, bf16[256,2048]{1,0:T(8,128)(2,1)} %collective-permute-done.3.refs_1_), custom_call_target="tpu_custom_call" | custom-call | tf_op jit(solution)/shard_map/pallas_call | solution.py:211
  45.7 6.6 %collective-permute-done.9 = bf16[256,1024]{1,0:T(8,128)(2,1)} collective-permute-done((bf16[256,1024]{1,0:T(8,128)(2,1)}, bf16[256,1024]{1,0:T(8,128)(2,1)}, u32[]{:S(2)}, u32[]{:S(2)}) %collective-permute-start.9) | collective-permute-done | bytes 524320 | tf_op jit(solution)/shard_map/ppermute | solution.py:352
  52.2 3.0 %collective-permute-done.6 = bf16[256,2048]{1,0:T(8,128)(2,1)} collective-permute-done((bf16[256,2048]{1,0:T(8,128)(2,1)}, bf16[256,2048]{1,0:T(8,128)(2,1)}, u32[]{:S(2)}, u32[]{:S(2)}) %collective-permute-start.6) | collective-permute-done | bytes 1048608 | tf_op jit(solution)/shard_map/ppermute | solution.py:352
  55.2 4.8 %collective-permute-done.7 = bf16[256,2048]{1,0:T(8,128)(2,1)} collective-permute-done((bf16[256,2048]{1,0:T(8,128)(2,1)}, bf16[256,2048]{1,0:T(8,128)(2,1)}, u32[]{:S(2)}, u32[]{:S(2)}) %collective-permute-start.7) | collective-permute-done | bytes 1048608 | tf_op jit(solution)/shard_map/ppermute | solution.py:352
  60.0 0.6 collective-permute-done.8.refs_1_.refs_3_
  60.6 1.3 %broadcast_select_fusion.1.refs_4_.refs_0_ = bf16[256,2048]{1,0:T(8,128)(2,1)S(1)} fusion(bf16[256,2048]{1,0:T(8,128)(2,1)} %collective-permute-done.7, bf16[256,2048]{1,0:T(8,128)(2,1)} %collective-permute-done.6, pred[]{:T(512)S(6)} %or.3), kind=kLoop, calls=%fused_computation.2 | loop fusion | flops 524288 | bytes 3145729 | tf_op jit(solution)/shard_map/jit(_where)/select_n | solution.py:419
  62.0 1.3 collective-permute-start.10
  63.3 1.3 %collective-permute-start.11 = (bf16[256,2048]{1,0:T(8,128)(2,1)}, bf16[256,2048]{1,0:T(8,128)(2,1)S(1)}, u32[]{:S(2)}, u32[]{:S(2)}) collective-permute-start(bf16[256,2048]{1,0:T(8,128)(2,1)} %collective-permute-done.7), channel_id=1, source_target_pairs={{4,0},{8,12},{5,1},{9,13},{6,2},{10,14},{7,3},{11,15},{20,16},{24,... | collective-permute-start | bytes 3145736 | tf_op jit(solution)/shard_map/ppermute | solution.py:352
  64.6 2.6 %collective-permute-start.15 = (bf16[256,1024]{1,0:T(8,128)(2,1)S(1)}, bf16[256,1024]{1,0:T(8,128)(2,1)S(1)}, u32[]{:S(2)}, u32[]{:S(2)}) collective-permute-start(bf16[256,1024]{1,0:T(8,128)(2,1)S(1)} %copy-done.2), channel_id=1, source_target_pairs={{4,8},{8,4},{5,9},{9,5},{6,10},{10,6},{7,11},{11,7},{20,24},{24,20... | collective-permute-start | bytes 1572872 | tf_op jit(solution)/shard_map/ppermute | solution.py:352
  67.2 1.3 %collective-permute-start.13 = (bf16[256,1024]{1,0:T(8,128)(2,1)S(1)}, bf16[256,1024]{1,0:T(8,128)(2,1)S(1)}, u32[]{:S(2)}, u32[]{:S(2)}) collective-permute-start(bf16[256,1024]{1,0:T(8,128)(2,1)S(1)} %get-tuple-element.69.refs_6_.refs_2_), channel_id=1, source_target_pairs={{0,4},{12,8},{1,5},{13,9},{2,6},{14,10},{3,7},{15,11},{16,20},{28,... | collective-permute-start | bytes 1572872 | tf_op jit(solution)/shard_map/ppermute | solution.py:352
  68.5 2.7 %collective-permute-start.17 = (bf16[256,1024]{1,0:T(8,128)(2,1)}, bf16[256,1024]{1,0:T(8,128)(2,1)S(1)}, u32[]{:S(2)}, u32[]{:S(2)}) collective-permute-start(bf16[256,1024]{1,0:T(8,128)(2,1)} %collective-permute-done.9), channel_id=1, source_target_pairs={{4,8},{8,4},{5,9},{9,5},{6,10},{10,6},{7,11},{11,7},{20,24},{24,20... | collective-permute-start | bytes 1572872 | tf_op jit(solution)/shard_map/ppermute | solution.py:352
  71.2 5.7 %shard_map.87 = (bf16[42,128,128]{2,1,0:T(8,128)(2,1)S(1)}, f32[42,128,128]{2,1,0:T(8,128)S(1)}) custom-call(s32[8]{0:T(128)S(1)} %concatenate.15.place_ref, s32[84,3]{1,0:T(8,128)S(1)} %copy.11.table_ref, bf16[256,2048]{1,0:T(8,128)(2,1)} %collective-permute-done.1.refs_0_.refs_2_, bf16[256,2048]{1,0:T(8,128)(2,1)} %collective-permute-done.8.refs_1_.refs_3_, ...), custom_call_target="tpu_custom_call" | custom-call | tf_op jit(solution)/shard_map/pallas_call | solution.py:211
  77.0 6.7 %collective-permute-done.10.refs_5_.refs_1_ = bf16[256,2048]{1,0:T(8,128)(2,1)S(1)} collective-permute-done((bf16[256,2048]{1,0:T(8,128)(2,1)S(1)}, bf16[256,2048]{1,0:T(8,128)(2,1)S(1)}, u32[]{:S(2)}, u32[]{:S(2)}) %collective-permute-start.10) | collective-permute-done | bytes 1048608 | tf_op jit(solution)/shard_map/ppermute | solution.py:355
  83.7 0.6 collective-permute-done.11
  84.3 1.3 %broadcast_select_fusion.refs_0_ = bf16[256,2048]{1,0:T(8,128)(2,1)S(1)} fusion(bf16[256,2048]{1,0:T(8,128)(2,1)} %collective-permute-done.2, bf16[256,2048]{1,0:T(8,128)(2,1)S(1)} %collective-permute-done.11, pred[]{:T(512)S(6)} %or.3), kind=kLoop, calls=%fused_computation.1 | loop fusion | flops 524288 | bytes 3145729 | tf_op jit(solution)/shard_map/jit(_where)/select_n | solution.py:430
  85.6 0.7 collective-permute-start.12
  86.3 4.2 %collective-permute-start.16 = (bf16[256,1024]{1,0:T(8,128)(2,1)S(1)}, bf16[256,1024]{1,0:T(8,128)(2,1)S(1)}, u32[]{:S(2)}, u32[]{:S(2)}) collective-permute-start(bf16[256,1024]{1,0:T(8,128)(2,1)S(1)} %collective-permute-done.15.refs_10_.refs_6_), channel_id=1, source_target_pairs={{0,1},{1,0},{2,3},{3,2},{4,5},{5,4},{6,7},{7,6},{8,9},{9,8},{10,11... | collective-permute-start | bytes 1572872 | tf_op jit(solution)/shard_map/ppermute | solution.py:358
  90.6 1.5 %collective-permute-start.18 = (bf16[256,1024]{1,0:T(8,128)(2,1)S(1)}, bf16[256,1024]{1,0:T(8,128)(2,1)S(1)}, u32[]{:S(2)}, u32[]{:S(2)}) collective-permute-start(bf16[256,1024]{1,0:T(8,128)(2,1)S(1)} %collective-permute-done.17.refs_12_.refs_8_), channel_id=1, source_target_pairs={{0,1},{1,0},{2,3},{3,2},{4,5},{5,4},{6,7},{7,6},{8,9},{9,8},{10,11... | collective-permute-start | bytes 1572872 | tf_op jit(solution)/shard_map/ppermute | solution.py:358
  92.1 0.7 collective-permute-done.14.refs_9_.refs_5_
  92.8 0.8 collective-permute-done.18.refs_13_.refs_9_
  93.6 5.8 %shard_map.88 = (bf16[2,256,256]{2,1,0:T(8,128)(2,1)S(1)}, bf16[2,256,256]{2,1,0:T(8,128)(2,1)S(1)}, bf16[2,256,256]{2,1,0:T(8,128)(2,1)S(1)}) custom-call(s32[8]{0:T(128)S(1)} %concatenate.15.place_ref, bf16[256,2048]{1,0:T(8,128)(2,1)S(1)} %pad_maximum_fusion.refs_0_, bf16[256,2048]{1,0:T(8,128)(2,1)} %collective-permute-done.3.refs_1_, ...), custom_call_target="tpu_custom_call" | custom-call | tf_op jit(solution)/shard_map/pallas_call | solution.py:296
  99.4 1.3 %collective-permute-start.19 = (bf16[2,256,256]{2,1,0:T(8,128)(2,1)S(1)}, bf16[2,256,256]{2,1,0:T(8,128)(2,1)S(1)}, u32[]{:S(2)}, u32[]{:S(2)}) collective-permute-start(bf16[2,256,256]{2,1,0:T(8,128)(2,1)S(1)} %get-tuple-element.72), channel_id=1, source_target_pairs={{4,0},{8,12},{5,1},{9,13},{6,2},{10,14},{7,3},{11,15},{20,16},{24,... | collective-permute-start | bytes 786440 | tf_op jit(solution)/shard_map/ppermute | solution.py:352
  100.7 2.7 %collective-permute-start.20 = (bf16[2,256,256]{2,1,0:T(8,128)(2,1)S(1)}, bf16[2,256,256]{2,1,0:T(8,128)(2,1)S(1)}, u32[]{:S(2)}, u32[]{:S(2)}) collective-permute-start(bf16[2,256,256]{2,1,0:T(8,128)(2,1)S(1)} %get-tuple-element.73), channel_id=1, source_target_pairs={{4,8},{8,4},{5,9},{9,5},{6,10},{10,6},{7,11},{11,7},{20,24},{24,20... | collective-permute-start | bytes 786440 | tf_op jit(solution)/shard_map/ppermute | solution.py:352
  103.4 4.3 %shard_map.89 = (bf16[42,128,128]{2,1,0:T(8,128)(2,1)S(1)}, f32[42,128,128]{2,1,0:T(8,128)S(1)}) custom-call(s32[8]{0:T(128)S(1)} %concatenate.15.place_ref, s32[84,3]{1,0:T(8,128)S(1)} %copy.11.table_ref, bf16[256,2048]{1,0:T(8,128)(2,1)S(1)} %broadcast_select_fusion.1.refs_4_.refs_0_, bf16[256,2048]{1,0:T(8,128)(2,1)S(1)} %collective-permute-done.10.refs_5_.refs_1_, ...), custom_call_target="tpu_custom_call" | custom-call | tf_op jit(solution)/shard_map/pallas_call | solution.py:211
  107.8 2.3 %collective-permute-done.20 = bf16[2,256,256]{2,1,0:T(8,128)(2,1)S(1)} collective-permute-done((bf16[2,256,256]{2,1,0:T(8,128)(2,1)S(1)}, bf16[2,256,256]{2,1,0:T(8,128)(2,1)S(1)}, u32[]{:S(2)}, u32[]{:S(2)}) %collective-permute-start.20) | collective-permute-done | bytes 262176 | tf_op jit(solution)/shard_map/ppermute | solution.py:352
  110.1 1.2 collective-permute-start.25
  111.8 2.0 %shard_map.90 = bf16[2,256,256]{2,1,0:T(8,128)(2,1)S(1)} custom-call(s32[8]{0:T(128)S(1)} %concatenate.15.place_ref, bf16[256,2048]{1,0:T(8,128)(2,1)S(1)} %broadcast_select_fusion.refs_0_, bf16[256,2048]{1,0:T(8,128)(2,1)S(1)} %collective-permute-done.12.refs_1_.refs_2_, bf16[256,1024]{1,0:T(8,128)(2,1)S(1)} %get-tuple-element.69.refs_6_.refs_2_, ...), custom_call_target="tpu_custom_call" | custom-call | tf_op jit(solution)/shard_map/pallas_call | solution.py:296
  113.9 1.3 %collective-permute-start.21 = (bf16[2,256,256]{2,1,0:T(8,128)(2,1)S(1)}, bf16[2,256,256]{2,1,0:T(8,128)(2,1)S(1)}, u32[]{:S(2)}, u32[]{:S(2)}) collective-permute-start(bf16[2,256,256]{2,1,0:T(8,128)(2,1)S(1)} %collective-permute-done.20), channel_id=1, source_target_pairs={{4,0},{8,12},{5,1},{9,13},{6,2},{10,14},{7,3},{11,15},{20,16},{24,... | collective-permute-start | bytes 786440 | tf_op jit(solution)/shard_map/ppermute | solution.py:352
  115.2 2.5 %collective-permute-start.22 = (bf16[2,256,256]{2,1,0:T(8,128)(2,1)S(1)}, bf16[2,256,256]{2,1,0:T(8,128)(2,1)S(1)}, u32[]{:S(2)}, u32[]{:S(2)}) collective-permute-start(bf16[2,256,256]{2,1,0:T(8,128)(2,1)S(1)} %shard_map.90), channel_id=1, source_target_pairs={{4,8},{8,4},{5,9},{9,5},{6,10},{10,6},{7,11},{11,7},{20,24},{24,20... | collective-permute-start | bytes 786440 | tf_op jit(solution)/shard_map/ppermute | solution.py:352
  118.3 6.1 %shard_map.91 = f32[42,128,128]{2,1,0:T(8,128)} custom-call(s32[8]{0:T(128)S(1)} %concatenate.15.place_ref, s32[84,3]{1,0:T(8,128)S(1)} %copy.11.table_ref, bf16[256,2048]{1,0:T(8,128)(2,1)S(1)} %broadcast_select_fusion.refs_0_, bf16[256,2048]{1,0:T(8,128)(2,1)S(1)} %collective-permute-done.23.refs_1_, ...), custom_call_target="tpu_custom_call" | custom-call | tf_op jit(solution)/shard_map/pallas_call | solution.py:211
  124.7 1.2 collective-permute-start.27
  125.9 1.0 collective-permute-done.27.refs_5_
  126.9 1.6 %shard_map.92 = f32[512,512]{1,0:T(8,128)} custom-call(s32[8]{0:T(128)S(1)} %concatenate.15.place_ref, bf16[2,256,256]{2,1,0:T(8,128)(2,1)S(1)} %get-tuple-element.77.refs_0_, bf16[2,256,256]{2,1,0:T(8,128)(2,1)S(1)} %collective-permute-done.22.refs_1_, bf16[2,256,256]{2,1,0:T(8,128)(2,1)S(1)} %collective-permute-done.19.refs_2_, ...), custom_call_target="tpu_custom_call" | custom-call | tf_op jit(solution)/shard_map/pallas_call | solution.py:328
  (42 shorter events, 2.1 us)
Async XLA Ops:
  0.6 1.2 copy-start
  1.9 2.3 %collective-permute-start = (bf16[256,1024]{1,0:T(8,128)(2,1)S(1)}, bf16[256,1024]{1,0:T(8,128)(2,1)S(1)}, u32[]{:S(2)}, u32[]{:S(2)}) collective-permute-start(bf16[256,1024]{1,0:T(8,128)(2,1)S(1)} %constant_dynamic-slice_fusion.4), channel_id=1, source_target_pairs={{0,1},{1,0},{2,3},{3,2},{4,5},{5,4},{6,7},{7,6},{8,9},{9,8},{10,11... | collective-permute-start | bytes 1572872 | tf_op jit(solution)/shard_map/ppermute | solution.py:358
  2.7 10.7 %copy-start.5 = (s32[1,168,2]{1,2,0:T(2,128)S(1)}, s32[1,168,2]{1,2,0:T(2,128)}, u32[]{:S(2)}) copy-start(s32[1,168,2]{1,2,0:T(2,128)} %param.10) | copy-start | bytes 4036
  2.7 37.6 %copy-start.3 = (s32[4]{0:T(128)S(1)}, s32[4]{0:T(128)}, u32[]{:S(2)}) copy-start(s32[4]{0:T(128)} %constant.71.clone) | copy-start | bytes 52
  2.7 37.6 %copy-start.4 = (s32[4]{0:T(128)S(1)}, s32[4]{0:T(128)}, u32[]{:S(2)}) copy-start(s32[4]{0:T(128)} %constant.72.clone) | copy-start | bytes 52
  4.3 24.5 %collective-permute-start.1 = (bf16[256,2048]{1,0:T(8,128)(2,1)S(1)}, bf16[256,2048]{1,0:T(8,128)(2,1)}, u32[]{:S(2)}, u32[]{:S(2)}) collective-permute-start(bf16[256,2048]{1,0:T(8,128)(2,1)S(1)} %pad_maximum_fusion.refs_0_), channel_id=1, source_target_pairs={{0,4},{4,0},{8,12},{12,8},{1,5},{5,1},{9,13},{13,9},{2,6},{6,2},{1... | collective-permute-start | bytes 3145736 | tf_op jit(solution)/shard_map/ppermute | solution.py:352
  4.3 27.5 %collective-permute-start.2 = (bf16[256,2048]{1,0:T(8,128)(2,1)S(1)}, bf16[256,2048]{1,0:T(8,128)(2,1)}, u32[]{:S(2)}, u32[]{:S(2)}) collective-permute-start(bf16[256,2048]{1,0:T(8,128)(2,1)S(1)} %pad_maximum_fusion.refs_0_), channel_id=1, source_target_pairs={{4,8},{8,4},{5,9},{9,5},{6,10},{10,6},{7,11},{11,7},{20,24},{24,20... | collective-permute-start | bytes 3145736 | tf_op jit(solution)/shard_map/ppermute | solution.py:352
  8.8 23.9 %collective-permute-start.3 = (bf16[256,2048]{1,0:T(8,128)(2,1)S(1)}, bf16[256,2048]{1,0:T(8,128)(2,1)}, u32[]{:S(2)}, u32[]{:S(2)}) collective-permute-start(bf16[256,2048]{1,0:T(8,128)(2,1)S(1)} %pad_maximum_fusion.refs_0_), channel_id=1, source_target_pairs={{0,2},{2,0},{1,3},{3,1},{4,6},{6,4},{5,7},{7,5},{8,10},{10,8},{9,1... | collective-permute-start | bytes 3145736 | tf_op jit(solution)/shard_map/ppermute | solution.py:355
  12.2 2.9 %collective-permute-start.5 = (bf16[256,1024]{1,0:T(8,128)(2,1)S(1)}, bf16[256,1024]{1,0:T(8,128)(2,1)S(1)}, u32[]{:S(2)}, u32[]{:S(2)}) collective-permute-start(bf16[256,1024]{1,0:T(8,128)(2,1)S(1)} %get-tuple-element.69.refs_6_.refs_2_), channel_id=1, source_target_pairs={{0,1},{1,0},{2,3},{3,2},{4,5},{5,4},{6,7},{7,6},{8,9},{9,8},{10,11... | collective-permute-start | bytes 1572872 | tf_op jit(solution)/shard_map/ppermute | solution.py:358
  13.5 1.5 %collective-permute-start.4 = (s32[42,2]{0,1:T(2,128)S(1)}, s32[42,2]{0,1:T(2,128)S(1)}, u32[]{:S(2)}, u32[]{:S(2)}) collective-permute-start(s32[42,2]{0,1:T(2,128)S(1)} %fusion.1), channel_id=1, source_target_pairs={{0,1},{1,0},{2,3},{3,2},{4,5},{5,4},{6,7},{7,6},{8,9},{9,8},{10,11... | collective-permute-start | bytes 1016 | tf_op jit(solution)/shard_map/ppermute | solution.py:358
  32.7 22.5 %collective-permute-start.6 = (bf16[256,2048]{1,0:T(8,128)(2,1)}, bf16[256,2048]{1,0:T(8,128)(2,1)}, u32[]{:S(2)}, u32[]{:S(2)}) collective-permute-start(bf16[256,2048]{1,0:T(8,128)(2,1)} %collective-permute-done.2), channel_id=1, source_target_pairs={{4,0},{8,12},{5,1},{9,13},{6,2},{10,14},{7,3},{11,15},{20,16},{24,... | collective-permute-start | bytes 3145736 | tf_op jit(solution)/shard_map/ppermute | solution.py:352
  35.0 25.0 %collective-permute-start.7 = (bf16[256,2048]{1,0:T(8,128)(2,1)}, bf16[256,2048]{1,0:T(8,128)(2,1)}, u32[]{:S(2)}, u32[]{:S(2)}) collective-permute-start(bf16[256,2048]{1,0:T(8,128)(2,1)} %collective-permute-done.1.refs_0_.refs_2_), channel_id=1, source_target_pairs={{4,8},{8,4},{5,9},{9,5},{6,10},{10,6},{7,11},{11,7},{20,24},{24,20... | collective-permute-start | bytes 3145736 | tf_op jit(solution)/shard_map/ppermute | solution.py:352
  37.7 22.9 %collective-permute-start.8 = (bf16[256,2048]{1,0:T(8,128)(2,1)}, bf16[256,2048]{1,0:T(8,128)(2,1)}, u32[]{:S(2)}, u32[]{:S(2)}) collective-permute-start(bf16[256,2048]{1,0:T(8,128)(2,1)} %collective-permute-done.1.refs_0_.refs_2_), channel_id=1, source_target_pairs={{0,2},{2,0},{1,3},{3,1},{4,6},{6,4},{5,7},{7,5},{8,10},{10,8},{9,1... | collective-permute-start | bytes 3145736 | tf_op jit(solution)/shard_map/ppermute | solution.py:355
  39.0 13.3 %collective-permute-start.9 = (bf16[256,1024]{1,0:T(8,128)(2,1)}, bf16[256,1024]{1,0:T(8,128)(2,1)}, u32[]{:S(2)}, u32[]{:S(2)}) collective-permute-start(bf16[256,1024]{1,0:T(8,128)(2,1)} %get-tuple-element.49), channel_id=1, source_target_pairs={{0,4},{12,8},{1,5},{13,9},{2,6},{14,10},{3,7},{15,11},{16,20},{28,... | collective-permute-start | bytes 1572872 | tf_op jit(solution)/shard_map/ppermute | solution.py:352
  45.7 19.0 %copy-start.2 = (bf16[256,1024]{1,0:T(8,128)(2,1)S(1)}, bf16[256,1024]{1,0:T(8,128)(2,1)}, u32[]{:S(2)}) copy-start(bf16[256,1024]{1,0:T(8,128)(2,1)} %get-tuple-element.49) | copy-start | bytes 1572868
  62.0 21.7 %collective-permute-start.10 = (bf16[256,2048]{1,0:T(8,128)(2,1)S(1)}, bf16[256,2048]{1,0:T(8,128)(2,1)S(1)}, u32[]{:S(2)}, u32[]{:S(2)}) collective-permute-start(bf16[256,2048]{1,0:T(8,128)(2,1)S(1)} %broadcast_select_fusion.1.refs_4_.refs_0_), channel_id=1, source_target_pairs={{0,2},{2,0},{1,3},{3,1},{4,6},{6,4},{5,7},{7,5},{8,10},{10,8},{9,1... | collective-permute-start | bytes 3145736 | tf_op jit(solution)/shard_map/ppermute | solution.py:355
  63.3 21.0 %collective-permute-start.11 = (bf16[256,2048]{1,0:T(8,128)(2,1)}, bf16[256,2048]{1,0:T(8,128)(2,1)S(1)}, u32[]{:S(2)}, u32[]{:S(2)}) collective-permute-start(bf16[256,2048]{1,0:T(8,128)(2,1)} %collective-permute-done.7), channel_id=1, source_target_pairs={{4,0},{8,12},{5,1},{9,13},{6,2},{10,14},{7,3},{11,15},{20,16},{24,... | collective-permute-start | bytes 3145736 | tf_op jit(solution)/shard_map/ppermute | solution.py:352
  64.6 21.7 %collective-permute-start.15 = (bf16[256,1024]{1,0:T(8,128)(2,1)S(1)}, bf16[256,1024]{1,0:T(8,128)(2,1)S(1)}, u32[]{:S(2)}, u32[]{:S(2)}) collective-permute-start(bf16[256,1024]{1,0:T(8,128)(2,1)S(1)} %copy-done.2), channel_id=1, source_target_pairs={{4,8},{8,4},{5,9},{9,5},{6,10},{10,6},{7,11},{11,7},{20,24},{24,20... | collective-permute-start | bytes 1572872 | tf_op jit(solution)/shard_map/ppermute | solution.py:352
  67.2 23.3 %collective-permute-start.13 = (bf16[256,1024]{1,0:T(8,128)(2,1)S(1)}, bf16[256,1024]{1,0:T(8,128)(2,1)S(1)}, u32[]{:S(2)}, u32[]{:S(2)}) collective-permute-start(bf16[256,1024]{1,0:T(8,128)(2,1)S(1)} %get-tuple-element.69.refs_6_.refs_2_), channel_id=1, source_target_pairs={{0,4},{12,8},{1,5},{13,9},{2,6},{14,10},{3,7},{15,11},{16,20},{28,... | collective-permute-start | bytes 1572872 | tf_op jit(solution)/shard_map/ppermute | solution.py:352
  68.5 22.1 %collective-permute-start.17 = (bf16[256,1024]{1,0:T(8,128)(2,1)}, bf16[256,1024]{1,0:T(8,128)(2,1)S(1)}, u32[]{:S(2)}, u32[]{:S(2)}) collective-permute-start(bf16[256,1024]{1,0:T(8,128)(2,1)} %collective-permute-done.9), channel_id=1, source_target_pairs={{4,8},{8,4},{5,9},{9,5},{6,10},{10,6},{7,11},{11,7},{20,24},{24,20... | collective-permute-start | bytes 1572872 | tf_op jit(solution)/shard_map/ppermute | solution.py:352
  85.6 24.5 %collective-permute-start.12 = (bf16[256,2048]{1,0:T(8,128)(2,1)S(1)}, bf16[256,2048]{1,0:T(8,128)(2,1)S(1)}, u32[]{:S(2)}, u32[]{:S(2)}) collective-permute-start(bf16[256,2048]{1,0:T(8,128)(2,1)S(1)} %broadcast_select_fusion.refs_0_), channel_id=1, source_target_pairs={{0,2},{2,0},{1,3},{3,1},{4,6},{6,4},{5,7},{7,5},{8,10},{10,8},{9,1... | collective-permute-start | bytes 3145736 | tf_op jit(solution)/shard_map/ppermute | solution.py:355
  86.3 5.8 %collective-permute-start.16 = (bf16[256,1024]{1,0:T(8,128)(2,1)S(1)}, bf16[256,1024]{1,0:T(8,128)(2,1)S(1)}, u32[]{:S(2)}, u32[]{:S(2)}) collective-permute-start(bf16[256,1024]{1,0:T(8,128)(2,1)S(1)} %collective-permute-done.15.refs_10_.refs_6_), channel_id=1, source_target_pairs={{0,1},{1,0},{2,3},{3,2},{4,5},{5,4},{6,7},{7,6},{8,9},{9,8},{10,11... | collective-permute-start | bytes 1572872 | tf_op jit(solution)/shard_map/ppermute | solution.py:358
  90.5 2.3 %collective-permute-start.14 = (bf16[256,1024]{1,0:T(8,128)(2,1)S(1)}, bf16[256,1024]{1,0:T(8,128)(2,1)S(1)}, u32[]{:S(2)}, u32[]{:S(2)}) collective-permute-start(bf16[256,1024]{1,0:T(8,128)(2,1)S(1)} %collective-permute-done.13.refs_8_.refs_4_), channel_id=1, source_target_pairs={{0,1},{1,0},{2,3},{3,2},{4,5},{5,4},{6,7},{7,6},{8,9},{9,8},{10,11... | collective-permute-start | bytes 1572872 | tf_op jit(solution)/shard_map/ppermute | solution.py:358
  90.6 3.0 %collective-permute-start.18 = (bf16[256,1024]{1,0:T(8,128)(2,1)S(1)}, bf16[256,1024]{1,0:T(8,128)(2,1)S(1)}, u32[]{:S(2)}, u32[]{:S(2)}) collective-permute-start(bf16[256,1024]{1,0:T(8,128)(2,1)S(1)} %collective-permute-done.17.refs_12_.refs_8_), channel_id=1, source_target_pairs={{0,1},{1,0},{2,3},{3,2},{4,5},{5,4},{6,7},{7,6},{8,9},{9,8},{10,11... | collective-permute-start | bytes 1572872 | tf_op jit(solution)/shard_map/ppermute | solution.py:358
  99.4 8.4 %collective-permute-start.19 = (bf16[2,256,256]{2,1,0:T(8,128)(2,1)S(1)}, bf16[2,256,256]{2,1,0:T(8,128)(2,1)S(1)}, u32[]{:S(2)}, u32[]{:S(2)}) collective-permute-start(bf16[2,256,256]{2,1,0:T(8,128)(2,1)S(1)} %get-tuple-element.72), channel_id=1, source_target_pairs={{4,0},{8,12},{5,1},{9,13},{6,2},{10,14},{7,3},{11,15},{20,16},{24,... | collective-permute-start | bytes 786440 | tf_op jit(solution)/shard_map/ppermute | solution.py:352
  100.7 9.4 %collective-permute-start.20 = (bf16[2,256,256]{2,1,0:T(8,128)(2,1)S(1)}, bf16[2,256,256]{2,1,0:T(8,128)(2,1)S(1)}, u32[]{:S(2)}, u32[]{:S(2)}) collective-permute-start(bf16[2,256,256]{2,1,0:T(8,128)(2,1)S(1)} %get-tuple-element.73), channel_id=1, source_target_pairs={{4,8},{8,4},{5,9},{9,5},{6,10},{10,6},{7,11},{11,7},{20,24},{24,20... | collective-permute-start | bytes 786440 | tf_op jit(solution)/shard_map/ppermute | solution.py:352
  110.1 8.2 %collective-permute-start.25 = (bf16[42,128,128]{2,1,0:T(8,128)(2,1)S(1)}, bf16[42,128,128]{2,1,0:T(8,128)(2,1)S(1)}, u32[]{:S(2)}, u32[]{:S(2)}) collective-permute-start(bf16[42,128,128]{2,1,0:T(8,128)(2,1)S(1)} %get-tuple-element.84), channel_id=1, source_target_pairs={{0,1},{1,0},{2,3},{3,2},{4,5},{5,4},{6,7},{7,6},{8,9},{9,8},{10,11... | collective-permute-start | bytes 4128776 | tf_op jit(solution)/shard_map/ppermute | solution.py:358
  111.3 6.4 %collective-permute-start.23 = (bf16[256,2048]{1,0:T(8,128)(2,1)S(1)}, bf16[256,2048]{1,0:T(8,128)(2,1)S(1)}, u32[]{:S(2)}, u32[]{:S(2)}) collective-permute-start(bf16[256,2048]{1,0:T(8,128)(2,1)S(1)} %broadcast_select_fusion.refs_0_), channel_id=1, source_target_pairs={{0,1},{1,0},{2,3},{3,2},{4,5},{5,4},{6,7},{7,6},{8,9},{9,8},{10,11... | collective-permute-start | bytes 3145736 | tf_op jit(solution)/shard_map/ppermute | solution.py:358
  111.3 7.0 %collective-permute-start.24 = (bf16[256,2048]{1,0:T(8,128)(2,1)S(1)}, bf16[256,2048]{1,0:T(8,128)(2,1)S(1)}, u32[]{:S(2)}, u32[]{:S(2)}) collective-permute-start(bf16[256,2048]{1,0:T(8,128)(2,1)S(1)} %collective-permute-done.12.refs_1_.refs_2_), channel_id=1, source_target_pairs={{0,1},{1,0},{2,3},{3,2},{4,5},{5,4},{6,7},{7,6},{8,9},{9,8},{10,11... | collective-permute-start | bytes 3145736 | tf_op jit(solution)/shard_map/ppermute | solution.py:358
  113.8 13.0 %copy-start.1 = (f32[512]{0:T(512)S(1)}, f32[512]{0:T(512)}, u32[]{:S(2)}) copy-start(f32[512]{0:T(512)} %param.9) | copy-start | bytes 6148
  113.9 10.6 %collective-permute-start.21 = (bf16[2,256,256]{2,1,0:T(8,128)(2,1)S(1)}, bf16[2,256,256]{2,1,0:T(8,128)(2,1)S(1)}, u32[]{:S(2)}, u32[]{:S(2)}) collective-permute-start(bf16[2,256,256]{2,1,0:T(8,128)(2,1)S(1)} %collective-permute-done.20), channel_id=1, source_target_pairs={{4,0},{8,12},{5,1},{9,13},{6,2},{10,14},{7,3},{11,15},{20,16},{24,... | collective-permute-start | bytes 786440 | tf_op jit(solution)/shard_map/ppermute | solution.py:352
  115.2 9.5 %collective-permute-start.22 = (bf16[2,256,256]{2,1,0:T(8,128)(2,1)S(1)}, bf16[2,256,256]{2,1,0:T(8,128)(2,1)S(1)}, u32[]{:S(2)}, u32[]{:S(2)}) collective-permute-start(bf16[2,256,256]{2,1,0:T(8,128)(2,1)S(1)} %shard_map.90), channel_id=1, source_target_pairs={{4,8},{8,4},{5,9},{9,5},{6,10},{10,6},{7,11},{11,7},{20,24},{24,20... | collective-permute-start | bytes 786440 | tf_op jit(solution)/shard_map/ppermute | solution.py:352
  117.7 8.1 %collective-permute-start.26 = (bf16[256,256]{1,0:T(8,128)(2,1)S(1)}, bf16[256,256]{1,0:T(8,128)(2,1)S(1)}, u32[]{:S(2)}, u32[]{:S(2)}) collective-permute-start(bf16[256,256]{1,0:T(8,128)(2,1)S(1)} %fusion), channel_id=1, source_target_pairs={{0,1},{1,0},{2,3},{3,2},{4,5},{5,4},{6,7},{7,6},{8,9},{9,8},{10,11... | collective-permute-start | bytes 393224 | tf_op jit(solution)/shard_map/ppermute | solution.py:358
  124.7 2.2 %collective-permute-start.27 = (bf16[256,256]{1,0:T(8,128)(2,1)S(1)}, bf16[256,256]{1,0:T(8,128)(2,1)S(1)}, u32[]{:S(2)}, u32[]{:S(2)}) collective-permute-start(bf16[256,256]{1,0:T(8,128)(2,1)S(1)} %select_bitcast_fusion), channel_id=1, source_target_pairs={{0,1},{1,0},{2,3},{3,2},{4,5},{5,4},{6,7},{7,6},{8,9},{9,8},{10,11... | collective-permute-start | bytes 393224 | tf_op jit(solution)/shard_map/ppermute | solution.py:358

commit v8 on v7

--- a/solution.py
+++ b/solution.py
@@ -421,8 +421,9 @@
     outer_end = move(outer, TO_END)
     q_inner = move(q_other, INNER)
     q_far = move(q_end_other, INNER)
-    q_end = move(q_mine, TO_MID)
     sibling1, sum1 = tile_call(place, table, whole(near, near_x), [sum0], sibling0)
+    (q_late,) = after((q_mine,), sum1)
+    q_end = move(q_late, TO_MID)
 
     second, second_x, outer_end, inner, sum1, sibling1 = after(
         (second, second_x, outer_end, inner, sum1, sibling1)

time: 129 us -> 129 us (level)
  transfers between devices with their start and end apart: 28 -> 28, of which waited for: 16 -> 16; matrix products, arithmetic and copies ran while one was open for 3% -> 3% of each run, Pallas kernels for 23% -> 22%
where the time goes in v8:
time: 129 us; the launch traced here: 128 us
  waiting for transfers between devices  48.1 us (37%)
  starting transfers between devices  42.3 us (33%)
  Pallas kernels  30.5 us (24%)
  local copies, waits for them, and re-layouts  3.64 us (3%)
  other arithmetic  2.89 us (2%)
    ppermute x13, waiting for transfers between devices, move(): return lax.ppermute(value, 'ex', pairs)  34.4 us
    ppermute x13, starting transfers between devices, move(): return lax.ppermute(value, 'ex', pairs)  26.6 us
    pallas_call x4, Pallas kernels, tile_call(): pl.pallas_call(kernel, out_shape=outs + (scores.out_shape if scores else...  21.2 us
    ppermute x11, starting transfers between devices, swap(): return lax.ppermute(value, 'feat', CORE)  11.2 us
    ppermute x4, waiting for transfers between devices, across(): return lax.ppermute(value, 'feat', ACROSS)  8.31 us
    pallas_call x2, Pallas kernels, score_call(): pl.pallas_call(kernel, out_shape=scores.out_shape, in_specs=[smem] + [hbm...  7.75 us
    ppermute x11, waiting for transfers between devices, swap(): return lax.ppermute(value, 'feat', CORE)  5.44 us
    ppermute x4, starting transfers between devices, across(): return lax.ppermute(value, 'feat', ACROSS)  4.52 us
  transfers between devices with their start and end apart: 28, of which 16 were waited for; matrix products, arithmetic and copies ran while one was open for 3% of the time, Pallas kernels for 22%

profile of v8, /device:TPU:9, one launch (start us, length us, event | category | flops | bytes accessed | tf_op | source)
XLA Modules:
  0.0 128.5 jit_solution(5724289755826382757)
XLA Ops:
  0.7 1.2 copy-done
  1.9 0.7 collective-permute-start
  2.7 1.5 %collective-permute-done = bf16[256,1024]{1,0:T(8,128)(2,1)S(1)} collective-permute-done((bf16[256,1024]{1,0:T(8,128)(2,1)S(1)}, bf16[256,1024]{1,0:T(8,128)(2,1)S(1)}, u32[]{:S(2)}, u32[]{:S(2)}) %collective-permute-start) | collective-permute-done | bytes 524320 | tf_op jit(solution)/shard_map/ppermute | solution.py:358
  4.3 4.5 %collective-permute-start.2 = (bf16[256,2048]{1,0:T(8,128)(2,1)S(1)}, bf16[256,2048]{1,0:T(8,128)(2,1)}, u32[]{:S(2)}, u32[]{:S(2)}) collective-permute-start(bf16[256,2048]{1,0:T(8,128)(2,1)S(1)} %pad_maximum_fusion.refs_0_), channel_id=1, source_target_pairs={{4,8},{8,4},{5,9},{9,5},{6,10},{10,6},{7,11},{11,7},{20,24},{24,20... | collective-permute-start | bytes 3145736 | tf_op jit(solution)/shard_map/ppermute | solution.py:352
  8.8 1.3 collective-permute-start.3
  10.1 2.1 %constant_dynamic-slice_fusion.1 = (bf16[256,1024]{1,0:T(8,128)(2,1)}, bf16[256,1024]{1,0:T(8,128)(2,1)S(1)}) fusion(bf16[512,1024]{1,0:T(8,128)(2,1)} %param.8, s32[]{:T(128)S(6)} %select_n.73, s32[]{:T(128)S(6)} %mul.21), kind=kLoop, calls=%fused_computation.11 | loop fusion | bytes 2097160 | tf_op jit(solution)/shard_map/dynamic_slice | solution.py:403
  12.2 1.2 collective-permute-start.5
  13.5 1.4 %collective-permute-done.4 = s32[42,2]{0,1:T(2,128)S(1)} collective-permute-done((s32[42,2]{0,1:T(2,128)S(1)}, s32[42,2]{0,1:T(2,128)S(1)}, u32[]{:S(2)}, u32[]{:S(2)}) %collective-permute-start.4) | collective-permute-done | bytes 368 | tf_op jit(solution)/shard_map/ppermute | solution.py:358
  15.0 13.8 %collective-permute-done.1.refs_0_.refs_2_ = bf16[256,2048]{1,0:T(8,128)(2,1)} collective-permute-done((bf16[256,2048]{1,0:T(8,128)(2,1)S(1)}, bf16[256,2048]{1,0:T(8,128)(2,1)}, u32[]{:S(2)}, u32[]{:S(2)}) %collective-permute-start.1) | collective-permute-done | bytes 1048608 | tf_op jit(solution)/shard_map/ppermute | solution.py:352
  28.8 3.0 %collective-permute-done.2 = bf16[256,2048]{1,0:T(8,128)(2,1)} collective-permute-done((bf16[256,2048]{1,0:T(8,128)(2,1)S(1)}, bf16[256,2048]{1,0:T(8,128)(2,1)}, u32[]{:S(2)}, u32[]{:S(2)}) %collective-permute-start.2) | collective-permute-done | bytes 1048608 | tf_op jit(solution)/shard_map/ppermute | solution.py:352
  31.8 0.9 collective-permute-done.3.refs_1_
  32.7 2.3 %collective-permute-start.6 = (bf16[256,2048]{1,0:T(8,128)(2,1)}, bf16[256,2048]{1,0:T(8,128)(2,1)}, u32[]{:S(2)}, u32[]{:S(2)}) collective-permute-start(bf16[256,2048]{1,0:T(8,128)(2,1)} %collective-permute-done.2), channel_id=1, source_target_pairs={{4,0},{8,12},{5,1},{9,13},{6,2},{10,14},{7,3},{11,15},{20,16},{24,... | collective-permute-start | bytes 3145736 | tf_op jit(solution)/shard_map/ppermute | solution.py:352
  35.0 2.7 %collective-permute-start.7 = (bf16[256,2048]{1,0:T(8,128)(2,1)}, bf16[256,2048]{1,0:T(8,128)(2,1)}, u32[]{:S(2)}, u32[]{:S(2)}) collective-permute-start(bf16[256,2048]{1,0:T(8,128)(2,1)} %collective-permute-done.1.refs_0_.refs_2_), channel_id=1, source_target_pairs={{4,8},{8,4},{5,9},{9,5},{6,10},{10,6},{7,11},{11,7},{20,24},{24,20... | collective-permute-start | bytes 3145736 | tf_op jit(solution)/shard_map/ppermute | solution.py:352
  37.7 1.3 collective-permute-start.8
  39.0 1.3 collective-permute-start.9
  40.5 5.1 %shard_map.86 = (bf16[42,128,128]{2,1,0:T(8,128)(2,1)S(1)}, f32[42,128,128]{2,1,0:T(8,128)S(1)}) custom-call(s32[8]{0:T(128)S(1)} %concatenate.15.place_ref, s32[84,3]{1,0:T(8,128)S(1)} %copy.11.table_ref, bf16[256,2048]{1,0:T(8,128)(2,1)S(1)} %pad_maximum_fusion.refs_0_, bf16[256,2048]{1,0:T(8,128)(2,1)} %collective-permute-done.3.refs_1_), custom_call_target="tpu_custom_call" | custom-call | tf_op jit(solution)/shard_map/pallas_call | solution.py:211
  45.6 6.6 %collective-permute-done.9 = bf16[256,1024]{1,0:T(8,128)(2,1)} collective-permute-done((bf16[256,1024]{1,0:T(8,128)(2,1)}, bf16[256,1024]{1,0:T(8,128)(2,1)}, u32[]{:S(2)}, u32[]{:S(2)}) %collective-permute-start.9) | collective-permute-done | bytes 524320 | tf_op jit(solution)/shard_map/ppermute | solution.py:352
  52.2 3.0 %collective-permute-done.6 = bf16[256,2048]{1,0:T(8,128)(2,1)} collective-permute-done((bf16[256,2048]{1,0:T(8,128)(2,1)}, bf16[256,2048]{1,0:T(8,128)(2,1)}, u32[]{:S(2)}, u32[]{:S(2)}) %collective-permute-start.6) | collective-permute-done | bytes 1048608 | tf_op jit(solution)/shard_map/ppermute | solution.py:352
  55.2 4.8 %collective-permute-done.7 = bf16[256,2048]{1,0:T(8,128)(2,1)} collective-permute-done((bf16[256,2048]{1,0:T(8,128)(2,1)}, bf16[256,2048]{1,0:T(8,128)(2,1)}, u32[]{:S(2)}, u32[]{:S(2)}) %collective-permute-start.7) | collective-permute-done | bytes 1048608 | tf_op jit(solution)/shard_map/ppermute | solution.py:352
  60.0 0.6 collective-permute-done.8.refs_1_.refs_3_
  60.6 1.3 %broadcast_select_fusion.1.refs_4_.refs_0_ = bf16[256,2048]{1,0:T(8,128)(2,1)S(1)} fusion(bf16[256,2048]{1,0:T(8,128)(2,1)} %collective-permute-done.7, bf16[256,2048]{1,0:T(8,128)(2,1)} %collective-permute-done.6, pred[]{:T(512)S(6)} %or.3), kind=kLoop, calls=%fused_computation.2 | loop fusion | flops 524288 | bytes 3145729 | tf_op jit(solution)/shard_map/jit(_where)/select_n | solution.py:419
  62.0 1.3 collective-permute-start.10
  63.3 1.3 %collective-permute-start.11 = (bf16[256,2048]{1,0:T(8,128)(2,1)}, bf16[256,2048]{1,0:T(8,128)(2,1)S(1)}, u32[]{:S(2)}, u32[]{:S(2)}) collective-permute-start(bf16[256,2048]{1,0:T(8,128)(2,1)} %collective-permute-done.7), channel_id=1, source_target_pairs={{4,0},{8,12},{5,1},{9,13},{6,2},{10,14},{7,3},{11,15},{20,16},{24,... | collective-permute-start | bytes 3145736 | tf_op jit(solution)/shard_map/ppermute | solution.py:352
  64.6 2.6 %collective-permute-start.15 = (bf16[256,1024]{1,0:T(8,128)(2,1)S(1)}, bf16[256,1024]{1,0:T(8,128)(2,1)S(1)}, u32[]{:S(2)}, u32[]{:S(2)}) collective-permute-start(bf16[256,1024]{1,0:T(8,128)(2,1)S(1)} %copy-done.2), channel_id=1, source_target_pairs={{4,8},{8,4},{5,9},{9,5},{6,10},{10,6},{7,11},{11,7},{20,24},{24,20... | collective-permute-start | bytes 1572872 | tf_op jit(solution)/shard_map/ppermute | solution.py:352
  67.2 5.7 %shard_map.87 = (bf16[42,128,128]{2,1,0:T(8,128)(2,1)S(1)}, f32[42,128,128]{2,1,0:T(8,128)S(1)}) custom-call(s32[8]{0:T(128)S(1)} %concatenate.15.place_ref, s32[84,3]{1,0:T(8,128)S(1)} %copy.11.table_ref, bf16[256,2048]{1,0:T(8,128)(2,1)} %collective-permute-done.1.refs_0_.refs_2_, bf16[256,2048]{1,0:T(8,128)(2,1)} %collective-permute-done.8.refs_1_.refs_3_, ...), custom_call_target="tpu_custom_call" | custom-call | tf_op jit(solution)/shard_map/pallas_call | solution.py:211
  72.9 1.3 %collective-permute-start.13 = (bf16[256,1024]{1,0:T(8,128)(2,1)S(1)}, bf16[256,1024]{1,0:T(8,128)(2,1)S(1)}, u32[]{:S(2)}, u32[]{:S(2)}) collective-permute-start(bf16[256,1024]{1,0:T(8,128)(2,1)S(1)} %get-tuple-element.72.refs_6_.refs_2_), channel_id=1, source_target_pairs={{0,4},{12,8},{1,5},{13,9},{2,6},{14,10},{3,7},{15,11},{16,20},{28,... | collective-permute-start | bytes 1572872 | tf_op jit(solution)/shard_map/ppermute | solution.py:352
  74.2 2.7 %collective-permute-start.17 = (bf16[256,1024]{1,0:T(8,128)(2,1)}, bf16[256,1024]{1,0:T(8,128)(2,1)S(1)}, u32[]{:S(2)}, u32[]{:S(2)}) collective-permute-start(bf16[256,1024]{1,0:T(8,128)(2,1)} %collective-permute-done.9), channel_id=1, source_target_pairs={{4,8},{8,4},{5,9},{9,5},{6,10},{10,6},{7,11},{11,7},{20,24},{24,20... | collective-permute-start | bytes 1572872 | tf_op jit(solution)/shard_map/ppermute | solution.py:352
  76.9 6.8 %collective-permute-done.10.refs_5_.refs_1_ = bf16[256,2048]{1,0:T(8,128)(2,1)S(1)} collective-permute-done((bf16[256,2048]{1,0:T(8,128)(2,1)S(1)}, bf16[256,2048]{1,0:T(8,128)(2,1)S(1)}, u32[]{:S(2)}, u32[]{:S(2)}) %collective-permute-start.10) | collective-permute-done | bytes 1048608 | tf_op jit(solution)/shard_map/ppermute | solution.py:355
  83.7 0.6 collective-permute-done.11
  84.3 1.3 %broadcast_select_fusion.refs_0_ = bf16[256,2048]{1,0:T(8,128)(2,1)S(1)} fusion(bf16[256,2048]{1,0:T(8,128)(2,1)} %collective-permute-done.2, bf16[256,2048]{1,0:T(8,128)(2,1)S(1)} %collective-permute-done.11, pred[]{:T(512)S(6)} %or.3), kind=kLoop, calls=%fused_computation.1 | loop fusion | flops 524288 | bytes 3145729 | tf_op jit(solution)/shard_map/jit(_where)/select_n | solution.py:431
  85.6 0.7 collective-permute-start.12
  86.3 4.2 %collective-permute-start.16 = (bf16[256,1024]{1,0:T(8,128)(2,1)S(1)}, bf16[256,1024]{1,0:T(8,128)(2,1)S(1)}, u32[]{:S(2)}, u32[]{:S(2)}) collective-permute-start(bf16[256,1024]{1,0:T(8,128)(2,1)S(1)} %collective-permute-done.15.refs_10_.refs_6_), channel_id=1, source_target_pairs={{0,1},{1,0},{2,3},{3,2},{4,5},{5,4},{6,7},{7,6},{8,9},{9,8},{10,11... | collective-permute-start | bytes 1572872 | tf_op jit(solution)/shard_map/ppermute | solution.py:358
  90.6 1.5 %collective-permute-start.18 = (bf16[256,1024]{1,0:T(8,128)(2,1)S(1)}, bf16[256,1024]{1,0:T(8,128)(2,1)S(1)}, u32[]{:S(2)}, u32[]{:S(2)}) collective-permute-start(bf16[256,1024]{1,0:T(8,128)(2,1)S(1)} %collective-permute-done.17.refs_12_.refs_8_), channel_id=1, source_target_pairs={{0,1},{1,0},{2,3},{3,2},{4,5},{5,4},{6,7},{7,6},{8,9},{9,8},{10,11... | collective-permute-start | bytes 1572872 | tf_op jit(solution)/shard_map/ppermute | solution.py:358
  92.1 0.7 collective-permute-done.14.refs_9_.refs_5_
  92.8 0.8 collective-permute-done.18.refs_13_.refs_9_
  93.6 5.8 %shard_map.88 = (bf16[2,256,256]{2,1,0:T(8,128)(2,1)S(1)}, bf16[2,256,256]{2,1,0:T(8,128)(2,1)S(1)}, bf16[2,256,256]{2,1,0:T(8,128)(2,1)S(1)}) custom-call(s32[8]{0:T(128)S(1)} %concatenate.15.place_ref, bf16[256,2048]{1,0:T(8,128)(2,1)S(1)} %pad_maximum_fusion.refs_0_, bf16[256,2048]{1,0:T(8,128)(2,1)} %collective-permute-done.3.refs_1_, ...), custom_call_target="tpu_custom_call" | custom-call | tf_op jit(solution)/shard_map/pallas_call | solution.py:296
  99.4 1.3 %collective-permute-start.19 = (bf16[2,256,256]{2,1,0:T(8,128)(2,1)S(1)}, bf16[2,256,256]{2,1,0:T(8,128)(2,1)S(1)}, u32[]{:S(2)}, u32[]{:S(2)}) collective-permute-start(bf16[2,256,256]{2,1,0:T(8,128)(2,1)S(1)} %get-tuple-element.74), channel_id=1, source_target_pairs={{4,0},{8,12},{5,1},{9,13},{6,2},{10,14},{7,3},{11,15},{20,16},{24,... | collective-permute-start | bytes 786440 | tf_op jit(solution)/shard_map/ppermute | solution.py:352
  100.7 2.7 %collective-permute-start.20 = (bf16[2,256,256]{2,1,0:T(8,128)(2,1)S(1)}, bf16[2,256,256]{2,1,0:T(8,128)(2,1)S(1)}, u32[]{:S(2)}, u32[]{:S(2)}) collective-permute-start(bf16[2,256,256]{2,1,0:T(8,128)(2,1)S(1)} %get-tuple-element.75), channel_id=1, source_target_pairs={{4,8},{8,4},{5,9},{9,5},{6,10},{10,6},{7,11},{11,7},{20,24},{24,20... | collective-permute-start | bytes 786440 | tf_op jit(solution)/shard_map/ppermute | solution.py:352
  103.4 4.3 %shard_map.89 = (bf16[42,128,128]{2,1,0:T(8,128)(2,1)S(1)}, f32[42,128,128]{2,1,0:T(8,128)S(1)}) custom-call(s32[8]{0:T(128)S(1)} %concatenate.15.place_ref, s32[84,3]{1,0:T(8,128)S(1)} %copy.11.table_ref, bf16[256,2048]{1,0:T(8,128)(2,1)S(1)} %broadcast_select_fusion.1.refs_4_.refs_0_, bf16[256,2048]{1,0:T(8,128)(2,1)S(1)} %collective-permute-done.10.refs_5_.refs_1_, ...), custom_call_target="tpu_custom_call" | custom-call | tf_op jit(solution)/shard_map/pallas_call | solution.py:211
  107.8 2.3 %collective-permute-done.20 = bf16[2,256,256]{2,1,0:T(8,128)(2,1)S(1)} collective-permute-done((bf16[2,256,256]{2,1,0:T(8,128)(2,1)S(1)}, bf16[2,256,256]{2,1,0:T(8,128)(2,1)S(1)}, u32[]{:S(2)}, u32[]{:S(2)}) %collective-permute-start.20) | collective-permute-done | bytes 262176 | tf_op jit(solution)/shard_map/ppermute | solution.py:352
  110.1 1.2 collective-permute-start.25
  111.8 2.0 %shard_map.90 = bf16[2,256,256]{2,1,0:T(8,128)(2,1)S(1)} custom-call(s32[8]{0:T(128)S(1)} %concatenate.15.place_ref, bf16[256,2048]{1,0:T(8,128)(2,1)S(1)} %broadcast_select_fusion.refs_0_, bf16[256,2048]{1,0:T(8,128)(2,1)S(1)} %collective-permute-done.12.refs_1_.refs_2_, bf16[256,1024]{1,0:T(8,128)(2,1)S(1)} %get-tuple-element.72.refs_6_.refs_2_, ...), custom_call_target="tpu_custom_call" | custom-call | tf_op jit(solution)/shard_map/pallas_call | solution.py:296
  113.9 1.3 %collective-permute-start.21 = (bf16[2,256,256]{2,1,0:T(8,128)(2,1)S(1)}, bf16[2,256,256]{2,1,0:T(8,128)(2,1)S(1)}, u32[]{:S(2)}, u32[]{:S(2)}) collective-permute-start(bf16[2,256,256]{2,1,0:T(8,128)(2,1)S(1)} %collective-permute-done.20), channel_id=1, source_target_pairs={{4,0},{8,12},{5,1},{9,13},{6,2},{10,14},{7,3},{11,15},{20,16},{24,... | collective-permute-start | bytes 786440 | tf_op jit(solution)/shard_map/ppermute | solution.py:352
  115.2 2.5 %collective-permute-start.22 = (bf16[2,256,256]{2,1,0:T(8,128)(2,1)S(1)}, bf16[2,256,256]{2,1,0:T(8,128)(2,1)S(1)}, u32[]{:S(2)}, u32[]{:S(2)}) collective-permute-start(bf16[2,256,256]{2,1,0:T(8,128)(2,1)S(1)} %shard_map.90), channel_id=1, source_target_pairs={{4,8},{8,4},{5,9},{9,5},{6,10},{10,6},{7,11},{11,7},{20,24},{24,20... | collective-permute-start | bytes 786440 | tf_op jit(solution)/shard_map/ppermute | solution.py:352
  118.3 6.1 %shard_map.91 = f32[42,128,128]{2,1,0:T(8,128)} custom-call(s32[8]{0:T(128)S(1)} %concatenate.15.place_ref, s32[84,3]{1,0:T(8,128)S(1)} %copy.11.table_ref, bf16[256,2048]{1,0:T(8,128)(2,1)S(1)} %broadcast_select_fusion.refs_0_, bf16[256,2048]{1,0:T(8,128)(2,1)S(1)} %collective-permute-done.23.refs_1_, ...), custom_call_target="tpu_custom_call" | custom-call | tf_op jit(solution)/shard_map/pallas_call | solution.py:211
  124.7 1.2 collective-permute-start.27
  125.9 1.0 collective-permute-done.27.refs_5_
  126.9 1.6 %shard_map.92 = f32[512,512]{1,0:T(8,128)} custom-call(s32[8]{0:T(128)S(1)} %concatenate.15.place_ref, bf16[2,256,256]{2,1,0:T(8,128)(2,1)S(1)} %get-tuple-element.79.refs_0_, bf16[2,256,256]{2,1,0:T(8,128)(2,1)S(1)} %collective-permute-done.22.refs_1_, bf16[2,256,256]{2,1,0:T(8,128)(2,1)S(1)} %collective-permute-done.19.refs_2_, ...), custom_call_target="tpu_custom_call" | custom-call | tf_op jit(solution)/shard_map/pallas_call | solution.py:328
  (42 shorter events, 2.1 us)
Async XLA Ops:
  0.6 1.2 copy-start
  1.9 2.3 %collective-permute-start = (bf16[256,1024]{1,0:T(8,128)(2,1)S(1)}, bf16[256,1024]{1,0:T(8,128)(2,1)S(1)}, u32[]{:S(2)}, u32[]{:S(2)}) collective-permute-start(bf16[256,1024]{1,0:T(8,128)(2,1)S(1)} %constant_dynamic-slice_fusion.4), channel_id=1, source_target_pairs={{0,1},{1,0},{2,3},{3,2},{4,5},{5,4},{6,7},{7,6},{8,9},{9,8},{10,11... | collective-permute-start | bytes 1572872 | tf_op jit(solution)/shard_map/ppermute | solution.py:358
  2.7 10.7 %copy-start.5 = (s32[1,168,2]{1,2,0:T(2,128)S(1)}, s32[1,168,2]{1,2,0:T(2,128)}, u32[]{:S(2)}) copy-start(s32[1,168,2]{1,2,0:T(2,128)} %param.10) | copy-start | bytes 4036
  2.7 37.6 %copy-start.3 = (s32[4]{0:T(128)S(1)}, s32[4]{0:T(128)}, u32[]{:S(2)}) copy-start(s32[4]{0:T(128)} %constant.71.clone) | copy-start | bytes 52
  2.7 37.6 %copy-start.4 = (s32[4]{0:T(128)S(1)}, s32[4]{0:T(128)}, u32[]{:S(2)}) copy-start(s32[4]{0:T(128)} %constant.72.clone) | copy-start | bytes 52
  4.3 24.5 %collective-permute-start.1 = (bf16[256,2048]{1,0:T(8,128)(2,1)S(1)}, bf16[256,2048]{1,0:T(8,128)(2,1)}, u32[]{:S(2)}, u32[]{:S(2)}) collective-permute-start(bf16[256,2048]{1,0:T(8,128)(2,1)S(1)} %pad_maximum_fusion.refs_0_), channel_id=1, source_target_pairs={{0,4},{4,0},{8,12},{12,8},{1,5},{5,1},{9,13},{13,9},{2,6},{6,2},{1... | collective-permute-start | bytes 3145736 | tf_op jit(solution)/shard_map/ppermute | solution.py:352
  4.3 27.5 %collective-permute-start.2 = (bf16[256,2048]{1,0:T(8,128)(2,1)S(1)}, bf16[256,2048]{1,0:T(8,128)(2,1)}, u32[]{:S(2)}, u32[]{:S(2)}) collective-permute-start(bf16[256,2048]{1,0:T(8,128)(2,1)S(1)} %pad_maximum_fusion.refs_0_), channel_id=1, source_target_pairs={{4,8},{8,4},{5,9},{9,5},{6,10},{10,6},{7,11},{11,7},{20,24},{24,20... | collective-permute-start | bytes 3145736 | tf_op jit(solution)/shard_map/ppermute | solution.py:352
  8.8 23.9 %collective-permute-start.3 = (bf16[256,2048]{1,0:T(8,128)(2,1)S(1)}, bf16[256,2048]{1,0:T(8,128)(2,1)}, u32[]{:S(2)}, u32[]{:S(2)}) collective-permute-start(bf16[256,2048]{1,0:T(8,128)(2,1)S(1)} %pad_maximum_fusion.refs_0_), channel_id=1, source_target_pairs={{0,2},{2,0},{1,3},{3,1},{4,6},{6,4},{5,7},{7,5},{8,10},{10,8},{9,1... | collective-permute-start | bytes 3145736 | tf_op jit(solution)/shard_map/ppermute | solution.py:355
  12.2 2.9 %collective-permute-start.5 = (bf16[256,1024]{1,0:T(8,128)(2,1)S(1)}, bf16[256,1024]{1,0:T(8,128)(2,1)S(1)}, u32[]{:S(2)}, u32[]{:S(2)}) collective-permute-start(bf16[256,1024]{1,0:T(8,128)(2,1)S(1)} %get-tuple-element.72.refs_6_.refs_2_), channel_id=1, source_target_pairs={{0,1},{1,0},{2,3},{3,2},{4,5},{5,4},{6,7},{7,6},{8,9},{9,8},{10,11... | collective-permute-start | bytes 1572872 | tf_op jit(solution)/shard_map/ppermute | solution.py:358
  13.5 1.5 %collective-permute-start.4 = (s32[42,2]{0,1:T(2,128)S(1)}, s32[42,2]{0,1:T(2,128)S(1)}, u32[]{:S(2)}, u32[]{:S(2)}) collective-permute-start(s32[42,2]{0,1:T(2,128)S(1)} %fusion.1), channel_id=1, source_target_pairs={{0,1},{1,0},{2,3},{3,2},{4,5},{5,4},{6,7},{7,6},{8,9},{9,8},{10,11... | collective-permute-start | bytes 1016 | tf_op jit(solution)/shard_map/ppermute | solution.py:358
  32.7 22.5 %collective-permute-start.6 = (bf16[256,2048]{1,0:T(8,128)(2,1)}, bf16[256,2048]{1,0:T(8,128)(2,1)}, u32[]{:S(2)}, u32[]{:S(2)}) collective-permute-start(bf16[256,2048]{1,0:T(8,128)(2,1)} %collective-permute-done.2), channel_id=1, source_target_pairs={{4,0},{8,12},{5,1},{9,13},{6,2},{10,14},{7,3},{11,15},{20,16},{24,... | collective-permute-start | bytes 3145736 | tf_op jit(solution)/shard_map/ppermute | solution.py:352
  35.0 25.0 %collective-permute-start.7 = (bf16[256,2048]{1,0:T(8,128)(2,1)}, bf16[256,2048]{1,0:T(8,128)(2,1)}, u32[]{:S(2)}, u32[]{:S(2)}) collective-permute-start(bf16[256,2048]{1,0:T(8,128)(2,1)} %collective-permute-done.1.refs_0_.refs_2_), channel_id=1, source_target_pairs={{4,8},{8,4},{5,9},{9,5},{6,10},{10,6},{7,11},{11,7},{20,24},{24,20... | collective-permute-start | bytes 3145736 | tf_op jit(solution)/shard_map/ppermute | solution.py:352
  37.7 22.9 %collective-permute-start.8 = (bf16[256,2048]{1,0:T(8,128)(2,1)}, bf16[256,2048]{1,0:T(8,128)(2,1)}, u32[]{:S(2)}, u32[]{:S(2)}) collective-permute-start(bf16[256,2048]{1,0:T(8,128)(2,1)} %collective-permute-done.1.refs_0_.refs_2_), channel_id=1, source_target_pairs={{0,2},{2,0},{1,3},{3,1},{4,6},{6,4},{5,7},{7,5},{8,10},{10,8},{9,1... | collective-permute-start | bytes 3145736 | tf_op jit(solution)/shard_map/ppermute | solution.py:355
  39.0 13.3 %collective-permute-start.9 = (bf16[256,1024]{1,0:T(8,128)(2,1)}, bf16[256,1024]{1,0:T(8,128)(2,1)}, u32[]{:S(2)}, u32[]{:S(2)}) collective-permute-start(bf16[256,1024]{1,0:T(8,128)(2,1)} %get-tuple-element.50), channel_id=1, source_target_pairs={{0,4},{12,8},{1,5},{13,9},{2,6},{14,10},{3,7},{15,11},{16,20},{28,... | collective-permute-start | bytes 1572872 | tf_op jit(solution)/shard_map/ppermute | solution.py:352
  45.6 19.0 %copy-start.2 = (bf16[256,1024]{1,0:T(8,128)(2,1)S(1)}, bf16[256,1024]{1,0:T(8,128)(2,1)}, u32[]{:S(2)}) copy-start(bf16[256,1024]{1,0:T(8,128)(2,1)} %get-tuple-element.50) | copy-start | bytes 1572868
  62.0 21.7 %collective-permute-start.10 = (bf16[256,2048]{1,0:T(8,128)(2,1)S(1)}, bf16[256,2048]{1,0:T(8,128)(2,1)S(1)}, u32[]{:S(2)}, u32[]{:S(2)}) collective-permute-start(bf16[256,2048]{1,0:T(8,128)(2,1)S(1)} %broadcast_select_fusion.1.refs_4_.refs_0_), channel_id=1, source_target_pairs={{0,2},{2,0},{1,3},{3,1},{4,6},{6,4},{5,7},{7,5},{8,10},{10,8},{9,1... | collective-permute-start | bytes 3145736 | tf_op jit(solution)/shard_map/ppermute | solution.py:355
  63.3 21.0 %collective-permute-start.11 = (bf16[256,2048]{1,0:T(8,128)(2,1)}, bf16[256,2048]{1,0:T(8,128)(2,1)S(1)}, u32[]{:S(2)}, u32[]{:S(2)}) collective-permute-start(bf16[256,2048]{1,0:T(8,128)(2,1)} %collective-permute-done.7), channel_id=1, source_target_pairs={{4,0},{8,12},{5,1},{9,13},{6,2},{10,14},{7,3},{11,15},{20,16},{24,... | collective-permute-start | bytes 3145736 | tf_op jit(solution)/shard_map/ppermute | solution.py:352
  64.6 21.7 %collective-permute-start.15 = (bf16[256,1024]{1,0:T(8,128)(2,1)S(1)}, bf16[256,1024]{1,0:T(8,128)(2,1)S(1)}, u32[]{:S(2)}, u32[]{:S(2)}) collective-permute-start(bf16[256,1024]{1,0:T(8,128)(2,1)S(1)} %copy-done.2), channel_id=1, source_target_pairs={{4,8},{8,4},{5,9},{9,5},{6,10},{10,6},{7,11},{11,7},{20,24},{24,20... | collective-permute-start | bytes 1572872 | tf_op jit(solution)/shard_map/ppermute | solution.py:352
  72.9 17.7 %collective-permute-start.13 = (bf16[256,1024]{1,0:T(8,128)(2,1)S(1)}, bf16[256,1024]{1,0:T(8,128)(2,1)S(1)}, u32[]{:S(2)}, u32[]{:S(2)}) collective-permute-start(bf16[256,1024]{1,0:T(8,128)(2,1)S(1)} %get-tuple-element.72.refs_6_.refs_2_), channel_id=1, source_target_pairs={{0,4},{12,8},{1,5},{13,9},{2,6},{14,10},{3,7},{15,11},{16,20},{28,... | collective-permute-start | bytes 1572872 | tf_op jit(solution)/shard_map/ppermute | solution.py:352
  74.2 16.4 %collective-permute-start.17 = (bf16[256,1024]{1,0:T(8,128)(2,1)}, bf16[256,1024]{1,0:T(8,128)(2,1)S(1)}, u32[]{:S(2)}, u32[]{:S(2)}) collective-permute-start(bf16[256,1024]{1,0:T(8,128)(2,1)} %collective-permute-done.9), channel_id=1, source_target_pairs={{4,8},{8,4},{5,9},{9,5},{6,10},{10,6},{7,11},{11,7},{20,24},{24,20... | collective-permute-start | bytes 1572872 | tf_op jit(solution)/shard_map/ppermute | solution.py:352
  85.6 24.5 %collective-permute-start.12 = (bf16[256,2048]{1,0:T(8,128)(2,1)S(1)}, bf16[256,2048]{1,0:T(8,128)(2,1)S(1)}, u32[]{:S(2)}, u32[]{:S(2)}) collective-permute-start(bf16[256,2048]{1,0:T(8,128)(2,1)S(1)} %broadcast_select_fusion.refs_0_), channel_id=1, source_target_pairs={{0,2},{2,0},{1,3},{3,1},{4,6},{6,4},{5,7},{7,5},{8,10},{10,8},{9,1... | collective-permute-start | bytes 3145736 | tf_op jit(solution)/shard_map/ppermute | solution.py:355
  86.3 5.8 %collective-permute-start.16 = (bf16[256,1024]{1,0:T(8,128)(2,1)S(1)}, bf16[256,1024]{1,0:T(8,128)(2,1)S(1)}, u32[]{:S(2)}, u32[]{:S(2)}) collective-permute-start(bf16[256,1024]{1,0:T(8,128)(2,1)S(1)} %collective-permute-done.15.refs_10_.refs_6_), channel_id=1, source_target_pairs={{0,1},{1,0},{2,3},{3,2},{4,5},{5,4},{6,7},{7,6},{8,9},{9,8},{10,11... | collective-permute-start | bytes 1572872 | tf_op jit(solution)/shard_map/ppermute | solution.py:358
  90.5 2.3 %collective-permute-start.14 = (bf16[256,1024]{1,0:T(8,128)(2,1)S(1)}, bf16[256,1024]{1,0:T(8,128)(2,1)S(1)}, u32[]{:S(2)}, u32[]{:S(2)}) collective-permute-start(bf16[256,1024]{1,0:T(8,128)(2,1)S(1)} %collective-permute-done.13.refs_8_.refs_4_), channel_id=1, source_target_pairs={{0,1},{1,0},{2,3},{3,2},{4,5},{5,4},{6,7},{7,6},{8,9},{9,8},{10,11... | collective-permute-start | bytes 1572872 | tf_op jit(solution)/shard_map/ppermute | solution.py:358
  90.6 3.0 %collective-permute-start.18 = (bf16[256,1024]{1,0:T(8,128)(2,1)S(1)}, bf16[256,1024]{1,0:T(8,128)(2,1)S(1)}, u32[]{:S(2)}, u32[]{:S(2)}) collective-permute-start(bf16[256,1024]{1,0:T(8,128)(2,1)S(1)} %collective-permute-done.17.refs_12_.refs_8_), channel_id=1, source_target_pairs={{0,1},{1,0},{2,3},{3,2},{4,5},{5,4},{6,7},{7,6},{8,9},{9,8},{10,11... | collective-permute-start | bytes 1572872 | tf_op jit(solution)/shard_map/ppermute | solution.py:358
  99.4 8.3 %collective-permute-start.19 = (bf16[2,256,256]{2,1,0:T(8,128)(2,1)S(1)}, bf16[2,256,256]{2,1,0:T(8,128)(2,1)S(1)}, u32[]{:S(2)}, u32[]{:S(2)}) collective-permute-start(bf16[2,256,256]{2,1,0:T(8,128)(2,1)S(1)} %get-tuple-element.74), channel_id=1, source_target_pairs={{4,0},{8,12},{5,1},{9,13},{6,2},{10,14},{7,3},{11,15},{20,16},{24,... | collective-permute-start | bytes 786440 | tf_op jit(solution)/shard_map/ppermute | solution.py:352
  100.7 9.4 %collective-permute-start.20 = (bf16[2,256,256]{2,1,0:T(8,128)(2,1)S(1)}, bf16[2,256,256]{2,1,0:T(8,128)(2,1)S(1)}, u32[]{:S(2)}, u32[]{:S(2)}) collective-permute-start(bf16[2,256,256]{2,1,0:T(8,128)(2,1)S(1)} %get-tuple-element.75), channel_id=1, source_target_pairs={{4,8},{8,4},{5,9},{9,5},{6,10},{10,6},{7,11},{11,7},{20,24},{24,20... | collective-permute-start | bytes 786440 | tf_op jit(solution)/shard_map/ppermute | solution.py:352
  110.1 8.2 %collective-permute-start.25 = (bf16[42,128,128]{2,1,0:T(8,128)(2,1)S(1)}, bf16[42,128,128]{2,1,0:T(8,128)(2,1)S(1)}, u32[]{:S(2)}, u32[]{:S(2)}) collective-permute-start(bf16[42,128,128]{2,1,0:T(8,128)(2,1)S(1)} %get-tuple-element.86), channel_id=1, source_target_pairs={{0,1},{1,0},{2,3},{3,2},{4,5},{5,4},{6,7},{7,6},{8,9},{9,8},{10,11... | collective-permute-start | bytes 4128776 | tf_op jit(solution)/shard_map/ppermute | solution.py:358
  111.3 6.4 %collective-permute-start.23 = (bf16[256,2048]{1,0:T(8,128)(2,1)S(1)}, bf16[256,2048]{1,0:T(8,128)(2,1)S(1)}, u32[]{:S(2)}, u32[]{:S(2)}) collective-permute-start(bf16[256,2048]{1,0:T(8,128)(2,1)S(1)} %broadcast_select_fusion.refs_0_), channel_id=1, source_target_pairs={{0,1},{1,0},{2,3},{3,2},{4,5},{5,4},{6,7},{7,6},{8,9},{9,8},{10,11... | collective-permute-start | bytes 3145736 | tf_op jit(solution)/shard_map/ppermute | solution.py:358
  111.3 7.0 %collective-permute-start.24 = (bf16[256,2048]{1,0:T(8,128)(2,1)S(1)}, bf16[256,2048]{1,0:T(8,128)(2,1)S(1)}, u32[]{:S(2)}, u32[]{:S(2)}) collective-permute-start(bf16[256,2048]{1,0:T(8,128)(2,1)S(1)} %collective-permute-done.12.refs_1_.refs_2_), channel_id=1, source_target_pairs={{0,1},{1,0},{2,3},{3,2},{4,5},{5,4},{6,7},{7,6},{8,9},{9,8},{10,11... | collective-permute-start | bytes 3145736 | tf_op jit(solution)/shard_map/ppermute | solution.py:358
  113.8 13.0 %copy-start.1 = (f32[512]{0:T(512)S(1)}, f32[512]{0:T(512)}, u32[]{:S(2)}) copy-start(f32[512]{0:T(512)} %param.9) | copy-start | bytes 6148
  113.9 10.6 %collective-permute-start.21 = (bf16[2,256,256]{2,1,0:T(8,128)(2,1)S(1)}, bf16[2,256,256]{2,1,0:T(8,128)(2,1)S(1)}, u32[]{:S(2)}, u32[]{:S(2)}) collective-permute-start(bf16[2,256,256]{2,1,0:T(8,128)(2,1)S(1)} %collective-permute-done.20), channel_id=1, source_target_pairs={{4,0},{8,12},{5,1},{9,13},{6,2},{10,14},{7,3},{11,15},{20,16},{24,... | collective-permute-start | bytes 786440 | tf_op jit(solution)/shard_map/ppermute | solution.py:352
  115.2 9.5 %collective-permute-start.22 = (bf16[2,256,256]{2,1,0:T(8,128)(2,1)S(1)}, bf16[2,256,256]{2,1,0:T(8,128)(2,1)S(1)}, u32[]{:S(2)}, u32[]{:S(2)}) collective-permute-start(bf16[2,256,256]{2,1,0:T(8,128)(2,1)S(1)} %shard_map.90), channel_id=1, source_target_pairs={{4,8},{8,4},{5,9},{9,5},{6,10},{10,6},{7,11},{11,7},{20,24},{24,20... | collective-permute-start | bytes 786440 | tf_op jit(solution)/shard_map/ppermute | solution.py:352
  117.7 8.1 %collective-permute-start.26 = (bf16[256,256]{1,0:T(8,128)(2,1)S(1)}, bf16[256,256]{1,0:T(8,128)(2,1)S(1)}, u32[]{:S(2)}, u32[]{:S(2)}) collective-permute-start(bf16[256,256]{1,0:T(8,128)(2,1)S(1)} %fusion), channel_id=1, source_target_pairs={{0,1},{1,0},{2,3},{3,2},{4,5},{5,4},{6,7},{7,6},{8,9},{9,8},{10,11... | collective-permute-start | bytes 393224 | tf_op jit(solution)/shard_map/ppermute | solution.py:358
  124.7 2.2 %collective-permute-start.27 = (bf16[256,256]{1,0:T(8,128)(2,1)S(1)}, bf16[256,256]{1,0:T(8,128)(2,1)S(1)}, u32[]{:S(2)}, u32[]{:S(2)}) collective-permute-start(bf16[256,256]{1,0:T(8,128)(2,1)S(1)} %select_bitcast_fusion), channel_id=1, source_target_pairs={{0,1},{1,0},{2,3},{3,2},{4,5},{5,4},{6,7},{7,6},{8,9},{9,8},{10,11... | collective-permute-start | bytes 393224 | tf_op jit(solution)/shard_map/ppermute | solution.py:358

commit v9 on v7

--- a/solution.py
+++ b/solution.py
@@ -309,7 +309,7 @@
 
     def kernel(place_ref, *refs):
         late, core = place_ref[5], place_ref[6]
-        weight, out = refs[6], refs[7]
+        weight, result, out, sems = refs[6], refs[7], refs[8], refs[9]
 
         def put(i, block, own_rows):
             row = late if i == 0 else 1 - late
@@ -318,10 +318,17 @@
             down = pl.ds(pl.multiple_of(row * group, group), group)
             out[down, across] = block.astype(jnp.float32) * weight[:, across]
 
+        copies = []
         for i in range(2):
             pl.when(place_ref[0] == 1)(lambda i=i: put(i, refs[i][0], True))
             pl.when(place_ref[0] == 0)(lambda i=i: put(i, refs[2 + i][0], True))
             put(i, refs[4 + i][...], False)
+            row = late if i == 0 else 1 - late
+            down = pl.ds(pl.multiple_of(row * group, group), group)
+            copies.append(pltpu.make_async_copy(out.at[down], result.at[down], sems.at[i]))
+            copies[i].start()
+        for copy in copies:
+            copy.wait()
 
     smem = pl.BlockSpec(memory_space=pltpu.SMEM)
     vmem = pl.BlockSpec(memory_space=pltpu.VMEM)
@@ -329,7 +336,11 @@
         kernel,
         out_shape=jax.ShapeDtypeStruct((2 * group, 2 * count), jnp.float32),
         in_specs=[smem] + [vmem] * 7,
-        out_specs=vmem,
+        out_specs=pl.BlockSpec(memory_space=pltpu.HBM),
+        scratch_shapes=[
+            pltpu.VMEM((2 * group, 2 * count), jnp.float32),
+            pltpu.SemaphoreType.DMA((2,)),
+        ],
         compiler_params=pltpu.CompilerParams(vmem_limit_bytes=8 * 2**20),
         cost_estimate=pl.CostEstimate(flops=0, bytes_accessed=0, transcendentals=0),
     )(place, *on_middle, *on_ends, *swapped, weights)

time: 129 us -> 129 us (level)
  transfers between devices with their start and end apart: 28 -> 28, of which waited for: 16 -> 16; matrix products, arithmetic and copies ran while one was open for 3% -> 3% of each run, Pallas kernels for 23% -> 22%
where the time goes in v9:
time: 129 us
  waiting for transfers between devices  48.2 us (37%)
  starting transfers between devices  42.3 us (33%)
  Pallas kernels  30.5 us (24%)
  local copies, waits for them, and re-layouts  3.64 us (3%)
  other arithmetic  2.89 us (2%)
    ppermute x13, waiting for transfers between devices, move(): return lax.ppermute(value, 'ex', pairs)  34.4 us
    ppermute x13, starting transfers between devices, move(): return lax.ppermute(value, 'ex', pairs)  26.6 us
    pallas_call x4, Pallas kernels, tile_call(): pl.pallas_call(kernel, out_shape=outs + (scores.out_shape if scores else...  21.1 us
    ppermute x11, starting transfers between devices, swap(): return lax.ppermute(value, 'feat', CORE)  11.2 us
    ppermute x4, waiting for transfers between devices, across(): return lax.ppermute(value, 'feat', ACROSS)  8.3 us
    pallas_call x2, Pallas kernels, score_call(): pl.pallas_call(kernel, out_shape=scores.out_shape, in_specs=[smem] + [hbm...  7.75 us
    ppermute x11, waiting for transfers between devices, swap(): return lax.ppermute(value, 'feat', CORE)  5.44 us
    ppermute x4, starting transfers between devices, across(): return lax.ppermute(value, 'feat', ACROSS)  4.52 us
  transfers between devices with their start and end apart: 28, of which 16 were waited for; matrix products, arithmetic and copies ran while one was open for 3% of the time, Pallas kernels for 22%

profile of v9, /device:TPU:9, one launch (start us, length us, event | category | flops | bytes accessed | tf_op | source)
XLA Modules:
  0.0 128.6 jit_solution(8240231450968332387)
XLA Ops:
  0.7 1.2 copy-done
  1.9 0.7 collective-permute-start
  2.7 1.5 %collective-permute-done = bf16[256,1024]{1,0:T(8,128)(2,1)S(1)} collective-permute-done((bf16[256,1024]{1,0:T(8,128)(2,1)S(1)}, bf16[256,1024]{1,0:T(8,128)(2,1)S(1)}, u32[]{:S(2)}, u32[]{:S(2)}) %collective-permute-start) | collective-permute-done | bytes 524320 | tf_op jit(solution)/shard_map/ppermute | solution.py:369
  4.3 4.5 %collective-permute-start.2 = (bf16[256,2048]{1,0:T(8,128)(2,1)S(1)}, bf16[256,2048]{1,0:T(8,128)(2,1)}, u32[]{:S(2)}, u32[]{:S(2)}) collective-permute-start(bf16[256,2048]{1,0:T(8,128)(2,1)S(1)} %pad_maximum_fusion.refs_0_), channel_id=1, source_target_pairs={{4,8},{8,4},{5,9},{9,5},{6,10},{10,6},{7,11},{11,7},{20,24},{24,20... | collective-permute-start | bytes 3145736 | tf_op jit(solution)/shard_map/ppermute | solution.py:363
  8.8 1.3 collective-permute-start.3
  10.1 2.1 %constant_dynamic-slice_fusion.1 = (bf16[256,1024]{1,0:T(8,128)(2,1)}, bf16[256,1024]{1,0:T(8,128)(2,1)S(1)}) fusion(bf16[512,1024]{1,0:T(8,128)(2,1)} %param.8, s32[]{:T(128)S(6)} %select_n.73, s32[]{:T(128)S(6)} %mul.21), kind=kLoop, calls=%fused_computation.11 | loop fusion | bytes 2097160 | tf_op jit(solution)/shard_map/dynamic_slice | solution.py:414
  12.2 1.2 collective-permute-start.5
  13.5 1.4 %collective-permute-done.4 = s32[42,2]{0,1:T(2,128)S(1)} collective-permute-done((s32[42,2]{0,1:T(2,128)S(1)}, s32[42,2]{0,1:T(2,128)S(1)}, u32[]{:S(2)}, u32[]{:S(2)}) %collective-permute-start.4) | collective-permute-done | bytes 368 | tf_op jit(solution)/shard_map/ppermute | solution.py:369
  15.0 13.8 %collective-permute-done.1.refs_0_.refs_2_ = bf16[256,2048]{1,0:T(8,128)(2,1)} collective-permute-done((bf16[256,2048]{1,0:T(8,128)(2,1)S(1)}, bf16[256,2048]{1,0:T(8,128)(2,1)}, u32[]{:S(2)}, u32[]{:S(2)}) %collective-permute-start.1) | collective-permute-done | bytes 1048608 | tf_op jit(solution)/shard_map/ppermute | solution.py:363
  28.8 3.0 %collective-permute-done.2 = bf16[256,2048]{1,0:T(8,128)(2,1)} collective-permute-done((bf16[256,2048]{1,0:T(8,128)(2,1)S(1)}, bf16[256,2048]{1,0:T(8,128)(2,1)}, u32[]{:S(2)}, u32[]{:S(2)}) %collective-permute-start.2) | collective-permute-done | bytes 1048608 | tf_op jit(solution)/shard_map/ppermute | solution.py:363
  31.8 0.9 collective-permute-done.3.refs_1_
  32.7 2.3 %collective-permute-start.6 = (bf16[256,2048]{1,0:T(8,128)(2,1)}, bf16[256,2048]{1,0:T(8,128)(2,1)}, u32[]{:S(2)}, u32[]{:S(2)}) collective-permute-start(bf16[256,2048]{1,0:T(8,128)(2,1)} %collective-permute-done.2), channel_id=1, source_target_pairs={{4,0},{8,12},{5,1},{9,13},{6,2},{10,14},{7,3},{11,15},{20,16},{24,... | collective-permute-start | bytes 3145736 | tf_op jit(solution)/shard_map/ppermute | solution.py:363
  35.0 2.7 %collective-permute-start.7 = (bf16[256,2048]{1,0:T(8,128)(2,1)}, bf16[256,2048]{1,0:T(8,128)(2,1)}, u32[]{:S(2)}, u32[]{:S(2)}) collective-permute-start(bf16[256,2048]{1,0:T(8,128)(2,1)} %collective-permute-done.1.refs_0_.refs_2_), channel_id=1, source_target_pairs={{4,8},{8,4},{5,9},{9,5},{6,10},{10,6},{7,11},{11,7},{20,24},{24,20... | collective-permute-start | bytes 3145736 | tf_op jit(solution)/shard_map/ppermute | solution.py:363
  37.7 1.3 collective-permute-start.8
  39.0 1.3 collective-permute-start.9
  40.5 5.1 %shard_map.86 = (bf16[42,128,128]{2,1,0:T(8,128)(2,1)S(1)}, f32[42,128,128]{2,1,0:T(8,128)S(1)}) custom-call(s32[8]{0:T(128)S(1)} %concatenate.15.place_ref, s32[84,3]{1,0:T(8,128)S(1)} %copy.11.table_ref, bf16[256,2048]{1,0:T(8,128)(2,1)S(1)} %pad_maximum_fusion.refs_0_, bf16[256,2048]{1,0:T(8,128)(2,1)} %collective-permute-done.3.refs_1_), custom_call_target="tpu_custom_call" | custom-call | tf_op jit(solution)/shard_map/pallas_call | solution.py:211
  45.6 6.6 %collective-permute-done.9 = bf16[256,1024]{1,0:T(8,128)(2,1)} collective-permute-done((bf16[256,1024]{1,0:T(8,128)(2,1)}, bf16[256,1024]{1,0:T(8,128)(2,1)}, u32[]{:S(2)}, u32[]{:S(2)}) %collective-permute-start.9) | collective-permute-done | bytes 524320 | tf_op jit(solution)/shard_map/ppermute | solution.py:363
  52.2 3.0 %collective-permute-done.6 = bf16[256,2048]{1,0:T(8,128)(2,1)} collective-permute-done((bf16[256,2048]{1,0:T(8,128)(2,1)}, bf16[256,2048]{1,0:T(8,128)(2,1)}, u32[]{:S(2)}, u32[]{:S(2)}) %collective-permute-start.6) | collective-permute-done | bytes 1048608 | tf_op jit(solution)/shard_map/ppermute | solution.py:363
  55.2 4.8 %collective-permute-done.7 = bf16[256,2048]{1,0:T(8,128)(2,1)} collective-permute-done((bf16[256,2048]{1,0:T(8,128)(2,1)}, bf16[256,2048]{1,0:T(8,128)(2,1)}, u32[]{:S(2)}, u32[]{:S(2)}) %collective-permute-start.7) | collective-permute-done | bytes 1048608 | tf_op jit(solution)/shard_map/ppermute | solution.py:363
  60.0 0.6 collective-permute-done.8.refs_1_.refs_3_
  60.6 1.3 %broadcast_select_fusion.1.refs_4_.refs_0_ = bf16[256,2048]{1,0:T(8,128)(2,1)S(1)} fusion(bf16[256,2048]{1,0:T(8,128)(2,1)} %collective-permute-done.7, bf16[256,2048]{1,0:T(8,128)(2,1)} %collective-permute-done.6, pred[]{:T(512)S(6)} %or.3), kind=kLoop, calls=%fused_computation.2 | loop fusion | flops 524288 | bytes 3145729 | tf_op jit(solution)/shard_map/jit(_where)/select_n | solution.py:430
  62.0 1.3 collective-permute-start.10
  63.3 1.3 %collective-permute-start.11 = (bf16[256,2048]{1,0:T(8,128)(2,1)}, bf16[256,2048]{1,0:T(8,128)(2,1)S(1)}, u32[]{:S(2)}, u32[]{:S(2)}) collective-permute-start(bf16[256,2048]{1,0:T(8,128)(2,1)} %collective-permute-done.7), channel_id=1, source_target_pairs={{4,0},{8,12},{5,1},{9,13},{6,2},{10,14},{7,3},{11,15},{20,16},{24,... | collective-permute-start | bytes 3145736 | tf_op jit(solution)/shard_map/ppermute | solution.py:363
  64.6 2.6 %collective-permute-start.15 = (bf16[256,1024]{1,0:T(8,128)(2,1)S(1)}, bf16[256,1024]{1,0:T(8,128)(2,1)S(1)}, u32[]{:S(2)}, u32[]{:S(2)}) collective-permute-start(bf16[256,1024]{1,0:T(8,128)(2,1)S(1)} %copy-done.2), channel_id=1, source_target_pairs={{4,8},{8,4},{5,9},{9,5},{6,10},{10,6},{7,11},{11,7},{20,24},{24,20... | collective-permute-start | bytes 1572872 | tf_op jit(solution)/shard_map/ppermute | solution.py:363
  67.2 1.3 %collective-permute-start.13 = (bf16[256,1024]{1,0:T(8,128)(2,1)S(1)}, bf16[256,1024]{1,0:T(8,128)(2,1)S(1)}, u32[]{:S(2)}, u32[]{:S(2)}) collective-permute-start(bf16[256,1024]{1,0:T(8,128)(2,1)S(1)} %get-tuple-element.69.refs_6_.refs_2_), channel_id=1, source_target_pairs={{0,4},{12,8},{1,5},{13,9},{2,6},{14,10},{3,7},{15,11},{16,20},{28,... | collective-permute-start | bytes 1572872 | tf_op jit(solution)/shard_map/ppermute | solution.py:363
  68.5 2.7 %collective-permute-start.17 = (bf16[256,1024]{1,0:T(8,128)(2,1)}, bf16[256,1024]{1,0:T(8,128)(2,1)S(1)}, u32[]{:S(2)}, u32[]{:S(2)}) collective-permute-start(bf16[256,1024]{1,0:T(8,128)(2,1)} %collective-permute-done.9), channel_id=1, source_target_pairs={{4,8},{8,4},{5,9},{9,5},{6,10},{10,6},{7,11},{11,7},{20,24},{24,20... | collective-permute-start | bytes 1572872 | tf_op jit(solution)/shard_map/ppermute | solution.py:363
  71.2 5.7 %shard_map.87 = (bf16[42,128,128]{2,1,0:T(8,128)(2,1)S(1)}, f32[42,128,128]{2,1,0:T(8,128)S(1)}) custom-call(s32[8]{0:T(128)S(1)} %concatenate.15.place_ref, s32[84,3]{1,0:T(8,128)S(1)} %copy.11.table_ref, bf16[256,2048]{1,0:T(8,128)(2,1)} %collective-permute-done.1.refs_0_.refs_2_, bf16[256,2048]{1,0:T(8,128)(2,1)} %collective-permute-done.8.refs_1_.refs_3_, ...), custom_call_target="tpu_custom_call" | custom-call | tf_op jit(solution)/shard_map/pallas_call | solution.py:211
  76.9 6.8 %collective-permute-done.10.refs_5_.refs_1_ = bf16[256,2048]{1,0:T(8,128)(2,1)S(1)} collective-permute-done((bf16[256,2048]{1,0:T(8,128)(2,1)S(1)}, bf16[256,2048]{1,0:T(8,128)(2,1)S(1)}, u32[]{:S(2)}, u32[]{:S(2)}) %collective-permute-start.10) | collective-permute-done | bytes 1048608 | tf_op jit(solution)/shard_map/ppermute | solution.py:366
  83.7 0.6 collective-permute-done.11
  84.3 1.3 %broadcast_select_fusion.refs_0_ = bf16[256,2048]{1,0:T(8,128)(2,1)S(1)} fusion(bf16[256,2048]{1,0:T(8,128)(2,1)} %collective-permute-done.2, bf16[256,2048]{1,0:T(8,128)(2,1)S(1)} %collective-permute-done.11, pred[]{:T(512)S(6)} %or.3), kind=kLoop, calls=%fused_computation.1 | loop fusion | flops 524288 | bytes 3145729 | tf_op jit(solution)/shard_map/jit(_where)/select_n | solution.py:441
  85.6 0.7 collective-permute-start.12
  86.3 4.2 %collective-permute-start.16 = (bf16[256,1024]{1,0:T(8,128)(2,1)S(1)}, bf16[256,1024]{1,0:T(8,128)(2,1)S(1)}, u32[]{:S(2)}, u32[]{:S(2)}) collective-permute-start(bf16[256,1024]{1,0:T(8,128)(2,1)S(1)} %collective-permute-done.15.refs_10_.refs_6_), channel_id=1, source_target_pairs={{0,1},{1,0},{2,3},{3,2},{4,5},{5,4},{6,7},{7,6},{8,9},{9,8},{10,11... | collective-permute-start | bytes 1572872 | tf_op jit(solution)/shard_map/ppermute | solution.py:369
  90.6 1.5 %collective-permute-start.18 = (bf16[256,1024]{1,0:T(8,128)(2,1)S(1)}, bf16[256,1024]{1,0:T(8,128)(2,1)S(1)}, u32[]{:S(2)}, u32[]{:S(2)}) collective-permute-start(bf16[256,1024]{1,0:T(8,128)(2,1)S(1)} %collective-permute-done.17.refs_12_.refs_8_), channel_id=1, source_target_pairs={{0,1},{1,0},{2,3},{3,2},{4,5},{5,4},{6,7},{7,6},{8,9},{9,8},{10,11... | collective-permute-start | bytes 1572872 | tf_op jit(solution)/shard_map/ppermute | solution.py:369
  92.1 0.7 collective-permute-done.14.refs_9_.refs_5_
  92.8 0.8 collective-permute-done.18.refs_13_.refs_9_
  93.6 5.8 %shard_map.88 = (bf16[2,256,256]{2,1,0:T(8,128)(2,1)S(1)}, bf16[2,256,256]{2,1,0:T(8,128)(2,1)S(1)}, bf16[2,256,256]{2,1,0:T(8,128)(2,1)S(1)}) custom-call(s32[8]{0:T(128)S(1)} %concatenate.15.place_ref, bf16[256,2048]{1,0:T(8,128)(2,1)S(1)} %pad_maximum_fusion.refs_0_, bf16[256,2048]{1,0:T(8,128)(2,1)} %collective-permute-done.3.refs_1_, ...), custom_call_target="tpu_custom_call" | custom-call | tf_op jit(solution)/shard_map/pallas_call | solution.py:296
  99.4 1.3 %collective-permute-start.19 = (bf16[2,256,256]{2,1,0:T(8,128)(2,1)S(1)}, bf16[2,256,256]{2,1,0:T(8,128)(2,1)S(1)}, u32[]{:S(2)}, u32[]{:S(2)}) collective-permute-start(bf16[2,256,256]{2,1,0:T(8,128)(2,1)S(1)} %get-tuple-element.72), channel_id=1, source_target_pairs={{4,0},{8,12},{5,1},{9,13},{6,2},{10,14},{7,3},{11,15},{20,16},{24,... | collective-permute-start | bytes 786440 | tf_op jit(solution)/shard_map/ppermute | solution.py:363
  100.7 2.7 %collective-permute-start.20 = (bf16[2,256,256]{2,1,0:T(8,128)(2,1)S(1)}, bf16[2,256,256]{2,1,0:T(8,128)(2,1)S(1)}, u32[]{:S(2)}, u32[]{:S(2)}) collective-permute-start(bf16[2,256,256]{2,1,0:T(8,128)(2,1)S(1)} %get-tuple-element.73), channel_id=1, source_target_pairs={{4,8},{8,4},{5,9},{9,5},{6,10},{10,6},{7,11},{11,7},{20,24},{24,20... | collective-permute-start | bytes 786440 | tf_op jit(solution)/shard_map/ppermute | solution.py:363
  103.4 4.3 %shard_map.89 = (bf16[42,128,128]{2,1,0:T(8,128)(2,1)S(1)}, f32[42,128,128]{2,1,0:T(8,128)S(1)}) custom-call(s32[8]{0:T(128)S(1)} %concatenate.15.place_ref, s32[84,3]{1,0:T(8,128)S(1)} %copy.11.table_ref, bf16[256,2048]{1,0:T(8,128)(2,1)S(1)} %broadcast_select_fusion.1.refs_4_.refs_0_, bf16[256,2048]{1,0:T(8,128)(2,1)S(1)} %collective-permute-done.10.refs_5_.refs_1_, ...), custom_call_target="tpu_custom_call" | custom-call | tf_op jit(solution)/shard_map/pallas_call | solution.py:211
  107.8 2.3 %collective-permute-done.20 = bf16[2,256,256]{2,1,0:T(8,128)(2,1)S(1)} collective-permute-done((bf16[2,256,256]{2,1,0:T(8,128)(2,1)S(1)}, bf16[2,256,256]{2,1,0:T(8,128)(2,1)S(1)}, u32[]{:S(2)}, u32[]{:S(2)}) %collective-permute-start.20) | collective-permute-done | bytes 262176 | tf_op jit(solution)/shard_map/ppermute | solution.py:363
  110.1 1.2 collective-permute-start.25
  111.8 2.0 %shard_map.90 = bf16[2,256,256]{2,1,0:T(8,128)(2,1)S(1)} custom-call(s32[8]{0:T(128)S(1)} %concatenate.15.place_ref, bf16[256,2048]{1,0:T(8,128)(2,1)S(1)} %broadcast_select_fusion.refs_0_, bf16[256,2048]{1,0:T(8,128)(2,1)S(1)} %collective-permute-done.12.refs_1_.refs_2_, bf16[256,1024]{1,0:T(8,128)(2,1)S(1)} %get-tuple-element.69.refs_6_.refs_2_, ...), custom_call_target="tpu_custom_call" | custom-call | tf_op jit(solution)/shard_map/pallas_call | solution.py:296
  113.9 1.3 %collective-permute-start.21 = (bf16[2,256,256]{2,1,0:T(8,128)(2,1)S(1)}, bf16[2,256,256]{2,1,0:T(8,128)(2,1)S(1)}, u32[]{:S(2)}, u32[]{:S(2)}) collective-permute-start(bf16[2,256,256]{2,1,0:T(8,128)(2,1)S(1)} %collective-permute-done.20), channel_id=1, source_target_pairs={{4,0},{8,12},{5,1},{9,13},{6,2},{10,14},{7,3},{11,15},{20,16},{24,... | collective-permute-start | bytes 786440 | tf_op jit(solution)/shard_map/ppermute | solution.py:363
  115.2 2.5 %collective-permute-start.22 = (bf16[2,256,256]{2,1,0:T(8,128)(2,1)S(1)}, bf16[2,256,256]{2,1,0:T(8,128)(2,1)S(1)}, u32[]{:S(2)}, u32[]{:S(2)}) collective-permute-start(bf16[2,256,256]{2,1,0:T(8,128)(2,1)S(1)} %shard_map.90), channel_id=1, source_target_pairs={{4,8},{8,4},{5,9},{9,5},{6,10},{10,6},{7,11},{11,7},{20,24},{24,20... | collective-permute-start | bytes 786440 | tf_op jit(solution)/shard_map/ppermute | solution.py:363
  118.3 6.1 %shard_map.91 = f32[42,128,128]{2,1,0:T(8,128)} custom-call(s32[8]{0:T(128)S(1)} %concatenate.15.place_ref, s32[84,3]{1,0:T(8,128)S(1)} %copy.11.table_ref, bf16[256,2048]{1,0:T(8,128)(2,1)S(1)} %broadcast_select_fusion.refs_0_, bf16[256,2048]{1,0:T(8,128)(2,1)S(1)} %collective-permute-done.23.refs_1_, ...), custom_call_target="tpu_custom_call" | custom-call | tf_op jit(solution)/shard_map/pallas_call | solution.py:211
  124.7 1.2 collective-permute-start.27
  125.9 1.0 collective-permute-done.27.refs_5_
  126.9 1.6 %shard_map.92 = f32[512,512]{1,0:T(8,128)} custom-call(s32[8]{0:T(128)S(1)} %concatenate.15.place_ref, bf16[2,256,256]{2,1,0:T(8,128)(2,1)S(1)} %get-tuple-element.77.refs_0_, bf16[2,256,256]{2,1,0:T(8,128)(2,1)S(1)} %collective-permute-done.22.refs_1_, bf16[2,256,256]{2,1,0:T(8,128)(2,1)S(1)} %collective-permute-done.19.refs_2_, ...), custom_call_target="tpu_custom_call" | custom-call | tf_op jit(solution)/shard_map/pallas_call | solution.py:335
  (42 shorter events, 2.1 us)
Async XLA Ops:
  0.6 1.2 copy-start
  1.9 2.3 %collective-permute-start = (bf16[256,1024]{1,0:T(8,128)(2,1)S(1)}, bf16[256,1024]{1,0:T(8,128)(2,1)S(1)}, u32[]{:S(2)}, u32[]{:S(2)}) collective-permute-start(bf16[256,1024]{1,0:T(8,128)(2,1)S(1)} %constant_dynamic-slice_fusion.4), channel_id=1, source_target_pairs={{0,1},{1,0},{2,3},{3,2},{4,5},{5,4},{6,7},{7,6},{8,9},{9,8},{10,11... | collective-permute-start | bytes 1572872 | tf_op jit(solution)/shard_map/ppermute | solution.py:369
  2.7 10.7 %copy-start.5 = (s32[1,168,2]{1,2,0:T(2,128)S(1)}, s32[1,168,2]{1,2,0:T(2,128)}, u32[]{:S(2)}) copy-start(s32[1,168,2]{1,2,0:T(2,128)} %param.10) | copy-start | bytes 4036
  2.7 37.6 %copy-start.3 = (s32[4]{0:T(128)S(1)}, s32[4]{0:T(128)}, u32[]{:S(2)}) copy-start(s32[4]{0:T(128)} %constant.71.clone) | copy-start | bytes 52
  2.7 37.6 %copy-start.4 = (s32[4]{0:T(128)S(1)}, s32[4]{0:T(128)}, u32[]{:S(2)}) copy-start(s32[4]{0:T(128)} %constant.72.clone) | copy-start | bytes 52
  4.3 24.5 %collective-permute-start.1 = (bf16[256,2048]{1,0:T(8,128)(2,1)S(1)}, bf16[256,2048]{1,0:T(8,128)(2,1)}, u32[]{:S(2)}, u32[]{:S(2)}) collective-permute-start(bf16[256,2048]{1,0:T(8,128)(2,1)S(1)} %pad_maximum_fusion.refs_0_), channel_id=1, source_target_pairs={{0,4},{4,0},{8,12},{12,8},{1,5},{5,1},{9,13},{13,9},{2,6},{6,2},{1... | collective-permute-start | bytes 3145736 | tf_op jit(solution)/shard_map/ppermute | solution.py:363
  4.3 27.5 %collective-permute-start.2 = (bf16[256,2048]{1,0:T(8,128)(2,1)S(1)}, bf16[256,2048]{1,0:T(8,128)(2,1)}, u32[]{:S(2)}, u32[]{:S(2)}) collective-permute-start(bf16[256,2048]{1,0:T(8,128)(2,1)S(1)} %pad_maximum_fusion.refs_0_), channel_id=1, source_target_pairs={{4,8},{8,4},{5,9},{9,5},{6,10},{10,6},{7,11},{11,7},{20,24},{24,20... | collective-permute-start | bytes 3145736 | tf_op jit(solution)/shard_map/ppermute | solution.py:363
  8.8 23.9 %collective-permute-start.3 = (bf16[256,2048]{1,0:T(8,128)(2,1)S(1)}, bf16[256,2048]{1,0:T(8,128)(2,1)}, u32[]{:S(2)}, u32[]{:S(2)}) collective-permute-start(bf16[256,2048]{1,0:T(8,128)(2,1)S(1)} %pad_maximum_fusion.refs_0_), channel_id=1, source_target_pairs={{0,2},{2,0},{1,3},{3,1},{4,6},{6,4},{5,7},{7,5},{8,10},{10,8},{9,1... | collective-permute-start | bytes 3145736 | tf_op jit(solution)/shard_map/ppermute | solution.py:366
  12.2 2.9 %collective-permute-start.5 = (bf16[256,1024]{1,0:T(8,128)(2,1)S(1)}, bf16[256,1024]{1,0:T(8,128)(2,1)S(1)}, u32[]{:S(2)}, u32[]{:S(2)}) collective-permute-start(bf16[256,1024]{1,0:T(8,128)(2,1)S(1)} %get-tuple-element.69.refs_6_.refs_2_), channel_id=1, source_target_pairs={{0,1},{1,0},{2,3},{3,2},{4,5},{5,4},{6,7},{7,6},{8,9},{9,8},{10,11... | collective-permute-start | bytes 1572872 | tf_op jit(solution)/shard_map/ppermute | solution.py:369
  13.5 1.5 %collective-permute-start.4 = (s32[42,2]{0,1:T(2,128)S(1)}, s32[42,2]{0,1:T(2,128)S(1)}, u32[]{:S(2)}, u32[]{:S(2)}) collective-permute-start(s32[42,2]{0,1:T(2,128)S(1)} %fusion.1), channel_id=1, source_target_pairs={{0,1},{1,0},{2,3},{3,2},{4,5},{5,4},{6,7},{7,6},{8,9},{9,8},{10,11... | collective-permute-start | bytes 1016 | tf_op jit(solution)/shard_map/ppermute | solution.py:369
  32.7 22.5 %collective-permute-start.6 = (bf16[256,2048]{1,0:T(8,128)(2,1)}, bf16[256,2048]{1,0:T(8,128)(2,1)}, u32[]{:S(2)}, u32[]{:S(2)}) collective-permute-start(bf16[256,2048]{1,0:T(8,128)(2,1)} %collective-permute-done.2), channel_id=1, source_target_pairs={{4,0},{8,12},{5,1},{9,13},{6,2},{10,14},{7,3},{11,15},{20,16},{24,... | collective-permute-start | bytes 3145736 | tf_op jit(solution)/shard_map/ppermute | solution.py:363
  35.0 25.0 %collective-permute-start.7 = (bf16[256,2048]{1,0:T(8,128)(2,1)}, bf16[256,2048]{1,0:T(8,128)(2,1)}, u32[]{:S(2)}, u32[]{:S(2)}) collective-permute-start(bf16[256,2048]{1,0:T(8,128)(2,1)} %collective-permute-done.1.refs_0_.refs_2_), channel_id=1, source_target_pairs={{4,8},{8,4},{5,9},{9,5},{6,10},{10,6},{7,11},{11,7},{20,24},{24,20... | collective-permute-start | bytes 3145736 | tf_op jit(solution)/shard_map/ppermute | solution.py:363
  37.7 22.9 %collective-permute-start.8 = (bf16[256,2048]{1,0:T(8,128)(2,1)}, bf16[256,2048]{1,0:T(8,128)(2,1)}, u32[]{:S(2)}, u32[]{:S(2)}) collective-permute-start(bf16[256,2048]{1,0:T(8,128)(2,1)} %collective-permute-done.1.refs_0_.refs_2_), channel_id=1, source_target_pairs={{0,2},{2,0},{1,3},{3,1},{4,6},{6,4},{5,7},{7,5},{8,10},{10,8},{9,1... | collective-permute-start | bytes 3145736 | tf_op jit(solution)/shard_map/ppermute | solution.py:366
  39.0 13.3 %collective-permute-start.9 = (bf16[256,1024]{1,0:T(8,128)(2,1)}, bf16[256,1024]{1,0:T(8,128)(2,1)}, u32[]{:S(2)}, u32[]{:S(2)}) collective-permute-start(bf16[256,1024]{1,0:T(8,128)(2,1)} %get-tuple-element.49), channel_id=1, source_target_pairs={{0,4},{12,8},{1,5},{13,9},{2,6},{14,10},{3,7},{15,11},{16,20},{28,... | collective-permute-start | bytes 1572872 | tf_op jit(solution)/shard_map/ppermute | solution.py:363
  45.6 19.0 %copy-start.2 = (bf16[256,1024]{1,0:T(8,128)(2,1)S(1)}, bf16[256,1024]{1,0:T(8,128)(2,1)}, u32[]{:S(2)}) copy-start(bf16[256,1024]{1,0:T(8,128)(2,1)} %get-tuple-element.49) | copy-start | bytes 1572868
  62.0 21.7 %collective-permute-start.10 = (bf16[256,2048]{1,0:T(8,128)(2,1)S(1)}, bf16[256,2048]{1,0:T(8,128)(2,1)S(1)}, u32[]{:S(2)}, u32[]{:S(2)}) collective-permute-start(bf16[256,2048]{1,0:T(8,128)(2,1)S(1)} %broadcast_select_fusion.1.refs_4_.refs_0_), channel_id=1, source_target_pairs={{0,2},{2,0},{1,3},{3,1},{4,6},{6,4},{5,7},{7,5},{8,10},{10,8},{9,1... | collective-permute-start | bytes 3145736 | tf_op jit(solution)/shard_map/ppermute | solution.py:366
  63.3 21.0 %collective-permute-start.11 = (bf16[256,2048]{1,0:T(8,128)(2,1)}, bf16[256,2048]{1,0:T(8,128)(2,1)S(1)}, u32[]{:S(2)}, u32[]{:S(2)}) collective-permute-start(bf16[256,2048]{1,0:T(8,128)(2,1)} %collective-permute-done.7), channel_id=1, source_target_pairs={{4,0},{8,12},{5,1},{9,13},{6,2},{10,14},{7,3},{11,15},{20,16},{24,... | collective-permute-start | bytes 3145736 | tf_op jit(solution)/shard_map/ppermute | solution.py:363
  64.6 21.7 %collective-permute-start.15 = (bf16[256,1024]{1,0:T(8,128)(2,1)S(1)}, bf16[256,1024]{1,0:T(8,128)(2,1)S(1)}, u32[]{:S(2)}, u32[]{:S(2)}) collective-permute-start(bf16[256,1024]{1,0:T(8,128)(2,1)S(1)} %copy-done.2), channel_id=1, source_target_pairs={{4,8},{8,4},{5,9},{9,5},{6,10},{10,6},{7,11},{11,7},{20,24},{24,20... | collective-permute-start | bytes 1572872 | tf_op jit(solution)/shard_map/ppermute | solution.py:363
  67.2 23.3 %collective-permute-start.13 = (bf16[256,1024]{1,0:T(8,128)(2,1)S(1)}, bf16[256,1024]{1,0:T(8,128)(2,1)S(1)}, u32[]{:S(2)}, u32[]{:S(2)}) collective-permute-start(bf16[256,1024]{1,0:T(8,128)(2,1)S(1)} %get-tuple-element.69.refs_6_.refs_2_), channel_id=1, source_target_pairs={{0,4},{12,8},{1,5},{13,9},{2,6},{14,10},{3,7},{15,11},{16,20},{28,... | collective-permute-start | bytes 1572872 | tf_op jit(solution)/shard_map/ppermute | solution.py:363
  68.5 22.1 %collective-permute-start.17 = (bf16[256,1024]{1,0:T(8,128)(2,1)}, bf16[256,1024]{1,0:T(8,128)(2,1)S(1)}, u32[]{:S(2)}, u32[]{:S(2)}) collective-permute-start(bf16[256,1024]{1,0:T(8,128)(2,1)} %collective-permute-done.9), channel_id=1, source_target_pairs={{4,8},{8,4},{5,9},{9,5},{6,10},{10,6},{7,11},{11,7},{20,24},{24,20... | collective-permute-start | bytes 1572872 | tf_op jit(solution)/shard_map/ppermute | solution.py:363
  85.6 24.5 %collective-permute-start.12 = (bf16[256,2048]{1,0:T(8,128)(2,1)S(1)}, bf16[256,2048]{1,0:T(8,128)(2,1)S(1)}, u32[]{:S(2)}, u32[]{:S(2)}) collective-permute-start(bf16[256,2048]{1,0:T(8,128)(2,1)S(1)} %broadcast_select_fusion.refs_0_), channel_id=1, source_target_pairs={{0,2},{2,0},{1,3},{3,1},{4,6},{6,4},{5,7},{7,5},{8,10},{10,8},{9,1... | collective-permute-start | bytes 3145736 | tf_op jit(solution)/shard_map/ppermute | solution.py:366
  86.3 5.8 %collective-permute-start.16 = (bf16[256,1024]{1,0:T(8,128)(2,1)S(1)}, bf16[256,1024]{1,0:T(8,128)(2,1)S(1)}, u32[]{:S(2)}, u32[]{:S(2)}) collective-permute-start(bf16[256,1024]{1,0:T(8,128)(2,1)S(1)} %collective-permute-done.15.refs_10_.refs_6_), channel_id=1, source_target_pairs={{0,1},{1,0},{2,3},{3,2},{4,5},{5,4},{6,7},{7,6},{8,9},{9,8},{10,11... | collective-permute-start | bytes 1572872 | tf_op jit(solution)/shard_map/ppermute | solution.py:369
  90.5 2.3 %collective-permute-start.14 = (bf16[256,1024]{1,0:T(8,128)(2,1)S(1)}, bf16[256,1024]{1,0:T(8,128)(2,1)S(1)}, u32[]{:S(2)}, u32[]{:S(2)}) collective-permute-start(bf16[256,1024]{1,0:T(8,128)(2,1)S(1)} %collective-permute-done.13.refs_8_.refs_4_), channel_id=1, source_target_pairs={{0,1},{1,0},{2,3},{3,2},{4,5},{5,4},{6,7},{7,6},{8,9},{9,8},{10,11... | collective-permute-start | bytes 1572872 | tf_op jit(solution)/shard_map/ppermute | solution.py:369
  90.6 3.0 %collective-permute-start.18 = (bf16[256,1024]{1,0:T(8,128)(2,1)S(1)}, bf16[256,1024]{1,0:T(8,128)(2,1)S(1)}, u32[]{:S(2)}, u32[]{:S(2)}) collective-permute-start(bf16[256,1024]{1,0:T(8,128)(2,1)S(1)} %collective-permute-done.17.refs_12_.refs_8_), channel_id=1, source_target_pairs={{0,1},{1,0},{2,3},{3,2},{4,5},{5,4},{6,7},{7,6},{8,9},{9,8},{10,11... | collective-permute-start | bytes 1572872 | tf_op jit(solution)/shard_map/ppermute | solution.py:369
  99.4 8.4 %collective-permute-start.19 = (bf16[2,256,256]{2,1,0:T(8,128)(2,1)S(1)}, bf16[2,256,256]{2,1,0:T(8,128)(2,1)S(1)}, u32[]{:S(2)}, u32[]{:S(2)}) collective-permute-start(bf16[2,256,256]{2,1,0:T(8,128)(2,1)S(1)} %get-tuple-element.72), channel_id=1, source_target_pairs={{4,0},{8,12},{5,1},{9,13},{6,2},{10,14},{7,3},{11,15},{20,16},{24,... | collective-permute-start | bytes 786440 | tf_op jit(solution)/shard_map/ppermute | solution.py:363
  100.7 9.4 %collective-permute-start.20 = (bf16[2,256,256]{2,1,0:T(8,128)(2,1)S(1)}, bf16[2,256,256]{2,1,0:T(8,128)(2,1)S(1)}, u32[]{:S(2)}, u32[]{:S(2)}) collective-permute-start(bf16[2,256,256]{2,1,0:T(8,128)(2,1)S(1)} %get-tuple-element.73), channel_id=1, source_target_pairs={{4,8},{8,4},{5,9},{9,5},{6,10},{10,6},{7,11},{11,7},{20,24},{24,20... | collective-permute-start | bytes 786440 | tf_op jit(solution)/shard_map/ppermute | solution.py:363
  110.1 8.2 %collective-permute-start.25 = (bf16[42,128,128]{2,1,0:T(8,128)(2,1)S(1)}, bf16[42,128,128]{2,1,0:T(8,128)(2,1)S(1)}, u32[]{:S(2)}, u32[]{:S(2)}) collective-permute-start(bf16[42,128,128]{2,1,0:T(8,128)(2,1)S(1)} %get-tuple-element.84), channel_id=1, source_target_pairs={{0,1},{1,0},{2,3},{3,2},{4,5},{5,4},{6,7},{7,6},{8,9},{9,8},{10,11... | collective-permute-start | bytes 4128776 | tf_op jit(solution)/shard_map/ppermute | solution.py:369
  111.3 6.4 %collective-permute-start.23 = (bf16[256,2048]{1,0:T(8,128)(2,1)S(1)}, bf16[256,2048]{1,0:T(8,128)(2,1)S(1)}, u32[]{:S(2)}, u32[]{:S(2)}) collective-permute-start(bf16[256,2048]{1,0:T(8,128)(2,1)S(1)} %broadcast_select_fusion.refs_0_), channel_id=1, source_target_pairs={{0,1},{1,0},{2,3},{3,2},{4,5},{5,4},{6,7},{7,6},{8,9},{9,8},{10,11... | collective-permute-start | bytes 3145736 | tf_op jit(solution)/shard_map/ppermute | solution.py:369
  111.3 7.0 %collective-permute-start.24 = (bf16[256,2048]{1,0:T(8,128)(2,1)S(1)}, bf16[256,2048]{1,0:T(8,128)(2,1)S(1)}, u32[]{:S(2)}, u32[]{:S(2)}) collective-permute-start(bf16[256,2048]{1,0:T(8,128)(2,1)S(1)} %collective-permute-done.12.refs_1_.refs_2_), channel_id=1, source_target_pairs={{0,1},{1,0},{2,3},{3,2},{4,5},{5,4},{6,7},{7,6},{8,9},{9,8},{10,11... | collective-permute-start | bytes 3145736 | tf_op jit(solution)/shard_map/ppermute | solution.py:369
  113.8 13.0 %copy-start.1 = (f32[512]{0:T(512)S(1)}, f32[512]{0:T(512)}, u32[]{:S(2)}) copy-start(f32[512]{0:T(512)} %param.9) | copy-start | bytes 6148
  113.9 10.6 %collective-permute-start.21 = (bf16[2,256,256]{2,1,0:T(8,128)(2,1)S(1)}, bf16[2,256,256]{2,1,0:T(8,128)(2,1)S(1)}, u32[]{:S(2)}, u32[]{:S(2)}) collective-permute-start(bf16[2,256,256]{2,1,0:T(8,128)(2,1)S(1)} %collective-permute-done.20), channel_id=1, source_target_pairs={{4,0},{8,12},{5,1},{9,13},{6,2},{10,14},{7,3},{11,15},{20,16},{24,... | collective-permute-start | bytes 786440 | tf_op jit(solution)/shard_map/ppermute | solution.py:363
  115.2 9.5 %collective-permute-start.22 = (bf16[2,256,256]{2,1,0:T(8,128)(2,1)S(1)}, bf16[2,256,256]{2,1,0:T(8,128)(2,1)S(1)}, u32[]{:S(2)}, u32[]{:S(2)}) collective-permute-start(bf16[2,256,256]{2,1,0:T(8,128)(2,1)S(1)} %shard_map.90), channel_id=1, source_target_pairs={{4,8},{8,4},{5,9},{9,5},{6,10},{10,6},{7,11},{11,7},{20,24},{24,20... | collective-permute-start | bytes 786440 | tf_op jit(solution)/shard_map/ppermute | solution.py:363
  117.7 8.1 %collective-permute-start.26 = (bf16[256,256]{1,0:T(8,128)(2,1)S(1)}, bf16[256,256]{1,0:T(8,128)(2,1)S(1)}, u32[]{:S(2)}, u32[]{:S(2)}) collective-permute-start(bf16[256,256]{1,0:T(8,128)(2,1)S(1)} %fusion), channel_id=1, source_target_pairs={{0,1},{1,0},{2,3},{3,2},{4,5},{5,4},{6,7},{7,6},{8,9},{9,8},{10,11... | collective-permute-start | bytes 393224 | tf_op jit(solution)/shard_map/ppermute | solution.py:369
  124.7 2.2 %collective-permute-start.27 = (bf16[256,256]{1,0:T(8,128)(2,1)S(1)}, bf16[256,256]{1,0:T(8,128)(2,1)S(1)}, u32[]{:S(2)}, u32[]{:S(2)}) collective-permute-start(bf16[256,256]{1,0:T(8,128)(2,1)S(1)} %select_bitcast_fusion), channel_id=1, source_target_pairs={{0,1},{1,0},{2,3},{3,2},{4,5},{5,4},{6,7},{7,6},{8,9},{9,8},{10,11... | collective-permute-start | bytes 393224 | tf_op jit(solution)/shard_map/ppermute | solution.py:369
